TPU v7x, 32 devices: a whole 2x2x4 slice. The times are simulated.
32 devices in a mesh: dp: 8 (over y, x, core), mp: 4 (over z).
Axes of the slice: x: 2, y: 2, z: 4, core: 2. Of those that a mesh axis runs over, the one named last changes fastest.
Arguments:
- hidden_in: bfloat16 [32768, 768], P(('dp', 'mp')), may hold values from -6 to 6
- cotangent: bfloat16 [32768, 768], P(('dp', 'mp')), may hold values from -6 to 6
- query_lengths: int32 [32, 32], P(('dp', 'mp')), may hold values from 1 to 128, 1024 in all within a row
- passage_index: int32 [1024, 32], P(('dp', 'mp')), may hold values from 0 to 1023
- passages: bfloat16 [1024, 768], replicated, may hold values from -1.1953125 to 1.1953125
- w_query: bfloat16 [768, 768], P(None, 'mp'), may hold values from -0.21875 to 0.21875
- w_key: bfloat16 [768, 768], P(None, 'mp'), may hold values from -0.21875 to 0.21875
- w_value: bfloat16 [768, 768], P(None, 'mp'), may hold values from -0.21875 to 0.21875
- w_output: bfloat16 [768, 768], P('mp'), may hold values from -0.875 to 0.875
- w_up: bfloat16 [768, 3072], P(None, 'mp'), may hold values from -0.21875 to 0.21875
- w_down: bfloat16 [3072, 768], P('mp'), may hold values from -0.109375 to 0.109375
- b_query: bfloat16 [768], P('mp'), may hold values from -1.5 to 1.5
- b_value: bfloat16 [768], P('mp'), may hold values from -1.5 to 1.5
- b_output: bfloat16 [768], replicated, may hold values from -1.5 to 1.5
- b_up: bfloat16 [3072], P('mp'), may hold values from -1.5 to 1.5
- b_down: bfloat16 [768], replicated, may hold values from -1.5 to 1.5
- first_gain: bfloat16 [768], replicated, may hold values from 0.099609375 to 1.8984375
- first_shift: bfloat16 [768], replicated, may hold values from -1.5 to 1.5
- second_gain: bfloat16 [768], replicated, may hold values from 0.099609375 to 1.8984375
- second_shift: bfloat16 [768], replicated, may hold values from -1.5 to 1.5
Outputs:
- output: bfloat16 [32768, 768], P(('dp', 'mp'))
- scores: float32 [1024, 32], P(('dp', 'mp'))
- input_grad: float32 [32768, 768], P(('dp', 'mp'))
- w_query_grad: float32 [768, 768], P(None, 'mp')
- w_key_grad: float32 [768, 768], P(None, 'mp')
- w_value_grad: float32 [768, 768], P(None, 'mp')
- w_output_grad: float32 [768, 768], P('mp')
- w_up_grad: float32 [768, 3072], P(None, 'mp')
- w_down_grad: float32 [3072, 768], P('mp')
- b_query_grad: float32 [768], P('mp')
- b_value_grad: float32 [768], P('mp')
- b_output_grad: float32 [768], replicated
- b_up_grad: float32 [3072], P('mp')
- b_down_grad: float32 [768], replicated
- first_gain_grad: float32 [768], replicated
- first_shift_grad: float32 [768], replicated
- second_gain_grad: float32 [768], replicated
- second_shift_grad: float32 [768], replicated
Inputs may be any that keep to these rules, and one draw needn't show every extreme that they name: `query_lengths`: the 32 lengths of each row sum to 1024, and the longest query of every row has exactly 128 tokens.
All inputs are finite; a program needn't handle non-finite values.
Results may differ from a plain program's by a relative error of at most 0.015.
Values may be sent and summed in bfloat16 or wider, within the bound.
No kernel may reach another device: no remote copies, remote signals or barrier semaphores. Data moves between devices by JAX's collectives and lax.ppermute only.
A program may use at most 192 MiB of HBM per device.

v0:
```python
import jax
import jax.numpy as jnp
from jax import lax
from jax.sharding import PartitionSpec as P

HEAD_DIM = 64
ROW_LEN = 1024


SCALE = 0.125
EPSILON = 1e-12
CONTRACT_ROWS = (((0,), (0,)), ((), ()))
CONTRACT_COLS = (((1,), (1,)), ((), ()))


def segment_ids(lengths, width):
    ends = jnp.cumsum(lengths, axis=-1, dtype=jnp.int32)
    places = lax.broadcasted_iota(jnp.int32, (lengths.shape[0], width, lengths.shape[1]), 1)
    return jnp.sum((places >= ends[:, None, :]).astype(jnp.int32), axis=-1)


def normalize(totals, gain, shift):
    mean_val = jnp.mean(totals, axis=-1, keepdims=True)
    centred = totals - mean_val
    inv_std = lax.rsqrt(jnp.mean(centred * centred, axis=-1, keepdims=True) + EPSILON)
    unit_val = centred * inv_std
    return (unit_val * gain + shift, unit_val, inv_std)


def norm_back(grad_out, unit_val, inv_std, gain):
    scaled = grad_out * gain
    inner = (
        scaled
        - jnp.mean(scaled, axis=-1, keepdims=True)
        - unit_val * jnp.mean(scaled * unit_val, axis=-1, keepdims=True)
    )
    return (inv_std * inner, jnp.sum(grad_out * unit_val, axis=0), jnp.sum(grad_out, axis=0))


def gelu_slope(values):
    return (
        0.5 * (1.0 + lax.erf(values * 0.7071067811865476))
        + values * jnp.exp(-0.5 * values * values) * 0.3989422804014327
    )


def split_heads(block):
    return block.reshape(block.shape[0], block.shape[1] // HEAD_DIM, HEAD_DIM)


def score_block(query_heads, key_heads, seg_row):
    logits = (
        jnp.einsum("ihd,jhd->hij", query_heads, key_heads, preferred_element_type=jnp.float32)
        * SCALE
    )
    allowed = (seg_row[:, None] == seg_row[None, :])[None]
    return jnp.where(allowed, logits, -1e30)


def attend_row(packed):
    query_row, key_row, value_row, seg_row = packed
    logits = score_block(split_heads(query_row), split_heads(key_row), seg_row)
    peak = jnp.max(logits, axis=-1, keepdims=True)
    raised = jnp.exp(logits - peak)
    sums_row = jnp.sum(raised, axis=-1, keepdims=True)
    weights = (raised / sums_row).astype(jnp.bfloat16)
    context = jnp.einsum(
        "hij,jhd->ihd", weights, split_heads(value_row), preferred_element_type=jnp.float32
    )
    return (
        context.reshape(query_row.shape).astype(jnp.bfloat16),
        (peak + jnp.log(sums_row))[..., 0],
    )


def attend_back(packed):
    query_row, key_row, value_row, seg_row, log_total, context_grad = packed
    query_heads = split_heads(query_row)
    key_heads = split_heads(key_row)
    value_heads = split_heads(value_row)
    grad_heads = split_heads(context_grad)
    logits = score_block(query_heads, key_heads, seg_row)
    probs = jnp.exp(logits - log_total[..., None])
    weight_grad = jnp.einsum(
        "ihd,jhd->hij", grad_heads, value_heads, preferred_element_type=jnp.float32
    )
    logit_grad = (
        probs * (weight_grad - jnp.sum(weight_grad * probs, axis=-1, keepdims=True))
    ).astype(jnp.bfloat16)
    query_grad = (
        jnp.einsum("hij,jhd->ihd", logit_grad, key_heads, preferred_element_type=jnp.float32)
        * SCALE
    ).astype(jnp.bfloat16)
    key_grad = (
        jnp.einsum("hij,ihd->jhd", logit_grad, query_heads, preferred_element_type=jnp.float32)
        * SCALE
    ).astype(jnp.bfloat16)
    value_grad = jnp.einsum(
        "hij,ihd->jhd", probs.astype(jnp.bfloat16), grad_heads, preferred_element_type=jnp.float32
    ).astype(jnp.bfloat16)
    return (
        query_grad.reshape(query_row.shape),
        key_grad.reshape(query_row.shape),
        value_grad.reshape(query_row.shape),
    )


def per_device(
    hidden_in,
    cotangent,
    query_lengths,
    passage_index,
    passages,
    w_query,
    w_key,
    w_value,
    w_output,
    w_up,
    w_down,
    b_query,
    b_value,
    b_output,
    b_up,
    b_down,
    first_gain,
    first_shift,
    second_gain,
    second_shift,
):
    group_in, group_len = (
        lax.all_gather(hidden_in, "mp", axis=0, tiled=True),
        lax.all_gather(query_lengths, "mp", axis=0, tiled=True),
    )
    query_weight, key_weight, value_weight, out_weight = (w_query, w_key, w_value, w_output)
    up_weight, down_weight, query_bias, value_bias, up_bias = (w_up, w_down, b_query, b_value, b_up)
    group_tokens = group_in.shape[0]
    group_count = group_len.shape[0]
    group_seg = segment_ids(group_len, ROW_LEN)
    query_all = (
        jnp.dot(group_in, query_weight, preferred_element_type=jnp.float32) + query_bias
    ).astype(jnp.bfloat16)
    key_all = jnp.dot(group_in, key_weight, preferred_element_type=jnp.float32).astype(jnp.bfloat16)
    value_all = (
        jnp.dot(group_in, value_weight, preferred_element_type=jnp.float32) + value_bias
    ).astype(jnp.bfloat16)
    local_cols = query_all.shape[1]
    row_shape = (group_count, ROW_LEN, local_cols)
    query_rows = query_all.reshape(row_shape)
    key_rows = key_all.reshape(row_shape)
    value_rows = value_all.reshape(row_shape)
    context_rows, log_totals = lax.map(attend_row, (query_rows, key_rows, value_rows, group_seg))
    context_flat = context_rows.reshape(group_tokens, local_cols)
    attended = lax.psum_scatter(
        jnp.dot(context_flat, out_weight, preferred_element_type=jnp.float32),
        "mp",
        scatter_dimension=0,
        tiled=True,
    )
    first_norm, first_unit, first_inv = normalize(
        hidden_in.astype(jnp.float32) + attended + b_output, first_gain, first_shift
    )
    normed_group = lax.all_gather(first_norm.astype(jnp.bfloat16), "mp", axis=0, tiled=True)
    up_pre = jnp.dot(normed_group, up_weight, preferred_element_type=jnp.float32) + up_bias
    hidden_act = jax.nn.gelu(up_pre, approximate=False).astype(jnp.bfloat16)
    down_part = lax.psum_scatter(
        jnp.dot(hidden_act, down_weight, preferred_element_type=jnp.float32),
        "mp",
        scatter_dimension=0,
        tiled=True,
    )
    layer_out, second_unit, second_inv = normalize(
        first_norm + down_part + b_down, second_gain, second_shift
    )
    output = layer_out.astype(jnp.bfloat16)
    local_seg = segment_ids(query_lengths, ROW_LEN)
    row_local = query_lengths.shape[0]
    labels = lax.broadcasted_iota(jnp.int32, (1, query_lengths.shape[1], 1), 1)
    onehot = (local_seg[:, None, :] == labels).astype(jnp.float32)
    seg_sums = jnp.einsum(
        "rql,rld->rqd",
        onehot,
        layer_out.reshape(row_local, ROW_LEN, layer_out.shape[1]),
        precision=lax.Precision.HIGHEST,
    )
    means = (seg_sums / query_lengths[..., None].astype(jnp.float32)).reshape(
        -1, layer_out.shape[1]
    )
    picked = passages[passage_index].astype(jnp.float32)
    scores = jnp.einsum("qd,qpd->qp", means, picked, precision=lax.Precision.HIGHEST)
    second_grad, second_gain_grad, second_shift_grad = norm_back(
        cotangent.astype(jnp.float32), second_unit, second_inv, second_gain
    )
    down_local = second_grad.astype(jnp.bfloat16)
    b_down_grad = jnp.sum(down_local.astype(jnp.float32), axis=0)
    down_group = lax.all_gather(down_local, "mp", axis=0, tiled=True)
    w_down_grad = lax.dot_general(
        hidden_act, down_group, CONTRACT_ROWS, preferred_element_type=jnp.float32
    )
    act_grad = lax.dot_general(
        down_group, down_weight, CONTRACT_COLS, preferred_element_type=jnp.float32
    )
    up_grad = (act_grad * gelu_slope(up_pre)).astype(jnp.bfloat16)
    b_up_grad = jnp.sum(up_grad.astype(jnp.float32), axis=0)
    w_up_grad = lax.dot_general(
        normed_group, up_grad, CONTRACT_ROWS, preferred_element_type=jnp.float32
    )
    normed_grad = (
        lax.psum_scatter(
            lax.dot_general(up_grad, up_weight, CONTRACT_COLS, preferred_element_type=jnp.float32),
            "mp",
            scatter_dimension=0,
            tiled=True,
        )
        + second_grad
    )
    first_grad, first_gain_grad, first_shift_grad = norm_back(
        normed_grad, first_unit, first_inv, first_gain
    )
    attended_local = first_grad.astype(jnp.bfloat16)
    b_output_grad = jnp.sum(attended_local.astype(jnp.float32), axis=0)
    attended_group = lax.all_gather(attended_local, "mp", axis=0, tiled=True)
    w_output_grad = lax.dot_general(
        context_flat, attended_group, CONTRACT_ROWS, preferred_element_type=jnp.float32
    )
    context_grad = lax.dot_general(
        attended_group, out_weight, CONTRACT_COLS, preferred_element_type=jnp.float32
    ).astype(jnp.bfloat16)
    query_grads, key_grads, value_grads = lax.map(
        attend_back,
        (query_rows, key_rows, value_rows, group_seg, log_totals, context_grad.reshape(row_shape)),
    )
    query_grad = query_grads.reshape(group_tokens, local_cols)
    key_grad = key_grads.reshape(group_tokens, local_cols)
    value_grad = value_grads.reshape(group_tokens, local_cols)
    b_query_grad = jnp.sum(query_grad.astype(jnp.float32), axis=0)
    b_value_grad = jnp.sum(value_grad.astype(jnp.float32), axis=0)
    w_query_grad = lax.dot_general(
        group_in, query_grad, CONTRACT_ROWS, preferred_element_type=jnp.float32
    )
    w_key_grad = lax.dot_general(
        group_in, key_grad, CONTRACT_ROWS, preferred_element_type=jnp.float32
    )
    w_value_grad = lax.dot_general(
        group_in, value_grad, CONTRACT_ROWS, preferred_element_type=jnp.float32
    )
    total_term = lax.dot_general(
        query_grad, query_weight, CONTRACT_COLS, preferred_element_type=jnp.float32
    )
    total_term = total_term + lax.dot_general(
        key_grad, key_weight, CONTRACT_COLS, preferred_element_type=jnp.float32
    )
    input_grad = (
        lax.psum_scatter(
            (
                total_term
                + lax.dot_general(
                    value_grad, value_weight, CONTRACT_COLS, preferred_element_type=jnp.float32
                )
            ).astype(jnp.bfloat16),
            "mp",
            scatter_dimension=0,
            tiled=True,
        ).astype(jnp.float32)
        + first_grad
    )
    (
        first_gain_grad,
        first_shift_grad,
        second_gain_grad,
        second_shift_grad,
        b_output_grad,
        b_down_grad,
    ) = lax.psum(
        (
            first_gain_grad,
            first_shift_grad,
            second_gain_grad,
            second_shift_grad,
            b_output_grad,
            b_down_grad,
        ),
        ("dp", "mp"),
    )
    (
        w_query_grad,
        w_key_grad,
        w_value_grad,
        w_output_grad,
        w_up_grad,
        w_down_grad,
        b_query_grad,
        b_value_grad,
        b_up_grad,
    ) = lax.psum(
        (
            w_query_grad,
            w_key_grad,
            w_value_grad,
            w_output_grad,
            w_up_grad,
            w_down_grad,
            b_query_grad,
            b_value_grad,
            b_up_grad,
        ),
        "dp",
    )
    return (
        output,
        scores,
        input_grad,
        w_query_grad,
        w_key_grad,
        w_value_grad,
        w_output_grad,
        w_up_grad,
        w_down_grad,
        b_query_grad,
        b_value_grad,
        b_output_grad,
        b_up_grad,
        b_down_grad,
        first_gain_grad,
        first_shift_grad,
        second_gain_grad,
        second_shift_grad,
    )


def solution(mesh):
    return jax.shard_map(
        per_device,
        mesh=mesh,
        in_specs=(
            P(("dp", "mp"), None),
            P(("dp", "mp"), None),
            P(("dp", "mp"), None),
            P(("dp", "mp"), None),
            P(),
            P(None, "mp"),
            P(None, "mp"),
            P(None, "mp"),
            P("mp", None),
            P(None, "mp"),
            P("mp", None),
            P("mp"),
            P("mp"),
            P(),
            P("mp"),
            P(),
            P(),
            P(),
            P(),
            P(),
        ),
        out_specs=(
            P(("dp", "mp"), None),
            P(("dp", "mp"), None),
            P(("dp", "mp"), None),
            P(None, "mp"),
            P(None, "mp"),
            P(None, "mp"),
            P("mp", None),
            P(None, "mp"),
            P("mp", None),
            P("mp"),
            P("mp"),
            P(),
            P("mp"),
            P(),
            P(),
            P(),
            P(),
            P(),
        ),
        check_vma=False,
    )
```

profile of v0, /device:TPU:0, one launch (start us, length us, event | category | flops | bytes accessed | tf_op | source)
XLA Modules:
  0.0 1731.5 jit_solution(8861995465992946694)
XLA Ops:
  9.3 12.7 all-gather
  22.4 105.3 %all-gather.6.cloned.1.call-done = bf16[4096,768]{1,0:T(8,128)(2,1)} async-done(((bf16[1024,768]{1,0:T(8,128)(2,1)}), bf16[4096,768]{1,0:T(8,128)(2,1)}) %all-gather.6.cloned.1.call-update) | async-done | bytes 6291472 | tf_op jit(solution)/shard_map/all_gather | solution.py:131
  141.5 93.5 %while.26 = (s32[]{:T(128)}, bf16[4,1024,192]{1,2,0:T(8,128)(2,1)}, f32[4,3,1024]{2,1,0:T(4,128)}, bf16[4,1024,192]{1,2,0:T(8,128)(2,1)S(1)}, s32[4,1024]{1,0:T(...) while((s32[]{:T(128)}, bf16[4,1024,192]{1,2,0:T(8,128)(2,1)}, ...), condition=%wide.region_5.6_spmd, body=%wide.region_2.5_spmd.sunk | while | flops 844297216 | bytes 46776432 | solution.py:151
  149.5 7.3 fusion.142
  172.9 7.3 fusion.142
  196.2 7.3 fusion.142
  219.5 7.3 fusion.142
  245.5 209.6 %reduce-scatter.5.cloned.1.call-done = f32[1024,768]{1,0:T(8,128)} async-done(((f32[4096,768]{1,0:T(8,128)}), f32[1024,768]{1,0:T(8,128)}) %reduce-scatter.5.cloned.1.call-update) | async-done | bytes 3145744 | tf_op jit(solution)/shard_map/reduce_scatter | solution.py:153
  460.9 116.5 %all-gather.8.cloned.1.call-done = bf16[4096,768]{1,0:T(8,128)(2,1)} async-done(((bf16[1024,768]{1,0:T(8,128)(2,1)}), bf16[4096,768]{1,0:T(8,128)(2,1)}) %all-gather.8.cloned.1.call-update) | async-done | bytes 6291472 | tf_op jit(solution)/shard_map/all_gather | solution.py:162
  577.4 34.2 %fusion.19 = (bf16[4096,768]{1,0:T(8,128)(2,1)S(1)}, f32[4096,768]{1,0:T(8,128)}) fusion(f32[768]{0:T(1024)S(1)} %convert_element_type.169, bf16[4096,768]{1,0:T(8,128)(2,1)} %all-gather.8.cloned.1.call-done, bf16[768,768]{1,0:T(8,128)(2,1)} %param.33), kind=kOutput, calls=%fused_computation.44 | convolution fusion | flops 5039456256 | bytes 26348544 | tf_op jit(solution)/shard_map/dot_general | solution.py:163
  614.2 8.0 fusion.62
  622.9 209.6 %reduce-scatter.7.cloned.1.call-done = f32[1024,768]{1,0:T(8,128)} async-done(((f32[4096,768]{1,0:T(8,128)}), f32[1024,768]{1,0:T(8,128)}) %reduce-scatter.7.cloned.1.call-update) | async-done | bytes 3145744 | tf_op jit(solution)/shard_map/reduce_scatter | solution.py:165
  843.9 116.5 %all-gather.10.cloned.1.call-done = bf16[4096,768]{1,0:T(8,128)(2,1)} async-done(((bf16[1024,768]{1,0:T(8,128)(2,1)}), bf16[4096,768]{1,0:T(8,128)(2,1)}) %all-gather.10.cloned.1.call-update) | async-done | bytes 6291472 | tf_op jit(solution)/shard_map/all_gather | solution.py:195
  960.5 13.1 convert_reduce_fusion
  976.2 8.2 fusion.63
  985.1 209.6 %reduce-scatter.9.cloned.1.call-done = f32[1024,768]{1,0:T(8,128)} async-done(((f32[4096,768]{1,0:T(8,128)}), f32[1024,768]{1,0:T(8,128)}) %reduce-scatter.9.cloned.1.call-update) | async-done | bytes 3145744 | tf_op jit(solution)/shard_map/reduce_scatter | solution.py:208
  1204.9 116.5 %all-gather.12.cloned.1.call-done = bf16[4096,768]{1,0:T(8,128)(2,1)} async-done(((bf16[1024,768]{1,0:T(8,128)(2,1)}), bf16[4096,768]{1,0:T(8,128)(2,1)}) %all-gather.12.cloned.1.call-update) | async-done | bytes 6291472 | tf_op jit(solution)/shard_map/all_gather | solution.py:221
  1330.6 126.0 %while.27 = (s32[]{:T(128)}, bf16[4,1024,192]{1,2,0:T(8,128)(2,1)}, bf16[4,1024,192]{1,2,0:T(8,128)(2,1)}, bf16[4,1024,192]{1,2,0:T(8,128)(2,1)S(1)}, bf16[4,102...) while((s32[]{:T(128)}, bf16[4,1024,192]{1,2,0:T(8,128)(2,1)}, ...), condition=%wide.region_21.22_spmd, body=%wide.region_19.21_spmd.sunk | while | flops 2062480384 | bytes 109674672 | solution.py:228
  1343.3 7.2 multiply_reduce_fusion.7
  1350.4 6.9 multiply_convert_fusion.2
  1374.7 7.2 multiply_reduce_fusion.7
  1381.9 6.9 multiply_convert_fusion.2
  1406.2 7.2 multiply_reduce_fusion.7
  1413.4 6.9 multiply_convert_fusion.2
  1437.6 7.2 multiply_reduce_fusion.7
  1472.5 12.8 add_convert_fusion
  1485.4 10.4 fusion.68
  1495.8 10.3 fusion.67
  1527.3 43.5 %all-reduce = (f32[768]{0:T(1024)}, f32[768]{0:T(1024)}, f32[768]{0:T(1024)}, f32[768]{0:T(1024)}, f32[768]{0:T(1024)}, /*index=5*/f32[768]{0:T(1024)}) all-reduce(f32[768]{0:T(1024)S(1)} %copy-done.40, f32[768]{0:T(1024)S(1)} %copy-done.37, f32[768]{0:T(1024)S(1)} %copy-done.38, ...), channel_id=1, replica_groups=mesh['dp'=8,'mp'=4] {'dp','mp'}, use_global_device_ids=true, to_apply=%region_34.35 | all-reduce | flops 4608 | bytes 36864 | tf_op jit(solution)/shard_map/psum | solution.py:273
  1572.8 14.3 all-reduce.1
  1587.1 8.4 reduce-scatter.11.cloned.1.call-done
  1599.8 115.4 %all-reduce.5.cloned.1.call-done = (f32[768,192]{0,1:T(8,128)}, f32[768,192]{0,1:T(8,128)}, f32[768,192]{0,1:T(8,128)}, f32[192,768]{1,0:T(8,128)}, f32[768,768]{1,0:T(8,128)}, /*index=5*/f32[768,768]{1,0:T(8,128)}) async-done(((f32[768,192]{0,1:T(8,128)}, f32[768,192]{0,1:T(8,128)}, f32[768,192]{0,1:T(8,128)}, f32[192,768]{1,0:T(8,128)}, f32[768,768]{1,0:T(8,128)}, /*index=5*/f32[768,768]{1,0:T(8,128)}), ...) | async-done | bytes 7077904 | tf_op jit(solution)/shard_map/psum | solution.py:294
  (304 shorter events, 262.7 us)
Async XLA Ops:
  7.2 1508.9 %copy-start = (bf16[1024,768]{1,0:T(8,128)(2,1)S(1)}, bf16[1024,768]{1,0:T(8,128)(2,1)}, u32[]{:S(2)}) copy-start(bf16[1024,768]{1,0:T(8,128)(2,1)} %param.28) | copy-start | bytes 4718596
  7.2 120.5 %all-gather.6.cloned.1.call-start = ((), (), s32[]{:S(2)}) async-start(), calls=%async_computation.4 | async-start | bytes 7864320 | tf_op jit(solution)/shard_map/all_gather | solution.py:131
  7.9 447.1 %reduce-scatter.5.cloned.1.call-start = ((), (), s32[]{:S(2)}) async-start(), calls=%async_computation.5 | async-start | bytes 15728640 | tf_op jit(solution)/shard_map/reduce_scatter | solution.py:153
  235.1 9.7 copy-start.4
  235.1 9.7 copy-start.28
  244.8 210.3 %copy-start.16 = (bf16[1024,768]{1,0:T(8,128)(2,1)S(1)}, bf16[1024,768]{1,0:T(8,128)(2,1)}, u32[]{:S(2)}) copy-start(bf16[1024,768]{1,0:T(8,128)(2,1)} %param.24) | copy-start | bytes 4718596
  244.8 332.6 %all-gather.8.cloned.1.call-start = ((), (), s32[]{:S(2)}) async-start(), calls=%async_computation.6 | async-start | bytes 7864320 | tf_op jit(solution)/shard_map/all_gather | solution.py:162
  460.8 371.6 %reduce-scatter.7.cloned.1.call-start = ((), (), s32[]{:S(2)}) async-start(), calls=%async_computation.7 | async-start | bytes 15728640 | tf_op jit(solution)/shard_map/reduce_scatter | solution.py:165
  460.9 153.3 %copy-start.54 = (bf16[768,768]{1,0:T(8,128)(2,1)S(1)}, bf16[768,768]{1,0:T(8,128)(2,1)}, u32[]{:S(2)}) copy-start(bf16[768,768]{1,0:T(8,128)(2,1)} %param.34) | copy-start | bytes 3538948
  622.2 338.2 %all-gather.10.cloned.1.call-start = ((), (), s32[]{:S(2)}) async-start(), calls=%async_computation.8 | async-start | bytes 7864320 | tf_op jit(solution)/shard_map/all_gather | solution.py:195
  622.9 571.7 %copy-start.31 = (f32[768]{0:T(1024)}, f32[768]{0:T(1024)S(1)}, u32[]{:S(2)}) copy-start(f32[768]{0:T(1024)S(1)} %convert_element_type.172) | copy-start | bytes 9220
  836.4 358.3 %copy-start.29 = (f32[1024]{0:T(1024)}, f32[1024]{0:T(1024)S(1)}, u32[]{:S(2)}) copy-start(f32[1024]{0:T(1024)S(1)} %broadcast_multiply_fusion.4) | copy-start | bytes 12292
  838.9 355.7 %copy-start.33 = (f32[1024]{0:T(1024)}, f32[1024]{0:T(1024)S(1)}, u32[]{:S(2)}) copy-start(f32[1024]{0:T(1024)S(1)} %add_rsqrt_fusion) | copy-start | bytes 12292
  843.9 350.7 %reduce-scatter.9.cloned.1.call-start = ((), (), s32[]{:S(2)}) async-start(), calls=%async_computation.9 | async-start | bytes 15728640 | tf_op jit(solution)/shard_map/reduce_scatter | solution.py:208
  960.5 15.7 copy-start.55
  984.4 337.0 %all-gather.12.cloned.1.call-start = ((), (), s32[]{:S(2)}) async-start(), calls=%async_computation.10 | async-start | bytes 7864320 | tf_op jit(solution)/shard_map/all_gather | solution.py:221
  985.1 216.4 %copy-start.35 = (f32[768]{0:T(1024)}, f32[768]{0:T(1024)S(1)}, u32[]{:S(2)}) copy-start(f32[768]{0:T(1024)S(1)} %convert_element_type.173) | copy-start | bytes 9220
  1194.6 6.8 copy-start.2
  1201.4 119.9 %copy-start.23 = (bf16[192,768]{1,0:T(8,128)(2,1)S(1)}, bf16[192,768]{1,0:T(8,128)(2,1)}, u32[]{:S(2)}) copy-start(bf16[192,768]{1,0:T(8,128)(2,1)} %param.32) | copy-start | bytes 884740
  1204.8 390.7 %reduce-scatter.11.cloned.1.call-start = ((), (), s32[]{:S(2)}) async-start(), calls=%async_computation.11 | async-start | bytes 7864320 | tf_op jit(solution)/shard_map/reduce_scatter | solution.py:253
  1458.3 7.8 copy-start.10
  1458.7 7.5 copy-start.12
  1458.8 13.7 copy-start.14
  1459.7 6.4 copy-start.27
  1485.4 229.9 %all-reduce.5.cloned.1.call-start = ((), (), s32[]{:S(2)}) async-start(), calls=%async_computation.12 | async-start | bytes 14155776 | tf_op jit(solution)/shard_map/psum | solution.py:294
  1485.4 20.7 %slice-start.2 = ((s8[6291456]{0:T(1024)(128)(4,1)}), s8[4194304]{0:T(1024)(128)(4,1)S(1)}, s32[]{:S(2)}) async-start(s8[6291456]{0:T(1024)(128)(4,1)} %bitcast.206), calls=%async_computation.15 | async-start | bytes 8388608
  1485.4 22.9 %slice-start = ((s8[6291456]{0:T(1024)(128)(4,1)}), s8[4194304]{0:T(1024)(128)(4,1)S(1)}, s32[]{:S(2)}) async-start(s8[6291456]{0:T(1024)(128)(4,1)} %bitcast.204), calls=%async_computation.13 | async-start | bytes 8388608
  1495.8 10.3 copy-start.9
  1495.8 10.3 slice-start.3
  1495.8 12.5 slice-start.1
  1525.3 47.5 %copy-start.44 = (f32[768]{0:T(1024)S(1)}, f32[768]{0:T(1024)}, u32[]{:S(2)}) copy-start(f32[768]{0:T(1024)} %get-tuple-element.261) | copy-start | bytes 9220
  1715.2 6.7 copy-start.18
  (42 other events, 127.9 us)
Sparse Core Ops, SparseCore 0:
  9.6 118.0 all-gather.5
  244.9 210.0 reduce-scatter.4
  460.9 116.3 all-gather.7
  622.3 210.0 reduce-scatter.6
  844.0 116.4 all-gather.9
  984.5 210.0 reduce-scatter.8
  1204.9 116.3 all-gather.11
  1485.5 110.0 reduce-scatter.10
  1600.7 114.4 all-reduce.4
where the time goes:
time: 1740 us; the launch traced here: 1730 us
  waiting for transfers between devices  1210 us (70%)
  matrix products  263 us (15%)
  other arithmetic  97 us (6%)
  local copies, waits for them, and re-layouts  77.5 us (4%)
  blocking collectives  70.5 us (4%)
    reduce_scatter x1, waiting for transfers between devices, per_device(): lax.psum_scatter(jnp.dot(context_flat, out_weight, preferred_element_type...  210 us
    reduce_scatter x1, waiting for transfers between devices, per_device(): lax.psum_scatter(lax.dot_general(up_grad, up_weight, CONTRACT_COLS, prefe...  210 us
    reduce_scatter x1, waiting for transfers between devices, per_device(): lax.psum_scatter(jnp.dot(hidden_act, down_weight, preferred_element_type=...  210 us
    all_gather x1, waiting for transfers between devices, per_device(): down_group = lax.all_gather(down_local, 'mp', axis=0, tiled=True)  117 us
    all_gather x1, waiting for transfers between devices, per_device(): attended_group = lax.all_gather(attended_local, 'mp', axis=0, tiled=True)  117 us
    all_gather x1, waiting for transfers between devices, per_device(): lax.all_gather(first_norm.astype(jnp.bfloat16), 'mp', axis=0, tiled=True)  116 us
    psum x1, waiting for transfers between devices, per_device(): lax.psum((w_query_grad, w_key_grad, w_value_grad, w_output_grad, w_up_gra...  115 us
    all_gather x1, waiting for transfers between devices, per_device(): lax.all_gather(hidden_in, 'mp', axis=0, tiled=True)  105 us
  transfers between devices with their start and end apart: 9, of which 9 were waited for; matrix products, arithmetic and copies ran while one was open for 3% of the time, Pallas kernels for 0%

commit v1 on v0

v1 whole, which is shorter than its diff:
```python
import functools

import jax
import jax.numpy as jnp
from jax import lax
from jax.experimental import pallas as pl
from jax.experimental.pallas import tpu as pltpu
from jax.sharding import PartitionSpec as P

HEAD_DIM = 64
SCALE = 0.125
EPSILON = 1e-12
MASKED = -1e30
BLOCK = 128
WINDOW = 384
GROUP = 4 * HEAD_DIM
ROW_BLOCK = 256
GRAIN = 16
MEBI = 1024 * 1024
NT = (((1,), (1,)), ((), ()))
TN = (((0,), (0,)), ((), ()))
BF = jnp.bfloat16
F32 = jnp.float32

CORE, XBIT, YBIT = 1, 2, 4


def params(mebi=48):
    return pltpu.CompilerParams(vmem_limit_bytes=mebi * MEBI)


def cost(us):
    return pl.CostEstimate(flops=int(us * 1e9), bytes_accessed=int(us * 3e6), transcendentals=0)


def shape(dims, dtype):
    return jax.ShapeDtypeStruct(dims, dtype)


def scalar_spec():
    return pl.BlockSpec(memory_space=pltpu.SMEM)


def held_spec():
    return pl.BlockSpec(memory_space=pltpu.VMEM)


def whole_spec(dims):
    return pl.BlockSpec(dims, lambda i: (0,) * len(dims), pipeline_mode=pl.Buffered(1))


def fixed_spec(dims):
    return pl.BlockSpec(dims, lambda i: (0,) * len(dims))


def rows_spec(rows, width):
    return pl.BlockSpec((rows, width), lambda i: (i, 0))


def token_spec():
    return pl.BlockSpec(memory_space=pl.ANY)


def swap(block, axis, bit, size):
    return lax.ppermute(block, axis, [(i, i ^ bit) for i in range(size)])


def after(value, *others):
    return lax.optimization_barrier((value, *others))[0]


def piece_heads_kernel(place, wq, wk, wv, wo, piece):
    core, plane = place[0], place[1]
    heads = piece.shape[1]
    for side, pair in enumerate(((wq, wk), (wv, wo))):

        @pl.when(core == side)
        def _():
            for t, ref in enumerate(pair):
                for h in range(heads):
                    start = pl.multiple_of(h * HEAD_DIM + plane * GRAIN, GRAIN)
                    piece[t, h] = ref[pl.ds(start, GRAIN), :]


def piece_heads(place, *weights):
    local, width = weights[0].shape
    heads = local // HEAD_DIM
    return pl.pallas_call(
        piece_heads_kernel,
        in_specs=[scalar_spec()] + [held_spec()] * 4,
        out_specs=held_spec(),
        out_shape=shape((2, heads, GRAIN, width), BF),
        compiler_params=params(16),
        cost_estimate=cost(1),
        name="piece_heads",
    )(place, *weights).reshape(2 * heads * GRAIN, width)


def piece_feed_kernel(place, wu, wd, turned, piece_up, piece_down):
    core, plane = place[0], place[1]
    sub = piece_up.shape[0]
    turned[...] = wu[...].astype(F32).T.astype(BF)
    start = pl.multiple_of((core * 4 + plane) * sub, GRAIN)
    piece_up[...] = turned[pl.ds(start, sub), :]
    piece_down[...] = wd[pl.ds(start, sub), :]


def piece_feed(place, wu, wd):
    width, hidden = wu.shape
    sub = hidden // 8
    return pl.pallas_call(
        piece_feed_kernel,
        in_specs=[scalar_spec()] + [held_spec()] * 2,
        out_specs=[held_spec()] * 3,
        out_shape=[shape((hidden, width), BF), shape((sub, width), BF), shape((sub, width), BF)],
        compiler_params=params(16),
        cost_estimate=cost(3),
        name="piece_feed",
    )(place, wu, wd)


def finish_feed_kernel(turn, place, *refs):
    core, plane = place[0], place[1]
    out = refs[10]
    into = refs[11] if turn else out
    sub = refs[0].shape[0]
    half = sub // 2
    for c in range(2):
        a, x, y, first, second = refs[5 * c : 5 * c + 5]
        for g, ref in enumerate((a, x, y)):
            start = pl.multiple_of(((core ^ c) * 4 + (plane ^ g)) * sub, GRAIN)
            into[pl.ds(start, sub), :] = ref[...].astype(F32)
        start = pl.multiple_of(((core ^ c) * 4 + (plane ^ 3)) * sub, GRAIN)
        into[pl.ds(start, half), :] = first[...].astype(F32)
        start = pl.multiple_of(((core ^ c) * 4 + (plane ^ 3)) * sub + half, GRAIN)
        into[pl.ds(start, half), :] = second[...].astype(F32)
    if turn:
        out[...] = into[...].T


def finish_feed(place, pieces, turn):
    sub, width = pieces[0].shape
    out = (width, 8 * sub) if turn else (8 * sub, width)
    return pl.pallas_call(
        functools.partial(finish_feed_kernel, turn),
        in_specs=[scalar_spec()] + [held_spec()] * 10,
        out_specs=held_spec(),
        out_shape=shape(out, F32),
        scratch_shapes=[pltpu.VMEM((8 * sub, width), F32)] if turn else [],
        compiler_params=params(24),
        cost_estimate=cost(3),
        name="finish_up" if turn else "finish_down",
    )(place, *pieces)


def finish_heads_kernel(place, *refs):
    core, plane = place[0], place[1]
    pieces, outs = refs[:10], refs[10:]
    heads = outs[0].shape[0] // HEAD_DIM
    half = heads * GRAIN
    for side in range(2):

        @pl.when(core == side)
        def _():
            for c in range(2):
                a, x, y, first, second = pieces[5 * c : 5 * c + 5]
                for t in range(2):
                    out = outs[2 * (side ^ c) + t]
                    for g, ref in enumerate((a, x, y, (first, second)[t])):
                        base = 0 if g == 3 else t * half
                        for h in range(heads):
                            at = pl.multiple_of(h * HEAD_DIM + (plane ^ g) * GRAIN, GRAIN)
                            rows = slice(base + h * GRAIN, base + (h + 1) * GRAIN)
                            out[pl.ds(at, GRAIN), :] = ref[rows, :].astype(F32)


def finish_heads(place, pieces):
    rows, width = pieces[0].shape
    local = rows // (2 * GRAIN) * HEAD_DIM
    return pl.pallas_call(
        finish_heads_kernel,
        in_specs=[scalar_spec()] + [held_spec()] * 10,
        out_specs=[held_spec()] * 4,
        out_shape=[shape((local, width), F32)] * 4,
        compiler_params=params(24),
        cost_estimate=cost(2),
        name="finish_heads",
    )(place, *pieces)


def plane_step(piece, n_dp):
    by_x = swap(piece, "dp", XBIT, n_dp)
    by_y = swap(piece, "dp", YBIT, n_dp)
    return by_x, by_y


def corner_step(by_x, by_y, n_dp):
    half = by_x.shape[0] // 2
    return swap(by_x[:half], "dp", YBIT, n_dp), swap(by_y[half:], "dp", XBIT, n_dp)


def core_step(pieces, n_dp):
    return [swap(p, "dp", CORE, n_dp) for p in pieces]


def shard_step(piece, n_mp):
    return jnp.concatenate([swap(piece, "mp", r, n_mp) for r in range(1, n_mp)], axis=0)


def add(*terms):
    total = terms[0].astype(F32)
    for term in terms[1:]:
        total = total + term.astype(F32)
    return total.astype(BF)


def chip_sum(keep, send, n_dp):
    got = swap(send, "dp", CORE, n_dp)
    half = keep.shape[1] // 2
    first, second = slice(0, half), slice(half, None)
    return (
        add(keep[0::2, first], got[0::2, first]),
        add(keep[1::2, first], got[1::2, first]),
        add(keep[0:2, second], got[0:2, second]),
        add(keep[2:4, second], got[2:4, second]),
    )


def plane_sum(parts, n_dp):
    keep_x, send_x, keep_y, send_y = parts
    got_x = swap(send_x, "dp", XBIT, n_dp)
    got_y = swap(send_y, "dp", YBIT, n_dp)
    return (
        add(keep_x[0], got_x[0]),
        add(keep_x[1], got_x[1]),
        add(keep_y[0], got_y[0]),
        add(keep_y[1], got_y[1]),
    )


def corner_sum(parts, n_dp):
    keep_first, send_first, keep_second, send_second = parts
    got_first = swap(send_first, "dp", YBIT, n_dp)
    got_second = swap(send_second, "dp", XBIT, n_dp)
    half = keep_first.shape[0]
    return [add(keep_first[i], got_first[i]) for i in range(half)] + [
        add(keep_second[i], got_second[i]) for i in range(half)
    ]


def shard_sum(parts, n_dp, n_mp):
    total = parts[0].astype(F32)
    for r in range(1, n_mp):
        total = total + swap(parts[r], "mp", r, n_mp).astype(F32)
    bit = 8
    while bit < n_dp:
        total = total + swap(total, "dp", bit, n_dp)
        bit *= 2
    return total.astype(BF)


def gather_sum(total, n_dp):
    by_x, by_y = plane_step(total, n_dp)
    mine = [total, by_x, by_y, *corner_step(by_x, by_y, n_dp)]
    return mine + core_step(mine, n_dp)


def project_kernel(place, x, wq, wk, wv, wo, bq, bv, *refs):
    pieces, (q, k, v, full) = refs[:10], refs[10:]
    core, plane = place[0], place[1]
    heads = wq.shape[0] // HEAD_DIM
    shards = 1 + pieces[0].shape[0] // (2 * heads * GRAIN)

    @pl.when(pl.program_id(0) == 0)
    def _():
        for kind, ref in enumerate((wq, wk, wv, wo)):
            for h in range(heads):
                for g in range(4):
                    at = pl.multiple_of(h * HEAD_DIM + (plane ^ g) * GRAIN, GRAIN)
                    to = h * HEAD_DIM + g * GRAIN
                    full[kind, to : to + GRAIN, :] = ref[pl.ds(at, GRAIN), :]
        for c in range(2):
            a, x_, y_, first, second = pieces[5 * c : 5 * c + 5]
            half = first.shape[0]
            for r in range(1, shards):
                for t in range(2):
                    for h in range(heads):
                        at = ((r - 1) * 2 + t) * heads * GRAIN + h * GRAIN
                        to = (r * heads + h) * HEAD_DIM
                        for g, ref in enumerate((a, x_, y_, first if at < half else second)):
                            row = at - half if g == 3 and at >= half else at
                            full[
                                (core ^ c) * 2 + t, to + g * GRAIN : to + (g + 1) * GRAIN, :
                            ] = ref[row : row + GRAIN, :]

    block = x[...]
    for kind, (out, bias) in enumerate(((q, bq), (k, None), (v, bv))):
        value = lax.dot_general(block, full[kind], NT, preferred_element_type=F32)
        if bias is not None:
            value = value + bias[...]
        out[...] = value.astype(BF)


def project(place, x, weights, bq, bv, pieces):
    rows, width = x.shape
    block = rows_spec(ROW_BLOCK, width)
    return pl.pallas_call(
        project_kernel,
        grid=(rows // ROW_BLOCK,),
        in_specs=[scalar_spec(), block]
        + [whole_spec(a.shape) for a in (*weights, bq, bv, *pieces)],
        out_specs=[block, block, block, fixed_spec((4, width, width))],
        out_shape=[shape((rows, width), BF)] * 3 + [shape((4, width, width), BF)],
        compiler_params=params(),
        cost_estimate=cost(7),
        name="project",
    )(place, x, *weights, bq, bv, *pieces)


def spread_heads(block):
    lane = lax.broadcasted_iota(jnp.int32, block.shape, 1) // HEAD_DIM
    return jnp.concatenate(
        [jnp.where(lane == h, block, jnp.zeros_like(block)) for h in range(4)], axis=0
    )


def gather_heads(stacked):
    rows = stacked.shape[0] // 4
    lane = lax.broadcasted_iota(jnp.int32, (rows, GROUP), 1) // HEAD_DIM
    out = stacked[:rows]
    for h in range(1, 4):
        out = jnp.where(lane == h, stacked[h * rows : (h + 1) * rows], out)
    return out


def window_start(step, rows):
    return pl.multiple_of(jnp.clip(step - 1, 0, (rows - WINDOW) // BLOCK) * BLOCK, BLOCK)


def attend_kernel(
    q, k, v, segc, segr, x, wo, bo, gain, shift, ctx, saved, unit, low
):
    start = window_start(pl.program_id(0), k.shape[0])
    near = pl.ds(start, WINDOW)
    penalty = jnp.where(segc[...] == segr[:, near], 0.0, MASKED)
    lane = lax.broadcasted_iota(jnp.int32, (BLOCK, 128), 1)
    keep = jnp.zeros((BLOCK, 128), F32)
    for group in range(q.shape[1] // GROUP):
        cols = slice(group * GROUP, (group + 1) * GROUP)
        stacked = spread_heads(q[:, cols] * SCALE)
        logits = lax.dot_general(stacked, k[near, cols], NT, preferred_element_type=F32)
        logits = logits.reshape(4, BLOCK, WINDOW) + penalty[None]
        peak = jnp.max(logits, axis=-1, keepdims=True)
        raised = jnp.exp(logits - peak)
        sums = jnp.sum(raised, axis=-1, keepdims=True)
        probs = (raised * (1.0 / sums)).astype(BF).reshape(4 * BLOCK, WINDOW)
        context = jnp.dot(probs, v[near, cols], preferred_element_type=F32)
        ctx[:, cols] = gather_heads(context).astype(BF)
        log_total = peak + jnp.log(sums)
        for h in range(4):
            keep = jnp.where(lane == group * 4 + h, log_total[h], keep)
    attended = jnp.dot(ctx[...], wo[0], preferred_element_type=F32) + bo[...]
    total = x[...].astype(F32) + attended
    centred = total - jnp.mean(total, axis=-1, keepdims=True)
    inv_std = lax.rsqrt(jnp.mean(centred * centred, axis=-1, keepdims=True) + EPSILON)
    unit_val = centred * inv_std
    unit[...] = unit_val
    low[...] = (unit_val * gain[...] + shift[...]).astype(BF)
    saved[...] = jnp.where(lane == 127, inv_std, keep)


def attend(q, k, v, segc, segr, x, full, bo, gain, shift):
    rows, width = q.shape
    block = rows_spec(BLOCK, width)
    return pl.pallas_call(
        attend_kernel,
        grid=(rows // BLOCK,),
        in_specs=[
            block,
            whole_spec((rows, width)),
            whole_spec((rows, width)),
            rows_spec(BLOCK, 1),
            whole_spec((1, rows)),
            block,
            pl.BlockSpec((1, width, width), lambda i: (3, 0, 0), pipeline_mode=pl.Buffered(1)),
            whole_spec((1, width)),
            whole_spec((1, width)),
            whole_spec((1, width)),
        ],
        out_specs=[block, rows_spec(BLOCK, 128), block, block],
        out_shape=[
            shape((rows, width), BF),
            shape((rows, 128), F32),
            shape((rows, width), F32),
            shape((rows, width), BF),
        ],
        compiler_params=params(),
        cost_estimate=cost(18),
        name="attend",
    )(q, k, v, segc, segr, x, full, bo, gain, shift)


def attend_back_kernel(q, k, v, do, saved, segc, segr, *refs):
    dq, dk, dv, sums, dk_sum, dv_sum = refs[-6:]
    step = pl.program_id(0)

    @pl.when(step == 0)
    def _():
        dk_sum[...] = jnp.zeros_like(dk_sum)
        dv_sum[...] = jnp.zeros_like(dv_sum)
        sums[...] = jnp.zeros_like(sums)

    start = window_start(step, k.shape[0])
    near = pl.ds(start, WINDOW)
    penalty = jnp.where(segc[...] == segr[:, near], 0.0, MASKED)
    for group in range(q.shape[1] // GROUP):
        cols = slice(group * GROUP, (group + 1) * GROUP)
        q4 = spread_heads(q[:, cols] * SCALE)
        do4 = spread_heads(do[:, cols])
        k4 = k[near, cols]
        logits = lax.dot_general(q4, k4, NT, preferred_element_type=F32)
        logits = logits.reshape(4, BLOCK, WINDOW) + penalty[None]
        lse = jnp.stack([saved[:, group * 4 + h : group * 4 + h + 1] for h in range(4)])
        probs = jnp.exp(logits - lse)
        weight_grad = lax.dot_general(
            do4, v[near, cols], NT, preferred_element_type=F32
        ).reshape(4, BLOCK, WINDOW)
        inner = jnp.sum(weight_grad * probs, axis=-1, keepdims=True)
        logit_grad = (probs * (weight_grad - inner)).astype(BF).reshape(4 * BLOCK, WINDOW)
        probs_low = probs.astype(BF).reshape(4 * BLOCK, WINDOW)
        dq_low = (
            gather_heads(jnp.dot(logit_grad, k4, preferred_element_type=F32)) * SCALE
        ).astype(BF)
        dq[:, cols] = dq_low
        sums[0:1, cols] += jnp.sum(dq_low.astype(F32), axis=0, keepdims=True)
        dk_sum[near, cols] += lax.dot_general(logit_grad, q4, TN, preferred_element_type=F32)
        dv_sum[near, cols] += lax.dot_general(probs_low, do4, TN, preferred_element_type=F32)

    @pl.when(step == pl.num_programs(0) - 1)
    def _():
        dk[...] = dk_sum[...].astype(BF)
        dv_low = dv_sum[...].astype(BF)
        dv[...] = dv_low
        sums[1:2, :] = jnp.sum(dv_low.astype(F32), axis=0, keepdims=True)


def attend_back(q, k, v, do, saved, segc, segr, *tokens):
    rows, width = q.shape
    block = rows_spec(BLOCK, width)
    full = whole_spec((rows, width))
    return pl.pallas_call(
        attend_back_kernel,
        grid=(rows // BLOCK,),
        in_specs=[
            block,
            full,
            full,
            block,
            rows_spec(BLOCK, 128),
            rows_spec(BLOCK, 1),
            whole_spec((1, rows)),
        ]
        + [token_spec() for _ in tokens],
        out_specs=[block, fixed_spec((rows, width)), fixed_spec((rows, width)), fixed_spec((8, width))],
        out_shape=[shape((rows, width), BF)] * 3 + [shape((8, width), F32)],
        scratch_shapes=[pltpu.VMEM((rows, width), F32)] * 2,
        compiler_params=params(),
        cost_estimate=cost(30),
        name="attend_back",
    )(q, k, v, do, saved, segc, segr, *tokens)


def feed_kernel(place, x, unit, cot, turned, own, bu, vectors, *refs):
    pieces, outs = refs[:20], refs[20:]
    act, slope, layer, output, second, down_grad, sums, wu, wd = outs
    core, plane = place[0], place[1]
    sub = own.shape[0] // 8
    shards = 1 + pieces[0].shape[0] // sub

    @pl.when(pl.program_id(0) == 0)
    def _():
        sums[...] = jnp.zeros_like(sums)
        for source, into, parts in ((turned, wu, pieces[:10]), (own, wd, pieces[10:])):
            for c in range(2):
                a, x_, y_, first, second_ = parts[5 * c : 5 * c + 5]
                for g in range(4):
                    at = pl.multiple_of(((core ^ c) * 4 + (plane ^ g)) * sub, GRAIN)
                    to = (c * 4 + g) * shards * sub
                    into[to : to + sub, :] = source[pl.ds(at, sub), :]
                    to = to + sub
                    for ref in ((a,), (x_,), (y_,), (first, second_))[g]:
                        into[to : to + ref.shape[0], :] = ref[...]
                        to = to + ref.shape[0]

    block = x[...]
    hidden = wu.shape[0]
    for at in range(0, hidden, 256):
        span = slice(at, at + 256)
        pre = (
            lax.dot_general(block, wu[span, :], NT, preferred_element_type=F32) + bu[:, span]
        )
        below = 0.5 * (1.0 + lax.erf(pre * 0.7071067811865476))
        density = jnp.exp(-0.5 * pre * pre) * 0.3989422804014327
        act[:, span] = (pre * below).astype(BF)
        slope[:, span] = (below + pre * density).astype(BF)
    down = jnp.dot(act[...], wd[...], preferred_element_type=F32)
    b_down, first_gain, first_shift, second_gain, second_shift = (
        vectors[i : i + 1, :] for i in range(5)
    )
    total = unit[...] * first_gain + first_shift + down + b_down
    centred = total - jnp.mean(total, axis=-1, keepdims=True)
    inv_std = lax.rsqrt(jnp.mean(centred * centred, axis=-1, keepdims=True) + EPSILON)
    unit_val = centred * inv_std
    layer_out = unit_val * second_gain + second_shift
    layer[...] = layer_out
    output[...] = layer_out.astype(BF)
    grad = cot[...].astype(F32)
    scaled = grad * second_gain
    inner = (
        scaled
        - jnp.mean(scaled, axis=-1, keepdims=True)
        - unit_val * jnp.mean(scaled * unit_val, axis=-1, keepdims=True)
    )
    second_grad = inv_std * inner
    second[...] = second_grad
    grad_low = second_grad.astype(BF)
    down_grad[...] = grad_low
    sums[0:1, :] += jnp.sum(grad_low.astype(F32), axis=0, keepdims=True)
    sums[1:2, :] += jnp.sum(grad * unit_val, axis=0, keepdims=True)
    sums[2:3, :] += jnp.sum(grad, axis=0, keepdims=True)


def feed(place, x, unit, cot, turned, own, bu, vectors, pieces):
    rows, width = x.shape
    hidden = bu.shape[1]
    block = rows_spec(ROW_BLOCK, width)
    wide = rows_spec(ROW_BLOCK, hidden)
    weight = fixed_spec((hidden, width))
    return pl.pallas_call(
        feed_kernel,
        grid=(rows // ROW_BLOCK,),
        in_specs=[scalar_spec(), block, block, block]
        + [whole_spec(a.shape) for a in (turned, own, bu, vectors, *pieces)],
        out_specs=[wide, wide, block, block, block, block, fixed_spec((8, width)), weight, weight],
        out_shape=[
            shape((rows, hidden), BF),
            shape((rows, hidden), BF),
            shape((rows, width), F32),
            shape((rows, width), BF),
            shape((rows, width), F32),
            shape((rows, width), BF),
            shape((8, width), F32),
            shape((hidden, width), BF),
            shape((hidden, width), BF),
        ],
        compiler_params=params(56),
        cost_estimate=cost(24),
        name="feed",
    )(place, x, unit, cot, turned, own, bu, vectors, *pieces)


def down_weight_kernel(act, grad, *refs):
    refs[-1][...] = lax.dot_general(
        act[...], grad[...], TN, preferred_element_type=F32
    ).astype(BF)


def down_weight(act, grad, side, *tokens):
    rows, hidden = act.shape
    width = grad.shape[1]
    span = hidden // 4
    return pl.pallas_call(
        down_weight_kernel,
        grid=(2,),
        in_specs=[
            pl.BlockSpec((rows, span), lambda j: (0, 2 * side + j)),
            whole_spec((rows, width)),
        ]
        + [token_spec() for _ in tokens],
        out_specs=rows_spec(span, width),
        out_shape=shape((hidden // 2, width), BF),
        compiler_params=params(),
        cost_estimate=cost(5),
        name="down_weight",
    )(act, grad, *tokens)


def feed_back_kernel(more, grad, x, wu, wd, slope, *refs):
    weight, bias, out, held = refs[-4:]
    base = refs[0]

    @pl.when(pl.program_id(0) == 0)
    def _():
        out[...] = base[...] if more else jnp.zeros_like(out)

    total = None
    for at in range(0, x.shape[0], ROW_BLOCK):
        span = slice(at, at + ROW_BLOCK)
        act_grad = lax.dot_general(grad[span, :], wd[...], NT, preferred_element_type=F32)
        low = (act_grad * slope[span, :].astype(F32)).astype(BF)
        held[span, :] = low
        term = jnp.sum(low.astype(F32), axis=0, keepdims=True)
        total = term if total is None else total + term
    bias[...] = total
    out[...] += jnp.dot(held[...], wu[...], preferred_element_type=F32)
    weight[...] = lax.dot_general(
        held[...], x[...], TN, preferred_element_type=F32
    ).astype(BF)


def feed_back(grad, x, wu, wd, slope, side, base, *tokens):
    rows, width = x.shape
    hidden = wu.shape[0]
    span = hidden // 4
    full = whole_spec((rows, width))
    weight = pl.BlockSpec((span, width), lambda j: (2 * side + j, 0))
    return pl.pallas_call(
        functools.partial(feed_back_kernel, base is not None),
        grid=(2,),
        in_specs=[full, full, weight, weight, pl.BlockSpec((rows, span), lambda j: (0, 2 * side + j))]
        + ([full] if base is not None else [])
        + [token_spec() for _ in tokens],
        out_specs=[
            rows_spec(span, width),
            pl.BlockSpec((1, span), lambda j: (0, j)),
            fixed_spec((rows, width)),
        ],
        out_shape=[
            shape((hidden // 2, width), BF),
            shape((1, hidden // 2), F32),
            shape((rows, width), F32),
        ],
        scratch_shapes=[pltpu.VMEM((rows, span), BF)],
        compiler_params=params(),
        cost_estimate=cost(11),
        name="feed_back",
    )(grad, x, wu, wd, slope, *(() if base is None else (base,)), *tokens)


def middle_kernel(normed, second, unit, saved, ctx, wo, gain, *refs):
    first, context_grad, weight, sums, held = refs[-5:]
    step = pl.program_id(0)
    grad = normed[...] + second[...]
    unit_val = unit[...]
    scaled = grad * gain[...]
    inner = (
        scaled
        - jnp.mean(scaled, axis=-1, keepdims=True)
        - unit_val * jnp.mean(scaled * unit_val, axis=-1, keepdims=True)
    )
    first_grad = saved[:, 127:128] * inner
    first[...] = first_grad
    low = first_grad.astype(BF)
    context_grad[...] = lax.dot_general(
        low, wo[0], NT, preferred_element_type=F32
    ).astype(BF)
    term = lax.dot_general(ctx[...], low, TN, preferred_element_type=F32)

    @pl.when(step == 0)
    def _():
        sums[...] = jnp.zeros_like(sums)
        held[...] = jnp.zeros_like(held)

    held[...] += term
    sums[0:1, :] += jnp.sum(low.astype(F32), axis=0, keepdims=True)
    sums[1:2, :] += jnp.sum(grad * unit_val, axis=0, keepdims=True)
    sums[2:3, :] += jnp.sum(grad, axis=0, keepdims=True)

    @pl.when(step == pl.num_programs(0) - 1)
    def _():
        weight[...] = held[...].astype(BF)


def middle(normed, second, unit, saved, ctx, full, gain, *tokens):
    rows, width = normed.shape
    block = rows_spec(ROW_BLOCK, width)
    return pl.pallas_call(
        middle_kernel,
        grid=(rows // ROW_BLOCK,),
        in_specs=[
            block,
            block,
            block,
            rows_spec(ROW_BLOCK, 128),
            block,
            pl.BlockSpec((1, width, width), lambda i: (3, 0, 0), pipeline_mode=pl.Buffered(1)),
            whole_spec((1, width)),
        ]
        + [token_spec() for _ in tokens],
        out_specs=[block, block, fixed_spec((width, width)), fixed_spec((8, width))],
        out_shape=[
            shape((rows, width), F32),
            shape((rows, width), BF),
            shape((width, width), BF),
            shape((8, width), F32),
        ],
        scratch_shapes=[pltpu.VMEM((width, width), F32)],
        compiler_params=params(),
        cost_estimate=cost(8),
        name="middle",
    )(normed, second, unit, saved, ctx, full, gain, *tokens)


def head_weights_kernel(place, dq, dk, dv, x, wo, *refs):
    keep, send, held = refs[-3:]
    core = place[0]
    shards, heads = keep.shape[1], keep.shape[3]
    for kind in range(4):
        if kind < 3:
            held[...] = lax.dot_general(
                (dq, dk, dv)[kind][...], x[...], TN, preferred_element_type=F32
            ).astype(BF)
        source = held if kind < 3 else wo
        for side in range(2):

            @pl.when(core == side)
            def _():
                out = keep if side == kind // 2 else send
                for r in range(shards):
                    for h in range(heads):
                        for g in range(4):
                            at = (r * heads + h) * HEAD_DIM + g * GRAIN
                            out[g, r, kind % 2, h] = source[at : at + GRAIN, :]


def head_weights(place, dq, dk, dv, x, wo, n_mp, *tokens):
    rows, width = x.shape
    heads = width // HEAD_DIM // n_mp
    dims = (4, n_mp, 2, heads, GRAIN, width)
    keep, send = pl.pallas_call(
        head_weights_kernel,
        in_specs=[scalar_spec()] + [held_spec()] * 5 + [token_spec() for _ in tokens],
        out_specs=[held_spec()] * 2,
        out_shape=[shape(dims, BF)] * 2,
        scratch_shapes=[pltpu.VMEM((width, width), BF)],
        compiler_params=params(),
        cost_estimate=cost(8),
        name="head_weights",
    )(place, dq, dk, dv, x, wo, *tokens)
    dims = (4, n_mp, 2 * heads * GRAIN, width)
    return keep.reshape(dims), send.reshape(dims)


def input_kernel(dq, dk, dv, full, first, *refs):
    out = refs[-1]
    total = first[...]
    for kind, ref in enumerate((dq, dk, dv)):
        total = total + jnp.dot(ref[...], full[kind], preferred_element_type=F32)
    out[...] = total


def input_gradient(dq, dk, dv, full, first, *tokens):
    rows, width = dq.shape
    block = rows_spec(ROW_BLOCK, width)
    return pl.pallas_call(
        input_kernel,
        grid=(rows // ROW_BLOCK,),
        in_specs=[
            block,
            block,
            block,
            pl.BlockSpec((3, width, width), lambda i: (0, 0, 0), pipeline_mode=pl.Buffered(1)),
            block,
        ]
        + [token_spec() for _ in tokens],
        out_specs=block,
        out_shape=shape((rows, width), F32),
        compiler_params=params(),
        cost_estimate=cost(6),
        name="input_gradient",
    )(dq, dk, dv, full, first, *tokens)


def score_kernel(out_ref, segr_ref, len_ref, table_ref, pick_ref, *refs):
    score_ref = refs[-1]
    queries = pick_ref.shape[0]
    rows = out_ref.shape[0]
    label = lax.broadcasted_iota(jnp.int32, (queries, rows), 0)
    onehot = (label == segr_ref[...]).astype(F32)
    sums = jnp.dot(
        onehot, out_ref[...], precision=lax.Precision.HIGHEST, preferred_element_type=F32
    )
    means = sums / len_ref[...].astype(F32)
    every = lax.dot_general(
        means,
        table_ref[...].astype(F32),
        NT,
        precision=lax.Precision.HIGHEST,
        preferred_element_type=F32,
    )
    at = lax.broadcasted_iota(jnp.int32, every.shape, 1)
    column = lax.broadcasted_iota(jnp.int32, pick_ref.shape, 1)
    result = jnp.zeros(pick_ref.shape, F32)
    for p in range(pick_ref.shape[1]):
        chosen = jnp.sum(
            jnp.where(at == pick_ref[:, p : p + 1], every, 0.0), axis=1, keepdims=True
        )
        result = jnp.where(column == p, chosen, result)
    score_ref[...] = result


def score(layer_out, segr, lengths, table, picks, *tokens):
    return pl.pallas_call(
        score_kernel,
        in_specs=[held_spec()] * 5 + [token_spec() for _ in tokens],
        out_specs=held_spec(),
        out_shape=shape(picks.shape, F32),
        compiler_params=params(),
        cost_estimate=cost(8),
        name="score",
    )(layer_out, segr, lengths, table, picks, *tokens)


def per_device(
    n_dp,
    n_mp,
    hidden_in,
    cotangent,
    query_lengths,
    passage_index,
    passages,
    w_query,
    w_key,
    w_value,
    w_output,
    w_up,
    w_down,
    b_query,
    b_value,
    b_output,
    b_up,
    b_down,
    first_gain,
    first_shift,
    second_gain,
    second_shift,
):
    rows, width = hidden_in.shape
    heads = w_query.shape[1] // HEAD_DIM
    sub = w_up.shape[1] // 8
    at_dp = lax.axis_index("dp")
    core, plane = at_dp & 1, (at_dp >> 1) & 3
    place = jnp.stack([core, plane]).astype(jnp.int32)
    own_heads = (w_query.T, w_key.T, w_value.T, w_output)

    heads_piece = piece_heads(place, *own_heads)
    turned, up_piece, down_piece = piece_feed(place, w_up, w_down)

    heads_shards = shard_step(heads_piece, n_mp)
    up_shards = shard_step(after(up_piece, heads_shards), n_mp)
    heads_plane = plane_step(heads_shards, n_dp)
    heads_corner = corner_step(*heads_plane, n_dp)
    heads_mine = [heads_shards, *heads_plane, *heads_corner]
    heads_pieces = heads_mine + core_step(heads_mine, n_dp)
    down_shards = shard_step(after(down_piece, up_shards, heads_plane[0]), n_mp)
    up_plane = plane_step(after(up_shards, *heads_corner), n_dp)
    up_corner = corner_step(*up_plane, n_dp)
    up_mine = [up_shards, *up_plane, *up_corner]
    up_pieces = up_mine + core_step(up_mine, n_dp)
    down_plane = plane_step(after(down_shards, *up_corner), n_dp)
    down_corner = corner_step(*down_plane, n_dp)
    down_mine = [down_shards, *down_plane, *down_corner]
    down_pieces = down_mine + core_step(down_mine, n_dp)

    order4 = (lax.broadcasted_iota(jnp.int32, (4, 4), 0) ^ plane) == lax.broadcasted_iota(
        jnp.int32, (4, 4), 1
    )
    order8 = (
        lax.broadcasted_iota(jnp.int32, (8, 8), 0) ^ (core * 4 + plane)
    ) == lax.broadcasted_iota(jnp.int32, (8, 8), 1)
    order4, order8 = order4.astype(F32), order8.astype(F32)
    exact = functools.partial(
        jnp.einsum, precision=lax.Precision.HIGHEST, preferred_element_type=F32
    )

    def turn_heads(vector):
        return exact("gk,thki->thgi", order4, vector.reshape(-1, heads, 4, GRAIN))

    def turn_hidden(vector):
        return exact("sk,ki->si", order8, vector.reshape(8, sub))

    local_bias = jnp.concatenate(
        [
            turn_heads(jnp.concatenate([b_query, b_value]).astype(F32)).reshape(-1),
            turn_hidden(b_up.astype(F32)).reshape(-1),
        ]
    )
    all_bias = jnp.stack(
        [local_bias] + [swap(local_bias, "mp", r, n_mp) for r in range(1, n_mp)]
    )
    cut = heads * HEAD_DIM
    query_bias = all_bias[:, :cut].reshape(1, -1)
    value_bias = all_bias[:, cut : 2 * cut].reshape(1, -1)
    up_bias = all_bias[:, 2 * cut :].reshape(n_mp, 8, sub).transpose(1, 0, 2).reshape(1, -1)

    ends = jnp.cumsum(query_lengths, axis=-1, dtype=jnp.int32)
    places = lax.broadcasted_iota(jnp.int32, (rows, query_lengths.shape[1]), 0)
    seg = jnp.sum((places >= ends).astype(jnp.int32), axis=-1)
    segc, segr = seg.reshape(rows, 1), seg.reshape(1, rows)
    vectors = jnp.stack(
        [b_down, first_gain, first_shift, second_gain, second_shift, b_output, b_output, b_output]
    ).astype(F32)

    query, key, value, full = project(
        place, hidden_in, own_heads, query_bias, value_bias, heads_pieces
    )
    context, saved, unit, low = attend(
        query, key, value, segc, segr, hidden_in, full, vectors[5:6], vectors[1:2], vectors[2:3]
    )
    act, slope, layer_out, output, second_grad, down_grad, second_sums, wu, wd = feed(
        place, low, unit, cotangent, turned, w_down, up_bias, vectors, up_pieces + down_pieces
    )

    dims = (4, n_mp, sub, width)
    down_send = down_weight(act, down_grad, 1)
    down_keep = down_weight(act, down_grad, 0)
    down_parts = chip_sum(down_keep.reshape(dims), down_send.reshape(dims), n_dp)
    up_send, bias_send, normed = feed_back(down_grad, low, wu, wd, slope, 1, None, down_keep)
    down_parts2 = plane_sum(down_parts, n_dp)
    up_keep, bias_keep, normed = feed_back(
        down_grad, low, wu, wd, slope, 0, normed, *down_parts
    )
    up_parts = chip_sum(up_keep.reshape(dims), up_send.reshape(dims), n_dp)
    first_grad, context_grad, wo_grad, first_sums = middle(
        normed, second_grad, unit, saved, context, full, vectors[1:2], *down_parts2
    )
    down_parts3 = corner_sum(down_parts2, n_dp)
    up_parts2 = plane_sum(up_parts, n_dp)
    dq, dk, dv, head_sums = attend_back(
        query, key, value, context_grad, saved, segc, segr, *down_parts3, *up_parts
    )
    down_total = shard_sum(down_parts3, n_dp, n_mp)
    up_parts3 = corner_sum(up_parts2, n_dp)
    heads_keep, heads_send = head_weights(
        place, dq, dk, dv, hidden_in, wo_grad, n_mp, down_total, *up_parts2
    )
    heads_parts = chip_sum(heads_keep, heads_send, n_dp)
    up_total = shard_sum(up_parts3, n_dp, n_mp)
    down_all = gather_sum(down_total, n_dp)
    input_grad = input_gradient(dq, dk, dv, full, first_grad, *up_parts3, heads_keep)
    heads_parts2 = plane_sum(heads_parts, n_dp)
    up_all = gather_sum(up_total, n_dp)
    scores = score(
        layer_out, segr, query_lengths.reshape(-1, 1), passages, passage_index, input_grad
    )
    heads_parts3 = corner_sum(heads_parts2, n_dp)
    heads_total = shard_sum(heads_parts3, n_dp, n_mp)
    heads_all = gather_sum(heads_total, n_dp)
    w_down_grad = finish_feed(place, down_all, False)
    w_up_grad = finish_feed(place, up_all, True)
    query_t, key_t, value_t, w_output_grad = finish_heads(place, heads_all)

    bias_grad = jnp.concatenate(
        [
            head_sums[0].reshape(n_mp, cut),
            head_sums[1].reshape(n_mp, cut),
            jnp.concatenate([bias_keep, bias_send], axis=1)
            .reshape(8, n_mp, sub)
            .transpose(1, 0, 2)
            .reshape(n_mp, -1),
        ],
        axis=1,
    )
    own_bias = bias_grad[0]
    for r in range(1, n_mp):
        own_bias = own_bias + swap(bias_grad[r], "mp", r, n_mp)
    own_bias = jnp.concatenate(
        [turn_heads(own_bias[: 2 * cut]).reshape(-1), turn_hidden(own_bias[2 * cut :]).reshape(-1)]
    )
    shared = jnp.concatenate([first_sums[:3], second_sums[:3]])
    bit = 1
    while bit < n_mp:
        shared = shared + swap(shared, "mp", bit, n_mp)
        bit *= 2
    every = jnp.concatenate([shared.reshape(-1), own_bias])
    bit = 1
    while bit < n_dp:
        every = every + swap(every, "dp", bit, n_dp)
        bit *= 2
    shared = every[: 6 * width].reshape(6, width)
    own_bias = every[6 * width :]
    return (
        output,
        scores,
        input_grad,
        query_t.T,
        key_t.T,
        value_t.T,
        w_output_grad,
        w_up_grad,
        w_down_grad,
        own_bias[:cut],
        own_bias[cut : 2 * cut],
        shared[0],
        own_bias[2 * cut :],
        shared[3],
        shared[1],
        shared[2],
        shared[4],
        shared[5],
    )


def solution(mesh):
    both, split = P(("dp", "mp"), None), P(None, "mp")
    return jax.shard_map(
        functools.partial(per_device, mesh.shape["dp"], mesh.shape["mp"]),
        mesh=mesh,
        in_specs=(both, both, both, both, P())
        + (split, split, split, P("mp", None), split, P("mp", None))
        + (P("mp"), P("mp"), P(), P("mp"), P(), P(), P(), P(), P()),
        out_specs=(both, both, both)
        + (split, split, split, P("mp", None), split, P("mp", None))
        + (P("mp"), P("mp"), P(), P("mp"), P(), P(), P(), P(), P()),
        check_vma=False,
    )
```

time: 1740 us -> 369 us (0.21)
  waiting for transfers between devices: 1210 us -> 73.4 us
  matrix products: 263 us -> 0.75 us
  Pallas kernels: 0 us -> 160 us
  starting transfers between devices: 0.37 us -> 86.7 us
  other arithmetic: 97 us -> 13.9 us
  blocking collectives: 70.5 us -> 0 us
  local copies, waits for them, and re-layouts: 77.5 us -> 27.7 us
    reduce_scatter x4 -> x0, waiting for transfers between devices: 637 us -> none  [the longest x1 210 us: per_device(): lax.psum_scatter(jnp.dot(context_flat, out_weight, preferred_element_type...]
    all_gather x4 -> x0, waiting for transfers between devices: 455 us -> none  [the longest x1 117 us: per_device(): down_group = lax.all_gather(down_local, 'mp', axis=0, tiled=True)]
    dot_general x48 -> x4, matrix products: 263 us -> 0.75 us  [the longest x2 0.39 us: turn_heads(): return exact('gk,thki->thgi', order4, vector.reshape(-1, heads, 4, GRAIN))]
    pallas_call x0 -> x17, Pallas kernels: none -> 160 us  [the longest x1 29.9 us: attend_back(): pl.pallas_call(attend_back_kernel, grid=(rows // BLOCK,), in_specs=[block...]
    psum x1 -> x0, waiting for transfers between devices: 115 us -> none  [per_device(): lax.psum((w_query_grad, w_key_grad, w_value_grad, w_output_grad, w_up_gra...]
    ppermute x0 -> x98, starting transfers between devices: none -> 86.7 us  [swap(): return lax.ppermute(block, axis, [(i, i ^ bit) for i in range(size)])]
    ppermute x0 -> x98, waiting for transfers between devices: none -> 73.4 us  [swap(): return lax.ppermute(block, axis, [(i, i ^ bit) for i in range(size)])]
    psum x2 -> x0, blocking collectives: 57.8 us -> none  [the longest x1 43.5 us: per_device(): lax.psum((first_gain_grad, first_shift_grad, second_gain_grad, second_shi...]
  transfers between devices with their start and end apart: 9 -> 98, of which waited for: 9 -> 30; matrix products, arithmetic and copies ran while one was open for 3% -> 7% of each run, Pallas kernels for 0% -> 24%
where the time goes in v1:
time: 369 us; the launch traced here: 365 us
  Pallas kernels  160 us (43%)
  starting transfers between devices  86.7 us (23%)
  waiting for transfers between devices  73.4 us (20%)
  local copies, waits for them, and re-layouts  27.7 us (8%)
  other arithmetic  13.9 us (4%)
    ppermute x98, starting transfers between devices, swap(): return lax.ppermute(block, axis, [(i, i ^ bit) for i in range(size)])  86.7 us
    ppermute x98, waiting for transfers between devices, swap(): return lax.ppermute(block, axis, [(i, i ^ bit) for i in range(size)])  73.4 us
    pallas_call x1, Pallas kernels, attend_back(): pl.pallas_call(attend_back_kernel, grid=(rows // BLOCK,), in_specs=[block...  29.9 us
    pallas_call x1, Pallas kernels, feed(): pl.pallas_call(feed_kernel, grid=(rows // ROW_BLOCK,), in_specs=[scalar_s...  25.6 us
    pallas_call x2, Pallas kernels, feed_back(): pl.pallas_call(functools.partial(feed_back_kernel, base is not None), gri...  24 us
    pallas_call x1, Pallas kernels, attend(): pl.pallas_call(attend_kernel, grid=(rows // BLOCK,), in_specs=[block, who...  20.8 us
    unnamed x119, local copies, waits for them, and re-layouts  19.5 us
    convert_element_type x15, other arithmetic, add(): return total.astype(BF)  11.4 us
  transfers between devices with their start and end apart: 98, of which 30 were waited for; matrix products, arithmetic and copies ran while one was open for 7% of the time, Pallas kernels for 24%

profile of v1, /device:TPU:0, one launch (start us, length us, event | category | flops | bytes accessed | tf_op | source)
XLA Modules:
  0.0 364.7 jit_solution(9023741381662159868)
XLA Ops:
  5.2 3.1 collective-permute-start.3
  8.3 2.6 collective-permute-start.4
  14.2 8.1 %collective-permute-done.4 = bf16[96,768]{1,0:T(8,128)(2,1)S(1)} collective-permute-done((bf16[96,768]{1,0:T(8,128)(2,1)S(1)}, bf16[96,768]{1,0:T(8,128)(2,1)S(1)}, u32[]{:S(2)}, u32[]{:S(2)}) %collective-permute-start.4) | collective-permute-done | bytes 147488 | tf_op jit(solution)/shard_map/ppermute | solution.py:65
  35.5 4.8 %collective-permute-done.16 = bf16[96,768]{1,0:T(8,128)(2,1)S(1)} collective-permute-done((bf16[96,768]{1,0:T(8,128)(2,1)S(1)}, bf16[96,768]{1,0:T(8,128)(2,1)S(1)}, u32[]{:S(2)}, u32[]{:S(2)}) %collective-permute-start.16) | collective-permute-done | bytes 147488 | tf_op jit(solution)/shard_map/ppermute | solution.py:65
  44.4 2.3 collective-permute-start.28
  50.5 3.0 collective-permute-done.18.refs_1_
  66.0 3.6 collective-permute-done
  71.0 3.2 collective-permute-done.1
  87.6 8.9 %project.1 = (bf16[1024,768]{1,0:T(8,128)(2,1)}, bf16[1024,768]{1,0:T(8,128)(2,1)}, bf16[1024,768]{1,0:T(8,128)(2,1)}, bf16[4,768,768]{2,1,0:T(8,128)(2,1)}) custom-call(s32[2]{0:T(128)S(1)} %pad_add_fusion.place, bf16[1024,768]{1,0:T(8,128)(2,1)} %x.5, bf16[192,768]{1,0:T(8,128)(2,1)S(1)} %bitcast.153, bf16[192,768]{1,0:T(8,128)(2,1)S(1)} %bitcast.155, ...), custom_call_target="tpu_custom_call" | custom-call | flops 7000000000 | bytes 21000000 | tf_op jit(solution)/shard_map/project/pallas_call | solution.py:307
  99.1 20.8 %attend.1 = (bf16[1024,768]{1,0:T(8,128)(2,1)S(1)}, f32[1024,128]{1,0:T(8,128)S(1)}, f32[1024,768]{1,0:T(8,128)}, bf16[1024,768]{1,0:T(8,128)(2,1)S(1)}) custom-call(bf16[1024,768]{1,0:T(8,128)(2,1)S(1)} %copy-done.28, bf16[1024,768]{1,0:T(8,128)(2,1)} %get-tuple-element.63.k, bf16[1024,768]{1,0:T(8,128)(2,1)} %get-tuple-element.64.v, ...), custom_call_target="tpu_custom_call" | custom-call | flops 17999998976 | bytes 54000000 | tf_op jit(solution)/shard_map/attend/pallas_call | solution.py:375
  122.3 25.6 %feed.1 = (bf16[1024,3072]{1,0:T(8,128)(2,1)}, bf16[1024,3072]{1,0:T(8,128)(2,1)}, f32[1024,768]{1,0:T(8,128)}, bf16[1024,768]{1,0:T(8,128)(2,1)}, f32[1024,768]...) custom-call(s32[2]{0:T(128)} %copy-done.14, ...), custom_call_target="tpu_custom_call" | custom-call | flops 24000000000 | bytes 72000000 | tf_op jit(solution)/shard_map/feed/pallas_call | solution.py:539
  149.3 5.3 %down_weight.3 = bf16[1536,768]{1,0:T(8,128)(2,1)} custom-call(bf16[1024,3072]{1,0:T(8,128)(2,1)} %get-tuple-element.81.act, bf16[1024,768]{1,0:T(8,128)(2,1)S(1)} %copy-done.21), custom_call_target="tpu_custom_call" | custom-call | flops 5000000000 | bytes 15000000 | tf_op jit(solution)/shard_map/down_weight/pallas_call | solution.py:572
  155.0 4.5 %down_weight.2.refs_0_ = bf16[1536,768]{1,0:T(8,128)(2,1)S(1)} custom-call(bf16[1024,3072]{1,0:T(8,128)(2,1)} %get-tuple-element.81.act, bf16[1024,768]{1,0:T(8,128)(2,1)S(1)} %copy-done.21), custom_call_target="tpu_custom_call" | custom-call | flops 5000000000 | bytes 15000000 | tf_op jit(solution)/shard_map/down_weight/pallas_call | solution.py:572
  160.9 11.3 %feed_back.2 = (bf16[1536,768]{1,0:T(8,128)(2,1)S(1)}, f32[1,1536]{1,0:T(1,128)S(1)}, f32[1024,768]{1,0:T(8,128)}) custom-call(bf16[1024,768]{1,0:T(8,128)(2,1)S(1)} %copy-done.22, bf16[1024,768]{1,0:T(8,128)(2,1)S(1)} %copy-done.27, bf16[3072,768]{1,0:T(8,128)(2,1)} %get-tuple-element.78.wu, bf16[3072,768]{1,0:T(8,128)(2,1)} %get-tuple-element.79.wd, ...), custom_call_target="tpu_custom_call" | custom-call | flops 11000000512 | bytes 33000000 | tf_op jit(solution)/shard_map/feed_back/pallas_call | solution.py:617
  178.0 12.7 %feed_back.3 = (bf16[1536,768]{1,0:T(8,128)(2,1)}, f32[1,1536]{1,0:T(1,128)S(1)}, f32[1024,768]{1,0:T(8,128)}) custom-call(bf16[1024,768]{1,0:T(8,128)(2,1)S(1)} %copy-done.22, bf16[1024,768]{1,0:T(8,128)(2,1)S(1)} %copy-done.27, bf16[3072,768]{1,0:T(8,128)(2,1)} %get-tuple-element.78.wu, bf16[3072,768]{1,0:T(8,128)(2,1)} %get-tuple-element.79.wd, ...), custom_call_target="tpu_custom_call" | custom-call | flops 11000000512 | bytes 33000000 | tf_op jit(solution)/shard_map/feed_back/pallas_call | solution.py:617
  190.6 3.0 add_convert_fusion.4
  198.1 10.0 %middle.1 = (f32[1024,768]{1,0:T(8,128)}, bf16[1024,768]{1,0:T(8,128)(2,1)S(1)}, bf16[768,768]{1,0:T(8,128)(2,1)S(1)}, f32[8,768]{1,0:T(8,128)S(1)}) custom-call(f32[1024,768]{1,0:T(8,128)} %get-tuple-element.83.normed, f32[1024,768]{1,0:T(8,128)} %get-tuple-element.84.second, f32[1024,768]{1,0:T(8,128)} %get-tuple-element.67.unit, ...), custom_call_target="tpu_custom_call" | custom-call | flops 8000000000 | bytes 24000000 | tf_op jit(solution)/shard_map/middle/pallas_call | solution.py:677
  210.0 5.2 %collective-permute-done.42 = bf16[2,96,768]{2,1,0:T(8,128)(2,1)S(1)} collective-permute-done((bf16[2,96,768]{2,1,0:T(8,128)(2,1)S(1)}, bf16[2,96,768]{2,1,0:T(8,128)(2,1)S(1)}, u32[]{:S(2)}, u32[]{:S(2)}) %collective-permute-start.42) | collective-permute-done | bytes 294944 | tf_op jit(solution)/shard_map/ppermute | solution.py:65
  215.4 3.9 %collective-permute-start.50 = (bf16[96,768]{1,0:T(8,128)(2,1)S(1)}, bf16[96,768]{1,0:T(8,128)(2,1)S(1)}, u32[]{:S(2)}, u32[]{:S(2)}) collective-permute-start(bf16[96,768]{1,0:T(8,128)(2,1)S(1)} %get-tuple-element.144.refs_2_), channel_id=1, source_target_pairs={{0,2},{1,3},{2,0},{3,1},{4,6},{5,7},{6,4},{7,5},{8,10},{9,11},{10,... | collective-permute-start | bytes 442376 | tf_op jit(solution)/shard_map/ppermute | solution.py:65
  222.1 7.6 %collective-permute-done.50 = bf16[96,768]{1,0:T(8,128)(2,1)S(1)} collective-permute-done((bf16[96,768]{1,0:T(8,128)(2,1)S(1)}, bf16[96,768]{1,0:T(8,128)(2,1)S(1)}, u32[]{:S(2)}, u32[]{:S(2)}) %collective-permute-start.50) | collective-permute-done | bytes 147488 | tf_op jit(solution)/shard_map/ppermute | solution.py:65
  229.8 29.9 %attend_back.1 = (bf16[1024,768]{1,0:T(8,128)(2,1)S(1)}, bf16[1024,768]{1,0:T(8,128)(2,1)}, bf16[1024,768]{1,0:T(8,128)(2,1)}, f32[8,768]{1,0:T(8,128)S(1)}) custom-call(bf16[1024,768]{1,0:T(8,128)(2,1)} %get-tuple-element.62.q, bf16[1024,768]{1,0:T(8,128)(2,1)} %get-tuple-element.63.k, bf16[1024,768]{1,0:T(8,128)(2,1)} %get-tuple-element.64.v, ...), custom_call_target="tpu_custom_call" | custom-call | flops 30000001024 | bytes 90000000 | tf_op jit(solution)/shard_map/attend_back/pallas_call | solution.py:451
  261.7 9.4 %head_weights.1 = (bf16[4,4,2,3,16,768]{5,4,3,2,1,0:T(8,128)(2,1)}, bf16[4,4,2,3,16,768]{5,4,3,2,1,0:T(8,128)(2,1)}) custom-call(s32[2]{0:T(128)S(1)} %copy-done.15, bf16[1024,768]{1,0:T(8,128)(2,1)S(1)} %get-tuple-element.90.dq, bf16[1024,768]{1,0:T(8,128)(2,1)S(1)} %copy-done.18, bf16[1024,768]{1,0:T(8,128)(2,1)} %get-tuple-element.92.dv, ...), custom_call_target="tpu_custom_call" | custom-call | flops 8000000000 | bytes 24000000 | tf_op jit(solution)/shard_map/head_weights/pallas_call | solution.py:730
  275.3 3.0 collective-permute-start.91
  280.1 2.4 collective-permute-done.46
  289.7 2.4 collective-permute-start.71
  292.6 3.8 %add_convert_fusion.3 = (bf16[2,2,96,768]{3,2,1,0:T(8,128)(2,1)S(1)}, bf16[2,2,96,768]{3,2,1,0:T(8,128)(2,1)S(1)}, bf16[2,2,96,768]{3,2,1,0:T(8,128)(2,1)S(1)}, bf16[2,2,96,768]{3,2,1,0:T(8,128)(2,1)}) fusion(bf16[4,4,96,768]{3,2,1,0:T(8,128)(2,1)} %collective-permute-done.52, bf16[4,4,96,768]{3,2,1,0:T(8,128)(2,1)} %bitcast.161), kind=kLoop, calls=%fused_computation.3 | loop fusion | flops 4718592 | bytes 7077888 | tf_op jit(solution)/shard_map/convert_element_type | solution.py:214
  303.1 8.9 %collective-permute-done.53 = bf16[2,2,96,768]{3,2,1,0:T(8,128)(2,1)} collective-permute-done((bf16[2,2,96,768]{3,2,1,0:T(8,128)(2,1)}, bf16[2,2,96,768]{3,2,1,0:T(8,128)(2,1)}, u32[]{:S(2)}, u32[]{:S(2)}) %collective-permute-start.53) | collective-permute-done | bytes 589856 | tf_op jit(solution)/shard_map/ppermute | solution.py:65
  316.4 8.2 %input_gradient.1.refs_0_ = f32[1024,768]{1,0:T(8,128)} custom-call(bf16[1024,768]{1,0:T(8,128)(2,1)S(1)} %copy-done.17, bf16[1024,768]{1,0:T(8,128)(2,1)S(1)} %copy-done.19, bf16[1024,768]{1,0:T(8,128)(2,1)S(1)} %copy-done.20, bf16[4,768,768]{2,1,0:T(8,128)(2,1)} %get-tuple-element.65.wo.full, f32[1024,768]{1,0:T(8,128)} %get-tuple-element.93.first, ...), custom_call_target="tpu_custom_call" | custom-call | flops 6000000000 | bytes 18000000 | tf_op jit(solution)/shard_map/input_gradient/pallas_call | solution.py:755
  327.6 3.8 %collective-permute-done.97 = f32[5760]{0:T(1024)S(1)} collective-permute-done((f32[5760]{0:T(1024)S(1)}, f32[5760]{0:T(1024)S(1)}, u32[]{:S(2)}, u32[]{:S(2)}) %collective-permute-start.97) | collective-permute-done | bytes 23072 | tf_op jit(solution)/shard_map/ppermute | solution.py:65
  333.4 2.3 collective-permute-start.59
  335.7 5.3 %score.1 = f32[32,32]{1,0:T(8,128)} custom-call(f32[1024,768]{1,0:T(8,128)S(1)} %copy-done.25, s32[1,1024]{1,0:T(1,128)S(1)} %bitcast.150, s32[32,1]{1,0:T(8,128)S(1)} %copy.46.len_ref, bf16[1024,768]{1,0:T(8,128)(2,1)S(1)} %copy-done.2, s32[32,32]{1,0:T(8,128)S(1)} %copy-done.13, f32[1024,768]{1,0:T(8,128)} %input_gradient.1.refs_0_), custom_call_target="tpu_custom_call" | custom-call | flops 8000000000 | bytes 24000000 | tf_op jit(solution)/shard_map/score/pallas_call | solution.py:803
  359.6 2.8 finish_up.1
  (401 shorter events, 131.3 us)
Async XLA Ops:
  8.3 14.0 %collective-permute-start.4 = (bf16[96,768]{1,0:T(8,128)(2,1)S(1)}, bf16[96,768]{1,0:T(8,128)(2,1)S(1)}, u32[]{:S(2)}, u32[]{:S(2)}) collective-permute-start(bf16[96,768]{1,0:T(8,128)(2,1)S(1)} %bitcast.159), channel_id=1, source_target_pairs={{0,2},{1,3},{2,0},{3,1},{4,6},{5,7},{6,4},{7,5},{8,10},{9,11},{10,... | collective-permute-start | bytes 442376 | tf_op jit(solution)/shard_map/ppermute | solution.py:65
  46.8 32.9 %collective-permute-start.10 = (bf16[288,768]{1,0:T(8,128)(2,1)S(1)}, bf16[288,768]{1,0:T(8,128)(2,1)S(1)}, u32[]{:S(2)}, u32[]{:S(2)}) collective-permute-start(bf16[288,768]{1,0:T(8,128)(2,1)S(1)} %constant_dynamic-update-slice_fusion.1.refs_0_), channel_id=1, source_target_pairs={{0,4},{4,0},{8,12},{12,8},{16,20},{20,16},{24,28},{28,24},{1,5},{5... | collective-permute-start | bytes 1327112 | tf_op jit(solution)/shard_map/ppermute | solution.py:65
  53.5 26.7 %collective-permute-start.22 = (bf16[288,768]{1,0:T(8,128)(2,1)}, bf16[288,768]{1,0:T(8,128)(2,1)}, u32[]{:S(2)}, u32[]{:S(2)}) collective-permute-start(bf16[288,768]{1,0:T(8,128)(2,1)} %constant_dynamic-update-slice_fusion.4.refs_0_), channel_id=1, source_target_pairs={{0,4},{4,0},{8,12},{12,8},{16,20},{20,16},{24,28},{28,24},{1,5},{5... | collective-permute-start | bytes 1327112 | tf_op jit(solution)/shard_map/ppermute | solution.py:65
  62.7 17.6 %collective-permute-start.30 = (bf16[288,768]{1,0:T(8,128)(2,1)}, bf16[288,768]{1,0:T(8,128)(2,1)}, u32[]{:S(2)}, u32[]{:S(2)}) collective-permute-start(bf16[288,768]{1,0:T(8,128)(2,1)} %constant_dynamic-update-slice_fusion.7.refs_10_), channel_id=1, source_target_pairs={{0,8},{4,12},{8,0},{12,4},{16,24},{20,28},{24,16},{28,20},{1,9},{5... | collective-permute-start | bytes 1327112 | tf_op jit(solution)/shard_map/ppermute | solution.py:65
  64.0 16.9 %collective-permute-start.31 = (bf16[288,768]{1,0:T(8,128)(2,1)}, bf16[288,768]{1,0:T(8,128)(2,1)}, u32[]{:S(2)}, u32[]{:S(2)}) collective-permute-start(bf16[288,768]{1,0:T(8,128)(2,1)} %constant_dynamic-update-slice_fusion.7.refs_10_), channel_id=1, source_target_pairs={{0,16},{4,20},{8,24},{12,28},{16,0},{20,4},{24,8},{28,12},{1,17},{... | collective-permute-start | bytes 1327112 | tf_op jit(solution)/shard_map/ppermute | solution.py:65
  83.9 13.1 %collective-permute-start.23 = (bf16[288,768]{1,0:T(8,128)(2,1)}, bf16[288,768]{1,0:T(8,128)(2,1)S(1)}, u32[]{:S(2)}, u32[]{:S(2)}) collective-permute-start(bf16[288,768]{1,0:T(8,128)(2,1)} %copy-done.32), channel_id=1, source_target_pairs={{0,4},{4,0},{8,12},{12,8},{16,20},{20,16},{24,28},{28,24},{1,5},{5... | collective-permute-start | bytes 1327112 | tf_op jit(solution)/shard_map/ppermute | solution.py:65
  85.0 12.6 %collective-permute-start.33 = (bf16[144,768]{1,0:T(8,128)(2,1)S(1)}, bf16[144,768]{1,0:T(8,128)(2,1)S(1)}, u32[]{:S(2)}, u32[]{:S(2)}) collective-permute-start(bf16[144,768]{1,0:T(8,128)(2,1)S(1)} %slice.496), channel_id=1, source_target_pairs={{0,8},{4,12},{8,0},{12,4},{16,24},{20,28},{24,16},{28,20},{1,9},{5... | collective-permute-start | bytes 663560 | tf_op jit(solution)/shard_map/ppermute | solution.py:65
  96.5 24.6 %collective-permute-start.24 = (bf16[288,768]{1,0:T(8,128)(2,1)}, bf16[288,768]{1,0:T(8,128)(2,1)S(1)}, u32[]{:S(2)}, u32[]{:S(2)}) collective-permute-start(bf16[288,768]{1,0:T(8,128)(2,1)} %collective-permute-done.19.refs_2_), channel_id=1, source_target_pairs={{0,4},{4,0},{8,12},{12,8},{16,20},{20,16},{24,28},{28,24},{1,5},{5... | collective-permute-start | bytes 1327112 | tf_op jit(solution)/shard_map/ppermute | solution.py:65
  96.6 24.5 %collective-permute-start.35 = (bf16[288,768]{1,0:T(8,128)(2,1)}, bf16[288,768]{1,0:T(8,128)(2,1)S(1)}, u32[]{:S(2)}, u32[]{:S(2)}) collective-permute-start(bf16[288,768]{1,0:T(8,128)(2,1)} %collective-permute-done.30.refs_11_), channel_id=1, source_target_pairs={{0,4},{4,0},{8,12},{12,8},{16,20},{20,16},{24,28},{28,24},{1,5},{5... | collective-permute-start | bytes 1327112 | tf_op jit(solution)/shard_map/ppermute | solution.py:65
  97.1 24.1 %collective-permute-start.36 = (bf16[288,768]{1,0:T(8,128)(2,1)}, bf16[288,768]{1,0:T(8,128)(2,1)S(1)}, u32[]{:S(2)}, u32[]{:S(2)}) collective-permute-start(bf16[288,768]{1,0:T(8,128)(2,1)} %collective-permute-done.31.refs_12_), channel_id=1, source_target_pairs={{0,4},{4,0},{8,12},{12,8},{16,20},{20,16},{24,28},{28,24},{1,5},{5... | collective-permute-start | bytes 1327112 | tf_op jit(solution)/shard_map/ppermute | solution.py:65
  97.2 23.9 %collective-permute-start.37 = (bf16[144,768]{1,0:T(8,128)(2,1)S(1)}, bf16[144,768]{1,0:T(8,128)(2,1)S(1)}, u32[]{:S(2)}, u32[]{:S(2)}) collective-permute-start(bf16[144,768]{1,0:T(8,128)(2,1)S(1)} %collective-permute-done.32.refs_13_), channel_id=1, source_target_pairs={{0,4},{4,0},{8,12},{12,8},{16,20},{20,16},{24,28},{28,24},{1,5},{5... | collective-permute-start | bytes 663560 | tf_op jit(solution)/shard_map/ppermute | solution.py:65
  97.6 23.5 %collective-permute-start.38 = (bf16[144,768]{1,0:T(8,128)(2,1)S(1)}, bf16[144,768]{1,0:T(8,128)(2,1)S(1)}, u32[]{:S(2)}, u32[]{:S(2)}) collective-permute-start(bf16[144,768]{1,0:T(8,128)(2,1)S(1)} %collective-permute-done.33.refs_14_), channel_id=1, source_target_pairs={{0,4},{4,0},{8,12},{12,8},{16,20},{20,16},{24,28},{28,24},{1,5},{5... | collective-permute-start | bytes 663560 | tf_op jit(solution)/shard_map/ppermute | solution.py:65
  154.6 17.7 %collective-permute-start.39 = (bf16[4,4,96,768]{3,2,1,0:T(8,128)(2,1)}, bf16[4,4,96,768]{3,2,1,0:T(8,128)(2,1)}, u32[]{:S(2)}, u32[]{:S(2)}) collective-permute-start(bf16[4,4,96,768]{3,2,1,0:T(8,128)(2,1)} %bitcast.14), channel_id=1, source_target_pairs={{0,4},{4,0},{8,12},{12,8},{16,20},{20,16},{24,28},{28,24},{1,5},{5... | collective-permute-start | bytes 7077896 | tf_op jit(solution)/shard_map/ppermute | solution.py:65
  172.2 18.4 %collective-permute-start.44 = (bf16[4,4,96,768]{3,2,1,0:T(8,128)(2,1)S(1)}, bf16[4,4,96,768]{3,2,1,0:T(8,128)(2,1)}, u32[]{:S(2)}, u32[]{:S(2)}) collective-permute-start(bf16[4,4,96,768]{3,2,1,0:T(8,128)(2,1)S(1)} %bitcast.151), channel_id=1, source_target_pairs={{0,4},{4,0},{8,12},{12,8},{16,20},{20,16},{24,28},{28,24},{1,5},{5... | collective-permute-start | bytes 7077896 | tf_op jit(solution)/shard_map/ppermute | solution.py:65
  174.6 19.8 %collective-permute-start.40 = (bf16[2,2,96,768]{3,2,1,0:T(8,128)(2,1)S(1)}, bf16[2,2,96,768]{3,2,1,0:T(8,128)(2,1)S(1)}, u32[]{:S(2)}, u32[]{:S(2)}) collective-permute-start(bf16[2,2,96,768]{3,2,1,0:T(8,128)(2,1)S(1)} %get-tuple-element.126.refs_2_), channel_id=1, source_target_pairs={{0,8},{4,12},{8,0},{12,4},{16,24},{20,28},{24,16},{28,20},{1,9},{5... | collective-permute-start | bytes 1769480 | tf_op jit(solution)/shard_map/ppermute | solution.py:65
  176.0 20.1 %collective-permute-start.41 = (bf16[2,2,96,768]{3,2,1,0:T(8,128)(2,1)S(1)}, bf16[2,2,96,768]{3,2,1,0:T(8,128)(2,1)S(1)}, u32[]{:S(2)}, u32[]{:S(2)}) collective-permute-start(bf16[2,2,96,768]{3,2,1,0:T(8,128)(2,1)S(1)} %get-tuple-element.124.refs_4_), channel_id=1, source_target_pairs={{0,16},{4,20},{8,24},{12,28},{16,0},{20,4},{24,8},{28,12},{1,17},{... | collective-permute-start | bytes 1769480 | tf_op jit(solution)/shard_map/ppermute | solution.py:65
  193.6 16.3 %collective-permute-start.45 = (bf16[2,2,96,768]{3,2,1,0:T(8,128)(2,1)S(1)}, bf16[2,2,96,768]{3,2,1,0:T(8,128)(2,1)S(1)}, u32[]{:S(2)}, u32[]{:S(2)}) collective-permute-start(bf16[2,2,96,768]{3,2,1,0:T(8,128)(2,1)S(1)} %get-tuple-element.122.refs_5_), channel_id=1, source_target_pairs={{0,8},{4,12},{8,0},{12,4},{16,24},{20,28},{24,16},{28,20},{1,9},{5... | collective-permute-start | bytes 1769480 | tf_op jit(solution)/shard_map/ppermute | solution.py:65
  193.9 26.0 %collective-permute-start.47 = (bf16[2,2,96,768]{3,2,1,0:T(8,128)(2,1)S(1)}, bf16[2,2,96,768]{3,2,1,0:T(8,128)(2,1)S(1)}, u32[]{:S(2)}, u32[]{:S(2)}) collective-permute-start(bf16[2,2,96,768]{3,2,1,0:T(8,128)(2,1)S(1)} %get-tuple-element.120.refs_7_), channel_id=1, source_target_pairs={{0,16},{4,20},{8,24},{12,28},{16,0},{20,4},{24,8},{28,12},{1,17},{... | collective-permute-start | bytes 1769480 | tf_op jit(solution)/shard_map/ppermute | solution.py:65
  194.6 20.7 %collective-permute-start.42 = (bf16[2,96,768]{2,1,0:T(8,128)(2,1)S(1)}, bf16[2,96,768]{2,1,0:T(8,128)(2,1)S(1)}, u32[]{:S(2)}, u32[]{:S(2)}) collective-permute-start(bf16[2,96,768]{2,1,0:T(8,128)(2,1)S(1)} %get-tuple-element.138.refs_1_), channel_id=1, source_target_pairs={{0,16},{4,20},{8,24},{12,28},{16,0},{20,4},{24,8},{28,12},{1,17},{... | collective-permute-start | bytes 884744 | tf_op jit(solution)/shard_map/ppermute | solution.py:65
  196.3 19.1 %collective-permute-start.43 = (bf16[2,96,768]{2,1,0:T(8,128)(2,1)S(1)}, bf16[2,96,768]{2,1,0:T(8,128)(2,1)S(1)}, u32[]{:S(2)}, u32[]{:S(2)}) collective-permute-start(bf16[2,96,768]{2,1,0:T(8,128)(2,1)S(1)} %get-tuple-element.136.refs_3_), channel_id=1, source_target_pairs={{0,8},{4,12},{8,0},{12,4},{16,24},{20,28},{24,16},{28,20},{1,9},{5... | collective-permute-start | bytes 884744 | tf_op jit(solution)/shard_map/ppermute | solution.py:65
  215.4 14.3 %collective-permute-start.50 = (bf16[96,768]{1,0:T(8,128)(2,1)S(1)}, bf16[96,768]{1,0:T(8,128)(2,1)S(1)}, u32[]{:S(2)}, u32[]{:S(2)}) collective-permute-start(bf16[96,768]{1,0:T(8,128)(2,1)S(1)} %get-tuple-element.144.refs_2_), channel_id=1, source_target_pairs={{0,2},{1,3},{2,0},{3,1},{4,6},{5,7},{6,4},{7,5},{8,10},{9,11},{10,... | collective-permute-start | bytes 442376 | tf_op jit(solution)/shard_map/ppermute | solution.py:65
  271.1 21.5 %collective-permute-start.52 = (bf16[4,4,96,768]{3,2,1,0:T(8,128)(2,1)}, bf16[4,4,96,768]{3,2,1,0:T(8,128)(2,1)}, u32[]{:S(2)}, u32[]{:S(2)}) collective-permute-start(bf16[4,4,96,768]{3,2,1,0:T(8,128)(2,1)} %bitcast.167), channel_id=1, source_target_pairs={{0,4},{4,0},{8,12},{12,8},{16,20},{20,16},{24,28},{28,24},{1,5},{5... | collective-permute-start | bytes 7077896 | tf_op jit(solution)/shard_map/ppermute | solution.py:65
  282.6 15.3 %collective-permute-start.69 = (bf16[96,768]{1,0:T(8,128)(2,1)S(1)}, bf16[96,768]{1,0:T(8,128)(2,1)S(1)}, u32[]{:S(2)}, u32[]{:S(2)}) collective-permute-start(bf16[96,768]{1,0:T(8,128)(2,1)S(1)} %fusion.26.refs_1_), channel_id=1, source_target_pairs={{0,1},{1,0},{2,3},{3,2},{4,5},{5,4},{6,7},{7,6},{8,9},{9,8},{10,11... | collective-permute-start | bytes 442376 | tf_op jit(solution)/shard_map/ppermute | solution.py:65
  288.1 12.5 %collective-permute-start.70 = (bf16[96,768]{1,0:T(8,128)(2,1)S(1)}, bf16[96,768]{1,0:T(8,128)(2,1)}, u32[]{:S(2)}, u32[]{:S(2)}) collective-permute-start(bf16[96,768]{1,0:T(8,128)(2,1)S(1)} %get-tuple-element.142.refs_2_), channel_id=1, source_target_pairs={{0,2},{1,3},{2,0},{3,1},{4,6},{5,7},{6,4},{7,5},{8,10},{9,11},{10,... | collective-permute-start | bytes 442376 | tf_op jit(solution)/shard_map/ppermute | solution.py:65
  296.4 15.5 %collective-permute-start.53 = (bf16[2,2,96,768]{3,2,1,0:T(8,128)(2,1)}, bf16[2,2,96,768]{3,2,1,0:T(8,128)(2,1)}, u32[]{:S(2)}, u32[]{:S(2)}) collective-permute-start(bf16[2,2,96,768]{3,2,1,0:T(8,128)(2,1)} %get-tuple-element.119), channel_id=1, source_target_pairs={{0,8},{4,12},{8,0},{12,4},{16,24},{20,28},{24,16},{28,20},{1,9},{5... | collective-permute-start | bytes 1769480 | tf_op jit(solution)/shard_map/ppermute | solution.py:65
  297.2 16.2 %collective-permute-start.56 = (bf16[2,2,96,768]{3,2,1,0:T(8,128)(2,1)S(1)}, bf16[2,2,96,768]{3,2,1,0:T(8,128)(2,1)S(1)}, u32[]{:S(2)}, u32[]{:S(2)}) collective-permute-start(bf16[2,2,96,768]{3,2,1,0:T(8,128)(2,1)S(1)} %get-tuple-element.117), channel_id=1, source_target_pairs={{0,16},{4,20},{8,24},{12,28},{16,0},{20,4},{24,8},{28,12},{1,17},{... | collective-permute-start | bytes 1769480 | tf_op jit(solution)/shard_map/ppermute | solution.py:65
  297.9 33.5 %collective-permute-start.81 = (bf16[96,768]{1,0:T(8,128)(2,1)S(1)}, bf16[96,768]{1,0:T(8,128)(2,1)S(1)}, u32[]{:S(2)}, u32[]{:S(2)}) collective-permute-start(bf16[96,768]{1,0:T(8,128)(2,1)S(1)} %get-tuple-element.114.refs_0_), channel_id=1, source_target_pairs={{0,8},{4,12},{8,0},{12,4},{16,24},{20,28},{24,16},{28,20},{1,9},{5... | collective-permute-start | bytes 442376 | tf_op jit(solution)/shard_map/ppermute | solution.py:65
  300.6 32.8 %collective-permute-start.82 = (bf16[96,768]{1,0:T(8,128)(2,1)S(1)}, bf16[96,768]{1,0:T(8,128)(2,1)S(1)}, u32[]{:S(2)}, u32[]{:S(2)}) collective-permute-start(bf16[96,768]{1,0:T(8,128)(2,1)S(1)} %get-tuple-element.114.refs_0_), channel_id=1, source_target_pairs={{0,16},{4,20},{8,24},{12,28},{16,0},{20,4},{24,8},{28,12},{1,17},{... | collective-permute-start | bytes 442376 | tf_op jit(solution)/shard_map/ppermute | solution.py:65
  302.3 22.4 %collective-permute-start.96 = (f32[5760]{0:T(1024)S(1)}, f32[5760]{0:T(1024)S(1)}, u32[]{:S(2)}, u32[]{:S(2)}) collective-permute-start(f32[5760]{0:T(1024)S(1)} %add.237), channel_id=1, source_target_pairs={{0,8},{4,12},{8,0},{12,4},{16,24},{20,28},{24,16},{28,20},{1,9},{5... | collective-permute-start | bytes 69128 | tf_op jit(solution)/shard_map/ppermute | solution.py:65
  313.3 14.2 %collective-permute-start.54 = (bf16[2,96,768]{2,1,0:T(8,128)(2,1)S(1)}, bf16[2,96,768]{2,1,0:T(8,128)(2,1)S(1)}, u32[]{:S(2)}, u32[]{:S(2)}) collective-permute-start(bf16[2,96,768]{2,1,0:T(8,128)(2,1)S(1)} %get-tuple-element.129), channel_id=1, source_target_pairs={{0,16},{4,20},{8,24},{12,28},{16,0},{20,4},{24,8},{28,12},{1,17},{... | collective-permute-start | bytes 884744 | tf_op jit(solution)/shard_map/ppermute | solution.py:65
  324.7 16.4 %collective-permute-start.72 = (bf16[96,768]{1,0:T(8,128)(2,1)S(1)}, bf16[96,768]{1,0:T(8,128)(2,1)S(1)}, u32[]{:S(2)}, u32[]{:S(2)}) collective-permute-start(bf16[96,768]{1,0:T(8,128)(2,1)S(1)} %get-tuple-element.112.refs_0_), channel_id=1, source_target_pairs={{0,8},{4,12},{8,0},{12,4},{16,24},{20,28},{24,16},{28,20},{1,9},{5... | collective-permute-start | bytes 442376 | tf_op jit(solution)/shard_map/ppermute | solution.py:65
  325.3 15.9 %collective-permute-start.73 = (bf16[96,768]{1,0:T(8,128)(2,1)S(1)}, bf16[96,768]{1,0:T(8,128)(2,1)S(1)}, u32[]{:S(2)}, u32[]{:S(2)}) collective-permute-start(bf16[96,768]{1,0:T(8,128)(2,1)S(1)} %get-tuple-element.112.refs_0_), channel_id=1, source_target_pairs={{0,16},{4,20},{8,24},{12,28},{16,0},{20,4},{24,8},{28,12},{1,17},{... | collective-permute-start | bytes 442376 | tf_op jit(solution)/shard_map/ppermute | solution.py:65
  (121 other events, 1276.7 us)

commit v2 on v1

v2 whole, which is shorter than its diff:
```python
import functools

import jax
import jax.numpy as jnp
from jax import lax
from jax.experimental import pallas as pl
from jax.experimental.pallas import tpu as pltpu
from jax.sharding import PartitionSpec as P

HEAD_DIM = 64
SCALE = 0.125
EPSILON = 1e-12
MASKED = -1e30
BLOCK = 128
WINDOW = 384
GROUP = 4 * HEAD_DIM
ROW_BLOCK = 256
GRAIN = 16
MEBI = 1024 * 1024
NT = (((1,), (1,)), ((), ()))
TN = (((0,), (0,)), ((), ()))
BF = jnp.bfloat16
F32 = jnp.float32

CORE, XBIT, YBIT = 1, 2, 4


def params(mebi=60):
    return pltpu.CompilerParams(vmem_limit_bytes=mebi * MEBI)


def cost(us):
    return pl.CostEstimate(flops=int(us * 5e9), bytes_accessed=int(us * 15e6), transcendentals=0)


def shape(dims, dtype):
    return jax.ShapeDtypeStruct(dims, dtype)


def scalar_spec():
    return pl.BlockSpec(memory_space=pltpu.SMEM)


def held_spec():
    return pl.BlockSpec(memory_space=pltpu.VMEM)


def whole_spec(dims):
    return pl.BlockSpec(dims, lambda i: (0,) * len(dims), pipeline_mode=pl.Buffered(1))


def fixed_spec(dims):
    return pl.BlockSpec(dims, lambda i: (0,) * len(dims))


def rows_spec(rows, width):
    return pl.BlockSpec((rows, width), lambda i: (i, 0))


def token_spec():
    return pl.BlockSpec(memory_space=pl.ANY)


def swap(block, axis, bit, size):
    return lax.ppermute(block, axis, [(i, i ^ bit) for i in range(size)])


def after(value, *others):
    return lax.optimization_barrier((value, *others))[0]


def neighbour(core, g):
    if g in (0, 3):
        return g
    return g ^ (3 * core)


def piece_heads_kernel(place, wq, wk, wv, wo, piece, sems):
    core, plane = place[0], place[1]
    heads = piece.shape[1]
    for side, pair in enumerate(((wq, wk), (wv, wo))):

        @pl.when(core == side)
        def _():
            copies = []
            for t, ref in enumerate(pair):
                for h in range(heads):
                    start = pl.multiple_of(h * HEAD_DIM + plane * GRAIN, GRAIN)
                    copies.append(
                        pltpu.make_async_copy(
                            ref.at[pl.ds(start, GRAIN), :], piece.at[t, h], sems.at[t * heads + h]
                        )
                    )
            for copy in copies:
                copy.start()
            for copy in copies:
                copy.wait()


def piece_heads(place, *weights):
    local, width = weights[0].shape
    heads = local // HEAD_DIM
    return pl.pallas_call(
        piece_heads_kernel,
        in_specs=[scalar_spec()] + [token_spec()] * 4,
        out_specs=held_spec(),
        out_shape=shape((2, heads, GRAIN, width), BF),
        scratch_shapes=[pltpu.SemaphoreType.DMA((2 * heads,))],
        compiler_params=params(),
        cost_estimate=cost(1),
        name="piece_heads",
    )(place, *weights).reshape(2 * heads * GRAIN, width)


def piece_feed_kernel(place, wu, wd, turned, piece_up, piece_down):
    core, plane = place[0], place[1]
    sub = piece_up.shape[0]
    turned[...] = wu[...].astype(F32).T.astype(BF)
    start = pl.multiple_of((core * 4 + plane) * sub, GRAIN)
    piece_up[...] = turned[pl.ds(start, sub), :]
    piece_down[...] = wd[pl.ds(start, sub), :]


def piece_feed(place, wu, wd):
    width, hidden = wu.shape
    sub = hidden // 8
    return pl.pallas_call(
        piece_feed_kernel,
        in_specs=[scalar_spec()] + [held_spec()] * 2,
        out_specs=[held_spec()] * 3,
        out_shape=[shape((hidden, width), BF), shape((sub, width), BF), shape((sub, width), BF)],
        compiler_params=params(),
        cost_estimate=cost(3),
        name="piece_feed",
    )(place, wu, wd)


def finish_feed_kernel(place, mine, other, up, down, held):
    core = place[0]
    sub = mine.shape[1] // 2
    for c, ref in enumerate((mine, other)):
        for g in range(4):
            start = pl.multiple_of(((core ^ c) * 4 + g) * sub, GRAIN)
            held[pl.ds(start, sub), :] = ref[g, :sub, :].astype(F32)
            down[pl.ds(start, sub), :] = ref[g, sub:, :].astype(F32)
    up[...] = held[...].T


def finish_feed(place, pieces, *tokens):
    _, rows, width = pieces[0].shape
    return pl.pallas_call(
        finish_feed_drop,
        in_specs=[scalar_spec()] + [held_spec()] * 2 + [token_spec() for _ in tokens],
        out_specs=[held_spec()] * 2,
        out_shape=[shape((width, 4 * rows), F32), shape((4 * rows, width), F32)],
        scratch_shapes=[pltpu.VMEM((4 * rows, width), F32)],
        compiler_params=params(),
        cost_estimate=cost(6),
        name="finish_feed",
    )(place, *pieces, *tokens)


def finish_feed_drop(place, mine, other, *refs):
    finish_feed_kernel(place, mine, other, *refs[-3:])


def finish_heads_kernel(place, mine, other, *outs):
    core = place[0]
    heads = outs[0].shape[0] // HEAD_DIM
    for side in range(2):

        @pl.when(core == side)
        def _():
            for c, ref in enumerate((mine, other)):
                for t in range(2):
                    out = outs[2 * (side ^ c) + t]
                    for g in range(4):
                        for h in range(heads):
                            at = h * HEAD_DIM + g * GRAIN
                            row = (t * heads + h) * GRAIN
                            out[at : at + GRAIN, :] = ref[g, row : row + GRAIN, :].astype(F32)


def finish_heads(place, pieces):
    _, rows, width = pieces[0].shape
    local = rows // (2 * GRAIN) * HEAD_DIM
    return pl.pallas_call(
        finish_heads_kernel,
        in_specs=[scalar_spec()] + [held_spec()] * 2,
        out_specs=[held_spec()] * 4,
        out_shape=[shape((local, width), F32)] * 4,
        compiler_params=params(),
        cost_estimate=cost(2),
        name="finish_heads",
    )(place, *pieces)


def shard_step(piece, n_mp):
    return [swap(piece, "mp", r, n_mp) for r in range(1, n_mp)]


def turn_swap(block, bits, n_dp):
    return lax.ppermute(block, "dp", [(i, i ^ bits[i & 1]) for i in range(n_dp)])


def first_swap(block, n_dp):
    return turn_swap(block, (XBIT, YBIT), n_dp)


def second_swap(block, n_dp):
    return turn_swap(block, (YBIT, XBIT), n_dp)


def core_swap(block, n_dp):
    return swap(block, "dp", CORE, n_dp)


def exchange(block, axis, groups=None):
    return lax.all_to_all(block, axis, 0, 0, axis_index_groups=groups, tiled=True)


def spread(block, n):
    return jnp.broadcast_to(block[None], (n, *block.shape))


def plane_groups(n_dp):
    return [[8 * e + 2 * g + c for g in range(4)] for e in range(n_dp // 8) for c in range(2)]


def add(*terms):
    total = terms[0].astype(F32)
    for term in terms[1:]:
        total = total + term.astype(F32)
    return total.astype(BF)


def chip_sum(keep, got):
    return add(keep[0::2], got[0::2]), add(keep[1::2], got[1::2])


def side_sum(stay, got):
    return add(stay[0], got[0]), add(stay[1], got[1])


def shard_swap(parts, n_mp):
    shard = lax.axis_index("mp")
    return [
        swap(lax.dynamic_index_in_dim(parts, shard ^ r, 0, keepdims=False), "mp", r, n_mp)
        for r in range(1, n_mp)
    ]


def shard_sum(own, got, n_dp):
    total = own.astype(F32)
    for part in got:
        total = total + part.astype(F32)
    bit = 8
    while bit < n_dp:
        total = total + swap(total, "dp", bit, n_dp)
        bit *= 2
    return total.astype(BF)


def plane_gather(four, n_dp):
    return exchange(four, "dp", plane_groups(n_dp))


def project_kernel(place, x, wq, wk, wv, wo, bq, bv, *refs):
    pieces, (q, k, v, full, sems) = refs[:8], refs[-5:]
    core, plane, shard = place[0], place[1], place[2]
    heads = wq.shape[0] // HEAD_DIM
    shards = 1 + pieces[0].shape[0] // (2 * heads * GRAIN)

    @pl.when(pl.program_id(0) == 0)
    def _():
        copies = []
        base = pl.multiple_of(shard * heads * HEAD_DIM, HEAD_DIM)
        for kind, ref in enumerate((wq, wk, wv, wo)):
            for h in range(heads):
                for g in range(4):
                    source = plane ^ neighbour(kind // 2, g)
                    at = pl.multiple_of(h * HEAD_DIM + source * GRAIN, GRAIN)
                    to = pl.multiple_of(base + h * HEAD_DIM + g * GRAIN, GRAIN)
                    copies.append(
                        pltpu.make_async_copy(
                            ref.at[pl.ds(at, GRAIN), :],
                            full.at[kind, pl.ds(to, GRAIN), :],
                            sems.at[len(copies)],
                        )
                    )
        for copy in copies:
            copy.start()
        for c in range(2):
            for g, ref in enumerate(pieces[4 * c : 4 * c + 4]):
                for r in range(1, shards):
                    base = pl.multiple_of((shard ^ r) * heads * HEAD_DIM, HEAD_DIM)
                    for t in range(2):
                        for h in range(heads):
                            row = (((r - 1) * 2 + t) * heads + h) * GRAIN
                            to = pl.multiple_of(base + h * HEAD_DIM + g * GRAIN, GRAIN)
                            full[(core ^ c) * 2 + t, pl.ds(to, GRAIN), :] = ref[
                                row : row + GRAIN, :
                            ]
        for copy in copies:
            copy.wait()

    block = x[...]
    for kind, (out, bias) in enumerate(((q, bq), (k, None), (v, bv))):
        value = lax.dot_general(block, full[kind], NT, preferred_element_type=F32)
        if bias is not None:
            value = value + bias[...]
        out[...] = value.astype(BF)


def project(place, x, weights, bq, bv, pieces, *tokens):
    rows, width = x.shape
    block = rows_spec(ROW_BLOCK, width)
    return pl.pallas_call(
        project_kernel,
        grid=(rows // ROW_BLOCK,),
        in_specs=[scalar_spec(), block]
        + [token_spec()] * 4
        + [whole_spec(a.shape) for a in (bq, bv, *pieces)]
        + [token_spec() for _ in tokens],
        out_specs=[block, block, block, fixed_spec((4, width, width))],
        out_shape=[shape((rows, width), BF)] * 3 + [shape((4, width, width), BF)],
        scratch_shapes=[pltpu.SemaphoreType.DMA((weights[0].shape[0] // GRAIN * 4,))],
        compiler_params=params(),
        cost_estimate=cost(10),
        name="project",
    )(place, x, *weights, bq, bv, *pieces, *tokens)


def spread_heads(block):
    lane = lax.broadcasted_iota(jnp.int32, block.shape, 1) // HEAD_DIM
    return jnp.concatenate(
        [jnp.where(lane == h, block, jnp.zeros_like(block)) for h in range(4)], axis=0
    )


def gather_heads(stacked):
    rows = stacked.shape[0] // 4
    lane = lax.broadcasted_iota(jnp.int32, (rows, GROUP), 1) // HEAD_DIM
    out = stacked[:rows]
    for h in range(1, 4):
        out = jnp.where(lane == h, stacked[h * rows : (h + 1) * rows], out)
    return out


def window_start(step, rows):
    return pl.multiple_of(jnp.clip(step - 1, 0, (rows - WINDOW) // BLOCK) * BLOCK, BLOCK)


def attend_kernel(part, q, k, v, segc, segr, x, wo, bo, gain, shift, *refs):
    ctx, saved, unit, low = refs[-4:]
    start = window_start(part * pl.num_programs(0) + pl.program_id(0), k.shape[0])
    near = pl.ds(start, WINDOW)
    penalty = jnp.where(segc[...] == segr[:, near], 0.0, MASKED)
    lane = lax.broadcasted_iota(jnp.int32, (BLOCK, 128), 1)
    groups = q.shape[1] // GROUP

    def score_group(group):
        cols = slice(group * GROUP, (group + 1) * GROUP)
        return lax.dot_general(
            spread_heads(q[:, cols] * SCALE), k[near, cols], NT, preferred_element_type=F32
        )

    keep = jnp.zeros((BLOCK, 128), F32)
    ahead = score_group(0)
    for group in range(groups):
        cols = slice(group * GROUP, (group + 1) * GROUP)
        logits = ahead.reshape(4, BLOCK, WINDOW) + penalty[None]
        if group + 1 < groups:
            ahead = score_group(group + 1)
        peak = jnp.max(logits, axis=-1, keepdims=True)
        raised = jnp.exp(logits - peak)
        sums = jnp.sum(raised, axis=-1, keepdims=True)
        context = jnp.dot(
            raised.astype(BF).reshape(4 * BLOCK, WINDOW), v[near, cols], preferred_element_type=F32
        )
        context = (context.reshape(4, BLOCK, GROUP) * (1.0 / sums)).reshape(4 * BLOCK, GROUP)
        ctx[:, cols] = gather_heads(context).astype(BF)
        log_total = peak + jnp.log(sums)
        for h in range(4):
            keep = jnp.where(lane == group * 4 + h, log_total[h], keep)
    attended = jnp.dot(ctx[...], wo[0], preferred_element_type=F32) + bo[...]
    total = x[...].astype(F32) + attended
    centred = total - jnp.mean(total, axis=-1, keepdims=True)
    inv_std = lax.rsqrt(jnp.mean(centred * centred, axis=-1, keepdims=True) + EPSILON)
    unit_val = centred * inv_std
    unit[...] = unit_val
    low[...] = (unit_val * gain[...] + shift[...]).astype(BF)
    saved[...] = jnp.where(lane == 127, inv_std, keep)


def attend(part, parts, q, k, v, segc, segr, x, full, bo, gain, shift, held, *tokens):
    rows, width = q.shape
    steps = rows // BLOCK // parts

    def block(wide):
        return pl.BlockSpec((BLOCK, wide), lambda i: (part * steps + i, 0))

    return pl.pallas_call(
        functools.partial(attend_kernel, part),
        grid=(steps,),
        in_specs=[
            block(width),
            whole_spec((rows, width)),
            whole_spec((rows, width)),
            block(1),
            whole_spec((1, rows)),
            block(width),
            pl.BlockSpec((1, width, width), lambda i: (3, 0, 0), pipeline_mode=pl.Buffered(1)),
            whole_spec((1, width)),
            whole_spec((1, width)),
            whole_spec((1, width)),
        ]
        + [token_spec() for _ in (*held, *tokens)],
        out_specs=[block(width), block(128), block(width), block(width)],
        out_shape=[
            shape((rows, width), BF),
            shape((rows, 128), F32),
            shape((rows, width), F32),
            shape((rows, width), BF),
        ],
        input_output_aliases={10 + i: i for i in range(len(held))},
        compiler_params=params(),
        cost_estimate=cost(16 / parts),
        name="attend",
    )(q, k, v, segc, segr, x, full, bo, gain, shift, *held, *tokens)


def attend_back_kernel(q, k, v, do, saved, inner, segc, segr, *refs):
    dq, dk, dv, sums, dk_sum, dv_sum = refs[-6:]
    step = pl.program_id(0)

    @pl.when(step == 0)
    def _():
        dk_sum[...] = jnp.zeros_like(dk_sum)
        dv_sum[...] = jnp.zeros_like(dv_sum)
        sums[...] = jnp.zeros_like(sums)

    start = window_start(step, k.shape[0])
    near = pl.ds(start, WINDOW)
    penalty = jnp.where(segc[...] == segr[:, near], 0.0, MASKED)
    for group in range(q.shape[1] // GROUP):
        cols = slice(group * GROUP, (group + 1) * GROUP)
        q4 = spread_heads(q[:, cols] * SCALE)
        do4 = spread_heads(do[:, cols])
        k4 = k[near, cols]
        logits = lax.dot_general(q4, k4, NT, preferred_element_type=F32)
        logits = logits.reshape(4, BLOCK, WINDOW) + penalty[None]
        lse = jnp.stack([saved[:, group * 4 + h : group * 4 + h + 1] for h in range(4)])
        mean_grad = jnp.stack([inner[:, group * 4 + h : group * 4 + h + 1] for h in range(4)])
        probs = jnp.exp(logits - lse)
        weight_grad = lax.dot_general(
            do4, v[near, cols], NT, preferred_element_type=F32
        ).reshape(4, BLOCK, WINDOW)
        logit_grad = (probs * (weight_grad - mean_grad)).astype(BF).reshape(4 * BLOCK, WINDOW)
        probs_low = probs.astype(BF).reshape(4 * BLOCK, WINDOW)
        dq_low = (
            gather_heads(jnp.dot(logit_grad, k4, preferred_element_type=F32)) * SCALE
        ).astype(BF)
        dq[:, cols] = dq_low
        sums[0:1, cols] += jnp.sum(dq_low.astype(F32), axis=0, keepdims=True)
        dk_sum[near, cols] += lax.dot_general(logit_grad, q4, TN, preferred_element_type=F32)
        dv_sum[near, cols] += lax.dot_general(probs_low, do4, TN, preferred_element_type=F32)

    @pl.when(step == pl.num_programs(0) - 1)
    def _():
        dk[...] = dk_sum[...].astype(BF)
        dv_low = dv_sum[...].astype(BF)
        dv[...] = dv_low
        sums[1:2, :] = jnp.sum(dv_low.astype(F32), axis=0, keepdims=True)


def attend_back(q, k, v, do, saved, inner, segc, segr, *tokens):
    rows, width = q.shape
    block = rows_spec(BLOCK, width)
    full = whole_spec((rows, width))
    return pl.pallas_call(
        attend_back_kernel,
        grid=(rows // BLOCK,),
        in_specs=[
            block,
            full,
            full,
            block,
            rows_spec(BLOCK, 128),
            rows_spec(BLOCK, 128),
            rows_spec(BLOCK, 1),
            whole_spec((1, rows)),
        ]
        + [token_spec() for _ in tokens],
        out_specs=[block, fixed_spec((rows, width)), fixed_spec((rows, width)), fixed_spec((8, width))],
        out_shape=[shape((rows, width), BF)] * 3 + [shape((8, width), F32)],
        scratch_shapes=[pltpu.VMEM((rows, width), F32)] * 2,
        compiler_params=params(),
        cost_estimate=cost(22),
        name="attend_back",
    )(q, k, v, do, saved, inner, segc, segr, *tokens)


def assemble(place, own, pieces, into):
    core, plane, shard = place[0], place[1], place[2]
    sub = own.shape[0] // 8
    shards = 1 + pieces[0].shape[0] // sub

    def rows(c, g, r):
        return pl.ds(pl.multiple_of(((c * 4 + g) * shards + (shard ^ r)) * sub, GRAIN), sub)

    for c in range(2):
        for g, ref in enumerate(pieces[4 * c : 4 * c + 4]):
            at = pl.multiple_of(((core ^ c) * 4 + (plane ^ neighbour(core ^ c, g))) * sub, GRAIN)
            into[rows(c, g, 0), :] = own[pl.ds(at, sub), :]
            for r in range(1, shards):
                into[rows(c, g, r), :] = ref[(r - 1) * sub : r * sub, :]


def feed_up_kernel(place, x, own, bu, *refs):
    pieces, (act, slope, wu) = refs[:8], refs[-3:]

    @pl.when(pl.program_id(0) == 0)
    def _():
        assemble(place, own, pieces, wu)

    block = x[...]
    for at in range(0, wu.shape[0], 256):
        span = slice(at, at + 256)
        pre = (
            lax.dot_general(block, wu[span, :], NT, preferred_element_type=F32) + bu[:, span]
        )
        below = 0.5 * (1.0 + lax.erf(pre * 0.7071067811865476))
        density = jnp.exp(-0.5 * pre * pre) * 0.3989422804014327
        act[:, span] = (pre * below).astype(BF)
        slope[:, span] = (below + pre * density).astype(BF)


def feed_up(place, x, own, bu, pieces, *tokens):
    rows, width = x.shape
    hidden = bu.shape[1]
    wide = rows_spec(ROW_BLOCK, hidden)
    return pl.pallas_call(
        feed_up_kernel,
        grid=(rows // ROW_BLOCK,),
        in_specs=[scalar_spec(), rows_spec(ROW_BLOCK, width)]
        + [whole_spec(a.shape) for a in (own, bu, *pieces)]
        + [token_spec() for _ in tokens],
        out_specs=[wide, wide, fixed_spec((hidden, width))],
        out_shape=[shape((rows, hidden), BF)] * 2 + [shape((hidden, width), BF)],
        compiler_params=params(),
        cost_estimate=cost(12),
        name="feed_up",
    )(place, x, own, bu, *pieces, *tokens)


def feed_down_kernel(place, act, unit, cot, own, vectors, *refs):
    pieces, outs = refs[:8], refs[-6:]
    layer, output, second, down_grad, sums, wd = outs

    @pl.when(pl.program_id(0) == 0)
    def _():
        sums[...] = jnp.zeros_like(sums)
        assemble(place, own, pieces, wd)

    down = jnp.dot(act[...], wd[...], preferred_element_type=F32)
    b_down, first_gain, first_shift, second_gain, second_shift = (
        vectors[i : i + 1, :] for i in range(5)
    )
    total = unit[...] * first_gain + first_shift + down + b_down
    centred = total - jnp.mean(total, axis=-1, keepdims=True)
    inv_std = lax.rsqrt(jnp.mean(centred * centred, axis=-1, keepdims=True) + EPSILON)
    unit_val = centred * inv_std
    layer_out = unit_val * second_gain + second_shift
    layer[...] = layer_out
    output[...] = layer_out.astype(BF)
    grad = cot[...].astype(F32)
    scaled = grad * second_gain
    inner = (
        scaled
        - jnp.mean(scaled, axis=-1, keepdims=True)
        - unit_val * jnp.mean(scaled * unit_val, axis=-1, keepdims=True)
    )
    second_grad = inv_std * inner
    second[...] = second_grad
    grad_low = second_grad.astype(BF)
    down_grad[...] = grad_low
    sums[0:1, :] += jnp.sum(grad_low.astype(F32), axis=0, keepdims=True)
    sums[1:2, :] += jnp.sum(grad * unit_val, axis=0, keepdims=True)
    sums[2:3, :] += jnp.sum(grad, axis=0, keepdims=True)


def feed_down(place, act, unit, cot, own, vectors, pieces):
    rows, hidden = act.shape
    width = unit.shape[1]
    block = rows_spec(ROW_BLOCK, width)
    return pl.pallas_call(
        feed_down_kernel,
        grid=(rows // ROW_BLOCK,),
        in_specs=[scalar_spec(), rows_spec(ROW_BLOCK, hidden), block, block]
        + [whole_spec(a.shape) for a in (own, vectors, *pieces)],
        out_specs=[block, block, block, block, fixed_spec((8, width)), fixed_spec((hidden, width))],
        out_shape=[
            shape((rows, width), F32),
            shape((rows, width), BF),
            shape((rows, width), F32),
            shape((rows, width), BF),
            shape((8, width), F32),
            shape((hidden, width), BF),
        ],
        compiler_params=params(),
        cost_estimate=cost(13),
        name="feed_down",
    )(place, act, unit, cot, own, vectors, *pieces)


def feed_back_kernel(grad, x, wu, wd, slope, act, keep, send, bias, out, held):
    step = pl.program_id(0)
    half = pl.num_programs(0) // 2
    chips, shards, _, sub, width = keep.shape

    @pl.when(step == 0)
    def _():
        out[...] = jnp.zeros_like(out)

    total = None
    for at in range(0, x.shape[0], ROW_BLOCK):
        span = slice(at, at + ROW_BLOCK)
        act_grad = lax.dot_general(grad[span, :], wd[...], NT, preferred_element_type=F32)
        low = (act_grad * slope[span, :].astype(F32)).astype(BF)
        held[span, :] = low
        term = jnp.sum(low.astype(F32), axis=0, keepdims=True)
        total = term if total is None else total + term
    bias[...] = jnp.broadcast_to(total, bias.shape[1:])[None]
    out[...] += jnp.dot(held[...], wu[...], preferred_element_type=F32)
    dims = (chips, shards, sub, width)
    up = lax.dot_general(held[...], x[...], TN, preferred_element_type=F32).astype(BF)
    down = lax.dot_general(act[...], grad[...], TN, preferred_element_type=F32).astype(BF)

    @pl.when(step < half)
    def _():
        send[:, :, 0] = up.reshape(dims)
        send[:, :, 1] = down.reshape(dims)

    @pl.when(step >= half)
    def _():
        keep[:, :, 0] = up.reshape(dims)
        keep[:, :, 1] = down.reshape(dims)


def feed_back(grad, x, wu, wd, slope, act, n_mp):
    rows, width = x.shape
    hidden = wu.shape[0]
    span = hidden // 4
    full = whole_spec((rows, width))
    weight = pl.BlockSpec((span, width), lambda j: ((j + 2) % 4, 0))
    wide = pl.BlockSpec((rows, span), lambda j: (0, (j + 2) % 4))
    dims = (4, n_mp, 2, hidden // 8 // n_mp, width)
    block = (2, *dims[1:])
    return pl.pallas_call(
        feed_back_kernel,
        grid=(4,),
        in_specs=[full, full, weight, weight, wide, wide],
        out_specs=[
            pl.BlockSpec(block, lambda j: (jnp.maximum(j - 2, 0), 0, 0, 0, 0)),
            pl.BlockSpec(block, lambda j: (jnp.minimum(j, 1), 0, 0, 0, 0)),
            pl.BlockSpec((1, 8, span), lambda j: ((j + 2) % 4, 0, 0)),
            fixed_spec((rows, width)),
        ],
        out_shape=[
            shape(dims, BF),
            shape(dims, BF),
            shape((4, 8, span), F32),
            shape((rows, width), F32),
        ],
        scratch_shapes=[pltpu.VMEM((rows, span), BF)],
        compiler_params=params(),
        cost_estimate=cost(27),
        name="feed_back",
    )(grad, x, wu, wd, slope, act)


def middle_kernel(normed, second, unit, saved, ctx, wo, gain, *refs):
    first, context_grad, inner_sum, weight, sums, held = refs[-6:]
    step = pl.program_id(0)
    grad = normed[...] + second[...]
    unit_val = unit[...]
    scaled = grad * gain[...]
    inner = (
        scaled
        - jnp.mean(scaled, axis=-1, keepdims=True)
        - unit_val * jnp.mean(scaled * unit_val, axis=-1, keepdims=True)
    )
    first_grad = saved[:, 127:128] * inner
    first[...] = first_grad
    low = first_grad.astype(BF)
    context_low = lax.dot_general(low, wo[0], NT, preferred_element_type=F32).astype(BF)
    context_grad[...] = context_low
    product = context_low.astype(F32) * ctx[...].astype(F32)
    high = product.astype(BF)
    rest = (product - high.astype(F32)).astype(BF)
    width = product.shape[1]
    head = lax.broadcasted_iota(jnp.int32, (width, 128), 0) // HEAD_DIM
    head = (head == lax.broadcasted_iota(jnp.int32, (width, 128), 1)).astype(BF)
    inner_sum[...] = jnp.dot(high, head, preferred_element_type=F32) + jnp.dot(
        rest, head, preferred_element_type=F32
    )
    term = lax.dot_general(ctx[...], low, TN, preferred_element_type=F32)

    @pl.when(step == 0)
    def _():
        sums[...] = jnp.zeros_like(sums)
        held[...] = jnp.zeros_like(held)

    held[...] += term
    sums[0:1, :] += jnp.sum(low.astype(F32), axis=0, keepdims=True)
    sums[1:2, :] += jnp.sum(grad * unit_val, axis=0, keepdims=True)
    sums[2:3, :] += jnp.sum(grad, axis=0, keepdims=True)

    @pl.when(step == pl.num_programs(0) - 1)
    def _():
        weight[...] = held[...].astype(BF)


def middle(normed, second, unit, saved, ctx, full, gain, *tokens):
    rows, width = normed.shape
    block = rows_spec(ROW_BLOCK, width)
    return pl.pallas_call(
        middle_kernel,
        grid=(rows // ROW_BLOCK,),
        in_specs=[
            block,
            block,
            block,
            rows_spec(ROW_BLOCK, 128),
            block,
            pl.BlockSpec((1, width, width), lambda i: (3, 0, 0), pipeline_mode=pl.Buffered(1)),
            whole_spec((1, width)),
        ]
        + [token_spec() for _ in tokens],
        out_specs=[block, block, rows_spec(ROW_BLOCK, 128), fixed_spec((width, width)), fixed_spec((8, width))],
        out_shape=[
            shape((rows, width), F32),
            shape((rows, width), BF),
            shape((rows, 128), F32),
            shape((width, width), BF),
            shape((8, width), F32),
        ],
        scratch_shapes=[pltpu.VMEM((width, width), F32)],
        compiler_params=params(),
        cost_estimate=cost(8),
        name="middle",
    )(normed, second, unit, saved, ctx, full, gain, *tokens)


def head_weights_kernel(place, dq, dk, dv, x, wo, *refs):
    keep, send, held = refs[-3:]
    core = place[0]
    shards, heads = keep.shape[1], keep.shape[3]
    for kind in range(4):
        if kind < 3:
            held[...] = lax.dot_general(
                (dq, dk, dv)[kind][...], x[...], TN, preferred_element_type=F32
            ).astype(BF)
        source = held if kind < 3 else wo
        for side in range(2):

            @pl.when(core == side)
            def _():
                out = keep if side == kind // 2 else send
                for r in range(shards):
                    for h in range(heads):
                        for g in range(4):
                            at = (r * heads + h) * HEAD_DIM + g * GRAIN
                            out[g, r, kind % 2, h] = source[at : at + GRAIN, :]


def head_weights(place, dq, dk, dv, x, wo, n_mp, *tokens):
    rows, width = x.shape
    heads = width // HEAD_DIM // n_mp
    dims = (4, n_mp, 2, heads, GRAIN, width)
    keep, send = pl.pallas_call(
        head_weights_kernel,
        in_specs=[scalar_spec()] + [held_spec()] * 5 + [token_spec() for _ in tokens],
        out_specs=[held_spec()] * 2,
        out_shape=[shape(dims, BF)] * 2,
        scratch_shapes=[pltpu.VMEM((width, width), BF)],
        compiler_params=params(),
        cost_estimate=cost(8),
        name="head_weights",
    )(place, dq, dk, dv, x, wo, *tokens)
    dims = (4, n_mp, 2 * heads * GRAIN, width)
    return keep.reshape(dims), send.reshape(dims)


def input_kernel(dq, dk, dv, full, first, *refs):
    out = refs[-1]
    total = first[...]
    for kind, ref in enumerate((dq, dk, dv)):
        total = total + jnp.dot(ref[...], full[kind], preferred_element_type=F32)
    out[...] = total


def input_gradient(dq, dk, dv, full, first, *tokens):
    rows, width = dq.shape
    block = rows_spec(ROW_BLOCK, width)
    return pl.pallas_call(
        input_kernel,
        grid=(rows // ROW_BLOCK,),
        in_specs=[
            block,
            block,
            block,
            pl.BlockSpec((3, width, width), lambda i: (0, 0, 0), pipeline_mode=pl.Buffered(1)),
            block,
        ]
        + [token_spec() for _ in tokens],
        out_specs=block,
        out_shape=shape((rows, width), F32),
        compiler_params=params(),
        cost_estimate=cost(6),
        name="input_gradient",
    )(dq, dk, dv, full, first, *tokens)


def score_kernel(out_ref, segr_ref, len_ref, table_ref, pick_ref, *refs):
    score_ref = refs[-1]
    queries = pick_ref.shape[0]
    rows = out_ref.shape[0]
    label = lax.broadcasted_iota(jnp.int32, (queries, rows), 0)
    onehot = (label == segr_ref[...]).astype(F32)
    sums = jnp.dot(
        onehot, out_ref[...], precision=lax.Precision.HIGHEST, preferred_element_type=F32
    )
    means = sums / len_ref[...].astype(F32)
    every = lax.dot_general(
        means,
        table_ref[...].astype(F32),
        NT,
        precision=lax.Precision.HIGHEST,
        preferred_element_type=F32,
    )
    at = lax.broadcasted_iota(jnp.int32, every.shape, 1)
    column = lax.broadcasted_iota(jnp.int32, pick_ref.shape, 1)
    result = jnp.zeros(pick_ref.shape, F32)
    for p in range(pick_ref.shape[1]):
        chosen = jnp.sum(
            jnp.where(at == pick_ref[:, p : p + 1], every, 0.0), axis=1, keepdims=True
        )
        result = jnp.where(column == p, chosen, result)
    score_ref[...] = result


def score(layer_out, segr, lengths, table, picks, *tokens):
    return pl.pallas_call(
        score_kernel,
        in_specs=[held_spec()] * 5 + [token_spec() for _ in tokens],
        out_specs=held_spec(),
        out_shape=shape(picks.shape, F32),
        compiler_params=params(),
        cost_estimate=cost(8),
        name="score",
    )(layer_out, segr, lengths, table, picks, *tokens)


def per_device(
    n_dp,
    n_mp,
    hidden_in,
    cotangent,
    query_lengths,
    passage_index,
    passages,
    w_query,
    w_key,
    w_value,
    w_output,
    w_up,
    w_down,
    b_query,
    b_value,
    b_output,
    b_up,
    b_down,
    first_gain,
    first_shift,
    second_gain,
    second_shift,
):
    rows, width = hidden_in.shape
    heads = w_query.shape[1] // HEAD_DIM
    sub = w_up.shape[1] // 8
    at_dp = lax.axis_index("dp")
    core, plane = at_dp & 1, (at_dp >> 1) & 3
    shard = lax.axis_index("mp")
    place = jnp.stack([core, plane, shard]).astype(jnp.int32)
    own_heads = (w_query.T, w_key.T, w_value.T, w_output)

    heads_piece = piece_heads(place, *own_heads)
    heads_parts = shard_step(heads_piece, n_mp)
    turned, up_piece, down_piece = piece_feed(place, w_up, w_down)
    heads_shards = jnp.concatenate(heads_parts)
    up_got = exchange(spread(after(up_piece, heads_shards), n_mp), "mp")
    heads_first = first_swap(heads_shards, n_dp)
    heads_second = second_swap(heads_shards, n_dp)
    heads_corner = second_swap(heads_first, n_dp)
    heads_mine = [heads_shards, heads_first, heads_second, heads_corner]
    heads_pieces = heads_mine + [core_swap(p, n_dp) for p in heads_mine]

    def others(got):
        return jnp.concatenate(
            [
                lax.dynamic_index_in_dim(got, shard ^ r, 0, keepdims=False)
                for r in range(1, n_mp)
            ]
        )

    ranks = lax.broadcasted_iota(jnp.int32, (4, 4), 0)
    places4 = lax.broadcasted_iota(jnp.int32, (4, 4), 1)
    turned_ranks = jnp.where((ranks == 1) | (ranks == 2), ranks ^ 3, ranks)
    order_q = ((plane ^ ranks) == places4).astype(F32)
    order_v = ((plane ^ turned_ranks) == places4).astype(F32)
    owner = (core ^ jnp.arange(2, dtype=jnp.int32)).reshape(2, 1, 1, 1)
    is_owner = (owner == jnp.arange(2, dtype=jnp.int32).reshape(1, 1, 2, 1)).astype(F32)
    order_up = jnp.where(owner == 0, order_q[None, :, None], order_v[None, :, None])
    order_up = (order_up * is_owner).reshape(8, 8)
    exact = functools.partial(
        jnp.einsum, precision=lax.Precision.HIGHEST, preferred_element_type=F32
    )
    cut = heads * HEAD_DIM

    def turn(vector, there="gk"):
        query = vector[:cut].reshape(-1, 4, GRAIN)
        value = vector[cut : 2 * cut].reshape(-1, 4, GRAIN)
        hidden = vector[2 * cut :].reshape(8, sub)
        to = "g" if there == "gk" else "k"
        frm = "k" if there == "gk" else "g"
        return jnp.concatenate(
            [
                exact(f"gk,t{frm}i->t{to}i", order_q, query).reshape(-1),
                exact(f"gk,t{frm}i->t{to}i", order_v, value).reshape(-1),
                exact(f"gk,{frm}i->{to}i", order_up, hidden).reshape(-1),
            ]
        )

    local_bias = turn(
        jnp.concatenate(after((b_query, b_value, b_up), heads_shards)).astype(F32)
    )
    all_bias = exchange(spread(after(local_bias, up_got), n_mp), "mp")
    query_bias = all_bias[:, :cut].reshape(1, -1)
    value_bias = all_bias[:, cut : 2 * cut].reshape(1, -1)
    up_bias = all_bias[:, 2 * cut :].reshape(n_mp, 8, sub).transpose(1, 0, 2).reshape(1, -1)

    up_shards = others(lax.optimization_barrier((up_got, *heads_pieces))[0])
    up_first = first_swap(up_shards, n_dp)
    up_second = second_swap(up_shards, n_dp)
    down_got = exchange(spread(after(down_piece, all_bias), n_mp), "mp")

    ends = jnp.cumsum(query_lengths, axis=-1, dtype=jnp.int32)
    places = lax.broadcasted_iota(jnp.int32, (rows, query_lengths.shape[1]), 0)
    seg = jnp.sum((places >= ends).astype(jnp.int32), axis=-1)
    segc, segr = seg.reshape(rows, 1), seg.reshape(1, rows)
    vectors = jnp.stack(
        [b_down, first_gain, first_shift, second_gain, second_shift, b_output, b_output, b_output]
    ).astype(F32)

    query, key, value, full = project(
        place, hidden_in, own_heads, query_bias, value_bias, heads_pieces, up_shards
    )
    up_first, up_second, down_got, query = lax.optimization_barrier(
        (up_first, up_second, down_got, query)
    )
    up_corner = second_swap(up_first, n_dp)
    up_mine = [up_shards, up_first, up_second]
    up_other = [core_swap(p, n_dp) for p in up_mine]
    down_shards = others(down_got)
    down_first = first_swap(down_shards, n_dp)
    down_second = second_swap(down_shards, n_dp)
    held = attend(
        0, 2, query, key, value, segc, segr, hidden_in, full,
        vectors[5:6], vectors[1:2], vectors[2:3], (), down_shards,
    )
    up_corner, down_first, down_second, *held = lax.optimization_barrier(
        (up_corner, down_first, down_second, *held)
    )
    up_pieces = up_mine + [up_corner] + up_other + [core_swap(up_corner, n_dp)]
    down_corner = second_swap(down_first, n_dp)
    down_mine = [down_shards, down_first, down_second]
    down_other = [core_swap(p, n_dp) for p in down_mine]
    context, saved, unit, low = attend(
        1, 2, query, key, value, segc, segr, hidden_in, full,
        vectors[5:6], vectors[1:2], vectors[2:3], held,
    )
    down_corner, low = lax.optimization_barrier((down_corner, low))
    down_pieces = down_mine + [down_corner] + down_other + [core_swap(down_corner, n_dp)]
    act, slope, wu = feed_up(place, low, turned, up_bias, up_pieces)
    layer_out, output, second_grad, down_grad, second_sums, wd = feed_down(
        place, act, unit, cotangent, w_down, vectors, down_pieces
    )

    feed_keep, feed_send, up_sums, normed = feed_back(
        down_grad, low, wu, wd, slope, act, n_mp
    )
    dims = (4, n_mp, 2 * sub, width)
    feed_keep = feed_keep.reshape(dims)
    got = core_swap(feed_send.reshape(dims), n_dp)
    first_grad, context_grad, inner, wo_grad, first_sums = middle(
        normed, second_grad, unit, saved, context, full, vectors[1:2]
    )
    got, context_grad = lax.optimization_barrier((got, context_grad))
    feed_stay, feed_go = chip_sum(feed_keep, got)
    got = first_swap(feed_go, n_dp)
    dq, dk, dv, head_sums = attend_back(
        query, key, value, context_grad, saved, inner, segc, segr, feed_go
    )
    every = jnp.concatenate(
        [second_sums, first_sums, head_sums, up_sums.reshape(-1, width)]
    )
    vector_got = swap(every, "mp", 1, n_mp)
    heads_keep, heads_send = head_weights(
        place, dq, dk, dv, hidden_in, wo_grad, n_mp, every
    )
    got, vector_got, heads_keep = lax.optimization_barrier((got, vector_got, heads_keep))
    feed_own, feed_go = side_sum(feed_stay, got)
    every = every + vector_got
    got = second_swap(feed_go, n_dp)
    vector_got = swap(every, "mp", 2, n_mp)
    heads_got = core_swap(heads_send, n_dp)
    input_grad = input_gradient(dq, dk, dv, full, first_grad, heads_keep, feed_go, every)
    got, vector_got, heads_got, input_grad = lax.optimization_barrier(
        (got, vector_got, heads_got, input_grad)
    )
    heads_stay, heads_go = chip_sum(heads_keep, heads_got)
    heads_got = first_swap(heads_go, n_dp)
    feed_parts = add(feed_own, got)
    feed_got = exchange(feed_parts, "mp")
    every = every + vector_got
    up_sums = every[24:].reshape(2, 2, 8, 2, n_mp, sub)[:, :, 0]
    own_bias = jnp.concatenate(
        [
            lax.dynamic_slice_in_dim(every[16:18], shard * cut, cut, axis=1).reshape(-1),
            lax.dynamic_index_in_dim(up_sums, shard, 3, keepdims=False).reshape(-1),
        ]
    )
    every = jnp.concatenate(
        [every[0:3].reshape(-1), every[8:11].reshape(-1), turn(own_bias, "kg")]
    )
    vector_got = core_swap(every, n_dp)
    scores = score(
        layer_out, segr, query_lengths.reshape(-1, 1), passages, passage_index,
        every, feed_parts, heads_go,
    )
    heads_got, vector_got, scores = lax.optimization_barrier((heads_got, vector_got, scores))
    heads_own, heads_go = side_sum(heads_stay, heads_got)
    heads_got = second_swap(heads_go, n_dp)
    every = every + vector_got
    vector_got = swap(every, "dp", XBIT, n_dp)
    feed_got, heads_got, vector_got = lax.optimization_barrier(
        (feed_got, heads_got, vector_got)
    )
    heads_parts = add(heads_own, heads_got)
    heads_got = shard_swap(heads_parts, n_mp)
    heads_own = lax.dynamic_index_in_dim(heads_parts, shard, 0, keepdims=False)
    feed_total = shard_sum(feed_got[0], [feed_got[r] for r in range(1, n_mp)], n_dp)
    feed_mine = plane_gather(spread(feed_total, 4), n_dp)
    every = every + vector_got
    vector_got = swap(every, "dp", YBIT, n_dp)
    feed_mine, vector_got, *heads_got = lax.optimization_barrier(
        (feed_mine, vector_got, *heads_got)
    )
    heads_total = shard_sum(heads_own, heads_got, n_dp)
    heads_mine = plane_gather(spread(heads_total, 4), n_dp)
    feed_other = core_swap(feed_mine, n_dp)
    every = every + vector_got
    bit = 8
    while bit < n_dp:
        every = every + swap(every, "dp", bit, n_dp)
        bit *= 2
    w_up_grad, w_down_grad = finish_feed(place, (feed_mine, feed_other), heads_total)
    heads_other = core_swap(after(heads_mine, w_up_grad), n_dp)
    query_t, key_t, value_t, w_output_grad = finish_heads(place, (heads_mine, heads_other))
    second_sums, first_sums = every[: 3 * width].reshape(3, width), every[3 * width : 6 * width].reshape(3, width)
    shared = [first_sums[0], second_sums[0], first_sums[1], first_sums[2], second_sums[1], second_sums[2]]
    own_bias = every[6 * width :]
    return (
        output,
        scores,
        input_grad,
        query_t.T,
        key_t.T,
        value_t.T,
        w_output_grad,
        w_up_grad,
        w_down_grad,
        own_bias[:cut],
        own_bias[cut : 2 * cut],
        shared[0],
        own_bias[2 * cut :],
        shared[1],
        shared[2],
        shared[3],
        shared[4],
        shared[5],
    )


def solution(mesh):
    both, split = P(("dp", "mp"), None), P(None, "mp")
    return jax.shard_map(
        functools.partial(per_device, mesh.shape["dp"], mesh.shape["mp"]),
        mesh=mesh,
        in_specs=(both, both, both, both, P())
        + (split, split, split, P("mp", None), split, P("mp", None))
        + (P("mp"), P("mp"), P(), P("mp"), P(), P(), P(), P(), P()),
        out_specs=(both, both, both)
        + (split, split, split, P("mp", None), split, P("mp", None))
        + (P("mp"), P("mp"), P(), P("mp"), P(), P(), P(), P(), P()),
        check_vma=False,
    )
```

time: 369 us -> 331 us (0.90)
  starting transfers between devices: 86.7 us -> 59.3 us
  local copies, waits for them, and re-layouts: 27.7 us -> 16.3 us
  waiting for transfers between devices: 73.4 us -> 62.5 us
  other arithmetic: 13.9 us -> 20.4 us
  Pallas kernels: 160 us -> 166 us
    ppermute x98 -> x27, starting transfers between devices: 86.7 us -> 20.1 us  [swap(): return lax.ppermute(block, axis, [(i, i ^ bit) for i in range(size)])]
    ppermute x98 -> x27, waiting for transfers between devices: 73.4 us -> 19.8 us  [swap(): return lax.ppermute(block, axis, [(i, i ^ bit) for i in range(size)])]
    ppermute x0 -> x13, waiting for transfers between devices: none -> 25.6 us  [turn_swap(): lax.ppermute(block, 'dp', [(i, i ^ bits[i & 1]) for i in range(n_dp)])]
    all_to_all x0 -> x6, starting transfers between devices: none -> 24.3 us  [exchange(): lax.all_to_all(block, axis, 0, 0, axis_index_groups=groups, tiled=True)]
    all_to_all x0 -> x6, waiting for transfers between devices: none -> 17.1 us  [exchange(): lax.all_to_all(block, axis, 0, 0, axis_index_groups=groups, tiled=True)]
    unnamed x119 -> x113, local copies, waits for them, and re-layouts: 19.5 us -> 3.13 us
    ppermute x0 -> x13, starting transfers between devices: none -> 14.9 us  [turn_swap(): lax.ppermute(block, 'dp', [(i, i ^ bits[i & 1]) for i in range(n_dp)])]
    pallas_call x1, Pallas kernels: 29.9 us -> 23.1 us  [attend_back(): pl.pallas_call(attend_back_kernel, grid=(rows // BLOCK,), in_specs=[block...]
  transfers between devices with their start and end apart: 98 -> 46, of which waited for: 30 -> 16; matrix products, arithmetic and copies ran while one was open for 7% -> 5% of each run, Pallas kernels for 24% -> 36%
where the time goes in v2:
time: 331 us; the launch traced here: 327 us
  Pallas kernels  166 us (50%)
  waiting for transfers between devices  62.5 us (19%)
  starting transfers between devices  59.3 us (18%)
  other arithmetic  20.4 us (6%)
  local copies, waits for them, and re-layouts  16.3 us (5%)
    pallas_call x1, Pallas kernels, feed_back(): pl.pallas_call(feed_back_kernel, grid=(4,), in_specs=[full, full, weight,...  29.3 us
    ppermute x13, waiting for transfers between devices, turn_swap(): lax.ppermute(block, 'dp', [(i, i ^ bits[i & 1]) for i in range(n_dp)])  25.6 us
    all_to_all x6, starting transfers between devices, exchange(): lax.all_to_all(block, axis, 0, 0, axis_index_groups=groups, tiled=True)  24.3 us
    pallas_call x1, Pallas kernels, attend_back(): pl.pallas_call(attend_back_kernel, grid=(rows // BLOCK,), in_specs=[block...  23.1 us
    pallas_call x2, Pallas kernels, attend(): pl.pallas_call(functools.partial(attend_kernel, part), grid=(steps,), in_...  21.2 us
    ppermute x27, starting transfers between devices, swap(): return lax.ppermute(block, axis, [(i, i ^ bit) for i in range(size)])  20.1 us
    ppermute x27, waiting for transfers between devices, swap(): return lax.ppermute(block, axis, [(i, i ^ bit) for i in range(size)])  19.8 us
    all_to_all x6, waiting for transfers between devices, exchange(): lax.all_to_all(block, axis, 0, 0, axis_index_groups=groups, tiled=True)  17.1 us
  transfers between devices with their start and end apart: 46, of which 16 were waited for; matrix products, arithmetic and copies ran while one was open for 5% of the time, Pallas kernels for 36%

profile of v2, /device:TPU:0, one launch (start us, length us, event | category | flops | bytes accessed | tf_op | source)
XLA Modules:
  0.0 327.2 jit_solution(17446164736227492375)
XLA Ops:
  3.5 3.1 collective-permute-start
  9.5 3.2 piece_feed.1
  12.9 7.9 %collective-permute-done.1 = bf16[96,768]{1,0:T(8,128)(2,1)S(1)} collective-permute-done((bf16[96,768]{1,0:T(8,128)(2,1)}, bf16[96,768]{1,0:T(8,128)(2,1)S(1)}, u32[]{:S(2)}, u32[]{:S(2)}) %collective-permute-start.1) | collective-permute-done | bytes 147488 | tf_op jit(solution)/shard_map/ppermute | solution.py:65
  24.8 4.6 %all-to-all-start = ((bf16[4,96,768]{2,1,0:T(8,128)(2,1)}), bf16[4,96,768]{2,1,0:T(8,128)(2,1)S(1)}, u32[]{:S(2)}, u32[]{:S(2)}) async-start(bf16[4,96,768]{2,1,0:T(8,128)(2,1)} %broadcast_in_dim.36), calls=%async_computation | async-start | bytes 1179648 | tf_op jit(solution)/shard_map/all_to_all | solution.py:219
  32.9 5.4 %collective-permute-done.4.refs_2_ = bf16[288,768]{1,0:T(8,128)(2,1)S(1)} collective-permute-done((bf16[288,768]{1,0:T(8,128)(2,1)S(1)}, bf16[288,768]{1,0:T(8,128)(2,1)S(1)}, u32[]{:S(2)}, u32[]{:S(2)}) %collective-permute-start.4) | collective-permute-done | bytes 442400 | tf_op jit(solution)/shard_map/ppermute | solution.py:203
  38.3 4.7 %collective-permute-done.5.refs_3_ = bf16[288,768]{1,0:T(8,128)(2,1)S(1)} collective-permute-done((bf16[288,768]{1,0:T(8,128)(2,1)S(1)}, bf16[288,768]{1,0:T(8,128)(2,1)S(1)}, u32[]{:S(2)}, u32[]{:S(2)}) %collective-permute-start.5) | collective-permute-done | bytes 442400 | tf_op jit(solution)/shard_map/ppermute | solution.py:203
  44.7 4.6 %all-to-all-start.1 = ((f32[4,1,1152]{2,1,0:T(1,128)}), f32[4,1,1152]{2,1,0:T(1,128)S(1)}, u32[]{:S(2)}, u32[]{:S(2)}) async-start(f32[4,1,1152]{2,1,0:T(1,128)} %broadcast_in_dim.62), calls=%async_computation.1 | async-start | bytes 36864 | tf_op jit(solution)/shard_map/all_to_all | solution.py:219
  51.0 3.9 %all-to-all-done.1 = f32[4,1,1152]{2,1,0:T(1,128)S(1)} async-done(((f32[4,1,1152]{2,1,0:T(1,128)}), f32[4,1,1152]{2,1,0:T(1,128)S(1)}, u32[]{:S(2)}, u32[]{:S(2)}) %all-to-all-start.1) | async-done | bytes 18464 | tf_op jit(solution)/shard_map/all_to_all | solution.py:219
  57.1 4.0 %all-to-all-start.2 = ((bf16[4,96,768]{2,1,0:T(8,128)(2,1)}), bf16[4,96,768]{2,1,0:T(8,128)(2,1)S(1)}, u32[]{:S(2)}, u32[]{:S(2)}) async-start(bf16[4,96,768]{2,1,0:T(8,128)(2,1)} %broadcast_in_dim.63), calls=%async_computation.2 | async-start | bytes 1179648 | tf_op jit(solution)/shard_map/all_to_all | solution.py:219
  64.2 9.9 %project.1 = (bf16[1024,768]{1,0:T(8,128)(2,1)}, bf16[1024,768]{1,0:T(8,128)(2,1)}, bf16[1024,768]{1,0:T(8,128)(2,1)}, bf16[4,768,768]{2,1,0:T(8,128)(2,1)}) custom-call(s32[3]{0:T(128)} %pad_add_fusion.place, bf16[1024,768]{1,0:T(8,128)(2,1)} %x.7, bf16[192,768]{1,0:T(8,128)(2,1)} %bitcast.105, bf16[192,768]{1,0:T(8,128)(2,1)} %bitcast.107, ...), custom_call_target="tpu_custom_call" | custom-call | flops 49999998976 | bytes 150000000 | tf_op jit(solution)/shard_map/project/pallas_call | solution.py:318
  79.4 10.6 %attend.2 = (bf16[1024,768]{1,0:T(8,128)(2,1)}, f32[1024,128]{1,0:T(8,128)}, f32[1024,768]{1,0:T(8,128)}, bf16[1024,768]{1,0:T(8,128)(2,1)}) custom-call(bf16[1024,768]{1,0:T(8,128)(2,1)} %get-tuple-element.116.q, bf16[1024,768]{1,0:T(8,128)(2,1)} %get-tuple-element.117.k, bf16[1024,768]{1,0:T(8,128)(2,1)} %get-tuple-element.118.v, s32[1024,1]{1,0:T(8,128)} %copy.73.segc, ...), custom_call_target="tpu_custom_call" | custom-call | flops 40000000000 | bytes 120000000 | tf_op jit(solution)/shard_map/attend/pallas_call | solution.py:403
  94.5 10.6 %attend.3 = (bf16[1024,768]{1,0:T(8,128)(2,1)}, f32[1024,128]{1,0:T(8,128)}, f32[1024,768]{1,0:T(8,128)}, bf16[1024,768]{1,0:T(8,128)(2,1)}) custom-call(bf16[1024,768]{1,0:T(8,128)(2,1)} %get-tuple-element.116.q, bf16[1024,768]{1,0:T(8,128)(2,1)} %get-tuple-element.117.k, ...), custom_call_target="tpu_custom_call", output_to_operand_aliasing={{0}: (10, {}), {1}: (11, {}), {2}: (12, {}), {3}: (13, {})} | custom-call | flops 40000000000 | bytes 120000000 | tf_op jit(solution)/shard_map/attend/pallas_call | solution.py:403
  106.7 14.7 %feed_up.1 = (bf16[1024,3072]{1,0:T(8,128)(2,1)}, bf16[1024,3072]{1,0:T(8,128)(2,1)}, bf16[3072,768]{1,0:T(8,128)(2,1)}) custom-call(s32[3]{0:T(128)} %pad_add_fusion.place, bf16[1024,768]{1,0:T(8,128)(2,1)} %get-tuple-element.130.x, bf16[768,768]{1,0:T(8,128)(2,1)} %get-tuple-element.131.own, f32[1,3072]{1,0:T(1,128)} %reshape.306.bu, ...), custom_call_target="tpu_custom_call" | custom-call | flops 60000002048 | bytes 180000000 | tf_op jit(solution)/shard_map/feed_up/pallas_call | solution.py:543
  122.3 14.9 %feed_down.1 = (f32[1024,768]{1,0:T(8,128)}, bf16[1024,768]{1,0:T(8,128)(2,1)}, f32[1024,768]{1,0:T(8,128)}, bf16[1024,768]{1,0:T(8,128)(2,1)}, f32[8,768]{1,0:T(8,128)}, /*index=5*/bf16[3072,768]{1,0:T(8,128)(2,1)}) custom-call(s32[3]{0:T(128)} %pad_add_fusion.place, bf16[1024,3072]{1,0:T(8,128)(2,1)} %get-tuple-element.134.act, ...), custom_call_target="tpu_custom_call" | custom-call | flops 65000001536 | bytes 195000000 | tf_op jit(solution)/shard_map/feed_down/pallas_call | solution.py:597
  137.2 29.3 %feed_back.1 = (bf16[4,4,2,96,768]{4,3,2,1,0:T(8,128)(2,1)}, bf16[4,4,2,96,768]{4,3,2,1,0:T(8,128)(2,1)}, f32[4,8,768]{2,1,0:T(8,128)}, f32[1024,768]{1,0:T(8,128)}) custom-call(bf16[1024,768]{1,0:T(8,128)(2,1)} %get-tuple-element.139.grad, bf16[1024,768]{1,0:T(8,128)(2,1)} %get-tuple-element.130.x, bf16[3072,768]{1,0:T(8,128)(2,1)} %get-tuple-element.140.wu, ...), custom_call_target="tpu_custom_call" | custom-call | flops 134999998464 | bytes 405000000 | tf_op jit(solution)/shard_map/feed_back/pallas_call | solution.py:660
  167.0 12.5 %middle.1 = (f32[1024,768]{1,0:T(8,128)}, bf16[1024,768]{1,0:T(8,128)(2,1)}, f32[1024,128]{1,0:T(8,128)}, bf16[768,768]{1,0:T(8,128)(2,1)}, f32[8,768]{1,0:T(8,128)}) custom-call(f32[1024,768]{1,0:T(8,128)} %get-tuple-element.145.normed, f32[1024,768]{1,0:T(8,128)} %get-tuple-element.146.second, f32[1024,768]{1,0:T(8,128)} %get-tuple-element.135.unit, ...), custom_call_target="tpu_custom_call" | custom-call | flops 40000000000 | bytes 120000000 | tf_op jit(solution)/shard_map/middle/pallas_call | solution.py:728
  179.5 5.7 %add_convert_fusion.1 = (bf16[2,4,192,768]{3,2,1,0:T(8,128)(2,1)}, bf16[2,4,192,768]{3,2,1,0:T(8,128)(2,1)}) fusion(bf16[4,4,192,768]{3,2,1,0:T(8,128)(2,1)} %collective-permute-done.24, bf16[4,4,192,768]{3,2,1,0:T(8,128)(2,1)} %bitcast.87), kind=kLoop, calls=%fused_computation.1 | loop fusion | flops 9437184 | bytes 14155776 | tf_op jit(solution)/shard_map/convert_element_type | solution.py:234
  186.0 23.1 %attend_back.1 = (bf16[1024,768]{1,0:T(8,128)(2,1)}, bf16[1024,768]{1,0:T(8,128)(2,1)}, bf16[1024,768]{1,0:T(8,128)(2,1)}, f32[8,768]{1,0:T(8,128)}) custom-call(bf16[1024,768]{1,0:T(8,128)(2,1)} %get-tuple-element.116.q, bf16[1024,768]{1,0:T(8,128)(2,1)} %get-tuple-element.117.k, bf16[1024,768]{1,0:T(8,128)(2,1)} %get-tuple-element.118.v, ...), custom_call_target="tpu_custom_call" | custom-call | flops 109999996928 | bytes 330000000 | tf_op jit(solution)/shard_map/attend_back/pallas_call | solution.py:481
  212.0 10.7 %head_weights.1 = (bf16[4,4,2,3,16,768]{5,4,3,2,1,0:T(8,128)(2,1)}, bf16[4,4,2,3,16,768]{5,4,3,2,1,0:T(8,128)(2,1)}) custom-call(s32[3]{0:T(128)} %pad_add_fusion.place, bf16[1024,768]{1,0:T(8,128)(2,1)} %get-tuple-element.157.dq, bf16[1024,768]{1,0:T(8,128)(2,1)} %get-tuple-element.158.dk, bf16[1024,768]{1,0:T(8,128)(2,1)} %get-tuple-element.159.dv, ...), custom_call_target="tpu_custom_call" | custom-call | flops 40000000000 | bytes 120000000 | tf_op jit(solution)/shard_map/head_weights/pallas_call | solution.py:782
  228.4 9.0 %input_gradient.1 = f32[1024,768]{1,0:T(8,128)} custom-call(bf16[1024,768]{1,0:T(8,128)(2,1)} %get-tuple-element.157.dq, bf16[1024,768]{1,0:T(8,128)(2,1)} %get-tuple-element.158.dk, bf16[1024,768]{1,0:T(8,128)(2,1)} %get-tuple-element.159.dv, bf16[4,768,768]{2,1,0:T(8,128)(2,1)} %get-tuple-element.119.wo.full, f32[1024,768]{1,0:T(8,128)} %get-tuple-element.166.first, ...), custom_call_target="tpu_custom_call" | custom-call | flops 30000001024 | bytes 90000000 | tf_op jit(solution)/shard_map/input_gradient/pallas_call | solution.py:807
  237.4 5.8 %collective-permute-done.27 = bf16[4,192,768]{2,1,0:T(8,128)(2,1)} collective-permute-done((bf16[4,192,768]{2,1,0:T(8,128)(2,1)S(1)}, bf16[4,192,768]{2,1,0:T(8,128)(2,1)}, u32[]{:S(2)}, u32[]{:S(2)}) %collective-permute-start.27) | collective-permute-done | bytes 1179680 | tf_op jit(solution)/shard_map/ppermute | solution.py:203
  253.8 3.8 %all-to-all-start.3 = ((bf16[4,192,768]{2,1,0:T(8,128)(2,1)}), bf16[4,192,768]{2,1,0:T(8,128)(2,1)S(1)}, u32[]{:S(2)}, u32[]{:S(2)}) async-start(bf16[4,192,768]{2,1,0:T(8,128)(2,1)} %fusion.refs_1_), calls=%async_computation.3 | async-start | bytes 2359296 | tf_op jit(solution)/shard_map/all_to_all | solution.py:219
  257.6 7.6 %score.1 = f32[32,32]{1,0:T(8,128)} custom-call(f32[1024,768]{1,0:T(8,128)} %get-tuple-element.169.out_ref, s32[1,1024]{1,0:T(1,128)} %bitcast.99, s32[32,1]{1,0:T(8,128)} %copy-done.18, bf16[1024,768]{1,0:T(8,128)(2,1)} %table_ref.1, s32[32,32]{1,0:T(8,128)} %pick_ref.1, f32[5760]{0:T(1024)} %concatenate.24.refs_0_, bf16[4,192,768]{2,1,0:T(8,128)(2,1)} %fusion.refs_1_, ...), custom_call_target="tpu_custom_call" | custom-call | flops 40000000000 | bytes 120000000 | tf_op jit(solution)/shard_map/score/pallas_call | solution.py:855
  265.2 3.4 %collective-permute-done.30 = bf16[2,4,96,768]{3,2,1,0:T(8,128)(2,1)} collective-permute-done((bf16[2,4,96,768]{3,2,1,0:T(8,128)(2,1)S(1)}, bf16[2,4,96,768]{3,2,1,0:T(8,128)(2,1)}, u32[]{:S(2)}, u32[]{:S(2)}) %collective-permute-start.30) | collective-permute-done | bytes 1179680 | tf_op jit(solution)/shard_map/ppermute | solution.py:203
  272.7 3.6 %collective-permute-done.33 = f32[5760]{0:T(1024)S(1)} collective-permute-done((f32[5760]{0:T(1024)S(1)}, f32[5760]{0:T(1024)S(1)}, u32[]{:S(2)}, u32[]{:S(2)}) %collective-permute-start.33) | collective-permute-done | bytes 23072 | tf_op jit(solution)/shard_map/ppermute | solution.py:65
  276.3 3.4 %collective-permute-done.32 = bf16[4,96,768]{2,1,0:T(8,128)(2,1)S(1)} collective-permute-done((bf16[4,96,768]{2,1,0:T(8,128)(2,1)S(1)}, bf16[4,96,768]{2,1,0:T(8,128)(2,1)S(1)}, u32[]{:S(2)}, u32[]{:S(2)}) %collective-permute-start.32) | collective-permute-done | bytes 589856 | tf_op jit(solution)/shard_map/ppermute | solution.py:203
  279.8 7.0 %all-to-all-done.3 = bf16[4,192,768]{2,1,0:T(8,128)(2,1)S(1)} async-done(((bf16[4,192,768]{2,1,0:T(8,128)(2,1)}), bf16[4,192,768]{2,1,0:T(8,128)(2,1)S(1)}, u32[]{:S(2)}, u32[]{:S(2)}) %all-to-all-start.3) | async-done | bytes 1179680 | tf_op jit(solution)/shard_map/all_to_all | solution.py:219
  288.0 3.5 %all-to-all-start.4 = ((bf16[4,192,768]{2,1,0:T(8,128)(2,1)}), bf16[4,192,768]{2,1,0:T(8,128)(2,1)S(1)}, u32[]{:S(2)}, u32[]{:S(2)}) async-start(bf16[4,192,768]{2,1,0:T(8,128)(2,1)} %broadcast_in_dim.65), calls=%async_computation.4 | async-start | bytes 2359296 | tf_op jit(solution)/shard_map/all_to_all | solution.py:219
  299.4 7.6 %collective-permute-done.34 = f32[5760]{0:T(1024)S(1)} collective-permute-done((f32[5760]{0:T(1024)S(1)}, f32[5760]{0:T(1024)S(1)}, u32[]{:S(2)}, u32[]{:S(2)}) %collective-permute-start.34) | collective-permute-done | bytes 23072 | tf_op jit(solution)/shard_map/ppermute | solution.py:65
  308.3 3.9 %all-to-all-start.5 = ((bf16[4,96,768]{2,1,0:T(8,128)(2,1)}), bf16[4,96,768]{2,1,0:T(8,128)(2,1)S(1)}, u32[]{:S(2)}, u32[]{:S(2)}) async-start(bf16[4,96,768]{2,1,0:T(8,128)(2,1)} %broadcast_in_dim.66), calls=%async_computation.5 | async-start | bytes 1179648 | tf_op jit(solution)/shard_map/all_to_all | solution.py:219
  312.2 4.7 %finish_feed.1 = (f32[768,768]{1,0:T(8,128)}, f32[768,768]{1,0:T(8,128)}) custom-call(s32[3]{0:T(128)} %pad_add_fusion.place, bf16[4,192,768]{2,1,0:T(8,128)(2,1)} %copy-done.3, bf16[4,192,768]{2,1,0:T(8,128)(2,1)} %collective-permute-done.38.other, bf16[96,768]{1,0:T(8,128)(2,1)} %copy-done.6), custom_call_target="tpu_custom_call" | custom-call | flops 30000001024 | bytes 90000000 | tf_op jit(solution)/shard_map/finish_feed/pallas_call | solution.py:151
  316.9 4.4 %all-to-all-done.5.mine = bf16[4,96,768]{2,1,0:T(8,128)(2,1)S(1)} async-done(((bf16[4,96,768]{2,1,0:T(8,128)(2,1)}), bf16[4,96,768]{2,1,0:T(8,128)(2,1)S(1)}, u32[]{:S(2)}, u32[]{:S(2)}) %all-to-all-start.5) | async-done | bytes 589856 | tf_op jit(solution)/shard_map/all_to_all | solution.py:219
  (278 shorter events, 74.2 us)
Async XLA Ops:
  6.6 14.2 %collective-permute-start.1 = (bf16[96,768]{1,0:T(8,128)(2,1)}, bf16[96,768]{1,0:T(8,128)(2,1)S(1)}, u32[]{:S(2)}, u32[]{:S(2)}) collective-permute-start(bf16[96,768]{1,0:T(8,128)(2,1)} %bitcast.111), channel_id=1, source_target_pairs={{0,2},{1,3},{2,0},{3,1},{4,6},{5,7},{6,4},{7,5},{8,10},{9,11},{10,... | collective-permute-start | bytes 442376 | tf_op jit(solution)/shard_map/ppermute | solution.py:65
  24.8 19.3 %all-to-all-start = ((bf16[4,96,768]{2,1,0:T(8,128)(2,1)}), bf16[4,96,768]{2,1,0:T(8,128)(2,1)S(1)}, u32[]{:S(2)}, u32[]{:S(2)}) async-start(bf16[4,96,768]{2,1,0:T(8,128)(2,1)} %broadcast_in_dim.36), calls=%async_computation | async-start | bytes 1179648 | tf_op jit(solution)/shard_map/all_to_all | solution.py:219
  31.5 30.5 %collective-permute-start.6 = (bf16[288,768]{1,0:T(8,128)(2,1)S(1)}, bf16[288,768]{1,0:T(8,128)(2,1)S(1)}, u32[]{:S(2)}, u32[]{:S(2)}) collective-permute-start(bf16[288,768]{1,0:T(8,128)(2,1)S(1)} %constant_dynamic-update-slice_fusion.refs_0_), channel_id=1, source_target_pairs={{0,4},{4,0},{8,12},{12,8},{16,20},{20,16},{24,28},{28,24},{1,5},{5... | collective-permute-start | bytes 1327112 | tf_op jit(solution)/shard_map/ppermute | solution.py:65
  32.6 29.3 %collective-permute-start.7 = (bf16[288,768]{1,0:T(8,128)(2,1)S(1)}, bf16[288,768]{1,0:T(8,128)(2,1)}, u32[]{:S(2)}, u32[]{:S(2)}) collective-permute-start(bf16[288,768]{1,0:T(8,128)(2,1)S(1)} %collective-permute-done.3.refs_1_), channel_id=1, source_target_pairs={{0,4},{4,0},{8,12},{12,8},{16,20},{20,16},{24,28},{28,24},{1,5},{5... | collective-permute-start | bytes 1327112 | tf_op jit(solution)/shard_map/ppermute | solution.py:65
  38.3 23.7 %collective-permute-start.8 = (bf16[288,768]{1,0:T(8,128)(2,1)S(1)}, bf16[288,768]{1,0:T(8,128)(2,1)}, u32[]{:S(2)}, u32[]{:S(2)}) collective-permute-start(bf16[288,768]{1,0:T(8,128)(2,1)S(1)} %collective-permute-done.4.refs_2_), channel_id=1, source_target_pairs={{0,4},{4,0},{8,12},{12,8},{16,20},{20,16},{24,28},{28,24},{1,5},{5... | collective-permute-start | bytes 1327112 | tf_op jit(solution)/shard_map/ppermute | solution.py:65
  43.0 18.9 %collective-permute-start.9 = (bf16[288,768]{1,0:T(8,128)(2,1)S(1)}, bf16[288,768]{1,0:T(8,128)(2,1)}, u32[]{:S(2)}, u32[]{:S(2)}) collective-permute-start(bf16[288,768]{1,0:T(8,128)(2,1)S(1)} %collective-permute-done.5.refs_3_), channel_id=1, source_target_pairs={{0,4},{4,0},{8,12},{12,8},{16,20},{20,16},{24,28},{28,24},{1,5},{5... | collective-permute-start | bytes 1327112 | tf_op jit(solution)/shard_map/ppermute | solution.py:65
  57.1 19.4 %all-to-all-start.2 = ((bf16[4,96,768]{2,1,0:T(8,128)(2,1)}), bf16[4,96,768]{2,1,0:T(8,128)(2,1)S(1)}, u32[]{:S(2)}, u32[]{:S(2)}) async-start(bf16[4,96,768]{2,1,0:T(8,128)(2,1)} %broadcast_in_dim.63), calls=%async_computation.2 | async-start | bytes 1179648 | tf_op jit(solution)/shard_map/all_to_all | solution.py:219
  62.1 12.5 %collective-permute-start.10 = (bf16[288,768]{1,0:T(8,128)(2,1)S(1)}, bf16[288,768]{1,0:T(8,128)(2,1)S(1)}, u32[]{:S(2)}, u32[]{:S(2)}) collective-permute-start(bf16[288,768]{1,0:T(8,128)(2,1)S(1)} %pad_maximum_fusion.refs_8_.refs_0_), channel_id=1, source_target_pairs={{0,8},{4,20},{8,0},{12,28},{16,24},{20,4},{24,16},{28,12},{1,9},{5... | collective-permute-start | bytes 1327112 | tf_op jit(solution)/shard_map/ppermute | solution.py:203
  62.7 12.6 %collective-permute-start.11 = (bf16[288,768]{1,0:T(8,128)(2,1)S(1)}, bf16[288,768]{1,0:T(8,128)(2,1)S(1)}, u32[]{:S(2)}, u32[]{:S(2)}) collective-permute-start(bf16[288,768]{1,0:T(8,128)(2,1)S(1)} %pad_maximum_fusion.refs_8_.refs_0_), channel_id=1, source_target_pairs={{0,16},{4,12},{8,24},{12,4},{16,0},{20,28},{24,8},{28,20},{1,17},{... | collective-permute-start | bytes 1327112 | tf_op jit(solution)/shard_map/ppermute | solution.py:203
  64.2 41.1 %collective-permute-start.16 = (bf16[288,768]{1,0:T(8,128)(2,1)S(1)}, bf16[288,768]{1,0:T(8,128)(2,1)}, u32[]{:S(2)}, u32[]{:S(2)}) collective-permute-start(bf16[288,768]{1,0:T(8,128)(2,1)S(1)} %pad_maximum_fusion.refs_8_.refs_0_), channel_id=1, source_target_pairs={{0,4},{4,0},{8,12},{12,8},{16,20},{20,16},{24,28},{28,24},{1,5},{5... | collective-permute-start | bytes 1327112 | tf_op jit(solution)/shard_map/ppermute | solution.py:65
  76.6 13.5 %collective-permute-start.13 = (bf16[288,768]{1,0:T(8,128)(2,1)S(1)}, bf16[288,768]{1,0:T(8,128)(2,1)S(1)}, u32[]{:S(2)}, u32[]{:S(2)}) collective-permute-start(bf16[288,768]{1,0:T(8,128)(2,1)S(1)} %pad_maximum_fusion.1.refs_0_), channel_id=1, source_target_pairs={{0,8},{4,20},{8,0},{12,28},{16,24},{20,4},{24,16},{28,12},{1,9},{5... | collective-permute-start | bytes 1327112 | tf_op jit(solution)/shard_map/ppermute | solution.py:203
  77.4 13.3 %collective-permute-start.14 = (bf16[288,768]{1,0:T(8,128)(2,1)S(1)}, bf16[288,768]{1,0:T(8,128)(2,1)S(1)}, u32[]{:S(2)}, u32[]{:S(2)}) collective-permute-start(bf16[288,768]{1,0:T(8,128)(2,1)S(1)} %pad_maximum_fusion.1.refs_0_), channel_id=1, source_target_pairs={{0,16},{4,12},{8,24},{12,4},{16,0},{20,28},{24,8},{28,20},{1,17},{... | collective-permute-start | bytes 1327112 | tf_op jit(solution)/shard_map/ppermute | solution.py:203
  78.7 14.5 %collective-permute-start.12 = (bf16[288,768]{1,0:T(8,128)(2,1)}, bf16[288,768]{1,0:T(8,128)(2,1)S(1)}, u32[]{:S(2)}, u32[]{:S(2)}) collective-permute-start(bf16[288,768]{1,0:T(8,128)(2,1)} %copy-done.44), channel_id=1, source_target_pairs={{0,16},{4,12},{8,24},{12,4},{16,0},{20,28},{24,8},{28,20},{1,17},{... | collective-permute-start | bytes 1327112 | tf_op jit(solution)/shard_map/ppermute | solution.py:203
  79.4 26.3 %collective-permute-start.17 = (bf16[288,768]{1,0:T(8,128)(2,1)}, bf16[288,768]{1,0:T(8,128)(2,1)S(1)}, u32[]{:S(2)}, u32[]{:S(2)}) collective-permute-start(bf16[288,768]{1,0:T(8,128)(2,1)} %copy-done.44), channel_id=1, source_target_pairs={{0,4},{4,0},{8,12},{12,8},{16,20},{20,16},{24,28},{28,24},{1,5},{5... | collective-permute-start | bytes 1327112 | tf_op jit(solution)/shard_map/ppermute | solution.py:65
  90.1 15.8 %collective-permute-start.18 = (bf16[288,768]{1,0:T(8,128)(2,1)S(1)}, bf16[288,768]{1,0:T(8,128)(2,1)S(1)}, u32[]{:S(2)}, u32[]{:S(2)}) collective-permute-start(bf16[288,768]{1,0:T(8,128)(2,1)S(1)} %copy-done.46), channel_id=1, source_target_pairs={{0,4},{4,0},{8,12},{12,8},{16,20},{20,16},{24,28},{28,24},{1,5},{5... | collective-permute-start | bytes 1327112 | tf_op jit(solution)/shard_map/ppermute | solution.py:65
  105.1 16.2 %collective-permute-start.20 = (bf16[288,768]{1,0:T(8,128)(2,1)S(1)}, bf16[288,768]{1,0:T(8,128)(2,1)}, u32[]{:S(2)}, u32[]{:S(2)}) collective-permute-start(bf16[288,768]{1,0:T(8,128)(2,1)S(1)} %copy-done.9), channel_id=1, source_target_pairs={{0,4},{4,0},{8,12},{12,8},{16,20},{20,16},{24,28},{28,24},{1,5},{5... | collective-permute-start | bytes 1327112 | tf_op jit(solution)/shard_map/ppermute | solution.py:65
  105.3 16.1 %collective-permute-start.21 = (bf16[288,768]{1,0:T(8,128)(2,1)S(1)}, bf16[288,768]{1,0:T(8,128)(2,1)S(1)}, u32[]{:S(2)}, u32[]{:S(2)}) collective-permute-start(bf16[288,768]{1,0:T(8,128)(2,1)S(1)} %collective-permute-done.13.refs_1_), channel_id=1, source_target_pairs={{0,4},{4,0},{8,12},{12,8},{16,20},{20,16},{24,28},{28,24},{1,5},{5... | collective-permute-start | bytes 1327112 | tf_op jit(solution)/shard_map/ppermute | solution.py:65
  105.7 15.7 %collective-permute-start.22 = (bf16[288,768]{1,0:T(8,128)(2,1)S(1)}, bf16[288,768]{1,0:T(8,128)(2,1)}, u32[]{:S(2)}, u32[]{:S(2)}) collective-permute-start(bf16[288,768]{1,0:T(8,128)(2,1)S(1)} %collective-permute-done.14.refs_2_), channel_id=1, source_target_pairs={{0,4},{4,0},{8,12},{12,8},{16,20},{20,16},{24,28},{28,24},{1,5},{5... | collective-permute-start | bytes 1327112 | tf_op jit(solution)/shard_map/ppermute | solution.py:65
  105.9 15.5 %collective-permute-start.23 = (bf16[288,768]{1,0:T(8,128)(2,1)S(1)}, bf16[288,768]{1,0:T(8,128)(2,1)S(1)}, u32[]{:S(2)}, u32[]{:S(2)}) collective-permute-start(bf16[288,768]{1,0:T(8,128)(2,1)S(1)} %collective-permute-done.15.refs_3_), channel_id=1, source_target_pairs={{0,4},{4,0},{8,12},{12,8},{16,20},{20,16},{24,28},{28,24},{1,5},{5... | collective-permute-start | bytes 1327112 | tf_op jit(solution)/shard_map/ppermute | solution.py:65
  166.5 13.0 %collective-permute-start.24 = (bf16[4,4,192,768]{3,2,1,0:T(8,128)(2,1)}, bf16[4,4,192,768]{3,2,1,0:T(8,128)(2,1)}, u32[]{:S(2)}, u32[]{:S(2)}) collective-permute-start(bf16[4,4,192,768]{3,2,1,0:T(8,128)(2,1)} %bitcast.102), channel_id=1, source_target_pairs={{0,4},{4,0},{8,12},{12,8},{16,20},{20,16},{24,28},{28,24},{1,5},{5... | collective-permute-start | bytes 14155784 | tf_op jit(solution)/shard_map/ppermute | solution.py:65
  185.2 37.5 %collective-permute-start.25 = (bf16[2,4,192,768]{3,2,1,0:T(8,128)(2,1)}, bf16[2,4,192,768]{3,2,1,0:T(8,128)(2,1)}, u32[]{:S(2)}, u32[]{:S(2)}) collective-permute-start(bf16[2,4,192,768]{3,2,1,0:T(8,128)(2,1)} %get-tuple-element.194.refs_0_), channel_id=1, source_target_pairs={{0,8},{4,20},{8,0},{12,28},{16,24},{20,4},{24,16},{28,12},{1,9},{5... | collective-permute-start | bytes 7077896 | tf_op jit(solution)/shard_map/ppermute | solution.py:203
  210.0 12.8 %collective-permute-start.26 = (f32[56,768]{1,0:T(8,128)S(1)}, f32[56,768]{1,0:T(8,128)S(1)}, u32[]{:S(2)}, u32[]{:S(2)}) collective-permute-start(f32[56,768]{1,0:T(8,128)S(1)} %pad_maximum_fusion.2.refs_0_), channel_id=1, source_target_pairs={{0,1},{1,0},{2,3},{3,2},{4,5},{5,4},{6,7},{7,6},{8,9},{9,8},{10,11... | collective-permute-start | bytes 516104 | tf_op jit(solution)/shard_map/ppermute | solution.py:65
  222.7 14.6 %collective-permute-start.29 = (bf16[4,4,96,768]{3,2,1,0:T(8,128)(2,1)}, bf16[4,4,96,768]{3,2,1,0:T(8,128)(2,1)}, u32[]{:S(2)}, u32[]{:S(2)}) collective-permute-start(bf16[4,4,96,768]{3,2,1,0:T(8,128)(2,1)} %bitcast.103), channel_id=1, source_target_pairs={{0,4},{4,0},{8,12},{12,8},{16,20},{20,16},{24,28},{28,24},{1,5},{5... | collective-permute-start | bytes 7077896 | tf_op jit(solution)/shard_map/ppermute | solution.py:65
  222.8 14.6 %collective-permute-start.28 = (f32[56,768]{1,0:T(8,128)S(1)}, f32[56,768]{1,0:T(8,128)S(1)}, u32[]{:S(2)}, u32[]{:S(2)}) collective-permute-start(f32[56,768]{1,0:T(8,128)S(1)} %fusion.19.refs_2_), channel_id=1, source_target_pairs={{0,2},{1,3},{2,0},{3,1},{4,6},{5,7},{6,4},{7,5},{8,10},{9,11},{10,... | collective-permute-start | bytes 516104 | tf_op jit(solution)/shard_map/ppermute | solution.py:65
  226.8 16.4 %collective-permute-start.27 = (bf16[4,192,768]{2,1,0:T(8,128)(2,1)S(1)}, bf16[4,192,768]{2,1,0:T(8,128)(2,1)}, u32[]{:S(2)}, u32[]{:S(2)}) collective-permute-start(bf16[4,192,768]{2,1,0:T(8,128)(2,1)S(1)} %fusion.1.refs_1_), channel_id=1, source_target_pairs={{0,16},{4,12},{8,24},{12,4},{16,0},{20,28},{24,8},{28,20},{1,17},{... | collective-permute-start | bytes 3538952 | tf_op jit(solution)/shard_map/ppermute | solution.py:203
  252.3 12.9 %collective-permute-start.31 = (f32[5760]{0:T(1024)}, f32[5760]{0:T(1024)}, u32[]{:S(2)}, u32[]{:S(2)}) collective-permute-start(f32[5760]{0:T(1024)} %concatenate.24.refs_0_), channel_id=1, source_target_pairs={{0,4},{4,0},{8,12},{12,8},{16,20},{20,16},{24,28},{28,24},{1,5},{5... | collective-permute-start | bytes 69128 | tf_op jit(solution)/shard_map/ppermute | solution.py:65
  252.3 16.3 %collective-permute-start.30 = (bf16[2,4,96,768]{3,2,1,0:T(8,128)(2,1)S(1)}, bf16[2,4,96,768]{3,2,1,0:T(8,128)(2,1)}, u32[]{:S(2)}, u32[]{:S(2)}) collective-permute-start(bf16[2,4,96,768]{3,2,1,0:T(8,128)(2,1)S(1)} %get-tuple-element.197.refs_2_), channel_id=1, source_target_pairs={{0,8},{4,20},{8,0},{12,28},{16,24},{20,4},{24,16},{28,12},{1,9},{5... | collective-permute-start | bytes 3538952 | tf_op jit(solution)/shard_map/ppermute | solution.py:203
  253.8 33.0 %all-to-all-start.3 = ((bf16[4,192,768]{2,1,0:T(8,128)(2,1)}), bf16[4,192,768]{2,1,0:T(8,128)(2,1)S(1)}, u32[]{:S(2)}, u32[]{:S(2)}) async-start(bf16[4,192,768]{2,1,0:T(8,128)(2,1)} %fusion.refs_1_), calls=%async_computation.3 | async-start | bytes 2359296 | tf_op jit(solution)/shard_map/all_to_all | solution.py:219
  288.0 19.0 %all-to-all-start.4 = ((bf16[4,192,768]{2,1,0:T(8,128)(2,1)}), bf16[4,192,768]{2,1,0:T(8,128)(2,1)S(1)}, u32[]{:S(2)}, u32[]{:S(2)}) async-start(bf16[4,192,768]{2,1,0:T(8,128)(2,1)} %broadcast_in_dim.65), calls=%async_computation.4 | async-start | bytes 2359296 | tf_op jit(solution)/shard_map/all_to_all | solution.py:219
  292.9 14.1 %collective-permute-start.35 = (bf16[96,768]{1,0:T(8,128)(2,1)S(1)}, bf16[96,768]{1,0:T(8,128)(2,1)S(1)}, u32[]{:S(2)}, u32[]{:S(2)}) collective-permute-start(bf16[96,768]{1,0:T(8,128)(2,1)S(1)} %get-tuple-element.200), channel_id=1, source_target_pairs={{0,1},{1,0},{2,3},{3,2},{4,5},{5,4},{6,7},{7,6},{8,9},{9,8},{10,11... | collective-permute-start | bytes 442376 | tf_op jit(solution)/shard_map/ppermute | solution.py:65
  293.0 14.0 %collective-permute-start.36 = (bf16[96,768]{1,0:T(8,128)(2,1)S(1)}, bf16[96,768]{1,0:T(8,128)(2,1)S(1)}, u32[]{:S(2)}, u32[]{:S(2)}) collective-permute-start(bf16[96,768]{1,0:T(8,128)(2,1)S(1)} %get-tuple-element.199), channel_id=1, source_target_pairs={{0,2},{1,3},{2,0},{3,1},{4,6},{5,7},{6,4},{7,5},{8,10},{9,11},{10,... | collective-permute-start | bytes 442376 | tf_op jit(solution)/shard_map/ppermute | solution.py:65
  308.3 13.0 %all-to-all-start.5 = ((bf16[4,96,768]{2,1,0:T(8,128)(2,1)}), bf16[4,96,768]{2,1,0:T(8,128)(2,1)S(1)}, u32[]{:S(2)}, u32[]{:S(2)}) async-start(bf16[4,96,768]{2,1,0:T(8,128)(2,1)} %broadcast_in_dim.66), calls=%async_computation.5 | async-start | bytes 1179648 | tf_op jit(solution)/shard_map/all_to_all | solution.py:219
  (69 other events, 807.8 us)

commit v3 on v2

--- a/solution.py
+++ b/solution.py
@@ -77,7 +77,7 @@
 
 def piece_heads_kernel(place, wq, wk, wv, wo, piece, sems):
     core, plane = place[0], place[1]
-    heads = piece.shape[1]
+    heads = piece.shape[0] // (2 * GRAIN)
     for side, pair in enumerate(((wq, wk), (wv, wo))):
 
         @pl.when(core == side)
@@ -86,9 +86,12 @@
             for t, ref in enumerate(pair):
                 for h in range(heads):
                     start = pl.multiple_of(h * HEAD_DIM + plane * GRAIN, GRAIN)
+                    to = (t * heads + h) * GRAIN
                     copies.append(
                         pltpu.make_async_copy(
-                            ref.at[pl.ds(start, GRAIN), :], piece.at[t, h], sems.at[t * heads + h]
+                            ref.at[pl.ds(start, GRAIN), :],
+                            piece.at[to : to + GRAIN, :],
+                            sems.at[t * heads + h],
                         )
                     )
             for copy in copies:
@@ -104,35 +107,41 @@
         piece_heads_kernel,
         in_specs=[scalar_spec()] + [token_spec()] * 4,
         out_specs=held_spec(),
-        out_shape=shape((2, heads, GRAIN, width), BF),
+        out_shape=shape((2 * heads * GRAIN, width), BF),
         scratch_shapes=[pltpu.SemaphoreType.DMA((2 * heads,))],
         compiler_params=params(),
         cost_estimate=cost(1),
         name="piece_heads",
-    )(place, *weights).reshape(2 * heads * GRAIN, width)
-
-
-def piece_feed_kernel(place, wu, wd, turned, piece_up, piece_down):
+    )(place, *weights)
+
+
+def piece_feed_kernel(place, wu, wd, rest, turned, piece_up, piece_down):
     core, plane = place[0], place[1]
-    sub = piece_up.shape[0]
+    sub = piece_down.shape[1]
     turned[...] = wu[...].astype(F32).T.astype(BF)
     start = pl.multiple_of((core * 4 + plane) * sub, GRAIN)
-    piece_up[...] = turned[pl.ds(start, sub), :]
-    piece_down[...] = wd[pl.ds(start, sub), :]
-
-
-def piece_feed(place, wu, wd):
+    for r in range(piece_up.shape[0]):
+        piece_up[r, :sub, :] = turned[pl.ds(start, sub), :]
+        piece_up[r, sub:, :] = rest[...]
+        piece_down[r] = wd[pl.ds(start, sub), :]
+
+
+def piece_feed(place, wu, wd, rest, n_mp):
     width, hidden = wu.shape
     sub = hidden // 8
     return pl.pallas_call(
         piece_feed_kernel,
-        in_specs=[scalar_spec()] + [held_spec()] * 2,
+        in_specs=[scalar_spec()] + [held_spec()] * 3,
         out_specs=[held_spec()] * 3,
-        out_shape=[shape((hidden, width), BF), shape((sub, width), BF), shape((sub, width), BF)],
+        out_shape=[
+            shape((hidden, width), BF),
+            shape((n_mp, sub + GRAIN, width), BF),
+            shape((n_mp, sub, width), BF),
+        ],
         compiler_params=params(),
         cost_estimate=cost(3),
         name="piece_feed",
-    )(place, wu, wd)
+    )(place, wu, wd, rest)
 
 
 def finish_feed_kernel(place, mine, other, up, down, held):
@@ -195,10 +204,6 @@
     )(place, *pieces)
 
 
-def shard_step(piece, n_mp):
-    return [swap(piece, "mp", r, n_mp) for r in range(1, n_mp)]
-
-
 def turn_swap(block, bits, n_dp):
     return lax.ppermute(block, "dp", [(i, i ^ bits[i & 1]) for i in range(n_dp)])
 
@@ -266,7 +271,8 @@
 
 
 def project_kernel(place, x, wq, wk, wv, wo, bq, bv, *refs):
-    pieces, (q, k, v, full, sems) = refs[:8], refs[-5:]
+    pieces, (q, k, v, out, full, sems, sem) = refs[:8], refs[-7:]
+    last = pltpu.make_async_copy(full, out, sem)
     core, plane, shard = place[0], place[1], place[2]
     heads = wq.shape[0] // HEAD_DIM
     shards = 1 + pieces[0].shape[0] // (2 * heads * GRAIN)
@@ -303,13 +309,18 @@
                             ]
         for copy in copies:
             copy.wait()
+        last.start()
 
     block = x[...]
-    for kind, (out, bias) in enumerate(((q, bq), (k, None), (v, bv))):
+    for kind, (into, bias) in enumerate(((q, bq), (k, None), (v, bv))):
         value = lax.dot_general(block, full[kind], NT, preferred_element_type=F32)
         if bias is not None:
             value = value + bias[...]
-        out[...] = value.astype(BF)
+        into[...] = value.astype(BF)
+
+    @pl.when(pl.program_id(0) == pl.num_programs(0) - 1)
+    def _():
+        last.wait()
 
 
 def project(place, x, weights, bq, bv, pieces, *tokens):
@@ -322,9 +333,13 @@
         + [token_spec()] * 4
         + [whole_spec(a.shape) for a in (bq, bv, *pieces)]
         + [token_spec() for _ in tokens],
-        out_specs=[block, block, block, fixed_spec((4, width, width))],
+        out_specs=[block, block, block, token_spec()],
         out_shape=[shape((rows, width), BF)] * 3 + [shape((4, width, width), BF)],
-        scratch_shapes=[pltpu.SemaphoreType.DMA((weights[0].shape[0] // GRAIN * 4,))],
+        scratch_shapes=[
+            pltpu.VMEM((4, width, width), BF),
+            pltpu.SemaphoreType.DMA((weights[0].shape[0] // GRAIN * 4,)),
+            pltpu.SemaphoreType.DMA,
+        ],
         compiler_params=params(),
         cost_estimate=cost(10),
         name="project",
@@ -430,7 +445,25 @@
     )(q, k, v, segc, segr, x, full, bo, gain, shift, *held, *tokens)
 
 
-def attend_back_kernel(q, k, v, do, saved, inner, segc, segr, *refs):
+def whole_order(rows, plane):
+    width = rows.shape[1]
+    rank = (lax.broadcasted_iota(jnp.int32, rows.shape, 1) // GRAIN) % 4
+    row = lax.broadcasted_iota(jnp.int32, rows.shape, 0)
+
+    def shifted(block, by):
+        return pltpu.roll(block, by % width, 1)
+
+    middle = jnp.where(rank == 1, shifted(rows, -GRAIN), shifted(rows, GRAIN))
+    swapped = (row == 7) & ((rank == 1) | (rank == 2))
+    rows = jnp.where(swapped, middle, rows)
+    for bit in (1, 2):
+        by = bit * GRAIN
+        other = jnp.where((rank & bit) == 0, shifted(rows, -by), shifted(rows, by))
+        rows = jnp.where((plane & bit) == 0, rows, other)
+    return rows
+
+
+def attend_back_kernel(place, q, k, v, do, saved, inner, segc, segr, *refs):
     dq, dk, dv, sums, dk_sum, dv_sum = refs[-6:]
     step = pl.program_id(0)
 
@@ -462,7 +495,7 @@
             gather_heads(jnp.dot(logit_grad, k4, preferred_element_type=F32)) * SCALE
         ).astype(BF)
         dq[:, cols] = dq_low
-        sums[0:1, cols] += jnp.sum(dq_low.astype(F32), axis=0, keepdims=True)
+        sums[6:7, cols] += jnp.sum(dq_low.astype(F32), axis=0, keepdims=True)
         dk_sum[near, cols] += lax.dot_general(logit_grad, q4, TN, preferred_element_type=F32)
         dv_sum[near, cols] += lax.dot_general(probs_low, do4, TN, preferred_element_type=F32)
 
@@ -471,10 +504,11 @@
         dk[...] = dk_sum[...].astype(BF)
         dv_low = dv_sum[...].astype(BF)
         dv[...] = dv_low
-        sums[1:2, :] = jnp.sum(dv_low.astype(F32), axis=0, keepdims=True)
-
-
-def attend_back(q, k, v, do, saved, inner, segc, segr, *tokens):
+        sums[7:8, :] = jnp.sum(dv_low.astype(F32), axis=0, keepdims=True)
+        sums[...] = whole_order(sums[...], place[1])
+
+
+def attend_back(place, q, k, v, do, saved, inner, segc, segr, *tokens):
     rows, width = q.shape
     block = rows_spec(BLOCK, width)
     full = whole_spec((rows, width))
@@ -482,6 +516,7 @@
         attend_back_kernel,
         grid=(rows // BLOCK,),
         in_specs=[
+            scalar_spec(),
             block,
             full,
             full,
@@ -498,7 +533,7 @@
         compiler_params=params(),
         cost_estimate=cost(22),
         name="attend_back",
-    )(q, k, v, do, saved, inner, segc, segr, *tokens)
+    )(place, q, k, v, do, saved, inner, segc, segr, *tokens)
 
 
 def assemble(place, own, pieces, into):
@@ -518,11 +553,13 @@
 
 
 def feed_up_kernel(place, x, own, bu, *refs):
-    pieces, (act, slope, wu) = refs[:8], refs[-3:]
+    pieces, (act, slope, out, wu, sem) = refs[:8], refs[-5:]
+    copy = pltpu.make_async_copy(wu, out, sem)
 
     @pl.when(pl.program_id(0) == 0)
     def _():
         assemble(place, own, pieces, wu)
+        copy.start()
 
     block = x[...]
     for at in range(0, wu.shape[0], 256):
@@ -535,6 +572,10 @@
         act[:, span] = (pre * below).astype(BF)
         slope[:, span] = (below + pre * density).astype(BF)
 
+    @pl.when(pl.program_id(0) == pl.num_programs(0) - 1)
+    def _():
+        copy.wait()
+
 
 def feed_up(place, x, own, bu, pieces, *tokens):
     rows, width = x.shape
@@ -546,8 +587,9 @@
         in_specs=[scalar_spec(), rows_spec(ROW_BLOCK, width)]
         + [whole_spec(a.shape) for a in (own, bu, *pieces)]
         + [token_spec() for _ in tokens],
-        out_specs=[wide, wide, fixed_spec((hidden, width))],
+        out_specs=[wide, wide, token_spec()],
         out_shape=[shape((rows, hidden), BF)] * 2 + [shape((hidden, width), BF)],
+        scratch_shapes=[pltpu.VMEM((hidden, width), BF), pltpu.SemaphoreType.DMA],
         compiler_params=params(),
         cost_estimate=cost(12),
         name="feed_up",
@@ -555,13 +597,15 @@
 
 
 def feed_down_kernel(place, act, unit, cot, own, vectors, *refs):
-    pieces, outs = refs[:8], refs[-6:]
-    layer, output, second, down_grad, sums, wd = outs
+    pieces, outs = refs[:8], refs[-8:]
+    layer, output, second, down_grad, sums, out, wd, sem = outs
+    copy = pltpu.make_async_copy(wd, out, sem)
 
     @pl.when(pl.program_id(0) == 0)
     def _():
         sums[...] = jnp.zeros_like(sums)
         assemble(place, own, pieces, wd)
+        copy.start()
 
     down = jnp.dot(act[...], wd[...], preferred_element_type=F32)
     b_down, first_gain, first_shift, second_gain, second_shift = (
@@ -585,9 +629,13 @@
     second[...] = second_grad
     grad_low = second_grad.astype(BF)
     down_grad[...] = grad_low
-    sums[0:1, :] += jnp.sum(grad_low.astype(F32), axis=0, keepdims=True)
-    sums[1:2, :] += jnp.sum(grad * unit_val, axis=0, keepdims=True)
-    sums[2:3, :] += jnp.sum(grad, axis=0, keepdims=True)
+    sums[3:4, :] += jnp.sum(grad_low.astype(F32), axis=0, keepdims=True)
+    sums[4:5, :] += jnp.sum(grad * unit_val, axis=0, keepdims=True)
+    sums[5:6, :] += jnp.sum(grad, axis=0, keepdims=True)
+
+    @pl.when(pl.program_id(0) == pl.num_programs(0) - 1)
+    def _():
+        copy.wait()
 
 
 def feed_down(place, act, unit, cot, own, vectors, pieces):
@@ -599,7 +647,7 @@
         grid=(rows // ROW_BLOCK,),
         in_specs=[scalar_spec(), rows_spec(ROW_BLOCK, hidden), block, block]
         + [whole_spec(a.shape) for a in (own, vectors, *pieces)],
-        out_specs=[block, block, block, block, fixed_spec((8, width)), fixed_spec((hidden, width))],
+        out_specs=[block, block, block, block, fixed_spec((8, width)), token_spec()],
         out_shape=[
             shape((rows, width), F32),
             shape((rows, width), BF),
@@ -608,6 +656,7 @@
             shape((8, width), F32),
             shape((hidden, width), BF),
         ],
+        scratch_shapes=[pltpu.VMEM((hidden, width), BF), pltpu.SemaphoreType.DMA],
         compiler_params=params(),
         cost_estimate=cost(13),
         name="feed_down",
@@ -622,6 +671,7 @@
     @pl.when(step == 0)
     def _():
         out[...] = jnp.zeros_like(out)
+        bias[...] = jnp.zeros_like(bias)
 
     total = None
     for at in range(0, x.shape[0], ROW_BLOCK):
@@ -631,7 +681,16 @@
         held[span, :] = low
         term = jnp.sum(low.astype(F32), axis=0, keepdims=True)
         total = term if total is None else total + term
-    bias[...] = jnp.broadcast_to(total, bias.shape[1:])[None]
+    for block in range(4):
+
+        @pl.when(step == (block + 2) % 4)
+        def _():
+            for g in range(chips):
+                for r in range(shards):
+                    at = (g * shards + r) * sub
+                    row = block * chips + g
+                    bias[row : row + 1, r * 128 : r * 128 + sub] = total[:, at : at + sub]
+
     out[...] += jnp.dot(held[...], wu[...], preferred_element_type=F32)
     dims = (chips, shards, sub, width)
     up = lax.dot_general(held[...], x[...], TN, preferred_element_type=F32).astype(BF)
@@ -664,13 +723,13 @@
         out_specs=[
             pl.BlockSpec(block, lambda j: (jnp.maximum(j - 2, 0), 0, 0, 0, 0)),
             pl.BlockSpec(block, lambda j: (jnp.minimum(j, 1), 0, 0, 0, 0)),
-            pl.BlockSpec((1, 8, span), lambda j: ((j + 2) % 4, 0, 0)),
+            fixed_spec((8, 128 * n_mp)),
             fixed_spec((rows, width)),
         ],
         out_shape=[
             shape(dims, BF),
             shape(dims, BF),
-            shape((4, 8, span), F32),
+            shape((8, 128 * n_mp), F32),
             shape((rows, width), F32),
         ],
         scratch_shapes=[pltpu.VMEM((rows, span), BF)],
@@ -896,24 +955,39 @@
     place = jnp.stack([core, plane, shard]).astype(jnp.int32)
     own_heads = (w_query.T, w_key.T, w_value.T, w_output)
 
+    cut = heads * HEAD_DIM
     heads_piece = piece_heads(place, *own_heads)
-    heads_parts = shard_step(heads_piece, n_mp)
-    turned, up_piece, down_piece = piece_feed(place, w_up, w_down)
+    bias_rows = jnp.stack(
+        [jnp.pad(b_query, (0, width - cut)), jnp.pad(b_value, (0, width - cut)), b_up]
+    )
+    turned, up_piece, down_piece = piece_feed(
+        place, w_up, w_down, after(jnp.pad(bias_rows, ((0, GRAIN - 3), (0, 0))), heads_piece), n_mp
+    )
+    heads_parts = [swap(after(heads_piece, down_piece), "mp", 1, n_mp)] + [
+        swap(heads_piece, "mp", r, n_mp) for r in range(2, n_mp)
+    ]
+    up_got = exchange(up_piece, "mp")
     heads_shards = jnp.concatenate(heads_parts)
-    up_got = exchange(spread(after(up_piece, heads_shards), n_mp), "mp")
     heads_first = first_swap(heads_shards, n_dp)
     heads_second = second_swap(heads_shards, n_dp)
-    heads_corner = second_swap(heads_first, n_dp)
+    heads_corner = second_swap(after(heads_first, heads_second), n_dp)
+    heads_other = [core_swap(p, n_dp) for p in (heads_shards, heads_first, heads_second)]
+    heads_corner, up_got = lax.optimization_barrier((heads_corner, up_got))
     heads_mine = [heads_shards, heads_first, heads_second, heads_corner]
-    heads_pieces = heads_mine + [core_swap(p, n_dp) for p in heads_mine]
+    heads_other = heads_other + [core_swap(heads_corner, n_dp)]
 
     def others(got):
         return jnp.concatenate(
             [
-                lax.dynamic_index_in_dim(got, shard ^ r, 0, keepdims=False)
+                lax.dynamic_index_in_dim(got, shard ^ r, 0, keepdims=False)[:sub]
                 for r in range(1, n_mp)
             ]
         )
+
+    up_shards = others(after(up_got, *heads_mine, *heads_other))
+    up_first = first_swap(up_shards, n_dp)
+    up_second = second_swap(up_shards, n_dp)
+    down_got = exchange(after(down_piece, up_got), "mp")
 
     ranks = lax.broadcasted_iota(jnp.int32, (4, 4), 0)
     places4 = lax.broadcasted_iota(jnp.int32, (4, 4), 1)
@@ -927,34 +1001,14 @@
     exact = functools.partial(
         jnp.einsum, precision=lax.Precision.HIGHEST, preferred_element_type=F32
     )
-    cut = heads * HEAD_DIM
-
-    def turn(vector, there="gk"):
-        query = vector[:cut].reshape(-1, 4, GRAIN)
-        value = vector[cut : 2 * cut].reshape(-1, 4, GRAIN)
-        hidden = vector[2 * cut :].reshape(8, sub)
-        to = "g" if there == "gk" else "k"
-        frm = "k" if there == "gk" else "g"
-        return jnp.concatenate(
-            [
-                exact(f"gk,t{frm}i->t{to}i", order_q, query).reshape(-1),
-                exact(f"gk,t{frm}i->t{to}i", order_v, value).reshape(-1),
-                exact(f"gk,{frm}i->{to}i", order_up, hidden).reshape(-1),
-            ]
-        )
-
-    local_bias = turn(
-        jnp.concatenate(after((b_query, b_value, b_up), heads_shards)).astype(F32)
-    )
-    all_bias = exchange(spread(after(local_bias, up_got), n_mp), "mp")
-    query_bias = all_bias[:, :cut].reshape(1, -1)
-    value_bias = all_bias[:, cut : 2 * cut].reshape(1, -1)
-    up_bias = all_bias[:, 2 * cut :].reshape(n_mp, 8, sub).transpose(1, 0, 2).reshape(1, -1)
-
-    up_shards = others(lax.optimization_barrier((up_got, *heads_pieces))[0])
-    up_first = first_swap(up_shards, n_dp)
-    up_second = second_swap(up_shards, n_dp)
-    down_got = exchange(spread(after(down_piece, all_bias), n_mp), "mp")
+    all_bias = up_got[:, sub : sub + 3].astype(F32)
+    by_head = (n_mp, heads, 4, GRAIN)
+    query_bias = exact("gk,zhki->zhgi", order_q, all_bias[:, 0, :cut].reshape(by_head))
+    value_bias = exact("gk,zhki->zhgi", order_v, all_bias[:, 1, :cut].reshape(by_head))
+    up_bias = exact("gk,zki->gzi", order_up, all_bias[:, 2].reshape(n_mp, 8, sub))
+    query_bias, value_bias, up_bias = (
+        b.reshape(1, -1) for b in (query_bias, value_bias, up_bias)
+    )
 
     ends = jnp.cumsum(query_lengths, axis=-1, dtype=jnp.int32)
     places = lax.broadcasted_iota(jnp.int32, (rows, query_lengths.shape[1]), 0)
@@ -965,7 +1019,7 @@
     ).astype(F32)
 
     query, key, value, full = project(
-        place, hidden_in, own_heads, query_bias, value_bias, heads_pieces, up_shards
+        place, hidden_in, own_heads, query_bias, value_bias, heads_mine + heads_other
     )
     up_first, up_second, down_got, query = lax.optimization_barrier(
         (up_first, up_second, down_got, query)
@@ -986,14 +1040,14 @@
     up_pieces = up_mine + [up_corner] + up_other + [core_swap(up_corner, n_dp)]
     down_corner = second_swap(down_first, n_dp)
     down_mine = [down_shards, down_first, down_second]
-    down_other = [core_swap(p, n_dp) for p in down_mine]
     context, saved, unit, low = attend(
         1, 2, query, key, value, segc, segr, hidden_in, full,
         vectors[5:6], vectors[1:2], vectors[2:3], held,
     )
     down_corner, low = lax.optimization_barrier((down_corner, low))
-    down_pieces = down_mine + [down_corner] + down_other + [core_swap(down_corner, n_dp)]
-    act, slope, wu = feed_up(place, low, turned, up_bias, up_pieces)
+    down_mine = down_mine + [down_corner]
+    down_pieces = down_mine + [core_swap(p, n_dp) for p in down_mine]
+    act, slope, wu = feed_up(place, low, turned, up_bias, up_pieces, down_corner)
     layer_out, output, second_grad, down_grad, second_sums, wd = feed_down(
         place, act, unit, cotangent, w_down, vectors, down_pieces
     )
@@ -1011,77 +1065,75 @@
     feed_stay, feed_go = chip_sum(feed_keep, got)
     got = first_swap(feed_go, n_dp)
     dq, dk, dv, head_sums = attend_back(
-        query, key, value, context_grad, saved, inner, segc, segr, feed_go
-    )
+        place, query, key, value, context_grad, saved, inner, segc, segr, feed_go
+    )
+    got, head_sums = lax.optimization_barrier((got, head_sums))
+    feed_own, feed_go = side_sum(feed_stay, got)
+    got = second_swap(feed_go, n_dp)
     every = jnp.concatenate(
-        [second_sums, first_sums, head_sums, up_sums.reshape(-1, width)]
+        [second_sums + first_sums + head_sums, exact("sk,si->ki", order_up, up_sums)], axis=1
     )
     vector_got = swap(every, "mp", 1, n_mp)
     heads_keep, heads_send = head_weights(
-        place, dq, dk, dv, hidden_in, wo_grad, n_mp, every
-    )
-    got, vector_got, heads_keep = lax.optimization_barrier((got, vector_got, heads_keep))
-    feed_own, feed_go = side_sum(feed_stay, got)
-    every = every + vector_got
-    got = second_swap(feed_go, n_dp)
-    vector_got = swap(every, "mp", 2, n_mp)
-    heads_got = core_swap(heads_send, n_dp)
-    input_grad = input_gradient(dq, dk, dv, full, first_grad, heads_keep, feed_go, every)
-    got, vector_got, heads_got, input_grad = lax.optimization_barrier(
-        (got, vector_got, heads_got, input_grad)
-    )
+        place, dq, dk, dv, hidden_in, wo_grad, n_mp, every, feed_go
+    )
+    got, heads_keep = lax.optimization_barrier((got, heads_keep))
+    feed_parts = add(feed_own, got)
+    heads_got = core_swap(after(heads_send, feed_parts), n_dp)
+    feed_got = exchange(feed_parts, "mp")
     heads_stay, heads_go = chip_sum(heads_keep, heads_got)
     heads_got = first_swap(heads_go, n_dp)
-    feed_parts = add(feed_own, got)
-    feed_got = exchange(feed_parts, "mp")
-    every = every + vector_got
-    up_sums = every[24:].reshape(2, 2, 8, 2, n_mp, sub)[:, :, 0]
-    own_bias = jnp.concatenate(
-        [
-            lax.dynamic_slice_in_dim(every[16:18], shard * cut, cut, axis=1).reshape(-1),
-            lax.dynamic_index_in_dim(up_sums, shard, 3, keepdims=False).reshape(-1),
-        ]
-    )
-    every = jnp.concatenate(
-        [every[0:3].reshape(-1), every[8:11].reshape(-1), turn(own_bias, "kg")]
-    )
+    every = every + after(vector_got, heads_go)
     vector_got = core_swap(every, n_dp)
-    scores = score(
-        layer_out, segr, query_lengths.reshape(-1, 1), passages, passage_index,
-        every, feed_parts, heads_go,
-    )
-    heads_got, vector_got, scores = lax.optimization_barrier((heads_got, vector_got, scores))
+    input_grad = input_gradient(dq, dk, dv, full, first_grad, heads_go, every)
+    heads_got, vector_got, input_grad = lax.optimization_barrier(
+        (heads_got, vector_got, input_grad)
+    )
     heads_own, heads_go = side_sum(heads_stay, heads_got)
     heads_got = second_swap(heads_go, n_dp)
-    every = every + vector_got
-    vector_got = swap(every, "dp", XBIT, n_dp)
-    feed_got, heads_got, vector_got = lax.optimization_barrier(
-        (feed_got, heads_got, vector_got)
+    every = every + after(vector_got, heads_go)
+    bit = 2
+    while bit < n_mp:
+        vector_got = swap(every, "mp", bit, n_mp)
+        bit *= 2
+    feed_got, heads_go = lax.optimization_barrier((feed_got, heads_go))
+    feed_total = shard_sum(feed_got[0], [feed_got[r] for r in range(1, n_mp)], n_dp)
+    feed_four = spread(feed_total, 4)
+    feed_mine = plane_gather(feed_four, n_dp)
+    heads_got, vector_got, feed_four = lax.optimization_barrier(
+        (heads_got, vector_got, feed_four)
     )
     heads_parts = add(heads_own, heads_got)
     heads_got = shard_swap(heads_parts, n_mp)
     heads_own = lax.dynamic_index_in_dim(heads_parts, shard, 0, keepdims=False)
-    feed_total = shard_sum(feed_got[0], [feed_got[r] for r in range(1, n_mp)], n_dp)
-    feed_mine = plane_gather(spread(feed_total, 4), n_dp)
+    every = every + after(vector_got, heads_parts)
+    vector_got = swap(every, "dp", XBIT, n_dp)
+    scores = score(
+        layer_out, segr, query_lengths.reshape(-1, 1), passages, passage_index,
+        heads_parts, every,
+    )
+    vector_got, scores = lax.optimization_barrier((vector_got, scores))
     every = every + vector_got
     vector_got = swap(every, "dp", YBIT, n_dp)
-    feed_mine, vector_got, *heads_got = lax.optimization_barrier(
-        (feed_mine, vector_got, *heads_got)
-    )
+    feed_mine, *heads_got = lax.optimization_barrier((feed_mine, *heads_got, scores))[:n_mp]
     heads_total = shard_sum(heads_own, heads_got, n_dp)
     heads_mine = plane_gather(spread(heads_total, 4), n_dp)
     feed_other = core_swap(feed_mine, n_dp)
-    every = every + vector_got
+    every = every + after(vector_got, heads_total)
     bit = 8
     while bit < n_dp:
         every = every + swap(every, "dp", bit, n_dp)
         bit *= 2
-    w_up_grad, w_down_grad = finish_feed(place, (feed_mine, feed_other), heads_total)
-    heads_other = core_swap(after(heads_mine, w_up_grad), n_dp)
+    w_up_grad, w_down_grad = finish_feed(place, (feed_mine, feed_other), heads_total, every)
+    heads_mine, w_up_grad = lax.optimization_barrier((heads_mine, w_up_grad))
+    heads_other = core_swap(heads_mine, n_dp)
     query_t, key_t, value_t, w_output_grad = finish_heads(place, (heads_mine, heads_other))
-    second_sums, first_sums = every[: 3 * width].reshape(3, width), every[3 * width : 6 * width].reshape(3, width)
-    shared = [first_sums[0], second_sums[0], first_sums[1], first_sums[2], second_sums[1], second_sums[2]]
-    own_bias = every[6 * width :]
+    shared = every[:6, :width]
+    query_sums, value_sums = (
+        lax.dynamic_slice_in_dim(every[row, :width], shard * cut, cut) for row in (6, 7)
+    )
+    up_sums = lax.dynamic_slice_in_dim(every[:, width:], shard * 128, 128, axis=1)
+    up_sums = up_sums[:, :sub].reshape(-1)
     return (
         output,
         scores,
@@ -1092,13 +1144,13 @@
         w_output_grad,
         w_up_grad,
         w_down_grad,
-        own_bias[:cut],
-        own_bias[cut : 2 * cut],
+        query_sums,
+        value_sums,
         shared[0],
-        own_bias[2 * cut :],
+        up_sums,
+        shared[3],
         shared[1],
         shared[2],
-        shared[3],
         shared[4],
         shared[5],
     )

time: 331 us -> 310 us (0.937)
  waiting for transfers between devices: 62.5 us -> 40.6 us
  other arithmetic: 20.4 us -> 24.3 us
    ppermute x27, waiting for transfers between devices: 19.8 us -> 4.09 us  [swap(): return lax.ppermute(block, axis, [(i, i ^ bit) for i in range(size)])]
    all_to_all x6 -> x5, waiting for transfers between devices: 17.1 us -> 8.05 us  [exchange(): lax.all_to_all(block, axis, 0, 0, axis_index_groups=groups, tiled=True)]
    add x0 -> x5, other arithmetic: none -> 3.73 us  [the longest x2 2.19 us: per_device(): every = every + after(vector_got, heads_go)]
    broadcast_in_dim x5 -> x2, local copies, waits for them, and re-layouts: 5.37 us -> 1.94 us  [spread(): return jnp.broadcast_to(block[None], (n, *block.shape))]
    all_to_all x6 -> x5, starting transfers between devices: 24.3 us -> 21.5 us  [exchange(): lax.all_to_all(block, axis, 0, 0, axis_index_groups=groups, tiled=True)]
  transfers between devices with their start and end apart: 46 -> 45, of which waited for: 16 -> 12; matrix products, arithmetic and copies ran while one was open for 5% -> 8% of each run, Pallas kernels for 36% -> 38%
where the time goes in v3:
time: 310 us; the launch traced here: 306 us
  Pallas kernels  166 us (54%)
  starting transfers between devices  57.9 us (19%)
  waiting for transfers between devices  40.6 us (13%)
  other arithmetic  24.3 us (8%)
  local copies, waits for them, and re-layouts  13.6 us (4%)
    pallas_call x1, Pallas kernels, feed_back(): pl.pallas_call(feed_back_kernel, grid=(4,), in_specs=[full, full, weight,...  30.4 us
    ppermute x13, waiting for transfers between devices, turn_swap(): lax.ppermute(block, 'dp', [(i, i ^ bits[i & 1]) for i in range(n_dp)])  28.5 us
    pallas_call x1, Pallas kernels, attend_back(): pl.pallas_call(attend_back_kernel, grid=(rows // BLOCK,), in_specs=[scala...  23.6 us
    all_to_all x5, starting transfers between devices, exchange(): lax.all_to_all(block, axis, 0, 0, axis_index_groups=groups, tiled=True)  21.5 us
    pallas_call x2, Pallas kernels, attend(): pl.pallas_call(functools.partial(attend_kernel, part), grid=(steps,), in_...  21.2 us
    ppermute x27, starting transfers between devices, swap(): return lax.ppermute(block, axis, [(i, i ^ bit) for i in range(size)])  21.2 us
    convert_element_type x6, other arithmetic, add(): return total.astype(BF)  15.5 us
    ppermute x13, starting transfers between devices, turn_swap(): lax.ppermute(block, 'dp', [(i, i ^ bits[i & 1]) for i in range(n_dp)])  15.3 us
  transfers between devices with their start and end apart: 45, of which 12 were waited for; matrix products, arithmetic and copies ran while one was open for 8% of the time, Pallas kernels for 38%

profile of v3, /device:TPU:0, one launch (start us, length us, event | category | flops | bytes accessed | tf_op | source)
XLA Modules:
  0.0 306.1 jit_solution(10538644965293162219)
XLA Ops:
  3.6 4.1 %collective-permute-start.1 = (bf16[96,768]{1,0:T(8,128)(2,1)}, bf16[96,768]{1,0:T(8,128)(2,1)S(1)}, u32[]{:S(2)}, u32[]{:S(2)}) collective-permute-start(bf16[96,768]{1,0:T(8,128)(2,1)} %piece_heads.1), channel_id=1, source_target_pairs={{0,2},{1,3},{2,0},{3,1},{4,6},{5,7},{6,4},{7,5},{8,10},{9,11},{10,... | collective-permute-start | bytes 442376 | tf_op jit(solution)/shard_map/ppermute | solution.py:65
  9.8 3.6 %piece_feed.1 = (bf16[768,768]{1,0:T(8,128)(2,1)}, bf16[4,112,768]{2,1,0:T(8,128)(2,1)}, bf16[4,96,768]{2,1,0:T(8,128)(2,1)}) custom-call(s32[3]{0:T(128)} %pad_add_fusion.place, bf16[768,768]{1,0:T(8,128)(2,1)} %wu.1, bf16[768,768]{1,0:T(8,128)(2,1)} %own.1, bf16[16,768]{1,0:T(8,128)(2,1)} %fusion.14.rest), custom_call_target="tpu_custom_call" | custom-call | flops 15000000512 | bytes 45000000 | tf_op jit(solution)/shard_map/piece_feed/pallas_call | solution.py:132
  13.6 4.2 %all-to-all-start = ((bf16[4,112,768]{2,1,0:T(8,128)(2,1)}), bf16[4,112,768]{2,1,0:T(8,128)(2,1)S(1)}, u32[]{:S(2)}, u32[]{:S(2)}) async-start(bf16[4,112,768]{2,1,0:T(8,128)(2,1)} %get-tuple-element.112), calls=%async_computation | async-start | bytes 1376256 | tf_op jit(solution)/shard_map/all_to_all | solution.py:224
  19.5 3.6 %collective-permute-done = bf16[96,768]{1,0:T(8,128)(2,1)S(1)} collective-permute-done((bf16[96,768]{1,0:T(8,128)(2,1)S(1)}, bf16[96,768]{1,0:T(8,128)(2,1)S(1)}, u32[]{:S(2)}, u32[]{:S(2)}) %collective-permute-start) | collective-permute-done | bytes 147488 | tf_op jit(solution)/shard_map/ppermute | solution.py:65
  26.6 8.2 %collective-permute-done.3.refs_1_ = bf16[288,768]{1,0:T(8,128)(2,1)S(1)} collective-permute-done((bf16[288,768]{1,0:T(8,128)(2,1)S(1)}, bf16[288,768]{1,0:T(8,128)(2,1)S(1)}, u32[]{:S(2)}, u32[]{:S(2)}) %collective-permute-start.3) | collective-permute-done | bytes 442400 | tf_op jit(solution)/shard_map/ppermute | solution.py:208
  37.8 5.3 %collective-permute-done.5.refs_3_ = bf16[288,768]{1,0:T(8,128)(2,1)S(1)} collective-permute-done((bf16[288,768]{1,0:T(8,128)(2,1)S(1)}, bf16[288,768]{1,0:T(8,128)(2,1)S(1)}, u32[]{:S(2)}, u32[]{:S(2)}) %collective-permute-start.5) | collective-permute-done | bytes 442400 | tf_op jit(solution)/shard_map/ppermute | solution.py:208
  43.3 6.4 %all-to-all-start.1 = ((bf16[4,96,768]{2,1,0:T(8,128)(2,1)}), bf16[4,96,768]{2,1,0:T(8,128)(2,1)S(1)}, u32[]{:S(2)}, u32[]{:S(2)}) async-start(bf16[4,96,768]{2,1,0:T(8,128)(2,1)} %get-tuple-element.116), calls=%async_computation.1 | async-start | bytes 1179648 | tf_op jit(solution)/shard_map/all_to_all | solution.py:224
  54.8 9.8 %project.1 = (bf16[1024,768]{1,0:T(8,128)(2,1)}, bf16[1024,768]{1,0:T(8,128)(2,1)}, bf16[1024,768]{1,0:T(8,128)(2,1)}, bf16[4,768,768]{2,1,0:T(8,128)(2,1)}) custom-call(s32[3]{0:T(128)} %pad_add_fusion.place, bf16[1024,768]{1,0:T(8,128)(2,1)} %x.13, bf16[192,768]{1,0:T(8,128)(2,1)} %bitcast.89, bf16[192,768]{1,0:T(8,128)(2,1)} %bitcast.91, ...), custom_call_target="tpu_custom_call" | custom-call | flops 49999998976 | bytes 150000000 | tf_op jit(solution)/shard_map/project/pallas_call | solution.py:329
  69.9 10.6 %attend.2 = (bf16[1024,768]{1,0:T(8,128)(2,1)}, f32[1024,128]{1,0:T(8,128)}, f32[1024,768]{1,0:T(8,128)}, bf16[1024,768]{1,0:T(8,128)(2,1)}) custom-call(bf16[1024,768]{1,0:T(8,128)(2,1)} %get-tuple-element.120.q, bf16[1024,768]{1,0:T(8,128)(2,1)} %get-tuple-element.121.k, bf16[1024,768]{1,0:T(8,128)(2,1)} %get-tuple-element.122.v, s32[1024,1]{1,0:T(8,128)} %copy.52.segc, ...), custom_call_target="tpu_custom_call" | custom-call | flops 40000000000 | bytes 120000000 | tf_op jit(solution)/shard_map/attend/pallas_call | solution.py:418
  84.4 10.6 %attend.3 = (bf16[1024,768]{1,0:T(8,128)(2,1)}, f32[1024,128]{1,0:T(8,128)}, f32[1024,768]{1,0:T(8,128)}, bf16[1024,768]{1,0:T(8,128)(2,1)}) custom-call(bf16[1024,768]{1,0:T(8,128)(2,1)} %get-tuple-element.120.q, bf16[1024,768]{1,0:T(8,128)(2,1)} %get-tuple-element.121.k, ...), custom_call_target="tpu_custom_call", output_to_operand_aliasing={{0}: (10, {}), {1}: (11, {}), {2}: (12, {}), {3}: (13, {})} | custom-call | flops 40000000000 | bytes 120000000 | tf_op jit(solution)/shard_map/attend/pallas_call | solution.py:418
  96.4 13.6 %feed_up.1 = (bf16[1024,3072]{1,0:T(8,128)(2,1)}, bf16[1024,3072]{1,0:T(8,128)(2,1)}, bf16[3072,768]{1,0:T(8,128)(2,1)}) custom-call(s32[3]{0:T(128)} %pad_add_fusion.place, bf16[1024,768]{1,0:T(8,128)(2,1)} %get-tuple-element.134.x, bf16[768,768]{1,0:T(8,128)(2,1)} %get-tuple-element.135.own, f32[1,3072]{1,0:T(1,128)} %reshape.222.bu, ...), custom_call_target="tpu_custom_call" | custom-call | flops 60000002048 | bytes 180000000 | tf_op jit(solution)/shard_map/feed_up/pallas_call | solution.py:584
  111.1 14.1 %feed_down.1 = (f32[1024,768]{1,0:T(8,128)}, bf16[1024,768]{1,0:T(8,128)(2,1)}, f32[1024,768]{1,0:T(8,128)}, bf16[1024,768]{1,0:T(8,128)(2,1)}, f32[8,768]{1,0:T(8,128)}, /*index=5*/bf16[3072,768]{1,0:T(8,128)(2,1)}) custom-call(s32[3]{0:T(128)} %pad_add_fusion.place, bf16[1024,3072]{1,0:T(8,128)(2,1)} %get-tuple-element.139.act, ...), custom_call_target="tpu_custom_call" | custom-call | flops 65000001536 | bytes 195000000 | tf_op jit(solution)/shard_map/feed_down/pallas_call | solution.py:645
  125.2 30.4 %feed_back.1 = (bf16[4,4,2,96,768]{4,3,2,1,0:T(8,128)(2,1)}, bf16[4,4,2,96,768]{4,3,2,1,0:T(8,128)(2,1)}, f32[8,512]{1,0:T(8,128)}, f32[1024,768]{1,0:T(8,128)}) custom-call(bf16[1024,768]{1,0:T(8,128)(2,1)} %get-tuple-element.144.grad, bf16[1024,768]{1,0:T(8,128)(2,1)} %get-tuple-element.134.x, bf16[3072,768]{1,0:T(8,128)(2,1)} %get-tuple-element.145.wu, ...), custom_call_target="tpu_custom_call" | custom-call | flops 134999998464 | bytes 405000000 | tf_op jit(solution)/shard_map/feed_back/pallas_call | solution.py:719
  157.6 12.5 %middle.1 = (f32[1024,768]{1,0:T(8,128)}, bf16[1024,768]{1,0:T(8,128)(2,1)}, f32[1024,128]{1,0:T(8,128)}, bf16[768,768]{1,0:T(8,128)(2,1)}, f32[8,768]{1,0:T(8,128)}) custom-call(f32[1024,768]{1,0:T(8,128)} %get-tuple-element.148.normed, f32[1024,768]{1,0:T(8,128)} %get-tuple-element.149.second, f32[1024,768]{1,0:T(8,128)} %get-tuple-element.140.unit, ...), custom_call_target="tpu_custom_call" | custom-call | flops 40000000000 | bytes 120000000 | tf_op jit(solution)/shard_map/middle/pallas_call | solution.py:787
  170.1 5.3 %add_convert_fusion = (bf16[2,4,192,768]{3,2,1,0:T(8,128)(2,1)S(1)}, bf16[2,4,192,768]{3,2,1,0:T(8,128)(2,1)}) fusion(bf16[4,4,192,768]{3,2,1,0:T(8,128)(2,1)} %collective-permute-done.24, bf16[4,4,192,768]{3,2,1,0:T(8,128)(2,1)} %bitcast.76), kind=kLoop, calls=%fused_computation | loop fusion | flops 9437184 | bytes 14155776 | tf_op jit(solution)/shard_map/convert_element_type | solution.py:239
  176.9 23.6 %attend_back.1 = (bf16[1024,768]{1,0:T(8,128)(2,1)}, bf16[1024,768]{1,0:T(8,128)(2,1)}, bf16[1024,768]{1,0:T(8,128)(2,1)}, f32[8,768]{1,0:T(8,128)}) custom-call(s32[3]{0:T(128)} %pad_add_fusion.place, bf16[1024,768]{1,0:T(8,128)(2,1)} %get-tuple-element.120.q, bf16[1024,768]{1,0:T(8,128)(2,1)} %get-tuple-element.121.k, ...), custom_call_target="tpu_custom_call" | custom-call | flops 109999996928 | bytes 330000000 | tf_op jit(solution)/shard_map/attend_back/pallas_call | solution.py:515
  200.6 4.0 %collective-permute-done.25 = bf16[2,4,192,768]{3,2,1,0:T(8,128)(2,1)} collective-permute-done((bf16[2,4,192,768]{3,2,1,0:T(8,128)(2,1)}, bf16[2,4,192,768]{3,2,1,0:T(8,128)(2,1)}, u32[]{:S(2)}, u32[]{:S(2)}) %collective-permute-start.25) | collective-permute-done | bytes 2359328 | tf_op jit(solution)/shard_map/ppermute | solution.py:208
  208.5 10.6 %head_weights.1 = (bf16[4,4,2,3,16,768]{5,4,3,2,1,0:T(8,128)(2,1)}, bf16[4,4,2,3,16,768]{5,4,3,2,1,0:T(8,128)(2,1)}) custom-call(s32[3]{0:T(128)} %pad_add_fusion.place, bf16[1024,768]{1,0:T(8,128)(2,1)} %get-tuple-element.163.dq, bf16[1024,768]{1,0:T(8,128)(2,1)} %get-tuple-element.164.dk, bf16[1024,768]{1,0:T(8,128)(2,1)} %get-tuple-element.165.dv, ...), custom_call_target="tpu_custom_call" | custom-call | flops 40000000000 | bytes 120000000 | tf_op jit(solution)/shard_map/head_weights/pallas_call | solution.py:841
  219.1 3.3 %collective-permute-done.27 = bf16[4,192,768]{2,1,0:T(8,128)(2,1)} collective-permute-done((bf16[4,192,768]{2,1,0:T(8,128)(2,1)S(1)}, bf16[4,192,768]{2,1,0:T(8,128)(2,1)}, u32[]{:S(2)}, u32[]{:S(2)}) %collective-permute-start.27) | collective-permute-done | bytes 1179680 | tf_op jit(solution)/shard_map/ppermute | solution.py:208
  222.5 3.1 %fusion = bf16[4,192,768]{2,1,0:T(8,128)(2,1)} fusion(bf16[4,192,768]{2,1,0:T(8,128)(2,1)} %collective-permute-done.27, bf16[2,4,192,768]{3,2,1,0:T(8,128)(2,1)S(1)} %get-tuple-element.206, bf16[2,4,192,768]{3,2,1,0:T(8,128)(2,1)} %collective-permute-done.25), kind=kLoop, calls=%fused_computation.3 | loop fusion | flops 4718592 | bytes 4718592 | tf_op jit(solution)/shard_map/convert_element_type | solution.py:239
  227.2 3.6 %all-to-all-start.2 = ((bf16[4,192,768]{2,1,0:T(8,128)(2,1)}), bf16[4,192,768]{2,1,0:T(8,128)(2,1)S(1)}, u32[]{:S(2)}, u32[]{:S(2)}) async-start(bf16[4,192,768]{2,1,0:T(8,128)(2,1)} %fusion), calls=%async_computation.2 | async-start | bytes 2359296 | tf_op jit(solution)/shard_map/all_to_all | solution.py:224
  230.9 3.0 add_convert_fusion.2
  236.5 9.0 %input_gradient.1 = f32[1024,768]{1,0:T(8,128)} custom-call(bf16[1024,768]{1,0:T(8,128)(2,1)} %get-tuple-element.163.dq, bf16[1024,768]{1,0:T(8,128)(2,1)} %get-tuple-element.164.dk, bf16[1024,768]{1,0:T(8,128)(2,1)} %get-tuple-element.165.dv, bf16[4,768,768]{2,1,0:T(8,128)(2,1)} %get-tuple-element.123.wo.full, f32[1024,768]{1,0:T(8,128)} %get-tuple-element.173.first, ...), custom_call_target="tpu_custom_call" | custom-call | flops 30000001024 | bytes 90000000 | tf_op jit(solution)/shard_map/input_gradient/pallas_call | solution.py:866
  245.5 4.8 %collective-permute-done.29 = bf16[2,4,96,768]{3,2,1,0:T(8,128)(2,1)} collective-permute-done((bf16[2,4,96,768]{3,2,1,0:T(8,128)(2,1)S(1)}, bf16[2,4,96,768]{3,2,1,0:T(8,128)(2,1)}, u32[]{:S(2)}, u32[]{:S(2)}) %collective-permute-start.29) | collective-permute-done | bytes 1179680 | tf_op jit(solution)/shard_map/ppermute | solution.py:208
  254.1 2.9 collective-permute-start.32
  257.0 4.3 %all-to-all-done.2 = bf16[4,192,768]{2,1,0:T(8,128)(2,1)S(1)} async-done(((bf16[4,192,768]{2,1,0:T(8,128)(2,1)}), bf16[4,192,768]{2,1,0:T(8,128)(2,1)S(1)}, u32[]{:S(2)}, u32[]{:S(2)}) %all-to-all-start.2) | async-done | bytes 1179680 | tf_op jit(solution)/shard_map/all_to_all | solution.py:224
  262.5 3.8 %all-to-all-start.3 = ((bf16[4,192,768]{2,1,0:T(8,128)(2,1)}), bf16[4,192,768]{2,1,0:T(8,128)(2,1)S(1)}, u32[]{:S(2)}, u32[]{:S(2)}) async-start(bf16[4,192,768]{2,1,0:T(8,128)(2,1)} %broadcast_in_dim.44), calls=%async_computation.3 | async-start | bytes 2359296 | tf_op jit(solution)/shard_map/all_to_all | solution.py:224
  275.0 7.6 %score.1 = f32[32,32]{1,0:T(8,128)} custom-call(f32[1024,768]{1,0:T(8,128)} %get-tuple-element.181.out_ref, s32[1,1024]{1,0:T(1,128)} %bitcast.82, s32[32,1]{1,0:T(8,128)} %copy-done.17, bf16[1024,768]{1,0:T(8,128)(2,1)} %table_ref.1, s32[32,32]{1,0:T(8,128)} %pick_ref.1, bf16[4,96,768]{2,1,0:T(8,128)(2,1)} %copy-done, f32[8,1280]{1,0:T(8,128)} %copy-done.12), custom_call_target="tpu_custom_call" | custom-call | flops 40000000000 | bytes 120000000 | tf_op jit(solution)/shard_map/score/pallas_call | solution.py:914
  287.3 3.5 %all-to-all-start.4 = ((bf16[4,96,768]{2,1,0:T(8,128)(2,1)}), bf16[4,96,768]{2,1,0:T(8,128)(2,1)S(1)}, u32[]{:S(2)}, u32[]{:S(2)}) async-start(bf16[4,96,768]{2,1,0:T(8,128)(2,1)} %broadcast_in_dim.45), calls=%async_computation.4 | async-start | bytes 1179648 | tf_op jit(solution)/shard_map/all_to_all | solution.py:224
  292.5 4.7 %finish_feed.1 = (f32[768,768]{1,0:T(8,128)}, f32[768,768]{1,0:T(8,128)}) custom-call(s32[3]{0:T(128)} %pad_add_fusion.place, bf16[4,192,768]{2,1,0:T(8,128)(2,1)} %copy-done.3, bf16[4,192,768]{2,1,0:T(8,128)(2,1)} %copy-done.33, bf16[96,768]{1,0:T(8,128)(2,1)} %copy-done.5, f32[8,1280]{1,0:T(8,128)} %add.135.refs_1_), custom_call_target="tpu_custom_call" | custom-call | flops 30000001024 | bytes 90000000 | tf_op jit(solution)/shard_map/finish_feed/pallas_call | solution.py:160
  297.2 2.9 all-to-all-done.4.mine
  303.0 2.8 finish_heads.1
  (246 shorter events, 64.4 us)
Async XLA Ops:
  3.6 19.6 %collective-permute-start.1 = (bf16[96,768]{1,0:T(8,128)(2,1)}, bf16[96,768]{1,0:T(8,128)(2,1)S(1)}, u32[]{:S(2)}, u32[]{:S(2)}) collective-permute-start(bf16[96,768]{1,0:T(8,128)(2,1)} %piece_heads.1), channel_id=1, source_target_pairs={{0,2},{1,3},{2,0},{3,1},{4,6},{5,7},{6,4},{7,5},{8,10},{9,11},{10,... | collective-permute-start | bytes 442376 | tf_op jit(solution)/shard_map/ppermute | solution.py:65
  7.7 15.5 %collective-permute-start.2 = (bf16[96,768]{1,0:T(8,128)(2,1)}, bf16[96,768]{1,0:T(8,128)(2,1)S(1)}, u32[]{:S(2)}, u32[]{:S(2)}) collective-permute-start(bf16[96,768]{1,0:T(8,128)(2,1)} %piece_heads.1), channel_id=1, source_target_pairs={{0,3},{1,2},{2,1},{3,0},{4,7},{5,6},{6,5},{7,4},{8,11},{9,10},{10,... | collective-permute-start | bytes 442376 | tf_op jit(solution)/shard_map/ppermute | solution.py:65
  13.6 24.2 %all-to-all-start = ((bf16[4,112,768]{2,1,0:T(8,128)(2,1)}), bf16[4,112,768]{2,1,0:T(8,128)(2,1)S(1)}, u32[]{:S(2)}, u32[]{:S(2)}) async-start(bf16[4,112,768]{2,1,0:T(8,128)(2,1)} %get-tuple-element.112), calls=%async_computation | async-start | bytes 1376256 | tf_op jit(solution)/shard_map/all_to_all | solution.py:224
  37.3 15.3 %collective-permute-start.6 = (bf16[288,768]{1,0:T(8,128)(2,1)S(1)}, bf16[288,768]{1,0:T(8,128)(2,1)}, u32[]{:S(2)}, u32[]{:S(2)}) collective-permute-start(bf16[288,768]{1,0:T(8,128)(2,1)S(1)} %constant_dynamic-update-slice_fusion.refs_0_), channel_id=1, source_target_pairs={{0,4},{4,0},{8,12},{12,8},{16,20},{20,16},{24,28},{28,24},{1,5},{5... | collective-permute-start | bytes 1327112 | tf_op jit(solution)/shard_map/ppermute | solution.py:65
  37.3 15.3 %collective-permute-start.7 = (bf16[288,768]{1,0:T(8,128)(2,1)S(1)}, bf16[288,768]{1,0:T(8,128)(2,1)}, u32[]{:S(2)}, u32[]{:S(2)}) collective-permute-start(bf16[288,768]{1,0:T(8,128)(2,1)S(1)} %collective-permute-done.3.refs_1_), channel_id=1, source_target_pairs={{0,4},{4,0},{8,12},{12,8},{16,20},{20,16},{24,28},{28,24},{1,5},{5... | collective-permute-start | bytes 1327112 | tf_op jit(solution)/shard_map/ppermute | solution.py:65
  37.8 14.8 %collective-permute-start.8 = (bf16[288,768]{1,0:T(8,128)(2,1)S(1)}, bf16[288,768]{1,0:T(8,128)(2,1)}, u32[]{:S(2)}, u32[]{:S(2)}) collective-permute-start(bf16[288,768]{1,0:T(8,128)(2,1)S(1)} %collective-permute-done.4.refs_2_), channel_id=1, source_target_pairs={{0,4},{4,0},{8,12},{12,8},{16,20},{20,16},{24,28},{28,24},{1,5},{5... | collective-permute-start | bytes 1327112 | tf_op jit(solution)/shard_map/ppermute | solution.py:65
  43.3 22.9 %all-to-all-start.1 = ((bf16[4,96,768]{2,1,0:T(8,128)(2,1)}), bf16[4,96,768]{2,1,0:T(8,128)(2,1)S(1)}, u32[]{:S(2)}, u32[]{:S(2)}) async-start(bf16[4,96,768]{2,1,0:T(8,128)(2,1)} %get-tuple-element.116), calls=%async_computation.1 | async-start | bytes 1179648 | tf_op jit(solution)/shard_map/all_to_all | solution.py:224
  52.7 12.6 %collective-permute-start.10 = (bf16[288,768]{1,0:T(8,128)(2,1)S(1)}, bf16[288,768]{1,0:T(8,128)(2,1)S(1)}, u32[]{:S(2)}, u32[]{:S(2)}) collective-permute-start(bf16[288,768]{1,0:T(8,128)(2,1)S(1)} %pad_maximum_fusion.refs_0_), channel_id=1, source_target_pairs={{0,8},{4,20},{8,0},{12,28},{16,24},{20,4},{24,16},{28,12},{1,9},{5... | collective-permute-start | bytes 1327112 | tf_op jit(solution)/shard_map/ppermute | solution.py:208
  54.8 40.6 %collective-permute-start.16 = (bf16[288,768]{1,0:T(8,128)(2,1)S(1)}, bf16[288,768]{1,0:T(8,128)(2,1)}, u32[]{:S(2)}, u32[]{:S(2)}) collective-permute-start(bf16[288,768]{1,0:T(8,128)(2,1)S(1)} %pad_maximum_fusion.refs_0_), channel_id=1, source_target_pairs={{0,4},{4,0},{8,12},{12,8},{16,20},{20,16},{24,28},{28,24},{1,5},{5... | collective-permute-start | bytes 1327112 | tf_op jit(solution)/shard_map/ppermute | solution.py:65
  66.3 16.9 %collective-permute-start.13 = (bf16[288,768]{1,0:T(8,128)(2,1)S(1)}, bf16[288,768]{1,0:T(8,128)(2,1)S(1)}, u32[]{:S(2)}, u32[]{:S(2)}) collective-permute-start(bf16[288,768]{1,0:T(8,128)(2,1)S(1)} %pad_maximum_fusion.1.refs_0_), channel_id=1, source_target_pairs={{0,8},{4,20},{8,0},{12,28},{16,24},{20,4},{24,16},{28,12},{1,9},{5... | collective-permute-start | bytes 1327112 | tf_op jit(solution)/shard_map/ppermute | solution.py:208
  67.9 15.3 %collective-permute-start.14 = (bf16[288,768]{1,0:T(8,128)(2,1)S(1)}, bf16[288,768]{1,0:T(8,128)(2,1)S(1)}, u32[]{:S(2)}, u32[]{:S(2)}) collective-permute-start(bf16[288,768]{1,0:T(8,128)(2,1)S(1)} %pad_maximum_fusion.1.refs_0_), channel_id=1, source_target_pairs={{0,16},{4,12},{8,24},{12,4},{16,0},{20,28},{24,8},{28,20},{1,17},{... | collective-permute-start | bytes 1327112 | tf_op jit(solution)/shard_map/ppermute | solution.py:208
  68.4 14.2 %collective-permute-start.12 = (bf16[288,768]{1,0:T(8,128)(2,1)S(1)}, bf16[288,768]{1,0:T(8,128)(2,1)S(1)}, u32[]{:S(2)}, u32[]{:S(2)}) collective-permute-start(bf16[288,768]{1,0:T(8,128)(2,1)S(1)} %collective-permute-done.10.refs_1_), channel_id=1, source_target_pairs={{0,16},{4,12},{8,24},{12,4},{16,0},{20,28},{24,8},{28,20},{1,17},{... | collective-permute-start | bytes 1327112 | tf_op jit(solution)/shard_map/ppermute | solution.py:208
  69.9 25.7 %collective-permute-start.17 = (bf16[288,768]{1,0:T(8,128)(2,1)S(1)}, bf16[288,768]{1,0:T(8,128)(2,1)S(1)}, u32[]{:S(2)}, u32[]{:S(2)}) collective-permute-start(bf16[288,768]{1,0:T(8,128)(2,1)S(1)} %collective-permute-done.10.refs_1_), channel_id=1, source_target_pairs={{0,4},{4,0},{8,12},{12,8},{16,20},{20,16},{24,28},{28,24},{1,5},{5... | collective-permute-start | bytes 1327112 | tf_op jit(solution)/shard_map/ppermute | solution.py:65
  82.5 13.4 %collective-permute-start.18 = (bf16[288,768]{1,0:T(8,128)(2,1)}, bf16[288,768]{1,0:T(8,128)(2,1)}, u32[]{:S(2)}, u32[]{:S(2)}) collective-permute-start(bf16[288,768]{1,0:T(8,128)(2,1)} %collective-permute-done.11.refs_2_), channel_id=1, source_target_pairs={{0,4},{4,0},{8,12},{12,8},{16,20},{20,16},{24,28},{28,24},{1,5},{5... | collective-permute-start | bytes 1327112 | tf_op jit(solution)/shard_map/ppermute | solution.py:65
  83.2 11.8 %collective-permute-start.15 = (bf16[288,768]{1,0:T(8,128)(2,1)S(1)}, bf16[288,768]{1,0:T(8,128)(2,1)S(1)}, u32[]{:S(2)}, u32[]{:S(2)}) collective-permute-start(bf16[288,768]{1,0:T(8,128)(2,1)S(1)} %collective-permute-done.13.refs_1_), channel_id=1, source_target_pairs={{0,16},{4,12},{8,24},{12,4},{16,0},{20,28},{24,8},{28,20},{1,17},{... | collective-permute-start | bytes 1327112 | tf_op jit(solution)/shard_map/ppermute | solution.py:208
  84.2 11.9 %collective-permute-start.19 = (bf16[288,768]{1,0:T(8,128)(2,1)S(1)}, bf16[288,768]{1,0:T(8,128)(2,1)}, u32[]{:S(2)}, u32[]{:S(2)}) collective-permute-start(bf16[288,768]{1,0:T(8,128)(2,1)S(1)} %collective-permute-done.12.refs_3_), channel_id=1, source_target_pairs={{0,4},{4,0},{8,12},{12,8},{16,20},{20,16},{24,28},{28,24},{1,5},{5... | collective-permute-start | bytes 1327112 | tf_op jit(solution)/shard_map/ppermute | solution.py:65
  95.0 15.0 %collective-permute-start.20 = (bf16[288,768]{1,0:T(8,128)(2,1)S(1)}, bf16[288,768]{1,0:T(8,128)(2,1)}, u32[]{:S(2)}, u32[]{:S(2)}) collective-permute-start(bf16[288,768]{1,0:T(8,128)(2,1)S(1)} %copy-done.8), channel_id=1, source_target_pairs={{0,4},{4,0},{8,12},{12,8},{16,20},{20,16},{24,28},{28,24},{1,5},{5... | collective-permute-start | bytes 1327112 | tf_op jit(solution)/shard_map/ppermute | solution.py:65
  95.4 14.6 %collective-permute-start.21 = (bf16[288,768]{1,0:T(8,128)(2,1)S(1)}, bf16[288,768]{1,0:T(8,128)(2,1)S(1)}, u32[]{:S(2)}, u32[]{:S(2)}) collective-permute-start(bf16[288,768]{1,0:T(8,128)(2,1)S(1)} %collective-permute-done.13.refs_1_), channel_id=1, source_target_pairs={{0,4},{4,0},{8,12},{12,8},{16,20},{20,16},{24,28},{28,24},{1,5},{5... | collective-permute-start | bytes 1327112 | tf_op jit(solution)/shard_map/ppermute | solution.py:65
  95.6 14.4 %collective-permute-start.22 = (bf16[288,768]{1,0:T(8,128)(2,1)S(1)}, bf16[288,768]{1,0:T(8,128)(2,1)S(1)}, u32[]{:S(2)}, u32[]{:S(2)}) collective-permute-start(bf16[288,768]{1,0:T(8,128)(2,1)S(1)} %collective-permute-done.14.refs_2_), channel_id=1, source_target_pairs={{0,4},{4,0},{8,12},{12,8},{16,20},{20,16},{24,28},{28,24},{1,5},{5... | collective-permute-start | bytes 1327112 | tf_op jit(solution)/shard_map/ppermute | solution.py:65
  96.0 14.0 %collective-permute-start.23 = (bf16[288,768]{1,0:T(8,128)(2,1)S(1)}, bf16[288,768]{1,0:T(8,128)(2,1)S(1)}, u32[]{:S(2)}, u32[]{:S(2)}) collective-permute-start(bf16[288,768]{1,0:T(8,128)(2,1)S(1)} %collective-permute-done.15.refs_8_.refs_3_), channel_id=1, source_target_pairs={{0,4},{4,0},{8,12},{12,8},{16,20},{20,16},{24,28},{28,24},{1,5},{5... | collective-permute-start | bytes 1327112 | tf_op jit(solution)/shard_map/ppermute | solution.py:65
  155.6 14.5 %collective-permute-start.24 = (bf16[4,4,192,768]{3,2,1,0:T(8,128)(2,1)}, bf16[4,4,192,768]{3,2,1,0:T(8,128)(2,1)}, u32[]{:S(2)}, u32[]{:S(2)}) collective-permute-start(bf16[4,4,192,768]{3,2,1,0:T(8,128)(2,1)} %bitcast.87), channel_id=1, source_target_pairs={{0,4},{4,0},{8,12},{12,8},{16,20},{20,16},{24,28},{28,24},{1,5},{5... | collective-permute-start | bytes 14155784 | tf_op jit(solution)/shard_map/ppermute | solution.py:65
  175.4 29.2 %collective-permute-start.25 = (bf16[2,4,192,768]{3,2,1,0:T(8,128)(2,1)}, bf16[2,4,192,768]{3,2,1,0:T(8,128)(2,1)}, u32[]{:S(2)}, u32[]{:S(2)}) collective-permute-start(bf16[2,4,192,768]{3,2,1,0:T(8,128)(2,1)} %get-tuple-element.207.refs_0_), channel_id=1, source_target_pairs={{0,8},{4,20},{8,0},{12,28},{16,24},{20,4},{24,16},{28,12},{1,9},{5... | collective-permute-start | bytes 7077896 | tf_op jit(solution)/shard_map/ppermute | solution.py:208
  206.1 16.4 %collective-permute-start.27 = (bf16[4,192,768]{2,1,0:T(8,128)(2,1)S(1)}, bf16[4,192,768]{2,1,0:T(8,128)(2,1)}, u32[]{:S(2)}, u32[]{:S(2)}) collective-permute-start(bf16[4,192,768]{2,1,0:T(8,128)(2,1)S(1)} %fusion.1.refs_1_), channel_id=1, source_target_pairs={{0,16},{4,12},{8,24},{12,4},{16,0},{20,28},{24,8},{28,20},{1,17},{... | collective-permute-start | bytes 3538952 | tf_op jit(solution)/shard_map/ppermute | solution.py:208
  227.2 34.0 %all-to-all-start.2 = ((bf16[4,192,768]{2,1,0:T(8,128)(2,1)}), bf16[4,192,768]{2,1,0:T(8,128)(2,1)S(1)}, u32[]{:S(2)}, u32[]{:S(2)}) async-start(bf16[4,192,768]{2,1,0:T(8,128)(2,1)} %fusion), calls=%async_computation.2 | async-start | bytes 2359296 | tf_op jit(solution)/shard_map/all_to_all | solution.py:224
  233.9 16.4 %collective-permute-start.29 = (bf16[2,4,96,768]{3,2,1,0:T(8,128)(2,1)S(1)}, bf16[2,4,96,768]{3,2,1,0:T(8,128)(2,1)}, u32[]{:S(2)}, u32[]{:S(2)}) collective-permute-start(bf16[2,4,96,768]{3,2,1,0:T(8,128)(2,1)S(1)} %get-tuple-element.209.refs_0_), channel_id=1, source_target_pairs={{0,8},{4,20},{8,0},{12,28},{16,24},{20,4},{24,16},{28,12},{1,9},{5... | collective-permute-start | bytes 3538952 | tf_op jit(solution)/shard_map/ppermute | solution.py:208
  251.5 14.8 %collective-permute-start.31 = (bf16[4,96,768]{2,1,0:T(8,128)(2,1)S(1)}, bf16[4,96,768]{2,1,0:T(8,128)(2,1)S(1)}, u32[]{:S(2)}, u32[]{:S(2)}) collective-permute-start(bf16[4,96,768]{2,1,0:T(8,128)(2,1)S(1)} %fusion.4), channel_id=1, source_target_pairs={{0,16},{4,12},{8,24},{12,4},{16,0},{20,28},{24,8},{28,20},{1,17},{... | collective-permute-start | bytes 1769480 | tf_op jit(solution)/shard_map/ppermute | solution.py:208
  254.1 12.2 %collective-permute-start.32 = (f32[8,1280]{1,0:T(8,128)}, f32[8,1280]{1,0:T(8,128)}, u32[]{:S(2)}, u32[]{:S(2)}) collective-permute-start(f32[8,1280]{1,0:T(8,128)} %add.123), channel_id=1, source_target_pairs={{0,2},{1,3},{2,0},{3,1},{4,6},{5,7},{6,4},{7,5},{8,10},{9,11},{10,... | collective-permute-start | bytes 122888 | tf_op jit(solution)/shard_map/ppermute | solution.py:65
  262.5 20.5 %all-to-all-start.3 = ((bf16[4,192,768]{2,1,0:T(8,128)(2,1)}), bf16[4,192,768]{2,1,0:T(8,128)(2,1)S(1)}, u32[]{:S(2)}, u32[]{:S(2)}) async-start(bf16[4,192,768]{2,1,0:T(8,128)(2,1)} %broadcast_in_dim.44), calls=%async_computation.3 | async-start | bytes 2359296 | tf_op jit(solution)/shard_map/all_to_all | solution.py:224
  268.6 14.1 %collective-permute-start.33 = (f32[8,1280]{1,0:T(8,128)S(1)}, f32[8,1280]{1,0:T(8,128)S(1)}, u32[]{:S(2)}, u32[]{:S(2)}) collective-permute-start(f32[8,1280]{1,0:T(8,128)S(1)} %add.129.refs_1_), channel_id=1, source_target_pairs={{0,8},{4,12},{8,0},{12,4},{16,24},{20,28},{24,16},{28,20},{1,9},{5... | collective-permute-start | bytes 122888 | tf_op jit(solution)/shard_map/ppermute | solution.py:65
  270.6 12.0 %collective-permute-start.34 = (bf16[96,768]{1,0:T(8,128)(2,1)S(1)}, bf16[96,768]{1,0:T(8,128)(2,1)S(1)}, u32[]{:S(2)}, u32[]{:S(2)}) collective-permute-start(bf16[96,768]{1,0:T(8,128)(2,1)S(1)} %get-tuple-element.215), channel_id=1, source_target_pairs={{0,1},{1,0},{2,3},{3,2},{4,5},{5,4},{6,7},{7,6},{8,9},{9,8},{10,11... | collective-permute-start | bytes 442376 | tf_op jit(solution)/shard_map/ppermute | solution.py:65
  270.6 12.4 %collective-permute-start.35 = (bf16[96,768]{1,0:T(8,128)(2,1)S(1)}, bf16[96,768]{1,0:T(8,128)(2,1)S(1)}, u32[]{:S(2)}, u32[]{:S(2)}) collective-permute-start(bf16[96,768]{1,0:T(8,128)(2,1)S(1)} %get-tuple-element.214), channel_id=1, source_target_pairs={{0,2},{1,3},{2,0},{3,1},{4,6},{5,7},{6,4},{7,5},{8,10},{9,11},{10,... | collective-permute-start | bytes 442376 | tf_op jit(solution)/shard_map/ppermute | solution.py:65
  287.3 12.8 %all-to-all-start.4 = ((bf16[4,96,768]{2,1,0:T(8,128)(2,1)}), bf16[4,96,768]{2,1,0:T(8,128)(2,1)S(1)}, u32[]{:S(2)}, u32[]{:S(2)}) async-start(bf16[4,96,768]{2,1,0:T(8,128)(2,1)} %broadcast_in_dim.45), calls=%async_computation.4 | async-start | bytes 1179648 | tf_op jit(solution)/shard_map/all_to_all | solution.py:224
  (62 other events, 548.9 us)

commit v4 on v3

--- a/solution.py
+++ b/solution.py
@@ -25,8 +25,8 @@
 CORE, XBIT, YBIT = 1, 2, 4
 
 
-def params(mebi=60):
-    return pltpu.CompilerParams(vmem_limit_bytes=mebi * MEBI)
+def params(mebi=60.5):
+    return pltpu.CompilerParams(vmem_limit_bytes=int(mebi * MEBI))
 
 
 def cost(us):
@@ -144,22 +144,24 @@
     )(place, wu, wd, rest)
 
 
-def finish_feed_kernel(place, mine, other, up, down, held):
-    core = place[0]
-    sub = mine.shape[1] // 2
-    for c, ref in enumerate((mine, other)):
-        for g in range(4):
-            start = pl.multiple_of(((core ^ c) * 4 + g) * sub, GRAIN)
-            held[pl.ds(start, sub), :] = ref[g, :sub, :].astype(F32)
-            down[pl.ds(start, sub), :] = ref[g, sub:, :].astype(F32)
+def finish_feed_kernel(place, *refs):
+    pieces, (up, down, held) = refs[:8], refs[-3:]
+    core, plane = place[0], place[1]
+    sub = pieces[0].shape[0] // 2
+    for c in range(2):
+        for g, ref in enumerate(pieces[4 * c : 4 * c + 4]):
+            chip = plane ^ neighbour(core ^ c, g)
+            start = pl.multiple_of(((core ^ c) * 4 + chip) * sub, GRAIN)
+            held[pl.ds(start, sub), :] = ref[:sub, :].astype(F32)
+            down[pl.ds(start, sub), :] = ref[sub:, :].astype(F32)
     up[...] = held[...].T
 
 
 def finish_feed(place, pieces, *tokens):
-    _, rows, width = pieces[0].shape
-    return pl.pallas_call(
-        finish_feed_drop,
-        in_specs=[scalar_spec()] + [held_spec()] * 2 + [token_spec() for _ in tokens],
+    rows, width = pieces[0].shape
+    return pl.pallas_call(
+        finish_feed_kernel,
+        in_specs=[scalar_spec()] + [held_spec()] * 8 + [token_spec() for _ in tokens],
         out_specs=[held_spec()] * 2,
         out_shape=[shape((width, 4 * rows), F32), shape((4 * rows, width), F32)],
         scratch_shapes=[pltpu.VMEM((4 * rows, width), F32)],
@@ -167,10 +169,6 @@
         cost_estimate=cost(6),
         name="finish_feed",
     )(place, *pieces, *tokens)
-
-
-def finish_feed_drop(place, mine, other, *refs):
-    finish_feed_kernel(place, mine, other, *refs[-3:])
 
 
 def finish_heads_kernel(place, mine, other, *outs):
@@ -245,14 +243,6 @@
 
 def side_sum(stay, got):
     return add(stay[0], got[0]), add(stay[1], got[1])
-
-
-def shard_swap(parts, n_mp):
-    shard = lax.axis_index("mp")
-    return [
-        swap(lax.dynamic_index_in_dim(parts, shard ^ r, 0, keepdims=False), "mp", r, n_mp)
-        for r in range(1, n_mp)
-    ]
 
 
 def shard_sum(own, got, n_dp):
@@ -663,7 +653,7 @@
     )(place, act, unit, cot, own, vectors, *pieces)
 
 
-def feed_back_kernel(grad, x, wu, wd, slope, act, keep, send, bias, out, held):
+def feed_back_kernel(place, grad, x, wu, wd, slope, act, keep, send, bias, out, held):
     step = pl.program_id(0)
     half = pl.num_programs(0) // 2
     chips, shards, _, sub, width = keep.shape
@@ -681,16 +671,17 @@
         held[span, :] = low
         term = jnp.sum(low.astype(F32), axis=0, keepdims=True)
         total = term if total is None else total + term
-    for block in range(4):
-
-        @pl.when(step == (block + 2) % 4)
-        def _():
-            for g in range(chips):
-                for r in range(shards):
-                    at = (g * shards + r) * sub
-                    row = block * chips + g
-                    bias[row : row + 1, r * 128 : r * 128 + sub] = total[:, at : at + sub]
-
+    core, plane = place[0], place[1]
+    owner = jnp.where(step < half, core ^ 1, core)
+    row = lax.broadcasted_iota(jnp.int32, (bias.shape[0], sub), 0)
+    for g in range(chips):
+        early = plane ^ jnp.where(owner == 0, neighbour(0, g), neighbour(1, g))
+        late = plane ^ jnp.where(owner == 0, neighbour(0, 2 + g), neighbour(1, 2 + g))
+        target = owner * 4 + jnp.where(lax.rem(step, half) == 0, early, late)
+        for r in range(shards):
+            at = (g * shards + r) * sub
+            lanes = slice(r * 128, r * 128 + sub)
+            bias[:, lanes] = jnp.where(row == target, total[:, at : at + sub], bias[:, lanes])
     out[...] += jnp.dot(held[...], wu[...], preferred_element_type=F32)
     dims = (chips, shards, sub, width)
     up = lax.dot_general(held[...], x[...], TN, preferred_element_type=F32).astype(BF)
@@ -707,7 +698,7 @@
         keep[:, :, 1] = down.reshape(dims)
 
 
-def feed_back(grad, x, wu, wd, slope, act, n_mp):
+def feed_back(place, grad, x, wu, wd, slope, act, n_mp):
     rows, width = x.shape
     hidden = wu.shape[0]
     span = hidden // 4
@@ -719,7 +710,7 @@
     return pl.pallas_call(
         feed_back_kernel,
         grid=(4,),
-        in_specs=[full, full, weight, weight, wide, wide],
+        in_specs=[scalar_spec(), full, full, weight, weight, wide, wide],
         out_specs=[
             pl.BlockSpec(block, lambda j: (jnp.maximum(j - 2, 0), 0, 0, 0, 0)),
             pl.BlockSpec(block, lambda j: (jnp.minimum(j, 1), 0, 0, 0, 0)),
@@ -736,11 +727,11 @@
         compiler_params=params(),
         cost_estimate=cost(27),
         name="feed_back",
-    )(grad, x, wu, wd, slope, act)
+    )(place, grad, x, wu, wd, slope, act)
 
 
 def middle_kernel(normed, second, unit, saved, ctx, wo, gain, *refs):
-    first, context_grad, inner_sum, weight, sums, held = refs[-6:]
+    first, context_grad, inner_sum, weight, sums, held, lows = refs[-7:]
     step = pl.program_id(0)
     grad = normed[...] + second[...]
     unit_val = unit[...]
@@ -764,21 +755,23 @@
     inner_sum[...] = jnp.dot(high, head, preferred_element_type=F32) + jnp.dot(
         rest, head, preferred_element_type=F32
     )
-    term = lax.dot_general(ctx[...], low, TN, preferred_element_type=F32)
+    at = pl.ds(pl.multiple_of(step * ROW_BLOCK, ROW_BLOCK), ROW_BLOCK)
+    lows[at, :] = low
+    held[at, :] = ctx[...]
 
     @pl.when(step == 0)
     def _():
         sums[...] = jnp.zeros_like(sums)
-        held[...] = jnp.zeros_like(held)
-
-    held[...] += term
+
     sums[0:1, :] += jnp.sum(low.astype(F32), axis=0, keepdims=True)
     sums[1:2, :] += jnp.sum(grad * unit_val, axis=0, keepdims=True)
     sums[2:3, :] += jnp.sum(grad, axis=0, keepdims=True)
 
     @pl.when(step == pl.num_programs(0) - 1)
     def _():
-        weight[...] = held[...].astype(BF)
+        weight[...] = lax.dot_general(
+            held[...], lows[...], TN, preferred_element_type=F32
+        ).astype(BF)
 
 
 def middle(normed, second, unit, saved, ctx, full, gain, *tokens):
@@ -805,7 +798,7 @@
             shape((width, width), BF),
             shape((8, width), F32),
         ],
-        scratch_shapes=[pltpu.VMEM((width, width), F32)],
+        scratch_shapes=[pltpu.VMEM((rows, width), BF)] * 2,
         compiler_params=params(),
         cost_estimate=cost(8),
         name="middle",
@@ -960,10 +953,9 @@
     bias_rows = jnp.stack(
         [jnp.pad(b_query, (0, width - cut)), jnp.pad(b_value, (0, width - cut)), b_up]
     )
-    turned, up_piece, down_piece = piece_feed(
-        place, w_up, w_down, after(jnp.pad(bias_rows, ((0, GRAIN - 3), (0, 0))), heads_piece), n_mp
-    )
-    heads_parts = [swap(after(heads_piece, down_piece), "mp", 1, n_mp)] + [
+    rest = jnp.pad(after(bias_rows, heads_piece), ((0, GRAIN - 3), (0, 0)))
+    turned, up_piece, down_piece = piece_feed(place, w_up, w_down, rest, n_mp)
+    heads_parts = [swap(after(heads_piece, rest), "mp", 1, n_mp)] + [
         swap(heads_piece, "mp", r, n_mp) for r in range(2, n_mp)
     ]
     up_got = exchange(up_piece, "mp")
@@ -987,7 +979,6 @@
     up_shards = others(after(up_got, *heads_mine, *heads_other))
     up_first = first_swap(up_shards, n_dp)
     up_second = second_swap(up_shards, n_dp)
-    down_got = exchange(after(down_piece, up_got), "mp")
 
     ranks = lax.broadcasted_iota(jnp.int32, (4, 4), 0)
     places4 = lax.broadcasted_iota(jnp.int32, (4, 4), 1)
@@ -1021,39 +1012,39 @@
     query, key, value, full = project(
         place, hidden_in, own_heads, query_bias, value_bias, heads_mine + heads_other
     )
-    up_first, up_second, down_got, query = lax.optimization_barrier(
-        (up_first, up_second, down_got, query)
-    )
+    up_first, up_second, query = lax.optimization_barrier((up_first, up_second, query))
+    down_got = exchange(after(down_piece, query), "mp")
     up_corner = second_swap(up_first, n_dp)
     up_mine = [up_shards, up_first, up_second]
     up_other = [core_swap(p, n_dp) for p in up_mine]
+    held = attend(
+        0, 2, query, key, value, segc, segr, hidden_in, full,
+        vectors[5:6], vectors[1:2], vectors[2:3], (),
+    )
+    up_corner, down_got, up_other, *held = lax.optimization_barrier(
+        (up_corner, down_got, up_other, *held)
+    )
+    up_pieces = up_mine + [up_corner] + up_other + [core_swap(up_corner, n_dp)]
     down_shards = others(down_got)
     down_first = first_swap(down_shards, n_dp)
     down_second = second_swap(down_shards, n_dp)
-    held = attend(
-        0, 2, query, key, value, segc, segr, hidden_in, full,
-        vectors[5:6], vectors[1:2], vectors[2:3], (), down_shards,
-    )
-    up_corner, down_first, down_second, *held = lax.optimization_barrier(
-        (up_corner, down_first, down_second, *held)
-    )
-    up_pieces = up_mine + [up_corner] + up_other + [core_swap(up_corner, n_dp)]
+    context, saved, unit, low = attend(
+        1, 2, query, key, value, segc, segr, hidden_in, full,
+        vectors[5:6], vectors[1:2], vectors[2:3], held, down_shards,
+    )
+    down_first, down_second, low = lax.optimization_barrier((down_first, down_second, low))
     down_corner = second_swap(down_first, n_dp)
     down_mine = [down_shards, down_first, down_second]
-    context, saved, unit, low = attend(
-        1, 2, query, key, value, segc, segr, hidden_in, full,
-        vectors[5:6], vectors[1:2], vectors[2:3], held,
-    )
-    down_corner, low = lax.optimization_barrier((down_corner, low))
-    down_mine = down_mine + [down_corner]
-    down_pieces = down_mine + [core_swap(p, n_dp) for p in down_mine]
-    act, slope, wu = feed_up(place, low, turned, up_bias, up_pieces, down_corner)
+    down_other = [core_swap(p, n_dp) for p in down_mine]
+    act, slope, wu = feed_up(place, low, turned, up_bias, up_pieces, *down_mine[1:])
+    down_corner, act = lax.optimization_barrier((down_corner, act))
+    down_pieces = down_mine + [down_corner] + down_other + [core_swap(down_corner, n_dp)]
     layer_out, output, second_grad, down_grad, second_sums, wd = feed_down(
         place, act, unit, cotangent, w_down, vectors, down_pieces
     )
 
     feed_keep, feed_send, up_sums, normed = feed_back(
-        down_grad, low, wu, wd, slope, act, n_mp
+        place, down_grad, low, wu, wd, slope, act, n_mp
     )
     dims = (4, n_mp, 2 * sub, width)
     feed_keep = feed_keep.reshape(dims)
@@ -1071,7 +1062,7 @@
     feed_own, feed_go = side_sum(feed_stay, got)
     got = second_swap(feed_go, n_dp)
     every = jnp.concatenate(
-        [second_sums + first_sums + head_sums, exact("sk,si->ki", order_up, up_sums)], axis=1
+        [second_sums + first_sums + head_sums, up_sums], axis=1
     )
     vector_got = swap(every, "mp", 1, n_mp)
     heads_keep, heads_send = head_weights(
@@ -1096,35 +1087,34 @@
     while bit < n_mp:
         vector_got = swap(every, "mp", bit, n_mp)
         bit *= 2
-    feed_got, heads_go = lax.optimization_barrier((feed_got, heads_go))
+    heads_parts = add(heads_own, heads_got)
+    feed_got, vector_got, heads_parts = lax.optimization_barrier(
+        (feed_got, vector_got, heads_parts)
+    )
+    heads_got = exchange(heads_parts, "mp")
+    every = every + after(vector_got, heads_parts)
+    feed_got, every = lax.optimization_barrier((feed_got, every))
     feed_total = shard_sum(feed_got[0], [feed_got[r] for r in range(1, n_mp)], n_dp)
-    feed_four = spread(feed_total, 4)
-    feed_mine = plane_gather(feed_four, n_dp)
-    heads_got, vector_got, feed_four = lax.optimization_barrier(
-        (heads_got, vector_got, feed_four)
-    )
-    heads_parts = add(heads_own, heads_got)
-    heads_got = shard_swap(heads_parts, n_mp)
-    heads_own = lax.dynamic_index_in_dim(heads_parts, shard, 0, keepdims=False)
-    every = every + after(vector_got, heads_parts)
+    feed_mine = [feed_total, first_swap(feed_total, n_dp), second_swap(feed_total, n_dp)]
+    feed_mine.append(swap(feed_total, "dp", XBIT | YBIT, n_dp))
     vector_got = swap(every, "dp", XBIT, n_dp)
     scores = score(
-        layer_out, segr, query_lengths.reshape(-1, 1), passages, passage_index,
-        heads_parts, every,
-    )
-    vector_got, scores = lax.optimization_barrier((vector_got, scores))
+        layer_out, segr, query_lengths.reshape(-1, 1), passages, passage_index, every
+    )
+    heads_got, vector_got, scores = lax.optimization_barrier((heads_got, vector_got, scores))
     every = every + vector_got
     vector_got = swap(every, "dp", YBIT, n_dp)
-    feed_mine, *heads_got = lax.optimization_barrier((feed_mine, *heads_got, scores))[:n_mp]
-    heads_total = shard_sum(heads_own, heads_got, n_dp)
-    heads_mine = plane_gather(spread(heads_total, 4), n_dp)
-    feed_other = core_swap(feed_mine, n_dp)
-    every = every + after(vector_got, heads_total)
+    heads_total = shard_sum(heads_got[0], [heads_got[r] for r in range(1, n_mp)], n_dp)
+    heads_four = spread(heads_total, 4)
+    heads_mine = plane_gather(heads_four, n_dp)
+    feed_mine = lax.optimization_barrier((*feed_mine, heads_four))[:4]
+    feed_other = [core_swap(p, n_dp) for p in feed_mine]
+    every = every + after(vector_got, heads_four)
     bit = 8
     while bit < n_dp:
         every = every + swap(every, "dp", bit, n_dp)
         bit *= 2
-    w_up_grad, w_down_grad = finish_feed(place, (feed_mine, feed_other), heads_total, every)
+    w_up_grad, w_down_grad = finish_feed(place, (*feed_mine, *feed_other), heads_four, every)
     heads_mine, w_up_grad = lax.optimization_barrier((heads_mine, w_up_grad))
     heads_other = core_swap(heads_mine, n_dp)
     query_t, key_t, value_t, w_output_grad = finish_heads(place, (heads_mine, heads_other))

time: 310 us -> 310 us (level)
  waiting for transfers between devices: 40.6 us -> 47.6 us
    ppermute x27 -> x28, starting transfers between devices: 21.2 us -> 14.4 us  [swap(): return lax.ppermute(block, axis, [(i, i ^ bit) for i in range(size)])]
    ppermute x27 -> x28, waiting for transfers between devices: 4.09 us -> 7.51 us  [swap(): return lax.ppermute(block, axis, [(i, i ^ bit) for i in range(size)])]
    ppermute x13 -> x15, waiting for transfers between devices: 28.5 us -> 31.8 us  [turn_swap(): lax.ppermute(block, 'dp', [(i, i ^ bits[i & 1]) for i in range(n_dp)])]
    ppermute x13 -> x15, starting transfers between devices: 15.3 us -> 18.5 us  [turn_swap(): lax.ppermute(block, 'dp', [(i, i ^ bits[i & 1]) for i in range(n_dp)])]
  transfers between devices with their start and end apart: 45 -> 48, of which waited for: 12 -> 14; matrix products, arithmetic and copies ran while one was open for 8% -> 6% of each run, Pallas kernels for 38% -> 38%
where the time goes in v4:
time: 310 us; the launch traced here: 304 us
  Pallas kernels  164 us (53%)
  starting transfers between devices  55.3 us (18%)
  waiting for transfers between devices  47.6 us (15%)
  other arithmetic  22.1 us (7%)
  local copies, waits for them, and re-layouts  13.1 us (4%)
    ppermute x15, waiting for transfers between devices, turn_swap(): lax.ppermute(block, 'dp', [(i, i ^ bits[i & 1]) for i in range(n_dp)])  31.8 us
    pallas_call x1, Pallas kernels, feed_back(): pl.pallas_call(feed_back_kernel, grid=(4,), in_specs=[scalar_spec(), full...  29.1 us
    pallas_call x1, Pallas kernels, attend_back(): pl.pallas_call(attend_back_kernel, grid=(rows // BLOCK,), in_specs=[scala...  23.6 us
    all_to_all x5, starting transfers between devices, exchange(): lax.all_to_all(block, axis, 0, 0, axis_index_groups=groups, tiled=True)  22.4 us
    pallas_call x2, Pallas kernels, attend(): pl.pallas_call(functools.partial(attend_kernel, part), grid=(steps,), in_...  21.2 us
    ppermute x15, starting transfers between devices, turn_swap(): lax.ppermute(block, 'dp', [(i, i ^ bits[i & 1]) for i in range(n_dp)])  18.5 us
    convert_element_type x6, other arithmetic, add(): return total.astype(BF)  16.3 us
    ppermute x28, starting transfers between devices, swap(): return lax.ppermute(block, axis, [(i, i ^ bit) for i in range(size)])  14.4 us
  transfers between devices with their start and end apart: 48, of which 14 were waited for; matrix products, arithmetic and copies ran while one was open for 6% of the time, Pallas kernels for 38%

profile of v4, /device:TPU:0, one launch (start us, length us, event | category | flops | bytes accessed | tf_op | source)
XLA Modules:
  0.0 304.4 jit_solution(14391618632416003147)
XLA Ops:
  1.3 2.3 piece_heads.1
  3.6 4.1 %collective-permute-start.1 = (bf16[96,768]{1,0:T(8,128)(2,1)}, bf16[96,768]{1,0:T(8,128)(2,1)S(1)}, u32[]{:S(2)}, u32[]{:S(2)}) collective-permute-start(bf16[96,768]{1,0:T(8,128)(2,1)} %piece_heads.1), channel_id=1, source_target_pairs={{0,2},{1,3},{2,0},{3,1},{4,6},{5,7},{6,4},{7,5},{8,10},{9,11},{10,... | collective-permute-start | bytes 442376 | tf_op jit(solution)/shard_map/ppermute | solution.py:65
  10.1 3.5 %piece_feed.1 = (bf16[768,768]{1,0:T(8,128)(2,1)}, bf16[4,112,768]{2,1,0:T(8,128)(2,1)}, bf16[4,96,768]{2,1,0:T(8,128)(2,1)}) custom-call(s32[3]{0:T(128)} %pad_add_fusion.place, bf16[768,768]{1,0:T(8,128)(2,1)} %wu.1, bf16[768,768]{1,0:T(8,128)(2,1)} %own.1, bf16[16,768]{1,0:T(8,128)(2,1)} %pad.13.rest), custom_call_target="tpu_custom_call" | custom-call | flops 15000000512 | bytes 45000000 | tf_op jit(solution)/shard_map/piece_feed/pallas_call | solution.py:132
  13.6 4.2 %all-to-all-start = ((bf16[4,112,768]{2,1,0:T(8,128)(2,1)}), bf16[4,112,768]{2,1,0:T(8,128)(2,1)S(1)}, u32[]{:S(2)}, u32[]{:S(2)}) async-start(bf16[4,112,768]{2,1,0:T(8,128)(2,1)} %get-tuple-element.118), calls=%async_computation | async-start | bytes 1376256 | tf_op jit(solution)/shard_map/all_to_all | solution.py:222
  24.8 8.2 %collective-permute-done.3.refs_1_ = bf16[288,768]{1,0:T(8,128)(2,1)S(1)} collective-permute-done((bf16[288,768]{1,0:T(8,128)(2,1)S(1)}, bf16[288,768]{1,0:T(8,128)(2,1)S(1)}, u32[]{:S(2)}, u32[]{:S(2)}) %collective-permute-start.3) | collective-permute-done | bytes 442400 | tf_op jit(solution)/shard_map/ppermute | solution.py:206
  36.0 5.3 %collective-permute-done.5.refs_3_ = bf16[288,768]{1,0:T(8,128)(2,1)S(1)} collective-permute-done((bf16[288,768]{1,0:T(8,128)(2,1)S(1)}, bf16[288,768]{1,0:T(8,128)(2,1)S(1)}, u32[]{:S(2)}, u32[]{:S(2)}) %collective-permute-start.5) | collective-permute-done | bytes 442400 | tf_op jit(solution)/shard_map/ppermute | solution.py:206
  47.2 9.7 %project.1 = (bf16[1024,768]{1,0:T(8,128)(2,1)}, bf16[1024,768]{1,0:T(8,128)(2,1)}, bf16[1024,768]{1,0:T(8,128)(2,1)}, bf16[4,768,768]{2,1,0:T(8,128)(2,1)}) custom-call(s32[3]{0:T(128)} %pad_add_fusion.place, bf16[1024,768]{1,0:T(8,128)(2,1)} %x.13, bf16[192,768]{1,0:T(8,128)(2,1)} %bitcast.80, bf16[192,768]{1,0:T(8,128)(2,1)} %bitcast.82, ...), custom_call_target="tpu_custom_call" | custom-call | flops 49999998976 | bytes 150000000 | tf_op jit(solution)/shard_map/project/pallas_call | solution.py:319
  59.0 7.2 %all-to-all-start.1 = ((bf16[4,96,768]{2,1,0:T(8,128)(2,1)}), bf16[4,96,768]{2,1,0:T(8,128)(2,1)S(1)}, u32[]{:S(2)}, u32[]{:S(2)}) async-start(bf16[4,96,768]{2,1,0:T(8,128)(2,1)} %get-tuple-element.126), calls=%async_computation.1 | async-start | bytes 1179648 | tf_op jit(solution)/shard_map/all_to_all | solution.py:222
  66.4 10.6 %attend.2 = (bf16[1024,768]{1,0:T(8,128)(2,1)}, f32[1024,128]{1,0:T(8,128)}, f32[1024,768]{1,0:T(8,128)}, bf16[1024,768]{1,0:T(8,128)(2,1)}) custom-call(bf16[1024,768]{1,0:T(8,128)(2,1)} %get-tuple-element.125.q, bf16[1024,768]{1,0:T(8,128)(2,1)} %get-tuple-element.128.k, bf16[1024,768]{1,0:T(8,128)(2,1)} %get-tuple-element.129.v, s32[1024,1]{1,0:T(8,128)} %copy.52.segc, ...), custom_call_target="tpu_custom_call" | custom-call | flops 40000000000 | bytes 120000000 | tf_op jit(solution)/shard_map/attend/pallas_call | solution.py:408
  77.1 5.3 %all-to-all-done.1 = bf16[4,96,768]{2,1,0:T(8,128)(2,1)S(1)} async-done(((bf16[4,96,768]{2,1,0:T(8,128)(2,1)}), bf16[4,96,768]{2,1,0:T(8,128)(2,1)S(1)}, u32[]{:S(2)}, u32[]{:S(2)}) %all-to-all-start.1) | async-done | bytes 589856 | tf_op jit(solution)/shard_map/all_to_all | solution.py:222
  86.0 10.6 %attend.3 = (bf16[1024,768]{1,0:T(8,128)(2,1)}, f32[1024,128]{1,0:T(8,128)}, f32[1024,768]{1,0:T(8,128)}, bf16[1024,768]{1,0:T(8,128)(2,1)}) custom-call(bf16[1024,768]{1,0:T(8,128)(2,1)} %get-tuple-element.125.q, bf16[1024,768]{1,0:T(8,128)(2,1)} %get-tuple-element.128.k, ...), custom_call_target="tpu_custom_call", output_to_operand_aliasing={{0}: (10, {}), {1}: (11, {}), {2}: (12, {}), {3}: (13, {})} | custom-call | flops 40000000000 | bytes 120000000 | tf_op jit(solution)/shard_map/attend/pallas_call | solution.py:408
  97.6 13.6 %feed_up.1 = (bf16[1024,3072]{1,0:T(8,128)(2,1)}, bf16[1024,3072]{1,0:T(8,128)(2,1)}, bf16[3072,768]{1,0:T(8,128)(2,1)}) custom-call(s32[3]{0:T(128)} %pad_add_fusion.place, bf16[1024,768]{1,0:T(8,128)(2,1)} %get-tuple-element.142.x, bf16[768,768]{1,0:T(8,128)(2,1)} %get-tuple-element.143.own, f32[1,3072]{1,0:T(1,128)} %reshape.226.bu, ...), custom_call_target="tpu_custom_call" | custom-call | flops 60000002048 | bytes 180000000 | tf_op jit(solution)/shard_map/feed_up/pallas_call | solution.py:574
  113.8 14.1 %feed_down.1 = (f32[1024,768]{1,0:T(8,128)}, bf16[1024,768]{1,0:T(8,128)(2,1)}, f32[1024,768]{1,0:T(8,128)}, bf16[1024,768]{1,0:T(8,128)(2,1)}, f32[8,768]{1,0:T(8,128)}, /*index=5*/bf16[3072,768]{1,0:T(8,128)(2,1)}) custom-call(s32[3]{0:T(128)} %pad_add_fusion.place, bf16[1024,3072]{1,0:T(8,128)(2,1)} %get-tuple-element.150.act, ...), custom_call_target="tpu_custom_call" | custom-call | flops 65000001536 | bytes 195000000 | tf_op jit(solution)/shard_map/feed_down/pallas_call | solution.py:635
  127.9 29.1 %feed_back.1 = (bf16[4,4,2,96,768]{4,3,2,1,0:T(8,128)(2,1)}, bf16[4,4,2,96,768]{4,3,2,1,0:T(8,128)(2,1)}, f32[8,512]{1,0:T(8,128)}, f32[1024,768]{1,0:T(8,128)}) custom-call(s32[3]{0:T(128)} %pad_add_fusion.place, bf16[1024,768]{1,0:T(8,128)(2,1)} %get-tuple-element.154.grad, bf16[1024,768]{1,0:T(8,128)(2,1)} %get-tuple-element.142.x, ...), custom_call_target="tpu_custom_call" | custom-call | flops 134999998464 | bytes 405000000 | tf_op jit(solution)/shard_map/feed_back/pallas_call | solution.py:710
  157.2 11.9 %middle.1 = (f32[1024,768]{1,0:T(8,128)}, bf16[1024,768]{1,0:T(8,128)(2,1)}, f32[1024,128]{1,0:T(8,128)}, bf16[768,768]{1,0:T(8,128)(2,1)}, f32[8,768]{1,0:T(8,128)}) custom-call(f32[1024,768]{1,0:T(8,128)} %get-tuple-element.160.normed, f32[1024,768]{1,0:T(8,128)} %get-tuple-element.161.second, f32[1024,768]{1,0:T(8,128)} %get-tuple-element.151.unit, ...), custom_call_target="tpu_custom_call" | custom-call | flops 40000000000 | bytes 120000000 | tf_op jit(solution)/shard_map/middle/pallas_call | solution.py:780
  169.1 5.3 %add_convert_fusion = (bf16[2,4,192,768]{3,2,1,0:T(8,128)(2,1)}, bf16[2,4,192,768]{3,2,1,0:T(8,128)(2,1)S(1)}) fusion(bf16[4,4,192,768]{3,2,1,0:T(8,128)(2,1)} %collective-permute-done.24, bf16[4,4,192,768]{3,2,1,0:T(8,128)(2,1)} %bitcast.67), kind=kLoop, calls=%fused_computation | loop fusion | flops 9437184 | bytes 14155776 | tf_op jit(solution)/shard_map/convert_element_type | solution.py:237
  175.8 23.6 %attend_back.1 = (bf16[1024,768]{1,0:T(8,128)(2,1)}, bf16[1024,768]{1,0:T(8,128)(2,1)}, bf16[1024,768]{1,0:T(8,128)(2,1)}, f32[8,768]{1,0:T(8,128)}) custom-call(s32[3]{0:T(128)} %pad_add_fusion.place, bf16[1024,768]{1,0:T(8,128)(2,1)} %get-tuple-element.125.q, bf16[1024,768]{1,0:T(8,128)(2,1)} %get-tuple-element.128.k, ...), custom_call_target="tpu_custom_call" | custom-call | flops 109999996928 | bytes 330000000 | tf_op jit(solution)/shard_map/attend_back/pallas_call | solution.py:505
  199.4 4.2 %collective-permute-done.25 = bf16[2,4,192,768]{3,2,1,0:T(8,128)(2,1)} collective-permute-done((bf16[2,4,192,768]{3,2,1,0:T(8,128)(2,1)}, bf16[2,4,192,768]{3,2,1,0:T(8,128)(2,1)}, u32[]{:S(2)}, u32[]{:S(2)}) %collective-permute-start.25) | collective-permute-done | bytes 2359328 | tf_op jit(solution)/shard_map/ppermute | solution.py:206
  208.2 10.6 %head_weights.1 = (bf16[4,4,2,3,16,768]{5,4,3,2,1,0:T(8,128)(2,1)}, bf16[4,4,2,3,16,768]{5,4,3,2,1,0:T(8,128)(2,1)}) custom-call(s32[3]{0:T(128)} %pad_add_fusion.place, bf16[1024,768]{1,0:T(8,128)(2,1)} %get-tuple-element.170.dq, bf16[1024,768]{1,0:T(8,128)(2,1)} %get-tuple-element.171.dk, bf16[1024,768]{1,0:T(8,128)(2,1)} %get-tuple-element.172.dv, ...), custom_call_target="tpu_custom_call" | custom-call | flops 40000000000 | bytes 120000000 | tf_op jit(solution)/shard_map/head_weights/pallas_call | solution.py:834
  218.9 2.7 collective-permute-done.26
  221.6 3.1 %fusion = bf16[4,192,768]{2,1,0:T(8,128)(2,1)} fusion(bf16[4,192,768]{2,1,0:T(8,128)(2,1)} %collective-permute-done.26, bf16[2,4,192,768]{3,2,1,0:T(8,128)(2,1)S(1)} %get-tuple-element.221, bf16[2,4,192,768]{3,2,1,0:T(8,128)(2,1)} %collective-permute-done.25), kind=kLoop, calls=%fused_computation.3 | loop fusion | flops 4718592 | bytes 4718592 | tf_op jit(solution)/shard_map/convert_element_type | solution.py:237
  224.7 3.5 %all-to-all-start.2 = ((bf16[4,192,768]{2,1,0:T(8,128)(2,1)}), bf16[4,192,768]{2,1,0:T(8,128)(2,1)S(1)}, u32[]{:S(2)}, u32[]{:S(2)}) async-start(bf16[4,192,768]{2,1,0:T(8,128)(2,1)} %fusion), calls=%async_computation.2 | async-start | bytes 2359296 | tf_op jit(solution)/shard_map/all_to_all | solution.py:222
  229.5 3.0 add_convert_fusion.2
  235.4 9.0 %input_gradient.1 = f32[1024,768]{1,0:T(8,128)} custom-call(bf16[1024,768]{1,0:T(8,128)(2,1)} %get-tuple-element.170.dq, bf16[1024,768]{1,0:T(8,128)(2,1)} %get-tuple-element.171.dk, bf16[1024,768]{1,0:T(8,128)(2,1)} %get-tuple-element.172.dv, bf16[4,768,768]{2,1,0:T(8,128)(2,1)} %get-tuple-element.130.wo.full, f32[1024,768]{1,0:T(8,128)} %get-tuple-element.184.first, ...), custom_call_target="tpu_custom_call" | custom-call | flops 30000001024 | bytes 90000000 | tf_op jit(solution)/shard_map/input_gradient/pallas_call | solution.py:859
  244.4 4.6 %collective-permute-done.29 = bf16[2,4,96,768]{3,2,1,0:T(8,128)(2,1)} collective-permute-done((bf16[2,4,96,768]{3,2,1,0:T(8,128)(2,1)S(1)}, bf16[2,4,96,768]{3,2,1,0:T(8,128)(2,1)}, u32[]{:S(2)}, u32[]{:S(2)}) %collective-permute-start.29) | collective-permute-done | bytes 1179680 | tf_op jit(solution)/shard_map/ppermute | solution.py:206
  254.3 5.8 %collective-permute-done.32 = bf16[4,96,768]{2,1,0:T(8,128)(2,1)S(1)} collective-permute-done((bf16[4,96,768]{2,1,0:T(8,128)(2,1)S(1)}, bf16[4,96,768]{2,1,0:T(8,128)(2,1)S(1)}, u32[]{:S(2)}, u32[]{:S(2)}) %collective-permute-start.32) | collective-permute-done | bytes 589856 | tf_op jit(solution)/shard_map/ppermute | solution.py:206
  262.2 4.0 %all-to-all-start.3 = ((bf16[4,96,768]{2,1,0:T(8,128)(2,1)}), bf16[4,96,768]{2,1,0:T(8,128)(2,1)S(1)}, u32[]{:S(2)}, u32[]{:S(2)}) async-start(bf16[4,96,768]{2,1,0:T(8,128)(2,1)} %fusion.3), calls=%async_computation.3 | async-start | bytes 1179648 | tf_op jit(solution)/shard_map/all_to_all | solution.py:222
  271.3 7.6 %score.1 = f32[32,32]{1,0:T(8,128)} custom-call(f32[1024,768]{1,0:T(8,128)} %get-tuple-element.193.out_ref, s32[1,1024]{1,0:T(1,128)} %bitcast.73, s32[32,1]{1,0:T(8,128)} %copy-done.14, bf16[1024,768]{1,0:T(8,128)(2,1)} %table_ref.1, s32[32,32]{1,0:T(8,128)} %pick_ref.1, f32[8,1280]{1,0:T(8,128)} %copy-done.9), custom_call_target="tpu_custom_call" | custom-call | flops 40000000000 | bytes 120000000 | tf_op jit(solution)/shard_map/score/pallas_call | solution.py:907
  278.9 3.4 %collective-permute-done.33 = f32[8,1280]{1,0:T(8,128)S(1)} collective-permute-done((f32[8,1280]{1,0:T(8,128)S(1)}, f32[8,1280]{1,0:T(8,128)S(1)}, u32[]{:S(2)}, u32[]{:S(2)}) %collective-permute-start.33) | collective-permute-done | bytes 40992 | tf_op jit(solution)/shard_map/ppermute | solution.py:65
  286.0 3.5 %all-to-all-start.4 = ((bf16[4,96,768]{2,1,0:T(8,128)(2,1)}), bf16[4,96,768]{2,1,0:T(8,128)(2,1)S(1)}, u32[]{:S(2)}, u32[]{:S(2)}) async-start(bf16[4,96,768]{2,1,0:T(8,128)(2,1)} %broadcast_in_dim.38.refs_8_), calls=%async_computation.4 | async-start | bytes 1179648 | tf_op jit(solution)/shard_map/all_to_all | solution.py:222
  291.8 4.7 %finish_feed.1 = (f32[768,768]{1,0:T(8,128)}, f32[768,768]{1,0:T(8,128)}) custom-call(s32[3]{0:T(128)} %pad_add_fusion.place, bf16[192,768]{1,0:T(8,128)(2,1)} %copy-done.5, bf16[192,768]{1,0:T(8,128)(2,1)} %copy-done.46, bf16[192,768]{1,0:T(8,128)(2,1)} %copy-done.47, bf16[192,768]{1,0:T(8,128)(2,1)} %copy-done.48, bf16[192,768]{1,0:T(8,128)(2,1)} %copy-done.49, ...), custom_call_target="tpu_custom_call" | custom-call | flops 30000001024 | bytes 90000000 | tf_op jit(solution)/shard_map/finish_feed/pallas_call | solution.py:162
  301.3 2.8 finish_heads.1
  (259 shorter events, 61.3 us)
Async XLA Ops:
  3.6 17.6 %collective-permute-start.1 = (bf16[96,768]{1,0:T(8,128)(2,1)}, bf16[96,768]{1,0:T(8,128)(2,1)S(1)}, u32[]{:S(2)}, u32[]{:S(2)}) collective-permute-start(bf16[96,768]{1,0:T(8,128)(2,1)} %piece_heads.1), channel_id=1, source_target_pairs={{0,2},{1,3},{2,0},{3,1},{4,6},{5,7},{6,4},{7,5},{8,10},{9,11},{10,... | collective-permute-start | bytes 442376 | tf_op jit(solution)/shard_map/ppermute | solution.py:65
  7.7 13.5 %collective-permute-start.2 = (bf16[96,768]{1,0:T(8,128)(2,1)}, bf16[96,768]{1,0:T(8,128)(2,1)S(1)}, u32[]{:S(2)}, u32[]{:S(2)}) collective-permute-start(bf16[96,768]{1,0:T(8,128)(2,1)} %piece_heads.1), channel_id=1, source_target_pairs={{0,3},{1,2},{2,1},{3,0},{4,7},{5,6},{6,5},{7,4},{8,11},{9,10},{10,... | collective-permute-start | bytes 442376 | tf_op jit(solution)/shard_map/ppermute | solution.py:65
  9.8 11.4 %collective-permute-start = (bf16[96,768]{1,0:T(8,128)(2,1)}, bf16[96,768]{1,0:T(8,128)(2,1)S(1)}, u32[]{:S(2)}, u32[]{:S(2)}) collective-permute-start(bf16[96,768]{1,0:T(8,128)(2,1)} %piece_heads.1), channel_id=1, source_target_pairs={{0,1},{1,0},{2,3},{3,2},{4,5},{5,4},{6,7},{7,6},{8,9},{9,8},{10,11... | collective-permute-start | bytes 442376 | tf_op jit(solution)/shard_map/ppermute | solution.py:65
  13.6 22.5 %all-to-all-start = ((bf16[4,112,768]{2,1,0:T(8,128)(2,1)}), bf16[4,112,768]{2,1,0:T(8,128)(2,1)S(1)}, u32[]{:S(2)}, u32[]{:S(2)}) async-start(bf16[4,112,768]{2,1,0:T(8,128)(2,1)} %get-tuple-element.118), calls=%async_computation | async-start | bytes 1376256 | tf_op jit(solution)/shard_map/all_to_all | solution.py:222
  21.3 11.7 %collective-permute-start.3 = (bf16[288,768]{1,0:T(8,128)(2,1)S(1)}, bf16[288,768]{1,0:T(8,128)(2,1)S(1)}, u32[]{:S(2)}, u32[]{:S(2)}) collective-permute-start(bf16[288,768]{1,0:T(8,128)(2,1)S(1)} %constant_dynamic-update-slice_fusion.refs_0_), channel_id=1, source_target_pairs={{0,8},{4,20},{8,0},{12,28},{16,24},{20,4},{24,16},{28,12},{1,9},{5... | collective-permute-start | bytes 1327112 | tf_op jit(solution)/shard_map/ppermute | solution.py:206
  34.4 10.0 %collective-permute-start.6 = (bf16[288,768]{1,0:T(8,128)(2,1)S(1)}, bf16[288,768]{1,0:T(8,128)(2,1)S(1)}, u32[]{:S(2)}, u32[]{:S(2)}) collective-permute-start(bf16[288,768]{1,0:T(8,128)(2,1)S(1)} %constant_dynamic-update-slice_fusion.refs_0_), channel_id=1, source_target_pairs={{0,4},{4,0},{8,12},{12,8},{16,20},{20,16},{24,28},{28,24},{1,5},{5... | collective-permute-start | bytes 1327112 | tf_op jit(solution)/shard_map/ppermute | solution.py:65
  34.4 10.0 %collective-permute-start.7 = (bf16[288,768]{1,0:T(8,128)(2,1)S(1)}, bf16[288,768]{1,0:T(8,128)(2,1)}, u32[]{:S(2)}, u32[]{:S(2)}) collective-permute-start(bf16[288,768]{1,0:T(8,128)(2,1)S(1)} %collective-permute-done.3.refs_1_), channel_id=1, source_target_pairs={{0,4},{4,0},{8,12},{12,8},{16,20},{20,16},{24,28},{28,24},{1,5},{5... | collective-permute-start | bytes 1327112 | tf_op jit(solution)/shard_map/ppermute | solution.py:65
  45.1 12.8 %collective-permute-start.10 = (bf16[288,768]{1,0:T(8,128)(2,1)S(1)}, bf16[288,768]{1,0:T(8,128)(2,1)S(1)}, u32[]{:S(2)}, u32[]{:S(2)}) collective-permute-start(bf16[288,768]{1,0:T(8,128)(2,1)S(1)} %pad_maximum_fusion.refs_0_), channel_id=1, source_target_pairs={{0,8},{4,20},{8,0},{12,28},{16,24},{20,4},{24,16},{28,12},{1,9},{5... | collective-permute-start | bytes 1327112 | tf_op jit(solution)/shard_map/ppermute | solution.py:206
  46.6 11.3 %collective-permute-start.11 = (bf16[288,768]{1,0:T(8,128)(2,1)S(1)}, bf16[288,768]{1,0:T(8,128)(2,1)S(1)}, u32[]{:S(2)}, u32[]{:S(2)}) collective-permute-start(bf16[288,768]{1,0:T(8,128)(2,1)S(1)} %pad_maximum_fusion.refs_0_), channel_id=1, source_target_pairs={{0,16},{4,12},{8,24},{12,4},{16,0},{20,28},{24,8},{28,20},{1,17},{... | collective-permute-start | bytes 1327112 | tf_op jit(solution)/shard_map/ppermute | solution.py:206
  47.2 29.9 %collective-permute-start.13 = (bf16[288,768]{1,0:T(8,128)(2,1)S(1)}, bf16[288,768]{1,0:T(8,128)(2,1)}, u32[]{:S(2)}, u32[]{:S(2)}) collective-permute-start(bf16[288,768]{1,0:T(8,128)(2,1)S(1)} %pad_maximum_fusion.refs_0_), channel_id=1, source_target_pairs={{0,4},{4,0},{8,12},{12,8},{16,20},{20,16},{24,28},{28,24},{1,5},{5... | collective-permute-start | bytes 1327112 | tf_op jit(solution)/shard_map/ppermute | solution.py:65
  57.9 19.1 %collective-permute-start.12 = (bf16[288,768]{1,0:T(8,128)(2,1)S(1)}, bf16[288,768]{1,0:T(8,128)(2,1)S(1)}, u32[]{:S(2)}, u32[]{:S(2)}) collective-permute-start(bf16[288,768]{1,0:T(8,128)(2,1)S(1)} %collective-permute-done.10.refs_1_), channel_id=1, source_target_pairs={{0,16},{4,12},{8,24},{12,4},{16,0},{20,28},{24,8},{28,20},{1,17},{... | collective-permute-start | bytes 1327112 | tf_op jit(solution)/shard_map/ppermute | solution.py:206
  58.5 18.5 %collective-permute-start.14 = (bf16[288,768]{1,0:T(8,128)(2,1)S(1)}, bf16[288,768]{1,0:T(8,128)(2,1)S(1)}, u32[]{:S(2)}, u32[]{:S(2)}) collective-permute-start(bf16[288,768]{1,0:T(8,128)(2,1)S(1)} %collective-permute-done.10.refs_1_), channel_id=1, source_target_pairs={{0,4},{4,0},{8,12},{12,8},{16,20},{20,16},{24,28},{28,24},{1,5},{5... | collective-permute-start | bytes 1327112 | tf_op jit(solution)/shard_map/ppermute | solution.py:65
  59.0 23.3 %all-to-all-start.1 = ((bf16[4,96,768]{2,1,0:T(8,128)(2,1)}), bf16[4,96,768]{2,1,0:T(8,128)(2,1)S(1)}, u32[]{:S(2)}, u32[]{:S(2)}) async-start(bf16[4,96,768]{2,1,0:T(8,128)(2,1)} %get-tuple-element.126), calls=%async_computation.1 | async-start | bytes 1179648 | tf_op jit(solution)/shard_map/all_to_all | solution.py:222
  66.3 10.8 %collective-permute-start.15 = (bf16[288,768]{1,0:T(8,128)(2,1)S(1)}, bf16[288,768]{1,0:T(8,128)(2,1)S(1)}, u32[]{:S(2)}, u32[]{:S(2)}) collective-permute-start(bf16[288,768]{1,0:T(8,128)(2,1)S(1)} %collective-permute-done.11.refs_2_), channel_id=1, source_target_pairs={{0,4},{4,0},{8,12},{12,8},{16,20},{20,16},{24,28},{28,24},{1,5},{5... | collective-permute-start | bytes 1327112 | tf_op jit(solution)/shard_map/ppermute | solution.py:65
  82.4 14.2 %collective-permute-start.16 = (bf16[288,768]{1,0:T(8,128)(2,1)S(1)}, bf16[288,768]{1,0:T(8,128)(2,1)S(1)}, u32[]{:S(2)}, u32[]{:S(2)}) collective-permute-start(bf16[288,768]{1,0:T(8,128)(2,1)S(1)} %pad_maximum_fusion.1.refs_4_.refs_0_), channel_id=1, source_target_pairs={{0,8},{4,20},{8,0},{12,28},{16,24},{20,4},{24,16},{28,12},{1,9},{5... | collective-permute-start | bytes 1327112 | tf_op jit(solution)/shard_map/ppermute | solution.py:206
  83.7 13.0 %collective-permute-start.17 = (bf16[288,768]{1,0:T(8,128)(2,1)S(1)}, bf16[288,768]{1,0:T(8,128)(2,1)S(1)}, u32[]{:S(2)}, u32[]{:S(2)}) collective-permute-start(bf16[288,768]{1,0:T(8,128)(2,1)S(1)} %pad_maximum_fusion.1.refs_4_.refs_0_), channel_id=1, source_target_pairs={{0,16},{4,12},{8,24},{12,4},{16,0},{20,28},{24,8},{28,20},{1,17},{... | collective-permute-start | bytes 1327112 | tf_op jit(solution)/shard_map/ppermute | solution.py:206
  85.5 26.5 %collective-permute-start.20 = (bf16[288,768]{1,0:T(8,128)(2,1)S(1)}, bf16[288,768]{1,0:T(8,128)(2,1)S(1)}, u32[]{:S(2)}, u32[]{:S(2)}) collective-permute-start(bf16[288,768]{1,0:T(8,128)(2,1)S(1)} %pad_maximum_fusion.1.refs_4_.refs_0_), channel_id=1, source_target_pairs={{0,4},{4,0},{8,12},{12,8},{16,20},{20,16},{24,28},{28,24},{1,5},{5... | collective-permute-start | bytes 1327112 | tf_op jit(solution)/shard_map/ppermute | solution.py:65
  85.5 12.0 %collective-permute-start.19 = (bf16[288,768]{1,0:T(8,128)(2,1)S(1)}, bf16[288,768]{1,0:T(8,128)(2,1)}, u32[]{:S(2)}, u32[]{:S(2)}) collective-permute-start(bf16[288,768]{1,0:T(8,128)(2,1)S(1)} %collective-permute-done.12.refs_3_), channel_id=1, source_target_pairs={{0,4},{4,0},{8,12},{12,8},{16,20},{20,16},{24,28},{28,24},{1,5},{5... | collective-permute-start | bytes 1327112 | tf_op jit(solution)/shard_map/ppermute | solution.py:65
  96.7 14.5 %collective-permute-start.18 = (bf16[288,768]{1,0:T(8,128)(2,1)S(1)}, bf16[288,768]{1,0:T(8,128)(2,1)S(1)}, u32[]{:S(2)}, u32[]{:S(2)}) collective-permute-start(bf16[288,768]{1,0:T(8,128)(2,1)S(1)} %collective-permute-done.16.refs_8_.refs_1_), channel_id=1, source_target_pairs={{0,16},{4,12},{8,24},{12,4},{16,0},{20,28},{24,8},{28,20},{1,17},{... | collective-permute-start | bytes 1327112 | tf_op jit(solution)/shard_map/ppermute | solution.py:206
  96.9 15.0 %collective-permute-start.21 = (bf16[288,768]{1,0:T(8,128)(2,1)S(1)}, bf16[288,768]{1,0:T(8,128)(2,1)S(1)}, u32[]{:S(2)}, u32[]{:S(2)}) collective-permute-start(bf16[288,768]{1,0:T(8,128)(2,1)S(1)} %collective-permute-done.16.refs_8_.refs_1_), channel_id=1, source_target_pairs={{0,4},{4,0},{8,12},{12,8},{16,20},{20,16},{24,28},{28,24},{1,5},{5... | collective-permute-start | bytes 1327112 | tf_op jit(solution)/shard_map/ppermute | solution.py:65
  97.0 15.0 %collective-permute-start.22 = (bf16[288,768]{1,0:T(8,128)(2,1)S(1)}, bf16[288,768]{1,0:T(8,128)(2,1)}, u32[]{:S(2)}, u32[]{:S(2)}) collective-permute-start(bf16[288,768]{1,0:T(8,128)(2,1)S(1)} %collective-permute-done.17.refs_9_.refs_2_), channel_id=1, source_target_pairs={{0,4},{4,0},{8,12},{12,8},{16,20},{20,16},{24,28},{28,24},{1,5},{5... | collective-permute-start | bytes 1327112 | tf_op jit(solution)/shard_map/ppermute | solution.py:65
  157.0 12.1 %collective-permute-start.24 = (bf16[4,4,192,768]{3,2,1,0:T(8,128)(2,1)}, bf16[4,4,192,768]{3,2,1,0:T(8,128)(2,1)}, u32[]{:S(2)}, u32[]{:S(2)}) collective-permute-start(bf16[4,4,192,768]{3,2,1,0:T(8,128)(2,1)} %bitcast.78), channel_id=1, source_target_pairs={{0,4},{4,0},{8,12},{12,8},{16,20},{20,16},{24,28},{28,24},{1,5},{5... | collective-permute-start | bytes 14155784 | tf_op jit(solution)/shard_map/ppermute | solution.py:65
  174.5 29.2 %collective-permute-start.25 = (bf16[2,4,192,768]{3,2,1,0:T(8,128)(2,1)}, bf16[2,4,192,768]{3,2,1,0:T(8,128)(2,1)}, u32[]{:S(2)}, u32[]{:S(2)}) collective-permute-start(bf16[2,4,192,768]{3,2,1,0:T(8,128)(2,1)} %get-tuple-element.220.refs_0_), channel_id=1, source_target_pairs={{0,8},{4,20},{8,0},{12,28},{16,24},{20,4},{24,16},{28,12},{1,9},{5... | collective-permute-start | bytes 7077896 | tf_op jit(solution)/shard_map/ppermute | solution.py:206
  205.2 16.4 %collective-permute-start.26 = (bf16[4,192,768]{2,1,0:T(8,128)(2,1)S(1)}, bf16[4,192,768]{2,1,0:T(8,128)(2,1)}, u32[]{:S(2)}, u32[]{:S(2)}) collective-permute-start(bf16[4,192,768]{2,1,0:T(8,128)(2,1)S(1)} %fusion.2.refs_1_), channel_id=1, source_target_pairs={{0,16},{4,12},{8,24},{12,4},{16,0},{20,28},{24,8},{28,20},{1,17},{... | collective-permute-start | bytes 3538952 | tf_op jit(solution)/shard_map/ppermute | solution.py:206
  224.7 37.5 %all-to-all-start.2 = ((bf16[4,192,768]{2,1,0:T(8,128)(2,1)}), bf16[4,192,768]{2,1,0:T(8,128)(2,1)S(1)}, u32[]{:S(2)}, u32[]{:S(2)}) async-start(bf16[4,192,768]{2,1,0:T(8,128)(2,1)} %fusion), calls=%async_computation.2 | async-start | bytes 2359296 | tf_op jit(solution)/shard_map/all_to_all | solution.py:222
  232.6 16.4 %collective-permute-start.29 = (bf16[2,4,96,768]{3,2,1,0:T(8,128)(2,1)S(1)}, bf16[2,4,96,768]{3,2,1,0:T(8,128)(2,1)}, u32[]{:S(2)}, u32[]{:S(2)}) collective-permute-start(bf16[2,4,96,768]{3,2,1,0:T(8,128)(2,1)S(1)} %get-tuple-element.223.refs_0_), channel_id=1, source_target_pairs={{0,8},{4,20},{8,0},{12,28},{16,24},{20,4},{24,16},{28,12},{1,9},{5... | collective-permute-start | bytes 3538952 | tf_op jit(solution)/shard_map/ppermute | solution.py:206
  262.2 20.1 %all-to-all-start.3 = ((bf16[4,96,768]{2,1,0:T(8,128)(2,1)}), bf16[4,96,768]{2,1,0:T(8,128)(2,1)S(1)}, u32[]{:S(2)}, u32[]{:S(2)}) async-start(bf16[4,96,768]{2,1,0:T(8,128)(2,1)} %fusion.3), calls=%async_computation.3 | async-start | bytes 1179648 | tf_op jit(solution)/shard_map/all_to_all | solution.py:222
  266.4 16.0 %collective-permute-start.34 = (bf16[192,768]{1,0:T(8,128)(2,1)S(1)}, bf16[192,768]{1,0:T(8,128)(2,1)S(1)}, u32[]{:S(2)}, u32[]{:S(2)}) collective-permute-start(bf16[192,768]{1,0:T(8,128)(2,1)S(1)} %fusion.6.refs_0_), channel_id=1, source_target_pairs={{0,8},{4,20},{8,0},{12,28},{16,24},{20,4},{24,16},{28,12},{1,9},{5... | collective-permute-start | bytes 884744 | tf_op jit(solution)/shard_map/ppermute | solution.py:206
  267.8 14.6 %collective-permute-start.35 = (bf16[192,768]{1,0:T(8,128)(2,1)S(1)}, bf16[192,768]{1,0:T(8,128)(2,1)S(1)}, u32[]{:S(2)}, u32[]{:S(2)}) collective-permute-start(bf16[192,768]{1,0:T(8,128)(2,1)S(1)} %fusion.6.refs_0_), channel_id=1, source_target_pairs={{0,16},{4,12},{8,24},{12,4},{16,0},{20,28},{24,8},{28,20},{1,17},{... | collective-permute-start | bytes 884744 | tf_op jit(solution)/shard_map/ppermute | solution.py:206
  268.7 13.7 %collective-permute-start.36 = (bf16[192,768]{1,0:T(8,128)(2,1)S(1)}, bf16[192,768]{1,0:T(8,128)(2,1)S(1)}, u32[]{:S(2)}, u32[]{:S(2)}) collective-permute-start(bf16[192,768]{1,0:T(8,128)(2,1)S(1)} %fusion.6.refs_0_), channel_id=1, source_target_pairs={{0,24},{4,28},{8,16},{12,20},{16,8},{20,12},{24,0},{28,4},{1,25},{... | collective-permute-start | bytes 884744 | tf_op jit(solution)/shard_map/ppermute | solution.py:65
  270.0 12.3 %collective-permute-start.33 = (f32[8,1280]{1,0:T(8,128)S(1)}, f32[8,1280]{1,0:T(8,128)S(1)}, u32[]{:S(2)}, u32[]{:S(2)}) collective-permute-start(f32[8,1280]{1,0:T(8,128)S(1)} %add.125.refs_0_), channel_id=1, source_target_pairs={{0,8},{4,12},{8,0},{12,4},{16,24},{20,28},{24,16},{28,20},{1,9},{5... | collective-permute-start | bytes 122888 | tf_op jit(solution)/shard_map/ppermute | solution.py:65
  286.0 12.3 %all-to-all-start.4 = ((bf16[4,96,768]{2,1,0:T(8,128)(2,1)}), bf16[4,96,768]{2,1,0:T(8,128)(2,1)S(1)}, u32[]{:S(2)}, u32[]{:S(2)}) async-start(bf16[4,96,768]{2,1,0:T(8,128)(2,1)} %broadcast_in_dim.38.refs_8_), calls=%async_computation.4 | async-start | bytes 1179648 | tf_op jit(solution)/shard_map/all_to_all | solution.py:222
  (70 other events, 582.5 us)

commit v5 on v4

--- a/solution.py
+++ b/solution.py
@@ -806,25 +806,51 @@
 
 
 def head_weights_kernel(place, dq, dk, dv, x, wo, *refs):
-    keep, send, held = refs[-3:]
+    keep, send, pairs, loaded, held, sems, out_sems = refs[-7:]
     core = place[0]
     shards, heads = keep.shape[1], keep.shape[3]
+    width = x.shape[1]
+    copies = [
+        pltpu.make_async_copy(ref, loaded.at[n], sems.at[n])
+        for n, ref in enumerate((dq, dk, dv, x))
+    ] + [pltpu.make_async_copy(wo, loaded.at[4, :width, :], sems.at[4])]
+    for n in (3, 0, 1, 2, 4):
+        copies[n].start()
+    copies[3].wait()
+
+    def out_copy(pair, side):
+        return pltpu.make_async_copy(
+            pairs.at[pair], keep if side == pair else send, out_sems.at[pair]
+        )
+
     for kind in range(4):
         if kind < 3:
+            copies[kind].wait()
             held[...] = lax.dot_general(
-                (dq, dk, dv)[kind][...], x[...], TN, preferred_element_type=F32
+                loaded[kind], loaded[3], TN, preferred_element_type=F32
             ).astype(BF)
-        source = held if kind < 3 else wo
+        else:
+            copies[4].wait()
+        for r in range(shards):
+            for h in range(heads):
+                for g in range(4):
+                    at = (r * heads + h) * HEAD_DIM + g * GRAIN
+                    rows = slice(at, at + GRAIN)
+                    value = held[rows, :] if kind < 3 else loaded[4, rows, :]
+                    pairs[kind // 2, g, r, kind % 2, h] = value
         for side in range(2):
-
-            @pl.when(core == side)
-            def _():
-                out = keep if side == kind // 2 else send
-                for r in range(shards):
-                    for h in range(heads):
-                        for g in range(4):
-                            at = (r * heads + h) * HEAD_DIM + g * GRAIN
-                            out[g, r, kind % 2, h] = source[at : at + GRAIN, :]
+            if kind % 2 == 1:
+
+                @pl.when(core == side)
+                def _():
+                    out_copy(kind // 2, side).start()
+
+    for side in range(2):
+
+        @pl.when(core == side)
+        def _():
+            for pair in range(2):
+                out_copy(pair, side).wait()
 
 
 def head_weights(place, dq, dk, dv, x, wo, n_mp, *tokens):
@@ -833,12 +859,18 @@
     dims = (4, n_mp, 2, heads, GRAIN, width)
     keep, send = pl.pallas_call(
         head_weights_kernel,
-        in_specs=[scalar_spec()] + [held_spec()] * 5 + [token_spec() for _ in tokens],
-        out_specs=[held_spec()] * 2,
+        in_specs=[scalar_spec()] + [token_spec()] * 5 + [token_spec() for _ in tokens],
+        out_specs=[token_spec()] * 2,
         out_shape=[shape(dims, BF)] * 2,
-        scratch_shapes=[pltpu.VMEM((width, width), BF)],
-        compiler_params=params(),
-        cost_estimate=cost(8),
+        scratch_shapes=[
+            pltpu.VMEM((2, *dims), BF),
+            pltpu.VMEM((5, rows, width), BF),
+            pltpu.VMEM((width, width), BF),
+            pltpu.SemaphoreType.DMA((5,)),
+            pltpu.SemaphoreType.DMA((2,)),
+        ],
+        compiler_params=params(),
+        cost_estimate=cost(9),
         name="head_weights",
     )(place, dq, dk, dv, x, wo, *tokens)
     dims = (4, n_mp, 2 * heads * GRAIN, width)
@@ -1070,7 +1102,7 @@
     )
     got, heads_keep = lax.optimization_barrier((got, heads_keep))
     feed_parts = add(feed_own, got)
-    heads_got = core_swap(after(heads_send, feed_parts), n_dp)
+    heads_got = core_swap(after(heads_send, got), n_dp)
     feed_got = exchange(feed_parts, "mp")
     heads_stay, heads_go = chip_sum(heads_keep, heads_got)
     heads_got = first_swap(heads_go, n_dp)

time: 310 us -> 310 us (level)
  transfers between devices with their start and end apart: 48 -> 48, of which waited for: 14 -> 13; matrix products, arithmetic and copies ran while one was open for 6% -> 7% of each run, Pallas kernels for 38% -> 37%
where the time goes in v5:
time: 310 us; the launch traced here: 304 us
  Pallas kernels  162 us (52%)
  starting transfers between devices  58.3 us (19%)
  waiting for transfers between devices  46.5 us (15%)
  other arithmetic  22.1 us (7%)
  local copies, waits for them, and re-layouts  12.7 us (4%)
    ppermute x15, waiting for transfers between devices, turn_swap(): lax.ppermute(block, 'dp', [(i, i ^ bits[i & 1]) for i in range(n_dp)])  31.9 us
    pallas_call x1, Pallas kernels, feed_back(): pl.pallas_call(feed_back_kernel, grid=(4,), in_specs=[scalar_spec(), full...  29.1 us
    all_to_all x5, starting transfers between devices, exchange(): lax.all_to_all(block, axis, 0, 0, axis_index_groups=groups, tiled=True)  23.7 us
    pallas_call x1, Pallas kernels, attend_back(): pl.pallas_call(attend_back_kernel, grid=(rows // BLOCK,), in_specs=[scala...  23.6 us
    pallas_call x2, Pallas kernels, attend(): pl.pallas_call(functools.partial(attend_kernel, part), grid=(steps,), in_...  21.2 us
    ppermute x15, starting transfers between devices, turn_swap(): lax.ppermute(block, 'dp', [(i, i ^ bits[i & 1]) for i in range(n_dp)])  18.5 us
    convert_element_type x6, other arithmetic, add(): return total.astype(BF)  16.3 us
    ppermute x28, starting transfers between devices, swap(): return lax.ppermute(block, axis, [(i, i ^ bit) for i in range(size)])  16.1 us
  transfers between devices with their start and end apart: 48, of which 13 were waited for; matrix products, arithmetic and copies ran while one was open for 7% of the time, Pallas kernels for 37%

profile of v5, /device:TPU:0, one launch (start us, length us, event | category | flops | bytes accessed | tf_op | source)
XLA Modules:
  0.0 304.4 jit_solution(2829609249540295578)
XLA Ops:
  3.6 4.1 %collective-permute-start.1 = (bf16[96,768]{1,0:T(8,128)(2,1)}, bf16[96,768]{1,0:T(8,128)(2,1)S(1)}, u32[]{:S(2)}, u32[]{:S(2)}) collective-permute-start(bf16[96,768]{1,0:T(8,128)(2,1)} %piece_heads.1), channel_id=1, source_target_pairs={{0,2},{1,3},{2,0},{3,1},{4,6},{5,7},{6,4},{7,5},{8,10},{9,11},{10,... | collective-permute-start | bytes 442376 | tf_op jit(solution)/shard_map/ppermute | solution.py:65
  10.1 3.5 %piece_feed.1 = (bf16[768,768]{1,0:T(8,128)(2,1)}, bf16[4,112,768]{2,1,0:T(8,128)(2,1)}, bf16[4,96,768]{2,1,0:T(8,128)(2,1)}) custom-call(s32[3]{0:T(128)} %pad_add_fusion.place, bf16[768,768]{1,0:T(8,128)(2,1)} %wu.1, bf16[768,768]{1,0:T(8,128)(2,1)} %own.1, bf16[16,768]{1,0:T(8,128)(2,1)} %pad.13.rest), custom_call_target="tpu_custom_call" | custom-call | flops 15000000512 | bytes 45000000 | tf_op jit(solution)/shard_map/piece_feed/pallas_call | solution.py:132
  13.6 4.2 %all-to-all-start = ((bf16[4,112,768]{2,1,0:T(8,128)(2,1)}), bf16[4,112,768]{2,1,0:T(8,128)(2,1)S(1)}, u32[]{:S(2)}, u32[]{:S(2)}) async-start(bf16[4,112,768]{2,1,0:T(8,128)(2,1)} %get-tuple-element.118), calls=%async_computation | async-start | bytes 1376256 | tf_op jit(solution)/shard_map/all_to_all | solution.py:222
  24.8 8.2 %collective-permute-done.3.refs_1_ = bf16[288,768]{1,0:T(8,128)(2,1)S(1)} collective-permute-done((bf16[288,768]{1,0:T(8,128)(2,1)S(1)}, bf16[288,768]{1,0:T(8,128)(2,1)S(1)}, u32[]{:S(2)}, u32[]{:S(2)}) %collective-permute-start.3) | collective-permute-done | bytes 442400 | tf_op jit(solution)/shard_map/ppermute | solution.py:206
  36.0 5.3 %collective-permute-done.5.refs_3_ = bf16[288,768]{1,0:T(8,128)(2,1)S(1)} collective-permute-done((bf16[288,768]{1,0:T(8,128)(2,1)S(1)}, bf16[288,768]{1,0:T(8,128)(2,1)S(1)}, u32[]{:S(2)}, u32[]{:S(2)}) %collective-permute-start.5) | collective-permute-done | bytes 442400 | tf_op jit(solution)/shard_map/ppermute | solution.py:206
  47.2 9.7 %project.1 = (bf16[1024,768]{1,0:T(8,128)(2,1)}, bf16[1024,768]{1,0:T(8,128)(2,1)}, bf16[1024,768]{1,0:T(8,128)(2,1)}, bf16[4,768,768]{2,1,0:T(8,128)(2,1)}) custom-call(s32[3]{0:T(128)} %pad_add_fusion.place, bf16[1024,768]{1,0:T(8,128)(2,1)} %x.13, bf16[192,768]{1,0:T(8,128)(2,1)} %bitcast.81, bf16[192,768]{1,0:T(8,128)(2,1)} %bitcast.83, ...), custom_call_target="tpu_custom_call" | custom-call | flops 49999998976 | bytes 150000000 | tf_op jit(solution)/shard_map/project/pallas_call | solution.py:319
  59.0 7.2 %all-to-all-start.1 = ((bf16[4,96,768]{2,1,0:T(8,128)(2,1)}), bf16[4,96,768]{2,1,0:T(8,128)(2,1)S(1)}, u32[]{:S(2)}, u32[]{:S(2)}) async-start(bf16[4,96,768]{2,1,0:T(8,128)(2,1)} %get-tuple-element.126), calls=%async_computation.1 | async-start | bytes 1179648 | tf_op jit(solution)/shard_map/all_to_all | solution.py:222
  66.4 10.6 %attend.2 = (bf16[1024,768]{1,0:T(8,128)(2,1)}, f32[1024,128]{1,0:T(8,128)}, f32[1024,768]{1,0:T(8,128)}, bf16[1024,768]{1,0:T(8,128)(2,1)}) custom-call(bf16[1024,768]{1,0:T(8,128)(2,1)} %get-tuple-element.125.q, bf16[1024,768]{1,0:T(8,128)(2,1)} %get-tuple-element.128.k, bf16[1024,768]{1,0:T(8,128)(2,1)} %get-tuple-element.129.v, s32[1024,1]{1,0:T(8,128)} %copy.52.segc, ...), custom_call_target="tpu_custom_call" | custom-call | flops 40000000000 | bytes 120000000 | tf_op jit(solution)/shard_map/attend/pallas_call | solution.py:408
  77.1 5.3 %all-to-all-done.1 = bf16[4,96,768]{2,1,0:T(8,128)(2,1)S(1)} async-done(((bf16[4,96,768]{2,1,0:T(8,128)(2,1)}), bf16[4,96,768]{2,1,0:T(8,128)(2,1)S(1)}, u32[]{:S(2)}, u32[]{:S(2)}) %all-to-all-start.1) | async-done | bytes 589856 | tf_op jit(solution)/shard_map/all_to_all | solution.py:222
  86.0 10.6 %attend.3 = (bf16[1024,768]{1,0:T(8,128)(2,1)}, f32[1024,128]{1,0:T(8,128)}, f32[1024,768]{1,0:T(8,128)}, bf16[1024,768]{1,0:T(8,128)(2,1)}) custom-call(bf16[1024,768]{1,0:T(8,128)(2,1)} %get-tuple-element.125.q, bf16[1024,768]{1,0:T(8,128)(2,1)} %get-tuple-element.128.k, ...), custom_call_target="tpu_custom_call", output_to_operand_aliasing={{0}: (10, {}), {1}: (11, {}), {2}: (12, {}), {3}: (13, {})} | custom-call | flops 40000000000 | bytes 120000000 | tf_op jit(solution)/shard_map/attend/pallas_call | solution.py:408
  97.6 13.6 %feed_up.1 = (bf16[1024,3072]{1,0:T(8,128)(2,1)}, bf16[1024,3072]{1,0:T(8,128)(2,1)}, bf16[3072,768]{1,0:T(8,128)(2,1)}) custom-call(s32[3]{0:T(128)} %pad_add_fusion.place, bf16[1024,768]{1,0:T(8,128)(2,1)} %get-tuple-element.142.x, bf16[768,768]{1,0:T(8,128)(2,1)} %get-tuple-element.143.own, f32[1,3072]{1,0:T(1,128)} %reshape.226.bu, ...), custom_call_target="tpu_custom_call" | custom-call | flops 60000002048 | bytes 180000000 | tf_op jit(solution)/shard_map/feed_up/pallas_call | solution.py:574
  113.8 14.1 %feed_down.1 = (f32[1024,768]{1,0:T(8,128)}, bf16[1024,768]{1,0:T(8,128)(2,1)}, f32[1024,768]{1,0:T(8,128)}, bf16[1024,768]{1,0:T(8,128)(2,1)}, f32[8,768]{1,0:T(8,128)}, /*index=5*/bf16[3072,768]{1,0:T(8,128)(2,1)}) custom-call(s32[3]{0:T(128)} %pad_add_fusion.place, bf16[1024,3072]{1,0:T(8,128)(2,1)} %get-tuple-element.150.act, ...), custom_call_target="tpu_custom_call" | custom-call | flops 65000001536 | bytes 195000000 | tf_op jit(solution)/shard_map/feed_down/pallas_call | solution.py:635
  127.9 29.1 %feed_back.1 = (bf16[4,4,2,96,768]{4,3,2,1,0:T(8,128)(2,1)}, bf16[4,4,2,96,768]{4,3,2,1,0:T(8,128)(2,1)}, f32[8,512]{1,0:T(8,128)}, f32[1024,768]{1,0:T(8,128)}) custom-call(s32[3]{0:T(128)} %pad_add_fusion.place, bf16[1024,768]{1,0:T(8,128)(2,1)} %get-tuple-element.154.grad, bf16[1024,768]{1,0:T(8,128)(2,1)} %get-tuple-element.142.x, ...), custom_call_target="tpu_custom_call" | custom-call | flops 134999998464 | bytes 405000000 | tf_op jit(solution)/shard_map/feed_back/pallas_call | solution.py:710
  157.2 11.9 %middle.1 = (f32[1024,768]{1,0:T(8,128)}, bf16[1024,768]{1,0:T(8,128)(2,1)}, f32[1024,128]{1,0:T(8,128)}, bf16[768,768]{1,0:T(8,128)(2,1)}, f32[8,768]{1,0:T(8,128)}) custom-call(f32[1024,768]{1,0:T(8,128)} %get-tuple-element.160.normed, f32[1024,768]{1,0:T(8,128)} %get-tuple-element.161.second, f32[1024,768]{1,0:T(8,128)} %get-tuple-element.151.unit, ...), custom_call_target="tpu_custom_call" | custom-call | flops 40000000000 | bytes 120000000 | tf_op jit(solution)/shard_map/middle/pallas_call | solution.py:780
  169.1 5.3 %add_convert_fusion = (bf16[2,4,192,768]{3,2,1,0:T(8,128)(2,1)}, bf16[2,4,192,768]{3,2,1,0:T(8,128)(2,1)S(1)}) fusion(bf16[4,4,192,768]{3,2,1,0:T(8,128)(2,1)} %collective-permute-done.24, bf16[4,4,192,768]{3,2,1,0:T(8,128)(2,1)} %bitcast.67), kind=kLoop, calls=%fused_computation | loop fusion | flops 9437184 | bytes 14155776 | tf_op jit(solution)/shard_map/convert_element_type | solution.py:237
  175.8 23.6 %attend_back.1 = (bf16[1024,768]{1,0:T(8,128)(2,1)}, bf16[1024,768]{1,0:T(8,128)(2,1)}, bf16[1024,768]{1,0:T(8,128)(2,1)}, f32[8,768]{1,0:T(8,128)}) custom-call(s32[3]{0:T(128)} %pad_add_fusion.place, bf16[1024,768]{1,0:T(8,128)(2,1)} %get-tuple-element.125.q, bf16[1024,768]{1,0:T(8,128)(2,1)} %get-tuple-element.128.k, ...), custom_call_target="tpu_custom_call" | custom-call | flops 109999996928 | bytes 330000000 | tf_op jit(solution)/shard_map/attend_back/pallas_call | solution.py:505
  199.4 4.2 %collective-permute-done.25 = bf16[2,4,192,768]{3,2,1,0:T(8,128)(2,1)} collective-permute-done((bf16[2,4,192,768]{3,2,1,0:T(8,128)(2,1)}, bf16[2,4,192,768]{3,2,1,0:T(8,128)(2,1)}, u32[]{:S(2)}, u32[]{:S(2)}) %collective-permute-start.25) | collective-permute-done | bytes 2359328 | tf_op jit(solution)/shard_map/ppermute | solution.py:206
  208.2 9.2 %head_weights.1 = (bf16[4,4,2,3,16,768]{5,4,3,2,1,0:T(8,128)(2,1)}, bf16[4,4,2,3,16,768]{5,4,3,2,1,0:T(8,128)(2,1)}) custom-call(s32[3]{0:T(128)} %pad_add_fusion.place, bf16[1024,768]{1,0:T(8,128)(2,1)} %get-tuple-element.170.dq, bf16[1024,768]{1,0:T(8,128)(2,1)} %get-tuple-element.171.dk, bf16[1024,768]{1,0:T(8,128)(2,1)} %get-tuple-element.172.dv, ...), custom_call_target="tpu_custom_call" | custom-call | flops 44999999488 | bytes 135000000 | tf_op jit(solution)/shard_map/head_weights/pallas_call | solution.py:860
  217.4 4.1 %collective-permute-done.26 = bf16[4,192,768]{2,1,0:T(8,128)(2,1)} collective-permute-done((bf16[4,192,768]{2,1,0:T(8,128)(2,1)S(1)}, bf16[4,192,768]{2,1,0:T(8,128)(2,1)}, u32[]{:S(2)}, u32[]{:S(2)}) %collective-permute-start.26) | collective-permute-done | bytes 1179680 | tf_op jit(solution)/shard_map/ppermute | solution.py:206
  221.6 3.1 %fusion = bf16[4,192,768]{2,1,0:T(8,128)(2,1)} fusion(bf16[4,192,768]{2,1,0:T(8,128)(2,1)} %collective-permute-done.26, bf16[2,4,192,768]{3,2,1,0:T(8,128)(2,1)S(1)} %get-tuple-element.221, bf16[2,4,192,768]{3,2,1,0:T(8,128)(2,1)} %collective-permute-done.25), kind=kLoop, calls=%fused_computation.3 | loop fusion | flops 4718592 | bytes 4718592 | tf_op jit(solution)/shard_map/convert_element_type | solution.py:237
  224.7 3.5 %all-to-all-start.2 = ((bf16[4,192,768]{2,1,0:T(8,128)(2,1)}), bf16[4,192,768]{2,1,0:T(8,128)(2,1)S(1)}, u32[]{:S(2)}, u32[]{:S(2)}) async-start(bf16[4,192,768]{2,1,0:T(8,128)(2,1)} %fusion), calls=%async_computation.2 | async-start | bytes 2359296 | tf_op jit(solution)/shard_map/all_to_all | solution.py:222
  228.2 3.0 add_convert_fusion.2
  234.1 9.0 %input_gradient.1 = f32[1024,768]{1,0:T(8,128)} custom-call(bf16[1024,768]{1,0:T(8,128)(2,1)} %get-tuple-element.170.dq, bf16[1024,768]{1,0:T(8,128)(2,1)} %get-tuple-element.171.dk, bf16[1024,768]{1,0:T(8,128)(2,1)} %get-tuple-element.172.dv, bf16[4,768,768]{2,1,0:T(8,128)(2,1)} %get-tuple-element.130.wo.full, f32[1024,768]{1,0:T(8,128)} %get-tuple-element.184.first, ...), custom_call_target="tpu_custom_call" | custom-call | flops 30000001024 | bytes 90000000 | tf_op jit(solution)/shard_map/input_gradient/pallas_call | solution.py:891
  243.1 4.5 %collective-permute-done.29 = bf16[2,4,96,768]{3,2,1,0:T(8,128)(2,1)} collective-permute-done((bf16[2,4,96,768]{3,2,1,0:T(8,128)(2,1)S(1)}, bf16[2,4,96,768]{3,2,1,0:T(8,128)(2,1)}, u32[]{:S(2)}, u32[]{:S(2)}) %collective-permute-start.29) | collective-permute-done | bytes 1179680 | tf_op jit(solution)/shard_map/ppermute | solution.py:206
  251.5 2.9 collective-permute-start.31
  254.3 4.5 %collective-permute-done.32 = bf16[4,96,768]{2,1,0:T(8,128)(2,1)S(1)} collective-permute-done((bf16[4,96,768]{2,1,0:T(8,128)(2,1)S(1)}, bf16[4,96,768]{2,1,0:T(8,128)(2,1)S(1)}, u32[]{:S(2)}, u32[]{:S(2)}) %collective-permute-start.32) | collective-permute-done | bytes 589856 | tf_op jit(solution)/shard_map/ppermute | solution.py:206
  260.9 5.3 %all-to-all-start.3 = ((bf16[4,96,768]{2,1,0:T(8,128)(2,1)}), bf16[4,96,768]{2,1,0:T(8,128)(2,1)S(1)}, u32[]{:S(2)}, u32[]{:S(2)}) async-start(bf16[4,96,768]{2,1,0:T(8,128)(2,1)} %fusion.3), calls=%async_computation.3 | async-start | bytes 1179648 | tf_op jit(solution)/shard_map/all_to_all | solution.py:222
  271.3 7.6 %score.1 = f32[32,32]{1,0:T(8,128)} custom-call(f32[1024,768]{1,0:T(8,128)} %get-tuple-element.193.out_ref, s32[1,1024]{1,0:T(1,128)} %bitcast.73, s32[32,1]{1,0:T(8,128)} %copy-done.14, bf16[1024,768]{1,0:T(8,128)(2,1)} %table_ref.1, s32[32,32]{1,0:T(8,128)} %pick_ref.1, f32[8,1280]{1,0:T(8,128)} %copy-done.9), custom_call_target="tpu_custom_call" | custom-call | flops 40000000000 | bytes 120000000 | tf_op jit(solution)/shard_map/score/pallas_call | solution.py:939
  278.9 3.4 %collective-permute-done.33 = f32[8,1280]{1,0:T(8,128)S(1)} collective-permute-done((f32[8,1280]{1,0:T(8,128)S(1)}, f32[8,1280]{1,0:T(8,128)S(1)}, u32[]{:S(2)}, u32[]{:S(2)}) %collective-permute-start.33) | collective-permute-done | bytes 40992 | tf_op jit(solution)/shard_map/ppermute | solution.py:65
  286.0 3.5 %all-to-all-start.4 = ((bf16[4,96,768]{2,1,0:T(8,128)(2,1)}), bf16[4,96,768]{2,1,0:T(8,128)(2,1)S(1)}, u32[]{:S(2)}, u32[]{:S(2)}) async-start(bf16[4,96,768]{2,1,0:T(8,128)(2,1)} %broadcast_in_dim.38.refs_8_), calls=%async_computation.4 | async-start | bytes 1179648 | tf_op jit(solution)/shard_map/all_to_all | solution.py:222
  291.8 4.7 %finish_feed.1 = (f32[768,768]{1,0:T(8,128)}, f32[768,768]{1,0:T(8,128)}) custom-call(s32[3]{0:T(128)} %pad_add_fusion.place, bf16[192,768]{1,0:T(8,128)(2,1)} %copy-done.5, bf16[192,768]{1,0:T(8,128)(2,1)} %copy-done.46, bf16[192,768]{1,0:T(8,128)(2,1)} %copy-done.47, bf16[192,768]{1,0:T(8,128)(2,1)} %copy-done.48, bf16[192,768]{1,0:T(8,128)(2,1)} %copy-done.49, ...), custom_call_target="tpu_custom_call" | custom-call | flops 30000001024 | bytes 90000000 | tf_op jit(solution)/shard_map/finish_feed/pallas_call | solution.py:162
  301.3 2.8 finish_heads.1
  (259 shorter events, 60.8 us)
Async XLA Ops:
  3.6 17.6 %collective-permute-start.1 = (bf16[96,768]{1,0:T(8,128)(2,1)}, bf16[96,768]{1,0:T(8,128)(2,1)S(1)}, u32[]{:S(2)}, u32[]{:S(2)}) collective-permute-start(bf16[96,768]{1,0:T(8,128)(2,1)} %piece_heads.1), channel_id=1, source_target_pairs={{0,2},{1,3},{2,0},{3,1},{4,6},{5,7},{6,4},{7,5},{8,10},{9,11},{10,... | collective-permute-start | bytes 442376 | tf_op jit(solution)/shard_map/ppermute | solution.py:65
  7.7 13.5 %collective-permute-start.2 = (bf16[96,768]{1,0:T(8,128)(2,1)}, bf16[96,768]{1,0:T(8,128)(2,1)S(1)}, u32[]{:S(2)}, u32[]{:S(2)}) collective-permute-start(bf16[96,768]{1,0:T(8,128)(2,1)} %piece_heads.1), channel_id=1, source_target_pairs={{0,3},{1,2},{2,1},{3,0},{4,7},{5,6},{6,5},{7,4},{8,11},{9,10},{10,... | collective-permute-start | bytes 442376 | tf_op jit(solution)/shard_map/ppermute | solution.py:65
  9.8 11.4 %collective-permute-start = (bf16[96,768]{1,0:T(8,128)(2,1)}, bf16[96,768]{1,0:T(8,128)(2,1)S(1)}, u32[]{:S(2)}, u32[]{:S(2)}) collective-permute-start(bf16[96,768]{1,0:T(8,128)(2,1)} %piece_heads.1), channel_id=1, source_target_pairs={{0,1},{1,0},{2,3},{3,2},{4,5},{5,4},{6,7},{7,6},{8,9},{9,8},{10,11... | collective-permute-start | bytes 442376 | tf_op jit(solution)/shard_map/ppermute | solution.py:65
  13.6 22.5 %all-to-all-start = ((bf16[4,112,768]{2,1,0:T(8,128)(2,1)}), bf16[4,112,768]{2,1,0:T(8,128)(2,1)S(1)}, u32[]{:S(2)}, u32[]{:S(2)}) async-start(bf16[4,112,768]{2,1,0:T(8,128)(2,1)} %get-tuple-element.118), calls=%async_computation | async-start | bytes 1376256 | tf_op jit(solution)/shard_map/all_to_all | solution.py:222
  21.3 11.7 %collective-permute-start.3 = (bf16[288,768]{1,0:T(8,128)(2,1)S(1)}, bf16[288,768]{1,0:T(8,128)(2,1)S(1)}, u32[]{:S(2)}, u32[]{:S(2)}) collective-permute-start(bf16[288,768]{1,0:T(8,128)(2,1)S(1)} %constant_dynamic-update-slice_fusion.refs_0_), channel_id=1, source_target_pairs={{0,8},{4,20},{8,0},{12,28},{16,24},{20,4},{24,16},{28,12},{1,9},{5... | collective-permute-start | bytes 1327112 | tf_op jit(solution)/shard_map/ppermute | solution.py:206
  34.4 10.0 %collective-permute-start.7 = (bf16[288,768]{1,0:T(8,128)(2,1)S(1)}, bf16[288,768]{1,0:T(8,128)(2,1)}, u32[]{:S(2)}, u32[]{:S(2)}) collective-permute-start(bf16[288,768]{1,0:T(8,128)(2,1)S(1)} %collective-permute-done.3.refs_1_), channel_id=1, source_target_pairs={{0,4},{4,0},{8,12},{12,8},{16,20},{20,16},{24,28},{28,24},{1,5},{5... | collective-permute-start | bytes 1327112 | tf_op jit(solution)/shard_map/ppermute | solution.py:65
  45.1 12.8 %collective-permute-start.10 = (bf16[288,768]{1,0:T(8,128)(2,1)S(1)}, bf16[288,768]{1,0:T(8,128)(2,1)S(1)}, u32[]{:S(2)}, u32[]{:S(2)}) collective-permute-start(bf16[288,768]{1,0:T(8,128)(2,1)S(1)} %pad_maximum_fusion.refs_0_), channel_id=1, source_target_pairs={{0,8},{4,20},{8,0},{12,28},{16,24},{20,4},{24,16},{28,12},{1,9},{5... | collective-permute-start | bytes 1327112 | tf_op jit(solution)/shard_map/ppermute | solution.py:206
  46.6 11.3 %collective-permute-start.11 = (bf16[288,768]{1,0:T(8,128)(2,1)S(1)}, bf16[288,768]{1,0:T(8,128)(2,1)S(1)}, u32[]{:S(2)}, u32[]{:S(2)}) collective-permute-start(bf16[288,768]{1,0:T(8,128)(2,1)S(1)} %pad_maximum_fusion.refs_0_), channel_id=1, source_target_pairs={{0,16},{4,12},{8,24},{12,4},{16,0},{20,28},{24,8},{28,20},{1,17},{... | collective-permute-start | bytes 1327112 | tf_op jit(solution)/shard_map/ppermute | solution.py:206
  47.2 29.9 %collective-permute-start.13 = (bf16[288,768]{1,0:T(8,128)(2,1)S(1)}, bf16[288,768]{1,0:T(8,128)(2,1)}, u32[]{:S(2)}, u32[]{:S(2)}) collective-permute-start(bf16[288,768]{1,0:T(8,128)(2,1)S(1)} %pad_maximum_fusion.refs_0_), channel_id=1, source_target_pairs={{0,4},{4,0},{8,12},{12,8},{16,20},{20,16},{24,28},{28,24},{1,5},{5... | collective-permute-start | bytes 1327112 | tf_op jit(solution)/shard_map/ppermute | solution.py:65
  57.9 19.1 %collective-permute-start.12 = (bf16[288,768]{1,0:T(8,128)(2,1)S(1)}, bf16[288,768]{1,0:T(8,128)(2,1)S(1)}, u32[]{:S(2)}, u32[]{:S(2)}) collective-permute-start(bf16[288,768]{1,0:T(8,128)(2,1)S(1)} %collective-permute-done.10.refs_1_), channel_id=1, source_target_pairs={{0,16},{4,12},{8,24},{12,4},{16,0},{20,28},{24,8},{28,20},{1,17},{... | collective-permute-start | bytes 1327112 | tf_op jit(solution)/shard_map/ppermute | solution.py:206
  58.5 18.5 %collective-permute-start.14 = (bf16[288,768]{1,0:T(8,128)(2,1)S(1)}, bf16[288,768]{1,0:T(8,128)(2,1)S(1)}, u32[]{:S(2)}, u32[]{:S(2)}) collective-permute-start(bf16[288,768]{1,0:T(8,128)(2,1)S(1)} %collective-permute-done.10.refs_1_), channel_id=1, source_target_pairs={{0,4},{4,0},{8,12},{12,8},{16,20},{20,16},{24,28},{28,24},{1,5},{5... | collective-permute-start | bytes 1327112 | tf_op jit(solution)/shard_map/ppermute | solution.py:65
  59.0 23.3 %all-to-all-start.1 = ((bf16[4,96,768]{2,1,0:T(8,128)(2,1)}), bf16[4,96,768]{2,1,0:T(8,128)(2,1)S(1)}, u32[]{:S(2)}, u32[]{:S(2)}) async-start(bf16[4,96,768]{2,1,0:T(8,128)(2,1)} %get-tuple-element.126), calls=%async_computation.1 | async-start | bytes 1179648 | tf_op jit(solution)/shard_map/all_to_all | solution.py:222
  66.3 10.8 %collective-permute-start.15 = (bf16[288,768]{1,0:T(8,128)(2,1)S(1)}, bf16[288,768]{1,0:T(8,128)(2,1)S(1)}, u32[]{:S(2)}, u32[]{:S(2)}) collective-permute-start(bf16[288,768]{1,0:T(8,128)(2,1)S(1)} %collective-permute-done.11.refs_2_), channel_id=1, source_target_pairs={{0,4},{4,0},{8,12},{12,8},{16,20},{20,16},{24,28},{28,24},{1,5},{5... | collective-permute-start | bytes 1327112 | tf_op jit(solution)/shard_map/ppermute | solution.py:65
  82.4 14.2 %collective-permute-start.16 = (bf16[288,768]{1,0:T(8,128)(2,1)S(1)}, bf16[288,768]{1,0:T(8,128)(2,1)S(1)}, u32[]{:S(2)}, u32[]{:S(2)}) collective-permute-start(bf16[288,768]{1,0:T(8,128)(2,1)S(1)} %pad_maximum_fusion.1.refs_4_.refs_0_), channel_id=1, source_target_pairs={{0,8},{4,20},{8,0},{12,28},{16,24},{20,4},{24,16},{28,12},{1,9},{5... | collective-permute-start | bytes 1327112 | tf_op jit(solution)/shard_map/ppermute | solution.py:206
  83.7 13.0 %collective-permute-start.17 = (bf16[288,768]{1,0:T(8,128)(2,1)S(1)}, bf16[288,768]{1,0:T(8,128)(2,1)S(1)}, u32[]{:S(2)}, u32[]{:S(2)}) collective-permute-start(bf16[288,768]{1,0:T(8,128)(2,1)S(1)} %pad_maximum_fusion.1.refs_4_.refs_0_), channel_id=1, source_target_pairs={{0,16},{4,12},{8,24},{12,4},{16,0},{20,28},{24,8},{28,20},{1,17},{... | collective-permute-start | bytes 1327112 | tf_op jit(solution)/shard_map/ppermute | solution.py:206
  85.5 26.5 %collective-permute-start.20 = (bf16[288,768]{1,0:T(8,128)(2,1)S(1)}, bf16[288,768]{1,0:T(8,128)(2,1)S(1)}, u32[]{:S(2)}, u32[]{:S(2)}) collective-permute-start(bf16[288,768]{1,0:T(8,128)(2,1)S(1)} %pad_maximum_fusion.1.refs_4_.refs_0_), channel_id=1, source_target_pairs={{0,4},{4,0},{8,12},{12,8},{16,20},{20,16},{24,28},{28,24},{1,5},{5... | collective-permute-start | bytes 1327112 | tf_op jit(solution)/shard_map/ppermute | solution.py:65
  85.5 12.0 %collective-permute-start.19 = (bf16[288,768]{1,0:T(8,128)(2,1)S(1)}, bf16[288,768]{1,0:T(8,128)(2,1)}, u32[]{:S(2)}, u32[]{:S(2)}) collective-permute-start(bf16[288,768]{1,0:T(8,128)(2,1)S(1)} %collective-permute-done.12.refs_3_), channel_id=1, source_target_pairs={{0,4},{4,0},{8,12},{12,8},{16,20},{20,16},{24,28},{28,24},{1,5},{5... | collective-permute-start | bytes 1327112 | tf_op jit(solution)/shard_map/ppermute | solution.py:65
  96.7 14.5 %collective-permute-start.18 = (bf16[288,768]{1,0:T(8,128)(2,1)S(1)}, bf16[288,768]{1,0:T(8,128)(2,1)S(1)}, u32[]{:S(2)}, u32[]{:S(2)}) collective-permute-start(bf16[288,768]{1,0:T(8,128)(2,1)S(1)} %collective-permute-done.16.refs_8_.refs_1_), channel_id=1, source_target_pairs={{0,16},{4,12},{8,24},{12,4},{16,0},{20,28},{24,8},{28,20},{1,17},{... | collective-permute-start | bytes 1327112 | tf_op jit(solution)/shard_map/ppermute | solution.py:206
  96.9 15.0 %collective-permute-start.21 = (bf16[288,768]{1,0:T(8,128)(2,1)S(1)}, bf16[288,768]{1,0:T(8,128)(2,1)S(1)}, u32[]{:S(2)}, u32[]{:S(2)}) collective-permute-start(bf16[288,768]{1,0:T(8,128)(2,1)S(1)} %collective-permute-done.16.refs_8_.refs_1_), channel_id=1, source_target_pairs={{0,4},{4,0},{8,12},{12,8},{16,20},{20,16},{24,28},{28,24},{1,5},{5... | collective-permute-start | bytes 1327112 | tf_op jit(solution)/shard_map/ppermute | solution.py:65
  97.0 15.0 %collective-permute-start.22 = (bf16[288,768]{1,0:T(8,128)(2,1)S(1)}, bf16[288,768]{1,0:T(8,128)(2,1)}, u32[]{:S(2)}, u32[]{:S(2)}) collective-permute-start(bf16[288,768]{1,0:T(8,128)(2,1)S(1)} %collective-permute-done.17.refs_9_.refs_2_), channel_id=1, source_target_pairs={{0,4},{4,0},{8,12},{12,8},{16,20},{20,16},{24,28},{28,24},{1,5},{5... | collective-permute-start | bytes 1327112 | tf_op jit(solution)/shard_map/ppermute | solution.py:65
  157.0 12.1 %collective-permute-start.24 = (bf16[4,4,192,768]{3,2,1,0:T(8,128)(2,1)}, bf16[4,4,192,768]{3,2,1,0:T(8,128)(2,1)}, u32[]{:S(2)}, u32[]{:S(2)}) collective-permute-start(bf16[4,4,192,768]{3,2,1,0:T(8,128)(2,1)} %bitcast.78), channel_id=1, source_target_pairs={{0,4},{4,0},{8,12},{12,8},{16,20},{20,16},{24,28},{28,24},{1,5},{5... | collective-permute-start | bytes 14155784 | tf_op jit(solution)/shard_map/ppermute | solution.py:65
  174.5 29.2 %collective-permute-start.25 = (bf16[2,4,192,768]{3,2,1,0:T(8,128)(2,1)}, bf16[2,4,192,768]{3,2,1,0:T(8,128)(2,1)}, u32[]{:S(2)}, u32[]{:S(2)}) collective-permute-start(bf16[2,4,192,768]{3,2,1,0:T(8,128)(2,1)} %get-tuple-element.220.refs_0_), channel_id=1, source_target_pairs={{0,8},{4,20},{8,0},{12,28},{16,24},{20,4},{24,16},{28,12},{1,9},{5... | collective-permute-start | bytes 7077896 | tf_op jit(solution)/shard_map/ppermute | solution.py:206
  205.2 16.4 %collective-permute-start.26 = (bf16[4,192,768]{2,1,0:T(8,128)(2,1)S(1)}, bf16[4,192,768]{2,1,0:T(8,128)(2,1)}, u32[]{:S(2)}, u32[]{:S(2)}) collective-permute-start(bf16[4,192,768]{2,1,0:T(8,128)(2,1)S(1)} %fusion.2.refs_1_), channel_id=1, source_target_pairs={{0,16},{4,12},{8,24},{12,4},{16,0},{20,28},{24,8},{28,20},{1,17},{... | collective-permute-start | bytes 3538952 | tf_op jit(solution)/shard_map/ppermute | solution.py:206
  221.6 11.1 %collective-permute-start.27 = (f32[8,1280]{1,0:T(8,128)}, f32[8,1280]{1,0:T(8,128)}, u32[]{:S(2)}, u32[]{:S(2)}) collective-permute-start(f32[8,1280]{1,0:T(8,128)} %pad_maximum_fusion.2.refs_0_), channel_id=1, source_target_pairs={{0,1},{1,0},{2,3},{3,2},{4,5},{5,4},{6,7},{7,6},{8,9},{9,8},{10,11... | collective-permute-start | bytes 122888 | tf_op jit(solution)/shard_map/ppermute | solution.py:65
  224.7 36.2 %all-to-all-start.2 = ((bf16[4,192,768]{2,1,0:T(8,128)(2,1)}), bf16[4,192,768]{2,1,0:T(8,128)(2,1)S(1)}, u32[]{:S(2)}, u32[]{:S(2)}) async-start(bf16[4,192,768]{2,1,0:T(8,128)(2,1)} %fusion), calls=%async_computation.2 | async-start | bytes 2359296 | tf_op jit(solution)/shard_map/all_to_all | solution.py:222
  231.3 16.4 %collective-permute-start.29 = (bf16[2,4,96,768]{3,2,1,0:T(8,128)(2,1)S(1)}, bf16[2,4,96,768]{3,2,1,0:T(8,128)(2,1)}, u32[]{:S(2)}, u32[]{:S(2)}) collective-permute-start(bf16[2,4,96,768]{3,2,1,0:T(8,128)(2,1)S(1)} %get-tuple-element.223.refs_0_), channel_id=1, source_target_pairs={{0,8},{4,20},{8,0},{12,28},{16,24},{20,4},{24,16},{28,12},{1,9},{5... | collective-permute-start | bytes 3538952 | tf_op jit(solution)/shard_map/ppermute | solution.py:206
  260.9 21.4 %all-to-all-start.3 = ((bf16[4,96,768]{2,1,0:T(8,128)(2,1)}), bf16[4,96,768]{2,1,0:T(8,128)(2,1)S(1)}, u32[]{:S(2)}, u32[]{:S(2)}) async-start(bf16[4,96,768]{2,1,0:T(8,128)(2,1)} %fusion.3), calls=%async_computation.3 | async-start | bytes 1179648 | tf_op jit(solution)/shard_map/all_to_all | solution.py:222
  266.4 16.0 %collective-permute-start.34 = (bf16[192,768]{1,0:T(8,128)(2,1)S(1)}, bf16[192,768]{1,0:T(8,128)(2,1)S(1)}, u32[]{:S(2)}, u32[]{:S(2)}) collective-permute-start(bf16[192,768]{1,0:T(8,128)(2,1)S(1)} %fusion.6.refs_0_), channel_id=1, source_target_pairs={{0,8},{4,20},{8,0},{12,28},{16,24},{20,4},{24,16},{28,12},{1,9},{5... | collective-permute-start | bytes 884744 | tf_op jit(solution)/shard_map/ppermute | solution.py:206
  267.8 14.6 %collective-permute-start.35 = (bf16[192,768]{1,0:T(8,128)(2,1)S(1)}, bf16[192,768]{1,0:T(8,128)(2,1)S(1)}, u32[]{:S(2)}, u32[]{:S(2)}) collective-permute-start(bf16[192,768]{1,0:T(8,128)(2,1)S(1)} %fusion.6.refs_0_), channel_id=1, source_target_pairs={{0,16},{4,12},{8,24},{12,4},{16,0},{20,28},{24,8},{28,20},{1,17},{... | collective-permute-start | bytes 884744 | tf_op jit(solution)/shard_map/ppermute | solution.py:206
  268.7 13.7 %collective-permute-start.36 = (bf16[192,768]{1,0:T(8,128)(2,1)S(1)}, bf16[192,768]{1,0:T(8,128)(2,1)S(1)}, u32[]{:S(2)}, u32[]{:S(2)}) collective-permute-start(bf16[192,768]{1,0:T(8,128)(2,1)S(1)} %fusion.6.refs_0_), channel_id=1, source_target_pairs={{0,24},{4,28},{8,16},{12,20},{16,8},{20,12},{24,0},{28,4},{1,25},{... | collective-permute-start | bytes 884744 | tf_op jit(solution)/shard_map/ppermute | solution.py:65
  270.0 12.3 %collective-permute-start.33 = (f32[8,1280]{1,0:T(8,128)S(1)}, f32[8,1280]{1,0:T(8,128)S(1)}, u32[]{:S(2)}, u32[]{:S(2)}) collective-permute-start(f32[8,1280]{1,0:T(8,128)S(1)} %add.125.refs_0_), channel_id=1, source_target_pairs={{0,8},{4,12},{8,0},{12,4},{16,24},{20,28},{24,16},{28,20},{1,9},{5... | collective-permute-start | bytes 122888 | tf_op jit(solution)/shard_map/ppermute | solution.py:65
  286.0 12.3 %all-to-all-start.4 = ((bf16[4,96,768]{2,1,0:T(8,128)(2,1)}), bf16[4,96,768]{2,1,0:T(8,128)(2,1)S(1)}, u32[]{:S(2)}, u32[]{:S(2)}) async-start(bf16[4,96,768]{2,1,0:T(8,128)(2,1)} %broadcast_in_dim.38.refs_8_), calls=%async_computation.4 | async-start | bytes 1179648 | tf_op jit(solution)/shard_map/all_to_all | solution.py:222
  (70 other events, 584.3 us)

commit v6 on v5

--- a/solution.py
+++ b/solution.py
@@ -15,6 +15,7 @@
 WINDOW = 384
 GROUP = 4 * HEAD_DIM
 ROW_BLOCK = 256
+MIDDLE_BLOCK = 512
 GRAIN = 16
 MEBI = 1024 * 1024
 NT = (((1,), (1,)), ((), ()))
@@ -755,7 +756,7 @@
     inner_sum[...] = jnp.dot(high, head, preferred_element_type=F32) + jnp.dot(
         rest, head, preferred_element_type=F32
     )
-    at = pl.ds(pl.multiple_of(step * ROW_BLOCK, ROW_BLOCK), ROW_BLOCK)
+    at = pl.ds(pl.multiple_of(step * MIDDLE_BLOCK, MIDDLE_BLOCK), MIDDLE_BLOCK)
     lows[at, :] = low
     held[at, :] = ctx[...]
 
@@ -776,21 +777,21 @@
 
 def middle(normed, second, unit, saved, ctx, full, gain, *tokens):
     rows, width = normed.shape
-    block = rows_spec(ROW_BLOCK, width)
+    block = rows_spec(MIDDLE_BLOCK, width)
     return pl.pallas_call(
         middle_kernel,
-        grid=(rows // ROW_BLOCK,),
+        grid=(rows // MIDDLE_BLOCK,),
         in_specs=[
             block,
             block,
             block,
-            rows_spec(ROW_BLOCK, 128),
+            rows_spec(MIDDLE_BLOCK, 128),
             block,
             pl.BlockSpec((1, width, width), lambda i: (3, 0, 0), pipeline_mode=pl.Buffered(1)),
             whole_spec((1, width)),
         ]
         + [token_spec() for _ in tokens],
-        out_specs=[block, block, rows_spec(ROW_BLOCK, 128), fixed_spec((width, width)), fixed_spec((8, width))],
+        out_specs=[block, block, rows_spec(MIDDLE_BLOCK, 128), fixed_spec((width, width)), fixed_spec((8, width))],
         out_shape=[
             shape((rows, width), F32),
             shape((rows, width), BF),

time: 310 us -> 310 us (level)
  transfers between devices with their start and end apart: 48 -> 48, of which waited for: 13 -> 13; matrix products, arithmetic and copies ran while one was open for 7% -> 7% of each run, Pallas kernels for 37% -> 38%
where the time goes in v6:
time: 310 us; the launch traced here: 305 us
  Pallas kernels  163 us (53%)
  starting transfers between devices  58.3 us (19%)
  waiting for transfers between devices  46.5 us (15%)
  other arithmetic  22.1 us (7%)
  local copies, waits for them, and re-layouts  12.7 us (4%)
    ppermute x15, waiting for transfers between devices, turn_swap(): lax.ppermute(block, 'dp', [(i, i ^ bits[i & 1]) for i in range(n_dp)])  31.9 us
    pallas_call x1, Pallas kernels, feed_back(): pl.pallas_call(feed_back_kernel, grid=(4,), in_specs=[scalar_spec(), full...  29.1 us
    all_to_all x5, starting transfers between devices, exchange(): lax.all_to_all(block, axis, 0, 0, axis_index_groups=groups, tiled=True)  23.7 us
    pallas_call x1, Pallas kernels, attend_back(): pl.pallas_call(attend_back_kernel, grid=(rows // BLOCK,), in_specs=[scala...  23.5 us
    pallas_call x2, Pallas kernels, attend(): pl.pallas_call(functools.partial(attend_kernel, part), grid=(steps,), in_...  21.2 us
    ppermute x15, starting transfers between devices, turn_swap(): lax.ppermute(block, 'dp', [(i, i ^ bits[i & 1]) for i in range(n_dp)])  18.5 us
    convert_element_type x6, other arithmetic, add(): return total.astype(BF)  16.3 us
    ppermute x28, starting transfers between devices, swap(): return lax.ppermute(block, axis, [(i, i ^ bit) for i in range(size)])  16.1 us
  transfers between devices with their start and end apart: 48, of which 13 were waited for; matrix products, arithmetic and copies ran while one was open for 7% of the time, Pallas kernels for 38%

profile of v6, /device:TPU:0, one launch (start us, length us, event | category | flops | bytes accessed | tf_op | source)
XLA Modules:
  0.0 304.8 jit_solution(9387542008984663891)
XLA Ops:
  3.6 4.1 %collective-permute-start.1 = (bf16[96,768]{1,0:T(8,128)(2,1)}, bf16[96,768]{1,0:T(8,128)(2,1)S(1)}, u32[]{:S(2)}, u32[]{:S(2)}) collective-permute-start(bf16[96,768]{1,0:T(8,128)(2,1)} %piece_heads.1), channel_id=1, source_target_pairs={{0,2},{1,3},{2,0},{3,1},{4,6},{5,7},{6,4},{7,5},{8,10},{9,11},{10,... | collective-permute-start | bytes 442376 | tf_op jit(solution)/shard_map/ppermute | solution.py:66
  10.1 3.5 %piece_feed.1 = (bf16[768,768]{1,0:T(8,128)(2,1)}, bf16[4,112,768]{2,1,0:T(8,128)(2,1)}, bf16[4,96,768]{2,1,0:T(8,128)(2,1)}) custom-call(s32[3]{0:T(128)} %pad_add_fusion.place, bf16[768,768]{1,0:T(8,128)(2,1)} %wu.1, bf16[768,768]{1,0:T(8,128)(2,1)} %own.1, bf16[16,768]{1,0:T(8,128)(2,1)} %pad.13.rest), custom_call_target="tpu_custom_call" | custom-call | flops 15000000512 | bytes 45000000 | tf_op jit(solution)/shard_map/piece_feed/pallas_call | solution.py:133
  13.6 4.2 %all-to-all-start = ((bf16[4,112,768]{2,1,0:T(8,128)(2,1)}), bf16[4,112,768]{2,1,0:T(8,128)(2,1)S(1)}, u32[]{:S(2)}, u32[]{:S(2)}) async-start(bf16[4,112,768]{2,1,0:T(8,128)(2,1)} %get-tuple-element.118), calls=%async_computation | async-start | bytes 1376256 | tf_op jit(solution)/shard_map/all_to_all | solution.py:223
  24.8 8.2 %collective-permute-done.3.refs_1_ = bf16[288,768]{1,0:T(8,128)(2,1)S(1)} collective-permute-done((bf16[288,768]{1,0:T(8,128)(2,1)S(1)}, bf16[288,768]{1,0:T(8,128)(2,1)S(1)}, u32[]{:S(2)}, u32[]{:S(2)}) %collective-permute-start.3) | collective-permute-done | bytes 442400 | tf_op jit(solution)/shard_map/ppermute | solution.py:207
  36.0 5.3 %collective-permute-done.5.refs_3_ = bf16[288,768]{1,0:T(8,128)(2,1)S(1)} collective-permute-done((bf16[288,768]{1,0:T(8,128)(2,1)S(1)}, bf16[288,768]{1,0:T(8,128)(2,1)S(1)}, u32[]{:S(2)}, u32[]{:S(2)}) %collective-permute-start.5) | collective-permute-done | bytes 442400 | tf_op jit(solution)/shard_map/ppermute | solution.py:207
  47.2 9.7 %project.1 = (bf16[1024,768]{1,0:T(8,128)(2,1)}, bf16[1024,768]{1,0:T(8,128)(2,1)}, bf16[1024,768]{1,0:T(8,128)(2,1)}, bf16[4,768,768]{2,1,0:T(8,128)(2,1)}) custom-call(s32[3]{0:T(128)} %pad_add_fusion.place, bf16[1024,768]{1,0:T(8,128)(2,1)} %x.13, bf16[192,768]{1,0:T(8,128)(2,1)} %bitcast.81, bf16[192,768]{1,0:T(8,128)(2,1)} %bitcast.83, ...), custom_call_target="tpu_custom_call" | custom-call | flops 49999998976 | bytes 150000000 | tf_op jit(solution)/shard_map/project/pallas_call | solution.py:320
  59.0 7.2 %all-to-all-start.1 = ((bf16[4,96,768]{2,1,0:T(8,128)(2,1)}), bf16[4,96,768]{2,1,0:T(8,128)(2,1)S(1)}, u32[]{:S(2)}, u32[]{:S(2)}) async-start(bf16[4,96,768]{2,1,0:T(8,128)(2,1)} %get-tuple-element.126), calls=%async_computation.1 | async-start | bytes 1179648 | tf_op jit(solution)/shard_map/all_to_all | solution.py:223
  66.4 10.6 %attend.2 = (bf16[1024,768]{1,0:T(8,128)(2,1)}, f32[1024,128]{1,0:T(8,128)}, f32[1024,768]{1,0:T(8,128)}, bf16[1024,768]{1,0:T(8,128)(2,1)}) custom-call(bf16[1024,768]{1,0:T(8,128)(2,1)} %get-tuple-element.125.q, bf16[1024,768]{1,0:T(8,128)(2,1)} %get-tuple-element.128.k, bf16[1024,768]{1,0:T(8,128)(2,1)} %get-tuple-element.129.v, s32[1024,1]{1,0:T(8,128)} %copy.52.segc, ...), custom_call_target="tpu_custom_call" | custom-call | flops 40000000000 | bytes 120000000 | tf_op jit(solution)/shard_map/attend/pallas_call | solution.py:409
  77.1 5.3 %all-to-all-done.1 = bf16[4,96,768]{2,1,0:T(8,128)(2,1)S(1)} async-done(((bf16[4,96,768]{2,1,0:T(8,128)(2,1)}), bf16[4,96,768]{2,1,0:T(8,128)(2,1)S(1)}, u32[]{:S(2)}, u32[]{:S(2)}) %all-to-all-start.1) | async-done | bytes 589856 | tf_op jit(solution)/shard_map/all_to_all | solution.py:223
  86.0 10.6 %attend.3 = (bf16[1024,768]{1,0:T(8,128)(2,1)}, f32[1024,128]{1,0:T(8,128)}, f32[1024,768]{1,0:T(8,128)}, bf16[1024,768]{1,0:T(8,128)(2,1)}) custom-call(bf16[1024,768]{1,0:T(8,128)(2,1)} %get-tuple-element.125.q, bf16[1024,768]{1,0:T(8,128)(2,1)} %get-tuple-element.128.k, ...), custom_call_target="tpu_custom_call", output_to_operand_aliasing={{0}: (10, {}), {1}: (11, {}), {2}: (12, {}), {3}: (13, {})} | custom-call | flops 40000000000 | bytes 120000000 | tf_op jit(solution)/shard_map/attend/pallas_call | solution.py:409
  97.6 13.6 %feed_up.1 = (bf16[1024,3072]{1,0:T(8,128)(2,1)}, bf16[1024,3072]{1,0:T(8,128)(2,1)}, bf16[3072,768]{1,0:T(8,128)(2,1)}) custom-call(s32[3]{0:T(128)} %pad_add_fusion.place, bf16[1024,768]{1,0:T(8,128)(2,1)} %get-tuple-element.142.x, bf16[768,768]{1,0:T(8,128)(2,1)} %get-tuple-element.143.own, f32[1,3072]{1,0:T(1,128)} %reshape.226.bu, ...), custom_call_target="tpu_custom_call" | custom-call | flops 60000002048 | bytes 180000000 | tf_op jit(solution)/shard_map/feed_up/pallas_call | solution.py:575
  113.8 14.1 %feed_down.1 = (f32[1024,768]{1,0:T(8,128)}, bf16[1024,768]{1,0:T(8,128)(2,1)}, f32[1024,768]{1,0:T(8,128)}, bf16[1024,768]{1,0:T(8,128)(2,1)}, f32[8,768]{1,0:T(8,128)}, /*index=5*/bf16[3072,768]{1,0:T(8,128)(2,1)}) custom-call(s32[3]{0:T(128)} %pad_add_fusion.place, bf16[1024,3072]{1,0:T(8,128)(2,1)} %get-tuple-element.150.act, ...), custom_call_target="tpu_custom_call" | custom-call | flops 65000001536 | bytes 195000000 | tf_op jit(solution)/shard_map/feed_down/pallas_call | solution.py:636
  127.9 29.1 %feed_back.1 = (bf16[4,4,2,96,768]{4,3,2,1,0:T(8,128)(2,1)}, bf16[4,4,2,96,768]{4,3,2,1,0:T(8,128)(2,1)}, f32[8,512]{1,0:T(8,128)}, f32[1024,768]{1,0:T(8,128)}) custom-call(s32[3]{0:T(128)} %pad_add_fusion.place, bf16[1024,768]{1,0:T(8,128)(2,1)} %get-tuple-element.154.grad, bf16[1024,768]{1,0:T(8,128)(2,1)} %get-tuple-element.142.x, ...), custom_call_target="tpu_custom_call" | custom-call | flops 134999998464 | bytes 405000000 | tf_op jit(solution)/shard_map/feed_back/pallas_call | solution.py:711
  157.2 12.3 %middle.1 = (f32[1024,768]{1,0:T(8,128)}, bf16[1024,768]{1,0:T(8,128)(2,1)}, f32[1024,128]{1,0:T(8,128)}, bf16[768,768]{1,0:T(8,128)(2,1)}, f32[8,768]{1,0:T(8,128)}) custom-call(f32[1024,768]{1,0:T(8,128)} %get-tuple-element.160.normed, f32[1024,768]{1,0:T(8,128)} %get-tuple-element.161.second, f32[1024,768]{1,0:T(8,128)} %get-tuple-element.151.unit, ...), custom_call_target="tpu_custom_call" | custom-call | flops 40000000000 | bytes 120000000 | tf_op jit(solution)/shard_map/middle/pallas_call | solution.py:781
  169.5 5.3 %add_convert_fusion = (bf16[2,4,192,768]{3,2,1,0:T(8,128)(2,1)}, bf16[2,4,192,768]{3,2,1,0:T(8,128)(2,1)S(1)}) fusion(bf16[4,4,192,768]{3,2,1,0:T(8,128)(2,1)} %collective-permute-done.24, bf16[4,4,192,768]{3,2,1,0:T(8,128)(2,1)} %bitcast.67), kind=kLoop, calls=%fused_computation | loop fusion | flops 9437184 | bytes 14155776 | tf_op jit(solution)/shard_map/convert_element_type | solution.py:238
  176.2 23.5 %attend_back.1 = (bf16[1024,768]{1,0:T(8,128)(2,1)}, bf16[1024,768]{1,0:T(8,128)(2,1)}, bf16[1024,768]{1,0:T(8,128)(2,1)}, f32[8,768]{1,0:T(8,128)}) custom-call(s32[3]{0:T(128)} %pad_add_fusion.place, bf16[1024,768]{1,0:T(8,128)(2,1)} %get-tuple-element.125.q, bf16[1024,768]{1,0:T(8,128)(2,1)} %get-tuple-element.128.k, ...), custom_call_target="tpu_custom_call" | custom-call | flops 109999996928 | bytes 330000000 | tf_op jit(solution)/shard_map/attend_back/pallas_call | solution.py:506
  199.8 4.2 %collective-permute-done.25 = bf16[2,4,192,768]{3,2,1,0:T(8,128)(2,1)} collective-permute-done((bf16[2,4,192,768]{3,2,1,0:T(8,128)(2,1)}, bf16[2,4,192,768]{3,2,1,0:T(8,128)(2,1)}, u32[]{:S(2)}, u32[]{:S(2)}) %collective-permute-start.25) | collective-permute-done | bytes 2359328 | tf_op jit(solution)/shard_map/ppermute | solution.py:207
  208.6 9.2 %head_weights.1 = (bf16[4,4,2,3,16,768]{5,4,3,2,1,0:T(8,128)(2,1)}, bf16[4,4,2,3,16,768]{5,4,3,2,1,0:T(8,128)(2,1)}) custom-call(s32[3]{0:T(128)} %pad_add_fusion.place, bf16[1024,768]{1,0:T(8,128)(2,1)} %get-tuple-element.170.dq, bf16[1024,768]{1,0:T(8,128)(2,1)} %get-tuple-element.171.dk, bf16[1024,768]{1,0:T(8,128)(2,1)} %get-tuple-element.172.dv, ...), custom_call_target="tpu_custom_call" | custom-call | flops 44999999488 | bytes 135000000 | tf_op jit(solution)/shard_map/head_weights/pallas_call | solution.py:861
  217.8 4.1 %collective-permute-done.26 = bf16[4,192,768]{2,1,0:T(8,128)(2,1)} collective-permute-done((bf16[4,192,768]{2,1,0:T(8,128)(2,1)S(1)}, bf16[4,192,768]{2,1,0:T(8,128)(2,1)}, u32[]{:S(2)}, u32[]{:S(2)}) %collective-permute-start.26) | collective-permute-done | bytes 1179680 | tf_op jit(solution)/shard_map/ppermute | solution.py:207
  222.0 3.1 %fusion = bf16[4,192,768]{2,1,0:T(8,128)(2,1)} fusion(bf16[4,192,768]{2,1,0:T(8,128)(2,1)} %collective-permute-done.26, bf16[2,4,192,768]{3,2,1,0:T(8,128)(2,1)S(1)} %get-tuple-element.221, bf16[2,4,192,768]{3,2,1,0:T(8,128)(2,1)} %collective-permute-done.25), kind=kLoop, calls=%fused_computation.3 | loop fusion | flops 4718592 | bytes 4718592 | tf_op jit(solution)/shard_map/convert_element_type | solution.py:238
  225.1 3.5 %all-to-all-start.2 = ((bf16[4,192,768]{2,1,0:T(8,128)(2,1)}), bf16[4,192,768]{2,1,0:T(8,128)(2,1)S(1)}, u32[]{:S(2)}, u32[]{:S(2)}) async-start(bf16[4,192,768]{2,1,0:T(8,128)(2,1)} %fusion), calls=%async_computation.2 | async-start | bytes 2359296 | tf_op jit(solution)/shard_map/all_to_all | solution.py:223
  228.6 3.0 add_convert_fusion.2
  234.5 9.0 %input_gradient.1 = f32[1024,768]{1,0:T(8,128)} custom-call(bf16[1024,768]{1,0:T(8,128)(2,1)} %get-tuple-element.170.dq, bf16[1024,768]{1,0:T(8,128)(2,1)} %get-tuple-element.171.dk, bf16[1024,768]{1,0:T(8,128)(2,1)} %get-tuple-element.172.dv, bf16[4,768,768]{2,1,0:T(8,128)(2,1)} %get-tuple-element.130.wo.full, f32[1024,768]{1,0:T(8,128)} %get-tuple-element.184.first, ...), custom_call_target="tpu_custom_call" | custom-call | flops 30000001024 | bytes 90000000 | tf_op jit(solution)/shard_map/input_gradient/pallas_call | solution.py:892
  243.5 4.5 %collective-permute-done.29 = bf16[2,4,96,768]{3,2,1,0:T(8,128)(2,1)} collective-permute-done((bf16[2,4,96,768]{3,2,1,0:T(8,128)(2,1)S(1)}, bf16[2,4,96,768]{3,2,1,0:T(8,128)(2,1)}, u32[]{:S(2)}, u32[]{:S(2)}) %collective-permute-start.29) | collective-permute-done | bytes 1179680 | tf_op jit(solution)/shard_map/ppermute | solution.py:207
  251.9 2.9 collective-permute-start.31
  254.7 4.5 %collective-permute-done.32 = bf16[4,96,768]{2,1,0:T(8,128)(2,1)S(1)} collective-permute-done((bf16[4,96,768]{2,1,0:T(8,128)(2,1)S(1)}, bf16[4,96,768]{2,1,0:T(8,128)(2,1)S(1)}, u32[]{:S(2)}, u32[]{:S(2)}) %collective-permute-start.32) | collective-permute-done | bytes 589856 | tf_op jit(solution)/shard_map/ppermute | solution.py:207
  261.3 5.3 %all-to-all-start.3 = ((bf16[4,96,768]{2,1,0:T(8,128)(2,1)}), bf16[4,96,768]{2,1,0:T(8,128)(2,1)S(1)}, u32[]{:S(2)}, u32[]{:S(2)}) async-start(bf16[4,96,768]{2,1,0:T(8,128)(2,1)} %fusion.3), calls=%async_computation.3 | async-start | bytes 1179648 | tf_op jit(solution)/shard_map/all_to_all | solution.py:223
  271.7 7.6 %score.1 = f32[32,32]{1,0:T(8,128)} custom-call(f32[1024,768]{1,0:T(8,128)} %get-tuple-element.193.out_ref, s32[1,1024]{1,0:T(1,128)} %bitcast.73, s32[32,1]{1,0:T(8,128)} %copy-done.14, bf16[1024,768]{1,0:T(8,128)(2,1)} %table_ref.1, s32[32,32]{1,0:T(8,128)} %pick_ref.1, f32[8,1280]{1,0:T(8,128)} %copy-done.9), custom_call_target="tpu_custom_call" | custom-call | flops 40000000000 | bytes 120000000 | tf_op jit(solution)/shard_map/score/pallas_call | solution.py:940
  279.3 3.4 %collective-permute-done.33 = f32[8,1280]{1,0:T(8,128)S(1)} collective-permute-done((f32[8,1280]{1,0:T(8,128)S(1)}, f32[8,1280]{1,0:T(8,128)S(1)}, u32[]{:S(2)}, u32[]{:S(2)}) %collective-permute-start.33) | collective-permute-done | bytes 40992 | tf_op jit(solution)/shard_map/ppermute | solution.py:66
  286.4 3.5 %all-to-all-start.4 = ((bf16[4,96,768]{2,1,0:T(8,128)(2,1)}), bf16[4,96,768]{2,1,0:T(8,128)(2,1)S(1)}, u32[]{:S(2)}, u32[]{:S(2)}) async-start(bf16[4,96,768]{2,1,0:T(8,128)(2,1)} %broadcast_in_dim.38.refs_8_), calls=%async_computation.4 | async-start | bytes 1179648 | tf_op jit(solution)/shard_map/all_to_all | solution.py:223
  292.2 4.7 %finish_feed.1 = (f32[768,768]{1,0:T(8,128)}, f32[768,768]{1,0:T(8,128)}) custom-call(s32[3]{0:T(128)} %pad_add_fusion.place, bf16[192,768]{1,0:T(8,128)(2,1)} %copy-done.5, bf16[192,768]{1,0:T(8,128)(2,1)} %copy-done.46, bf16[192,768]{1,0:T(8,128)(2,1)} %copy-done.47, bf16[192,768]{1,0:T(8,128)(2,1)} %copy-done.48, bf16[192,768]{1,0:T(8,128)(2,1)} %copy-done.49, ...), custom_call_target="tpu_custom_call" | custom-call | flops 30000001024 | bytes 90000000 | tf_op jit(solution)/shard_map/finish_feed/pallas_call | solution.py:163
  301.7 2.8 finish_heads.1
  (259 shorter events, 60.8 us)
Async XLA Ops:
  3.6 17.6 %collective-permute-start.1 = (bf16[96,768]{1,0:T(8,128)(2,1)}, bf16[96,768]{1,0:T(8,128)(2,1)S(1)}, u32[]{:S(2)}, u32[]{:S(2)}) collective-permute-start(bf16[96,768]{1,0:T(8,128)(2,1)} %piece_heads.1), channel_id=1, source_target_pairs={{0,2},{1,3},{2,0},{3,1},{4,6},{5,7},{6,4},{7,5},{8,10},{9,11},{10,... | collective-permute-start | bytes 442376 | tf_op jit(solution)/shard_map/ppermute | solution.py:66
  7.7 13.5 %collective-permute-start.2 = (bf16[96,768]{1,0:T(8,128)(2,1)}, bf16[96,768]{1,0:T(8,128)(2,1)S(1)}, u32[]{:S(2)}, u32[]{:S(2)}) collective-permute-start(bf16[96,768]{1,0:T(8,128)(2,1)} %piece_heads.1), channel_id=1, source_target_pairs={{0,3},{1,2},{2,1},{3,0},{4,7},{5,6},{6,5},{7,4},{8,11},{9,10},{10,... | collective-permute-start | bytes 442376 | tf_op jit(solution)/shard_map/ppermute | solution.py:66
  9.8 11.4 %collective-permute-start = (bf16[96,768]{1,0:T(8,128)(2,1)}, bf16[96,768]{1,0:T(8,128)(2,1)S(1)}, u32[]{:S(2)}, u32[]{:S(2)}) collective-permute-start(bf16[96,768]{1,0:T(8,128)(2,1)} %piece_heads.1), channel_id=1, source_target_pairs={{0,1},{1,0},{2,3},{3,2},{4,5},{5,4},{6,7},{7,6},{8,9},{9,8},{10,11... | collective-permute-start | bytes 442376 | tf_op jit(solution)/shard_map/ppermute | solution.py:66
  13.6 22.5 %all-to-all-start = ((bf16[4,112,768]{2,1,0:T(8,128)(2,1)}), bf16[4,112,768]{2,1,0:T(8,128)(2,1)S(1)}, u32[]{:S(2)}, u32[]{:S(2)}) async-start(bf16[4,112,768]{2,1,0:T(8,128)(2,1)} %get-tuple-element.118), calls=%async_computation | async-start | bytes 1376256 | tf_op jit(solution)/shard_map/all_to_all | solution.py:223
  21.3 11.7 %collective-permute-start.3 = (bf16[288,768]{1,0:T(8,128)(2,1)S(1)}, bf16[288,768]{1,0:T(8,128)(2,1)S(1)}, u32[]{:S(2)}, u32[]{:S(2)}) collective-permute-start(bf16[288,768]{1,0:T(8,128)(2,1)S(1)} %constant_dynamic-update-slice_fusion.refs_0_), channel_id=1, source_target_pairs={{0,8},{4,20},{8,0},{12,28},{16,24},{20,4},{24,16},{28,12},{1,9},{5... | collective-permute-start | bytes 1327112 | tf_op jit(solution)/shard_map/ppermute | solution.py:207
  34.4 10.0 %collective-permute-start.7 = (bf16[288,768]{1,0:T(8,128)(2,1)S(1)}, bf16[288,768]{1,0:T(8,128)(2,1)}, u32[]{:S(2)}, u32[]{:S(2)}) collective-permute-start(bf16[288,768]{1,0:T(8,128)(2,1)S(1)} %collective-permute-done.3.refs_1_), channel_id=1, source_target_pairs={{0,4},{4,0},{8,12},{12,8},{16,20},{20,16},{24,28},{28,24},{1,5},{5... | collective-permute-start | bytes 1327112 | tf_op jit(solution)/shard_map/ppermute | solution.py:66
  45.1 12.8 %collective-permute-start.10 = (bf16[288,768]{1,0:T(8,128)(2,1)S(1)}, bf16[288,768]{1,0:T(8,128)(2,1)S(1)}, u32[]{:S(2)}, u32[]{:S(2)}) collective-permute-start(bf16[288,768]{1,0:T(8,128)(2,1)S(1)} %pad_maximum_fusion.refs_0_), channel_id=1, source_target_pairs={{0,8},{4,20},{8,0},{12,28},{16,24},{20,4},{24,16},{28,12},{1,9},{5... | collective-permute-start | bytes 1327112 | tf_op jit(solution)/shard_map/ppermute | solution.py:207
  46.6 11.3 %collective-permute-start.11 = (bf16[288,768]{1,0:T(8,128)(2,1)S(1)}, bf16[288,768]{1,0:T(8,128)(2,1)S(1)}, u32[]{:S(2)}, u32[]{:S(2)}) collective-permute-start(bf16[288,768]{1,0:T(8,128)(2,1)S(1)} %pad_maximum_fusion.refs_0_), channel_id=1, source_target_pairs={{0,16},{4,12},{8,24},{12,4},{16,0},{20,28},{24,8},{28,20},{1,17},{... | collective-permute-start | bytes 1327112 | tf_op jit(solution)/shard_map/ppermute | solution.py:207
  47.2 29.9 %collective-permute-start.13 = (bf16[288,768]{1,0:T(8,128)(2,1)S(1)}, bf16[288,768]{1,0:T(8,128)(2,1)}, u32[]{:S(2)}, u32[]{:S(2)}) collective-permute-start(bf16[288,768]{1,0:T(8,128)(2,1)S(1)} %pad_maximum_fusion.refs_0_), channel_id=1, source_target_pairs={{0,4},{4,0},{8,12},{12,8},{16,20},{20,16},{24,28},{28,24},{1,5},{5... | collective-permute-start | bytes 1327112 | tf_op jit(solution)/shard_map/ppermute | solution.py:66
  57.9 19.1 %collective-permute-start.12 = (bf16[288,768]{1,0:T(8,128)(2,1)S(1)}, bf16[288,768]{1,0:T(8,128)(2,1)S(1)}, u32[]{:S(2)}, u32[]{:S(2)}) collective-permute-start(bf16[288,768]{1,0:T(8,128)(2,1)S(1)} %collective-permute-done.10.refs_1_), channel_id=1, source_target_pairs={{0,16},{4,12},{8,24},{12,4},{16,0},{20,28},{24,8},{28,20},{1,17},{... | collective-permute-start | bytes 1327112 | tf_op jit(solution)/shard_map/ppermute | solution.py:207
  58.5 18.5 %collective-permute-start.14 = (bf16[288,768]{1,0:T(8,128)(2,1)S(1)}, bf16[288,768]{1,0:T(8,128)(2,1)S(1)}, u32[]{:S(2)}, u32[]{:S(2)}) collective-permute-start(bf16[288,768]{1,0:T(8,128)(2,1)S(1)} %collective-permute-done.10.refs_1_), channel_id=1, source_target_pairs={{0,4},{4,0},{8,12},{12,8},{16,20},{20,16},{24,28},{28,24},{1,5},{5... | collective-permute-start | bytes 1327112 | tf_op jit(solution)/shard_map/ppermute | solution.py:66
  59.0 23.3 %all-to-all-start.1 = ((bf16[4,96,768]{2,1,0:T(8,128)(2,1)}), bf16[4,96,768]{2,1,0:T(8,128)(2,1)S(1)}, u32[]{:S(2)}, u32[]{:S(2)}) async-start(bf16[4,96,768]{2,1,0:T(8,128)(2,1)} %get-tuple-element.126), calls=%async_computation.1 | async-start | bytes 1179648 | tf_op jit(solution)/shard_map/all_to_all | solution.py:223
  66.3 10.8 %collective-permute-start.15 = (bf16[288,768]{1,0:T(8,128)(2,1)S(1)}, bf16[288,768]{1,0:T(8,128)(2,1)S(1)}, u32[]{:S(2)}, u32[]{:S(2)}) collective-permute-start(bf16[288,768]{1,0:T(8,128)(2,1)S(1)} %collective-permute-done.11.refs_2_), channel_id=1, source_target_pairs={{0,4},{4,0},{8,12},{12,8},{16,20},{20,16},{24,28},{28,24},{1,5},{5... | collective-permute-start | bytes 1327112 | tf_op jit(solution)/shard_map/ppermute | solution.py:66
  82.4 14.2 %collective-permute-start.16 = (bf16[288,768]{1,0:T(8,128)(2,1)S(1)}, bf16[288,768]{1,0:T(8,128)(2,1)S(1)}, u32[]{:S(2)}, u32[]{:S(2)}) collective-permute-start(bf16[288,768]{1,0:T(8,128)(2,1)S(1)} %pad_maximum_fusion.1.refs_4_.refs_0_), channel_id=1, source_target_pairs={{0,8},{4,20},{8,0},{12,28},{16,24},{20,4},{24,16},{28,12},{1,9},{5... | collective-permute-start | bytes 1327112 | tf_op jit(solution)/shard_map/ppermute | solution.py:207
  83.7 13.0 %collective-permute-start.17 = (bf16[288,768]{1,0:T(8,128)(2,1)S(1)}, bf16[288,768]{1,0:T(8,128)(2,1)S(1)}, u32[]{:S(2)}, u32[]{:S(2)}) collective-permute-start(bf16[288,768]{1,0:T(8,128)(2,1)S(1)} %pad_maximum_fusion.1.refs_4_.refs_0_), channel_id=1, source_target_pairs={{0,16},{4,12},{8,24},{12,4},{16,0},{20,28},{24,8},{28,20},{1,17},{... | collective-permute-start | bytes 1327112 | tf_op jit(solution)/shard_map/ppermute | solution.py:207
  85.5 26.5 %collective-permute-start.20 = (bf16[288,768]{1,0:T(8,128)(2,1)S(1)}, bf16[288,768]{1,0:T(8,128)(2,1)S(1)}, u32[]{:S(2)}, u32[]{:S(2)}) collective-permute-start(bf16[288,768]{1,0:T(8,128)(2,1)S(1)} %pad_maximum_fusion.1.refs_4_.refs_0_), channel_id=1, source_target_pairs={{0,4},{4,0},{8,12},{12,8},{16,20},{20,16},{24,28},{28,24},{1,5},{5... | collective-permute-start | bytes 1327112 | tf_op jit(solution)/shard_map/ppermute | solution.py:66
  85.5 12.0 %collective-permute-start.19 = (bf16[288,768]{1,0:T(8,128)(2,1)S(1)}, bf16[288,768]{1,0:T(8,128)(2,1)}, u32[]{:S(2)}, u32[]{:S(2)}) collective-permute-start(bf16[288,768]{1,0:T(8,128)(2,1)S(1)} %collective-permute-done.12.refs_3_), channel_id=1, source_target_pairs={{0,4},{4,0},{8,12},{12,8},{16,20},{20,16},{24,28},{28,24},{1,5},{5... | collective-permute-start | bytes 1327112 | tf_op jit(solution)/shard_map/ppermute | solution.py:66
  96.7 14.5 %collective-permute-start.18 = (bf16[288,768]{1,0:T(8,128)(2,1)S(1)}, bf16[288,768]{1,0:T(8,128)(2,1)S(1)}, u32[]{:S(2)}, u32[]{:S(2)}) collective-permute-start(bf16[288,768]{1,0:T(8,128)(2,1)S(1)} %collective-permute-done.16.refs_8_.refs_1_), channel_id=1, source_target_pairs={{0,16},{4,12},{8,24},{12,4},{16,0},{20,28},{24,8},{28,20},{1,17},{... | collective-permute-start | bytes 1327112 | tf_op jit(solution)/shard_map/ppermute | solution.py:207
  96.9 15.0 %collective-permute-start.21 = (bf16[288,768]{1,0:T(8,128)(2,1)S(1)}, bf16[288,768]{1,0:T(8,128)(2,1)S(1)}, u32[]{:S(2)}, u32[]{:S(2)}) collective-permute-start(bf16[288,768]{1,0:T(8,128)(2,1)S(1)} %collective-permute-done.16.refs_8_.refs_1_), channel_id=1, source_target_pairs={{0,4},{4,0},{8,12},{12,8},{16,20},{20,16},{24,28},{28,24},{1,5},{5... | collective-permute-start | bytes 1327112 | tf_op jit(solution)/shard_map/ppermute | solution.py:66
  97.0 15.0 %collective-permute-start.22 = (bf16[288,768]{1,0:T(8,128)(2,1)S(1)}, bf16[288,768]{1,0:T(8,128)(2,1)}, u32[]{:S(2)}, u32[]{:S(2)}) collective-permute-start(bf16[288,768]{1,0:T(8,128)(2,1)S(1)} %collective-permute-done.17.refs_9_.refs_2_), channel_id=1, source_target_pairs={{0,4},{4,0},{8,12},{12,8},{16,20},{20,16},{24,28},{28,24},{1,5},{5... | collective-permute-start | bytes 1327112 | tf_op jit(solution)/shard_map/ppermute | solution.py:66
  157.0 12.5 %collective-permute-start.24 = (bf16[4,4,192,768]{3,2,1,0:T(8,128)(2,1)}, bf16[4,4,192,768]{3,2,1,0:T(8,128)(2,1)}, u32[]{:S(2)}, u32[]{:S(2)}) collective-permute-start(bf16[4,4,192,768]{3,2,1,0:T(8,128)(2,1)} %bitcast.78), channel_id=1, source_target_pairs={{0,4},{4,0},{8,12},{12,8},{16,20},{20,16},{24,28},{28,24},{1,5},{5... | collective-permute-start | bytes 14155784 | tf_op jit(solution)/shard_map/ppermute | solution.py:66
  174.9 29.2 %collective-permute-start.25 = (bf16[2,4,192,768]{3,2,1,0:T(8,128)(2,1)}, bf16[2,4,192,768]{3,2,1,0:T(8,128)(2,1)}, u32[]{:S(2)}, u32[]{:S(2)}) collective-permute-start(bf16[2,4,192,768]{3,2,1,0:T(8,128)(2,1)} %get-tuple-element.220.refs_0_), channel_id=1, source_target_pairs={{0,8},{4,20},{8,0},{12,28},{16,24},{20,4},{24,16},{28,12},{1,9},{5... | collective-permute-start | bytes 7077896 | tf_op jit(solution)/shard_map/ppermute | solution.py:207
  205.6 16.4 %collective-permute-start.26 = (bf16[4,192,768]{2,1,0:T(8,128)(2,1)S(1)}, bf16[4,192,768]{2,1,0:T(8,128)(2,1)}, u32[]{:S(2)}, u32[]{:S(2)}) collective-permute-start(bf16[4,192,768]{2,1,0:T(8,128)(2,1)S(1)} %fusion.2.refs_1_), channel_id=1, source_target_pairs={{0,16},{4,12},{8,24},{12,4},{16,0},{20,28},{24,8},{28,20},{1,17},{... | collective-permute-start | bytes 3538952 | tf_op jit(solution)/shard_map/ppermute | solution.py:207
  222.0 11.1 %collective-permute-start.27 = (f32[8,1280]{1,0:T(8,128)}, f32[8,1280]{1,0:T(8,128)}, u32[]{:S(2)}, u32[]{:S(2)}) collective-permute-start(f32[8,1280]{1,0:T(8,128)} %pad_maximum_fusion.2.refs_0_), channel_id=1, source_target_pairs={{0,1},{1,0},{2,3},{3,2},{4,5},{5,4},{6,7},{7,6},{8,9},{9,8},{10,11... | collective-permute-start | bytes 122888 | tf_op jit(solution)/shard_map/ppermute | solution.py:66
  225.1 36.2 %all-to-all-start.2 = ((bf16[4,192,768]{2,1,0:T(8,128)(2,1)}), bf16[4,192,768]{2,1,0:T(8,128)(2,1)S(1)}, u32[]{:S(2)}, u32[]{:S(2)}) async-start(bf16[4,192,768]{2,1,0:T(8,128)(2,1)} %fusion), calls=%async_computation.2 | async-start | bytes 2359296 | tf_op jit(solution)/shard_map/all_to_all | solution.py:223
  231.7 16.4 %collective-permute-start.29 = (bf16[2,4,96,768]{3,2,1,0:T(8,128)(2,1)S(1)}, bf16[2,4,96,768]{3,2,1,0:T(8,128)(2,1)}, u32[]{:S(2)}, u32[]{:S(2)}) collective-permute-start(bf16[2,4,96,768]{3,2,1,0:T(8,128)(2,1)S(1)} %get-tuple-element.223.refs_0_), channel_id=1, source_target_pairs={{0,8},{4,20},{8,0},{12,28},{16,24},{20,4},{24,16},{28,12},{1,9},{5... | collective-permute-start | bytes 3538952 | tf_op jit(solution)/shard_map/ppermute | solution.py:207
  261.3 21.4 %all-to-all-start.3 = ((bf16[4,96,768]{2,1,0:T(8,128)(2,1)}), bf16[4,96,768]{2,1,0:T(8,128)(2,1)S(1)}, u32[]{:S(2)}, u32[]{:S(2)}) async-start(bf16[4,96,768]{2,1,0:T(8,128)(2,1)} %fusion.3), calls=%async_computation.3 | async-start | bytes 1179648 | tf_op jit(solution)/shard_map/all_to_all | solution.py:223
  266.8 16.0 %collective-permute-start.34 = (bf16[192,768]{1,0:T(8,128)(2,1)S(1)}, bf16[192,768]{1,0:T(8,128)(2,1)S(1)}, u32[]{:S(2)}, u32[]{:S(2)}) collective-permute-start(bf16[192,768]{1,0:T(8,128)(2,1)S(1)} %fusion.6.refs_0_), channel_id=1, source_target_pairs={{0,8},{4,20},{8,0},{12,28},{16,24},{20,4},{24,16},{28,12},{1,9},{5... | collective-permute-start | bytes 884744 | tf_op jit(solution)/shard_map/ppermute | solution.py:207
  268.2 14.6 %collective-permute-start.35 = (bf16[192,768]{1,0:T(8,128)(2,1)S(1)}, bf16[192,768]{1,0:T(8,128)(2,1)S(1)}, u32[]{:S(2)}, u32[]{:S(2)}) collective-permute-start(bf16[192,768]{1,0:T(8,128)(2,1)S(1)} %fusion.6.refs_0_), channel_id=1, source_target_pairs={{0,16},{4,12},{8,24},{12,4},{16,0},{20,28},{24,8},{28,20},{1,17},{... | collective-permute-start | bytes 884744 | tf_op jit(solution)/shard_map/ppermute | solution.py:207
  269.1 13.7 %collective-permute-start.36 = (bf16[192,768]{1,0:T(8,128)(2,1)S(1)}, bf16[192,768]{1,0:T(8,128)(2,1)S(1)}, u32[]{:S(2)}, u32[]{:S(2)}) collective-permute-start(bf16[192,768]{1,0:T(8,128)(2,1)S(1)} %fusion.6.refs_0_), channel_id=1, source_target_pairs={{0,24},{4,28},{8,16},{12,20},{16,8},{20,12},{24,0},{28,4},{1,25},{... | collective-permute-start | bytes 884744 | tf_op jit(solution)/shard_map/ppermute | solution.py:66
  270.4 12.3 %collective-permute-start.33 = (f32[8,1280]{1,0:T(8,128)S(1)}, f32[8,1280]{1,0:T(8,128)S(1)}, u32[]{:S(2)}, u32[]{:S(2)}) collective-permute-start(f32[8,1280]{1,0:T(8,128)S(1)} %add.125.refs_0_), channel_id=1, source_target_pairs={{0,8},{4,12},{8,0},{12,4},{16,24},{20,28},{24,16},{28,20},{1,9},{5... | collective-permute-start | bytes 122888 | tf_op jit(solution)/shard_map/ppermute | solution.py:66
  286.4 12.3 %all-to-all-start.4 = ((bf16[4,96,768]{2,1,0:T(8,128)(2,1)}), bf16[4,96,768]{2,1,0:T(8,128)(2,1)S(1)}, u32[]{:S(2)}, u32[]{:S(2)}) async-start(bf16[4,96,768]{2,1,0:T(8,128)(2,1)} %broadcast_in_dim.38.refs_8_), calls=%async_computation.4 | async-start | bytes 1179648 | tf_op jit(solution)/shard_map/all_to_all | solution.py:223
  (70 other events, 584.4 us)
